TPU v7x, 512 devices: a whole 4x4x16 slice. The times are simulated.
512 devices in a mesh: fsdp: 32 (over x, y, z_hi), head: 16 (over z_lo, core).
Axes of the slice: x: 4, y: 4, z: 16 (z_hi: 2, z_lo: 8; z = z_hi * 8 + z_lo), core: 2. Of those that a mesh axis runs over, the one named last changes fastest.
Arguments:
- query_latent: bfloat16 [512, 1536], P('fsdp'), may hold values from -6 to 6
- query_rope: bfloat16 [512, 128, 64], P('fsdp', 'head')
- lengths: int32 [512], replicated, may hold values from 256 to 2048, as said below
- kv_cache: bfloat16 [16384, 576], P('fsdp')
- w_uq: bfloat16 [128, 1536, 128], P('head', 'fsdp'), may hold values from -0.15625 to 0.15625
- w_uk: bfloat16 [128, 512, 128], P('head', 'fsdp'), may hold values from -0.5 to 0.5
- w_uv: bfloat16 [128, 512, 128], P('head', 'fsdp'), may hold values from -0.25 to 0.25
- w_out: bfloat16 [128, 128, 7168], P('head', 'fsdp'), may hold values from -0.5 to 0.5
Outputs:
- attended: bfloat16 [512, 7168], P('fsdp', 'head')
Inputs may be any that keep to these rules, and one draw needn't show every extreme that they name: `lengths`: every sequence has a row that sees its whole cache and a row that sees only 256 tokens.
All inputs are finite; a program needn't handle non-finite values.
Results may differ from a plain program's by a relative error of at most 0.025.
Values may be sent and summed in bfloat16 or wider, within the bound.
No kernel may reach another device: no remote copies, remote signals or barrier semaphores. Data moves between devices by JAX's collectives and lax.ppermute only.
A program may use at most 64 MiB of HBM per device.

v0:
```python
import math

import jax
import jax.numpy as jnp
from jax import lax
from jax.sharding import PartitionSpec as P


def as_sent(x):
    return jax.tree.map(lambda a: a.astype(jnp.bfloat16) if a.dtype == jnp.float32 else a, x)


def from_partner(block, axis, stride):
    count = lax.axis_size(axis)
    route = []
    for low in range(count):
        high = low | 1 << stride
        if high != low and high < count:
            route += [(low, high), (high, low)]
    return lax.ppermute(block, axis, route)


def local(query_latent, query_rope, lengths, kv_cache, w_uq, w_uk, w_uv, w_out):
    heads_here = w_uq.shape[0]
    per_slot = heads_here // 4
    position = lax.axis_index("fsdp")
    slot_index = position % 4
    copies = lax.axis_size("fsdp") // 4
    gathered = (
        lax.all_gather(w_uq, "fsdp", axis=1, tiled=True),
        lax.all_gather(w_uk, "fsdp", axis=1, tiled=True),
        lax.all_gather(w_uv, "fsdp", axis=1, tiled=True),
    )
    up_query, up_key, up_value = [
        lax.dynamic_slice_in_dim(piece, slot_index * per_slot, per_slot, 0) for piece in gathered
    ]
    out_proj = lax.all_to_all(
        jnp.tile(w_out, (copies, 1, 1)), "fsdp", split_axis=0, concat_axis=1, tiled=True
    )
    query_absorb = jnp.einsum(
        "hqn,hcn->hqc", up_query, up_key, preferred_element_type=jnp.float32
    ).astype(jnp.bfloat16)
    pieces = (query_latent, query_rope, kv_cache)
    for bit_index in range(2):
        partner = jax.tree.map(
            lambda part, own: part.astype(own.dtype),
            from_partner(as_sent(pieces), "fsdp", bit_index),
            pieces,
        )
        is_upper = position >> bit_index & 1 == 1
        pieces = tuple(
            (
                jnp.where(
                    is_upper,
                    jnp.concatenate([theirs, ours], axis=0),
                    jnp.concatenate([ours, theirs], axis=0),
                )
                for ours, theirs in zip(pieces, partner)
            )
        )
    latent_rows, rope_rows, cache_all = pieces
    row_count = latent_rows.shape[0]
    latent_width = query_absorb.shape[2]
    rope_width = rope_rows.shape[2]
    temper = 1.0 / math.sqrt(up_query.shape[2] + rope_width)
    rope_mine = lax.dynamic_slice_in_dim(rope_rows, slot_index * per_slot, per_slot, 1)
    rope_mine = jnp.transpose(rope_mine, (1, 0, 2))
    sequence = position // 4
    row_lengths = lax.dynamic_slice_in_dim(lengths, sequence * row_count, row_count, 0)
    visible = jnp.arange(cache_all.shape[0])[None, :] < row_lengths[:, None]
    query_lat = jnp.einsum(
        "rq,hqc->hrc", latent_rows, query_absorb, preferred_element_type=jnp.float32
    ).astype(jnp.bfloat16)
    query_full = jnp.concatenate([query_lat, rope_mine], axis=2)
    scores = (
        jnp.einsum("hrk,tk->hrt", query_full, cache_all, preferred_element_type=jnp.float32)
        * temper
    )
    scores = jnp.where(visible[None], scores, -1e30)
    weights_soft = jax.nn.softmax(scores, axis=-1).astype(jnp.bfloat16)
    context = jnp.einsum(
        "hrt,tc->hrc", weights_soft, cache_all[:, :latent_width], preferred_element_type=jnp.float32
    ).astype(jnp.bfloat16)
    partial_value = jnp.zeros((row_count, out_proj.shape[2]), jnp.float32)
    for head_slot in range(per_slot):
        out_absorb = jnp.dot(
            up_value[head_slot], out_proj[head_slot], preferred_element_type=jnp.float32
        ).astype(jnp.bfloat16)
        partial_value = partial_value + jnp.dot(
            context[head_slot], out_absorb, preferred_element_type=jnp.float32
        )
    result = lax.psum_scatter(
        partial_value.astype(jnp.bfloat16), "head", scatter_dimension=1, tiled=True
    ).astype(jnp.float32)
    for bit_index in (1, 0):
        half_rows = result.shape[0] // 2
        is_upper = position >> bit_index & 1 == 1
        lower_rows = result[:half_rows]
        upper_rows = result[half_rows:]
        kept_rows = jnp.where(is_upper, upper_rows, lower_rows)
        sent_rows = jnp.where(is_upper, lower_rows, upper_rows)
        result = kept_rows + from_partner(sent_rows.astype(jnp.bfloat16), "fsdp", bit_index).astype(
            sent_rows.dtype
        )
    return result.astype(jnp.bfloat16)


def solution(mesh):
    placed = (
        P("fsdp", None),
        P("fsdp", "head", None),
        P(),
        P("fsdp", None),
        P("head", "fsdp", None),
        P("head", "fsdp", None),
        P("head", "fsdp", None),
        P("head", "fsdp", None),
    )
    return jax.shard_map(
        local, mesh=mesh, in_specs=placed, out_specs=P("fsdp", "head"), check_vma=False
    )
```

profile of v0, /device:TPU:6, one launch (start us, length us, event | category | flops | bytes accessed | tf_op | source)
XLA Modules:
  0.0 718.3 jit_solution(1958936080893513475)
XLA Ops:
  6.5 4.1 tile.4
  10.6 21.0 %all-to-all-start = ((bf16[64,4,7168]{2,1,0:T(4,128)(2,1)}), bf16[64,4,7168]{2,1,0:T(4,128)(2,1)}, u32[]{:S(2)}, u32[]{:S(2)}) async-start(bf16[64,4,7168]{2,1,0:T(4,128)(2,1)} %bitcast.47), calls=%async_computation | async-start | bytes 7340032 | tf_op jit(solution)/shard_map/all_to_all | solution.py:37
  31.7 0.0 all-gather.6.cloned.1.call-start
  31.7 0.7 all-gather.6.cloned.1.call-update
  32.4 0.0 all-gather.4.cloned.1.call-start
  32.5 0.7 all-gather.4.cloned.1.call-update
  33.2 0.0 all-gather.8.cloned.1.call-start
  33.2 12.1 %collective-permute-start.4 = (bf16[512,576]{0,1:T(8,128)(2,1)S(1)}, bf16[512,576]{0,1:T(8,128)(2,1)S(1)}, u32[]{:S(2)}, u32[]{:S(2)}) collective-permute-start(bf16[512,576]{0,1:T(8,128)(2,1)S(1)} %copy-done.3), channel_id=1, source_target_pairs={{0,16},{16,0},{32,48},{48,32},{64,80},{80,64},{96,112},{112,96},{1... | collective-permute-start | bytes 1769480 | tf_op jit(solution)/shard_map/ppermute | solution.py:20
  45.3 0.3 copy.20
  45.6 117.9 %collective-permute-done.4 = bf16[512,576]{0,1:T(8,128)(2,1)S(1)} collective-permute-done((bf16[512,576]{0,1:T(8,128)(2,1)S(1)}, bf16[512,576]{0,1:T(8,128)(2,1)S(1)}, u32[]{:S(2)}, u32[]{:S(2)}) %collective-permute-start.4) | collective-permute-done | bytes 589856 | tf_op jit(solution)/shard_map/ppermute | solution.py:20
  163.6 0.3 copy.19
  163.9 0.6 maximum_select_fusion.1
  164.4 0.6 copy.23
  165.1 15.0 %collective-permute-start.5 = (bf16[1024,576]{0,1:T(8,128)(2,1)S(1)}, bf16[1024,576]{0,1:T(8,128)(2,1)}, u32[]{:S(2)}, u32[]{:S(2)}) collective-permute-start(bf16[1024,576]{0,1:T(8,128)(2,1)S(1)} %copy.23), channel_id=1, source_target_pairs={{0,32},{32,0},{16,48},{48,16},{64,96},{96,64},{80,112},{112,80},{1... | collective-permute-start | bytes 3538952 | tf_op jit(solution)/shard_map/ppermute | solution.py:20
  180.1 1.9 collective-permute-start.2
  182.0 12.6 %collective-permute-start = (bf16[16,1536]{1,0:T(8,128)(2,1)S(1)}, bf16[16,1536]{1,0:T(8,128)(2,1)S(1)}, u32[]{:S(2)}, u32[]{:S(2)}) collective-permute-start(bf16[16,1536]{1,0:T(8,128)(2,1)S(1)} %copy-done.4), channel_id=1, source_target_pairs={{0,16},{16,0},{32,48},{48,32},{64,80},{80,64},{96,112},{112,96},{1... | collective-permute-start | bytes 147464 | tf_op jit(solution)/shard_map/ppermute | solution.py:20
  194.7 0.0 all-gather.8.cloned.1.call-update
  194.7 0.0 reduce-scatter.4.cloned.1.call-start
  194.8 0.8 dynamic_slice.15
  195.5 11.5 %collective-permute-done.2 = bf16[16,8,64]{2,0,1:T(8,128)(2,1)S(1)} collective-permute-done((bf16[16,8,64]{2,0,1:T(8,128)(2,1)S(1)}, bf16[16,8,64]{2,0,1:T(8,128)(2,1)S(1)}, u32[]{:S(2)}, u32[]{:S(2)}) %collective-permute-start.2) | collective-permute-done | bytes 16416 | tf_op jit(solution)/shard_map/ppermute | solution.py:20
  207.0 49.2 %collective-permute-start.3 = (bf16[32,8,64]{2,0,1:T(8,128)(2,1)S(1)}, bf16[32,8,64]{2,0,1:T(8,128)(2,1)S(1)}, u32[]{:S(2)}, u32[]{:S(2)}) collective-permute-start(bf16[32,8,64]{2,0,1:T(8,128)(2,1)S(1)} %maximum_select_fusion.4), channel_id=1, source_target_pairs={{0,32},{32,0},{16,48},{48,16},{64,96},{96,64},{80,112},{112,80},{1... | collective-permute-start | bytes 98312 | tf_op jit(solution)/shard_map/ppermute | solution.py:20
  256.2 0.1 iota_compare_fusion
  256.4 2.1 collective-permute-done.3
  258.5 4.1 collective-permute-start.1
  262.6 1.7 copy.24
  264.3 2.2 maximum_select_fusion
  266.6 53.8 %all-gather.6.cloned.1.call-done = bf16[8,512,128]{2,1,0:T(8,128)(2,1)} async-done(((bf16[8,16,128]{2,1,0:T(8,128)(2,1)}), bf16[8,512,128]{2,1,0:T(8,128)(2,1)}) %all-gather.6.cloned.1.call-update) | async-done | bytes 1048592 | tf_op jit(solution)/shard_map/all_gather | solution.py:31
  320.4 142.8 %all-gather.4.cloned.1.call-done = bf16[8,1536,128]{2,1,0:T(8,128)(2,1)} async-done(((bf16[8,48,128]{2,1,0:T(8,128)(2,1)}), bf16[8,1536,128]{2,1,0:T(8,128)(2,1)}) %all-gather.4.cloned.1.call-update) | async-done | bytes 3145744 | tf_op jit(solution)/shard_map/all_gather | solution.py:30
  463.1 2.7 fusion.17
  465.9 2.9 fusion.9
  468.8 1.0 copy-done.1
  469.8 0.3 fusion.48
  470.1 2.3 fusion.15
  472.4 4.6 fusion.47
  477.0 3.9 squeeze.20
  480.9 1.5 squeeze.23
  482.4 95.5 %all-gather.8.cloned.1.call-done = bf16[8,512,128]{2,1,0:T(8,128)(2,1)} async-done(((bf16[8,16,128]{2,1,0:T(8,128)(2,1)}), bf16[8,512,128]{2,1,0:T(8,128)(2,1)}) %all-gather.8.cloned.1.call-update) | async-done | bytes 1048592 | tf_op jit(solution)/shard_map/all_gather | solution.py:32
  577.9 6.1 fusion.2
  584.0 4.9 fusion.1
  588.9 1.7 copy.29
  590.6 0.0 reduce-scatter.4.cloned.1.call-update
  590.6 99.3 %reduce-scatter.4.cloned.1.call-done = bf16[448,64]{1,0:T(8,128)(2,1)} async-done(((bf16[7168,64]{1,0:T(8,128)(2,1)}), bf16[448,64]{1,0:T(8,128)(2,1)}) %reduce-scatter.4.cloned.1.call-update) | async-done | bytes 57360
  689.9 1.0 copy.30
  690.9 3.4 collective-permute-start.6
  694.3 2.4 collective-permute-done.6
  696.8 5.0 collective-permute-start.7
  701.8 9.3 %collective-permute-done.7 = bf16[16,448]{1,0:T(8,128)(2,1)S(1)} collective-permute-done((bf16[16,448]{1,0:T(8,128)(2,1)S(1)}, bf16[16,448]{1,0:T(8,128)(2,1)S(1)}, u32[]{:S(2)}, u32[]{:S(2)}) %collective-permute-start.7) | collective-permute-done | bytes 14368 | tf_op jit(solution)/shard_map/ppermute | solution.py:20
  711.1 0.6 add_convert_fusion
  (23 shorter events, 0.1 us)
Async XLA Ops:
  10.6 22.6 %copy-start.3 = (bf16[512,576]{0,1:T(8,128)(2,1)S(1)}, bf16[512,576]{0,1:T(8,128)(2,1)}, u32[]{:S(2)}) copy-start(bf16[512,576]{0,1:T(8,128)(2,1)} %param.11) | copy-start | bytes 1769476
  10.6 461.7 %all-to-all-start = ((bf16[64,4,7168]{2,1,0:T(4,128)(2,1)}), bf16[64,4,7168]{2,1,0:T(4,128)(2,1)}, u32[]{:S(2)}, u32[]{:S(2)}) async-start(bf16[64,4,7168]{2,1,0:T(4,128)(2,1)} %bitcast.47), calls=%async_computation | async-start | bytes 7340032 | tf_op jit(solution)/shard_map/all_to_all | solution.py:37
  31.7 288.7 %all-gather.6.cloned.1.call-start = ((), (), s32[]{:S(2)}) async-start(), calls=%async_computation.3 | async-start | bytes 1081344 | tf_op jit(solution)/shard_map/all_gather | solution.py:31
  32.4 430.7 %all-gather.4.cloned.1.call-start = ((), (), s32[]{:S(2)}) async-start(), calls=%async_computation.2 | async-start | bytes 3244032 | tf_op jit(solution)/shard_map/all_gather | solution.py:30
  33.2 544.7 %all-gather.8.cloned.1.call-start = ((), (), s32[]{:S(2)}) async-start(), calls=%async_computation.4 | async-start | bytes 1081344 | tf_op jit(solution)/shard_map/all_gather | solution.py:32
  33.2 130.3 %collective-permute-start.4 = (bf16[512,576]{0,1:T(8,128)(2,1)S(1)}, bf16[512,576]{0,1:T(8,128)(2,1)S(1)}, u32[]{:S(2)}, u32[]{:S(2)}) collective-permute-start(bf16[512,576]{0,1:T(8,128)(2,1)S(1)} %copy-done.3), channel_id=1, source_target_pairs={{0,16},{16,0},{32,48},{48,32},{64,80},{80,64},{96,112},{112,96},{1... | collective-permute-start | bytes 1769480 | tf_op jit(solution)/shard_map/ppermute | solution.py:20
  163.9 16.2 %copy-start.5 = (bf16[16,8,64]{2,1,0:T(8,128)(2,1)S(1)}, bf16[16,8,64]{2,1,0:T(8,128)(2,1)}, u32[]{:S(2)}) copy-start(bf16[16,8,64]{2,1,0:T(8,128)(2,1)} %param.9) | copy-start | bytes 49156
  163.9 18.1 %copy-start.4 = (bf16[16,1536]{1,0:T(8,128)(2,1)S(1)}, bf16[16,1536]{1,0:T(8,128)(2,1)}, u32[]{:S(2)}) copy-start(bf16[16,1536]{1,0:T(8,128)(2,1)} %param.8) | copy-start | bytes 147460
  165.1 97.5 %collective-permute-start.5 = (bf16[1024,576]{0,1:T(8,128)(2,1)S(1)}, bf16[1024,576]{0,1:T(8,128)(2,1)}, u32[]{:S(2)}, u32[]{:S(2)}) collective-permute-start(bf16[1024,576]{0,1:T(8,128)(2,1)S(1)} %copy.23), channel_id=1, source_target_pairs={{0,32},{32,0},{16,48},{48,16},{64,96},{96,64},{80,112},{112,80},{1... | collective-permute-start | bytes 3538952 | tf_op jit(solution)/shard_map/ppermute | solution.py:20
  180.1 26.9 %collective-permute-start.2 = (bf16[16,8,64]{2,0,1:T(8,128)(2,1)S(1)}, bf16[16,8,64]{2,0,1:T(8,128)(2,1)S(1)}, u32[]{:S(2)}, u32[]{:S(2)}) collective-permute-start(bf16[16,8,64]{2,0,1:T(8,128)(2,1)S(1)} %copy.16), channel_id=1, source_target_pairs={{0,16},{16,0},{32,48},{48,32},{64,80},{80,64},{96,112},{112,96},{1... | collective-permute-start | bytes 49160 | tf_op jit(solution)/shard_map/ppermute | solution.py:20
  182.0 76.4 %collective-permute-start = (bf16[16,1536]{1,0:T(8,128)(2,1)S(1)}, bf16[16,1536]{1,0:T(8,128)(2,1)S(1)}, u32[]{:S(2)}, u32[]{:S(2)}) collective-permute-start(bf16[16,1536]{1,0:T(8,128)(2,1)S(1)} %copy-done.4), channel_id=1, source_target_pairs={{0,16},{16,0},{32,48},{48,32},{64,80},{80,64},{96,112},{112,96},{1... | collective-permute-start | bytes 147464 | tf_op jit(solution)/shard_map/ppermute | solution.py:20
  194.7 495.2 %reduce-scatter.4.cloned.1.call-start = ((), (), s32[]{:S(2)}) async-start(), calls=%async_computation.5 | async-start | bytes 1949696
  207.0 51.4 %collective-permute-start.3 = (bf16[32,8,64]{2,0,1:T(8,128)(2,1)S(1)}, bf16[32,8,64]{2,0,1:T(8,128)(2,1)S(1)}, u32[]{:S(2)}, u32[]{:S(2)}) collective-permute-start(bf16[32,8,64]{2,0,1:T(8,128)(2,1)S(1)} %maximum_select_fusion.4), channel_id=1, source_target_pairs={{0,32},{32,0},{16,48},{48,16},{64,96},{96,64},{80,112},{112,80},{1... | collective-permute-start | bytes 98312 | tf_op jit(solution)/shard_map/ppermute | solution.py:20
  258.5 8.1 %collective-permute-start.1 = (bf16[32,1536]{1,0:T(8,128)(2,1)S(1)}, bf16[32,1536]{1,0:T(8,128)(2,1)S(1)}, u32[]{:S(2)}, u32[]{:S(2)}) collective-permute-start(bf16[32,1536]{1,0:T(8,128)(2,1)S(1)} %maximum_select_fusion.3), channel_id=1, source_target_pairs={{0,32},{32,0},{16,48},{48,16},{64,96},{96,64},{80,112},{112,80},{1... | collective-permute-start | bytes 294920 | tf_op jit(solution)/shard_map/ppermute | solution.py:20
  465.8 4.3 copy-start
  468.8 1.0 copy-start.1
  482.4 101.6 %copy-start.2 = (bf16[128,7168]{1,0:T(8,128)(2,1)S(1)}, bf16[128,7168]{1,0:T(8,128)(2,1)}, u32[]{:S(2)}) copy-start(bf16[128,7168]{1,0:T(8,128)(2,1)} %squeeze.23) | copy-start | bytes 5505028
  690.9 5.8 collective-permute-start.6
  696.8 14.3 %collective-permute-start.7 = (bf16[16,448]{1,0:T(8,128)(2,1)S(1)}, bf16[16,448]{1,0:T(8,128)(2,1)S(1)}, u32[]{:S(2)}, u32[]{:S(2)}) collective-permute-start(bf16[16,448]{1,0:T(8,128)(2,1)S(1)} %select_convert_fusion.1), channel_id=1, source_target_pairs={{0,16},{16,0},{32,48},{48,32},{64,80},{80,64},{96,112},{112,96},{1... | collective-permute-start | bytes 43016 | tf_op jit(solution)/shard_map/ppermute | solution.py:20
Sparse Core Ops, SparseCore 0:
  36.6 283.7 all-gather.5
  324.5 138.6 all-gather.3
  467.3 110.6 all-gather.7
  590.8 99.1 reduce-scatter.3
where the time goes:
time: 719 us; the launch traced here: 718 us
  waiting for transfers between devices  536 us (75%)
  starting transfers between devices  124 us (17%)
  local copies, waits for them, and re-layouts  21.5 us (3%)
  matrix products  18.8 us (3%)
  between operations  13.5 us (2%)
    ppermute x8, waiting for transfers between devices, from_partner(): return lax.ppermute(block, axis, route)  143 us
    all_gather x1, waiting for transfers between devices, local(): lax.all_gather(w_uq, 'fsdp', axis=1, tiled=True)  143 us
    ppermute x8, starting transfers between devices, from_partner(): return lax.ppermute(block, axis, route)  103 us
    unnamed x5, waiting for transfers between devices  101 us
    all_gather x1, waiting for transfers between devices, local(): lax.all_gather(w_uv, 'fsdp', axis=1, tiled=True)  95.5 us
    all_gather x1, waiting for transfers between devices, local(): lax.all_gather(w_uk, 'fsdp', axis=1, tiled=True)  53.8 us
    all_to_all x1, starting transfers between devices, local(): lax.all_to_all(jnp.tile(w_out, (copies, 1, 1)), 'fsdp', split_axis=0, con...  21 us
  transfers between devices with their start and end apart: 13, of which 9 were waited for; matrix products, arithmetic and copies ran while one was open for 3% of the time, Pallas kernels for 0%

commit v1 on v0

v1 whole, which is shorter than its diff:
```python
import math

import jax
import jax.numpy as jnp
from jax import lax
from jax.experimental import pallas as pl
from jax.experimental.pallas import tpu as pltpu
from jax.sharding import Mesh, PartitionSpec as P

AXES = ("x", "yh", "yl", "zh", "zlh", "zll", "c")
SIZES = (4, 2, 2, 2, 4, 2, 2)
FSDP = ("x", "yh", "yl", "zh")
HEAD = ("zlh", "zll", "c")
PLANE = ("x", "yh", "yl")
COLUMN = ("zlh", "zll", "zh")
BF16 = jnp.bfloat16
F32 = jnp.float32
VMEM_LIMIT = 40 * 1024 * 1024


def swap(block, axis):
    return lax.ppermute(block, axis, [(0, 1), (1, 0)])


def pair(block, axis):
    theirs = swap(block, axis)
    upper = lax.axis_index(axis) == 1
    return jnp.where(
        upper,
        jnp.concatenate([theirs, block], axis=0),
        jnp.concatenate([block, theirs], axis=0),
    )


def exchange(blocks, axes):
    return lax.all_to_all(blocks, axes, 0, 0, tiled=True)


def dot(a, b):
    return jnp.dot(a, b, preferred_element_type=F32)


def dot_nt(a, b):
    return lax.dot_general(a, b, (((1,), (1,)), ((), ())), preferred_element_type=F32)


def attend_kernel(
    starts, latent, weights, rope, lengths, kv0, kv1, kv2, kv3, value_out, scores, *, sizes, temper
):
    rows, heads, n_uq, n_uk, n_uv, width = sizes
    caches = (kv0, kv1, kv2, kv3)
    per_block = kv0.shape[0]
    chunk = per_block * len(caches) // starts.shape[0]
    query = latent[...]
    limit = lengths[...]
    lanes = lax.broadcasted_iota(jnp.int32, (rows, chunk), 1)
    for h in range(heads):
        w_uq = weights[:, h, :, 0:n_uq, :].reshape(-1, weights.shape[-1])
        w_uk = weights[:, h, :, n_uq : n_uq + n_uk, :].reshape(-1, weights.shape[-1])
        q_nope = dot(query, w_uq).astype(BF16)
        q_lat = dot_nt(q_nope, w_uk).astype(BF16)
        rope_width = kv0.shape[1] - width
        q_rope = rope[:, h * rope_width : (h + 1) * rope_width]
        top = jnp.full((rows, 1), -1e30, F32)
        for b, cache in enumerate(caches):
            s = dot_nt(q_lat, cache[:, :width]) + dot_nt(q_rope, cache[:, width:])
            s = s * temper
            for i in range(per_block // chunk):
                k = b * (per_block // chunk) + i
                piece = s[:, i * chunk : (i + 1) * chunk]
                piece = jnp.where(lanes + starts[k] < limit, piece, -1e30)
                top = jnp.maximum(top, jnp.max(piece, axis=1, keepdims=True))
                scores[:, k * chunk : (k + 1) * chunk] = piece
        total = jnp.zeros((rows, 1), F32)
        context = jnp.zeros((rows, width), F32)
        for b, cache in enumerate(caches):
            p = jnp.exp(scores[:, b * per_block : (b + 1) * per_block] - top)
            total = total + jnp.sum(p, axis=1, keepdims=True)
            context = context + dot(p.astype(BF16), cache[:, :width])
        context = (context / total).astype(BF16)
        w_uv = weights[:, h, :, n_uq + n_uk :, :].reshape(-1, weights.shape[-1])
        vdim = w_uv.shape[1]
        value_out[:, h * vdim : (h + 1) * vdim] = dot(context, w_uv).astype(BF16)


def project_kernel(values, weights, out):
    total = None
    half = values.shape[3]
    for y in range(values.shape[1]):
        rows = values[:, y].reshape(-1, half)
        part = dot(rows, weights[y * half : (y + 1) * half, :])
        total = part if total is None else total + part
    out[...] = total.astype(BF16)


def local(query_latent, query_rope, lengths, kv_cache, w_uq, w_uk, w_uv, w_out):
    yl, zh, zll, core = (lax.axis_index(a) for a in ("yl", "zh", "zll", "c"))
    plane = 16
    tokens, kv_width = kv_cache.shape
    latent_width = w_uk.shape[1] * 32
    rope_width = kv_width - latent_width
    temper = 1.0 / math.sqrt(w_uq.shape[2] + rope_width)
    n_uq, n_uk, n_uv = w_uq.shape[1], w_uk.shape[1], w_uv.shape[1]

    stacked = jnp.concatenate([w_uq, w_uk, w_uv], axis=1)
    stacked = lax.all_to_all(stacked, "zh", 0, 1, tiled=True)
    quarter = tokens // 4
    piece = lax.dynamic_slice_in_dim(kv_cache, (core * 2 + zll) * quarter, quarter, 0)
    piece = swap(piece, "zh")
    near = swap(kv_cache, "yl")
    latent_rows = pair(query_latent, "zh")
    rope_rows = query_rope.reshape(query_rope.shape[0], -1)
    rope_rows = lax.all_to_all(rope_rows, "zh", 1, 0, tiled=True)

    heads = stacked.shape[0] // 2
    weights = jnp.broadcast_to(
        stacked.reshape((1, 2, heads) + stacked.shape[1:]),
        (plane // 2, 2, heads) + stacked.shape[1:],
    ).reshape((plane * heads,) + stacked.shape[1:])
    weights = exchange(weights, PLANE).reshape(plane, heads, 2, n_uq + n_uk + n_uv, -1)

    latent_rows = pair(latent_rows, "yl")
    rope_rows = lax.all_to_all(rope_rows, "yl", 1, 0, tiled=True)

    piece = jnp.concatenate([piece, swap(piece, "yl")], axis=0)
    piece = jnp.concatenate([piece, swap(piece, "zll")], axis=0)
    far = swap(piece, "c")
    starts = []
    for ylo in (yl, 1 - yl):
        for i in range(4):
            starts.append((ylo * 2 + zh) * tokens + i * quarter)
    for co in (core, 1 - core):
        for zo in (zll, 1 - zll):
            for ylo in (yl, 1 - yl):
                starts.append((ylo * 2 + 1 - zh) * tokens + (co * 2 + zo) * quarter)
    starts = jnp.stack(starts).astype(jnp.int32)

    rows = latent_rows.shape[0]
    sequence = lax.axis_index("x") * 2 + lax.axis_index("yh")
    row_lengths = lax.dynamic_slice_in_dim(lengths, sequence * rows, rows, 0)[:, None]
    vdim = w_uv.shape[2]
    vmem = pl.BlockSpec(memory_space=pltpu.VMEM)
    values = pl.pallas_call(
        lambda *refs: attend_kernel(
            *refs, sizes=(rows, heads, n_uq, n_uk, n_uv, latent_width), temper=temper
        ),
        out_shape=jax.ShapeDtypeStruct((rows, heads * vdim), BF16),
        in_specs=[pl.BlockSpec(memory_space=pltpu.SMEM)] + [vmem] * 8,
        out_specs=vmem,
        scratch_shapes=[pltpu.VMEM((rows, 4 * tokens), F32)],
        compiler_params=pltpu.CompilerParams(vmem_limit_bytes=VMEM_LIMIT),
        cost_estimate=pl.CostEstimate(flops=10**9, bytes_accessed=5 * 10**6, transcendentals=0),
        name="attend",
    )(starts, latent_rows, weights, rope_rows, row_lengths, kv_cache, near, piece, far)

    w_out, _ = lax.optimization_barrier((w_out, stacked))
    out_proj = lax.all_to_all(w_out, "zh", 0, 1, tiled=True)
    four, vpart, width = out_proj.shape
    columns = width // plane
    out_proj = out_proj.reshape(four, vpart, plane, columns)
    out_proj = exchange(jnp.transpose(out_proj, (2, 0, 1, 3)), PLANE)
    out_proj = jnp.transpose(out_proj, (1, 0, 2, 3)).reshape(four * plane * vpart, columns)

    gathered = exchange(
        jnp.broadcast_to(values[None], (plane,) + values.shape).reshape(-1, values.shape[1]), PLANE
    ).reshape(plane // 2, 2, rows, heads * vdim)
    all_rows = plane // 2 * rows
    partial_out = pl.pallas_call(
        project_kernel,
        out_shape=jax.ShapeDtypeStruct((all_rows, columns), BF16),
        in_specs=[vmem, vmem],
        out_specs=vmem,
        compiler_params=pltpu.CompilerParams(vmem_limit_bytes=VMEM_LIMIT),
        cost_estimate=pl.CostEstimate(flops=2 * 10**8, bytes_accessed=2 * 10**6, transcendentals=0),
        name="project",
    )(gathered, out_proj)

    total = exchange(partial_out, "c").reshape(2, all_rows // 2, columns)
    total = jnp.sum(total.astype(F32), axis=0).astype(BF16)
    total = exchange(total, COLUMN).reshape(16, all_rows // 32, columns)
    total = jnp.sum(total.astype(F32), axis=0).astype(BF16)
    route = []
    for xy in range(16):
        for z_hi in range(2):
            for z_lo in range(8):
                for c in range(2):
                    source = ((xy * 2 + z_hi) * 8 + z_lo) * 2 + c
                    route.append((source, (c * 16 + z_lo * 2 + z_hi) * 16 + xy))
    return lax.ppermute(total, AXES, route)


def solution(mesh):
    fine = Mesh(mesh.devices.reshape(SIZES), AXES)
    placed = (
        P(FSDP, None),
        P(FSDP, HEAD, None),
        P(),
        P(FSDP, None),
        P(HEAD, FSDP, None),
        P(HEAD, FSDP, None),
        P(HEAD, FSDP, None),
        P(HEAD, FSDP, None),
    )
    return jax.shard_map(
        local, mesh=fine, in_specs=placed, out_specs=P(FSDP, HEAD), check_vma=False
    )
```

time: 719 us -> 230 us (0.32)
  waiting for transfers between devices: 536 us -> 81 us
  starting transfers between devices: 124 us -> 60 us
  blocking collectives: 0 us -> 60.9 us
  matrix products: 18.8 us -> 0 us
  between operations: 13.5 us -> 0.31 us
    all_gather x3 -> x0, waiting for transfers between devices: 292 us -> none  [the longest x1 143 us: local(): lax.all_gather(w_uq, 'fsdp', axis=1, tiled=True)]
    ppermute x8, waiting for transfers between devices: 143 us -> 37.1 us  [the longest x7 31.3 us: swap(): return lax.ppermute(block, axis, [(0, 1), (1, 0)])]
    unnamed x5 -> x0, waiting for transfers between devices: 101 us -> none
    ppermute x8, starting transfers between devices: 103 us -> 26.4 us  [the longest x7 20.9 us: swap(): return lax.ppermute(block, axis, [(0, 1), (1, 0)])]
    all_to_all x0 -> x3, blocking collectives: none -> 60.9 us  [the longest x2 33.5 us: exchange(): return lax.all_to_all(blocks, axes, 0, 0, tiled=True)]
    all_to_all x1 -> x6, waiting for transfers between devices: 0.01 us -> 43.9 us  [the longest x1 21.3 us: local(): out_proj = lax.all_to_all(w_out, 'zh', 0, 1, tiled=True)]
    dot_general x5 -> x0, matrix products: 18.8 us -> none  [the longest x2 11 us: local(): jnp.dot(context[head_slot], out_absorb, preferred_element_type=jnp.float32)]
    all_to_all x1 -> x6, starting transfers between devices: 21 us -> 33.6 us  [the longest x3 23.5 us: exchange(): return lax.all_to_all(blocks, axes, 0, 0, tiled=True)]
  transfers between devices with their start and end apart: 13 -> 14, of which waited for: 9 -> 8; matrix products, arithmetic and copies ran while one was open for 3% -> 6% of each run, Pallas kernels for 0% -> 2%
where the time goes in v1:
time: 230 us; the launch traced here: 226 us
  waiting for transfers between devices  81 us (35%)
  blocking collectives  60.9 us (26%)
  starting transfers between devices  60 us (26%)
  local copies, waits for them, and re-layouts  17.5 us (8%)
  Pallas kernels  4.49 us (2%)
    all_to_all x2, blocking collectives, exchange(): return lax.all_to_all(blocks, axes, 0, 0, tiled=True)  33.5 us
    ppermute x7, waiting for transfers between devices, swap(): return lax.ppermute(block, axis, [(0, 1), (1, 0)])  31.3 us
    all_to_all x1, blocking collectives, local(): rope_rows = lax.all_to_all(rope_rows, 'zh', 1, 0, tiled=True)  27.5 us
    all_to_all x3, starting transfers between devices, exchange(): return lax.all_to_all(blocks, axes, 0, 0, tiled=True)  23.5 us
    all_to_all x1, waiting for transfers between devices, local(): out_proj = lax.all_to_all(w_out, 'zh', 0, 1, tiled=True)  21.3 us
    ppermute x7, starting transfers between devices, swap(): return lax.ppermute(block, axis, [(0, 1), (1, 0)])  20.9 us
    all_to_all x1, waiting for transfers between devices, local(): stacked = lax.all_to_all(stacked, 'zh', 0, 1, tiled=True)  13.3 us
    all_to_all x3, waiting for transfers between devices, exchange(): return lax.all_to_all(blocks, axes, 0, 0, tiled=True)  6.98 us
  transfers between devices with their start and end apart: 14, of which 8 were waited for; matrix products, arithmetic and copies ran while one was open for 6% of the time, Pallas kernels for 2%

profile of v1, /device:TPU:6, one launch (start us, length us, event | category | flops | bytes accessed | tf_op | source)
XLA Modules:
  0.0 226.1 jit_solution(4620192940433650291)
XLA Ops:
  0.0 0.9 all_to_all.74
  0.9 27.5 %all_to_all.99 = bf16[16,2,256]{2,0,1:T(8,128)(2,1)S(1)} all-to-all(bf16[16,2,256]{2,0,1:T(8,128)(2,1)S(1)} %copy.57), channel_id=1, replica_groups=mesh['x'=4,'yh'=2,'yl'=2,'zh'=2,'zlh'=4,'zll'=2,'c'=2] {'zh'}, dimensions={1} | all-to-all | bytes 32768 | tf_op jit(solution)/shard_map/all_to_all | solution.py:113
  28.3 0.6 copy.58
  29.0 3.2 %all-to-all-start.3 = ((bf16[32,2,128]{2,0,1:T(8,128)(2,1)}), bf16[32,2,128]{2,0,1:T(8,128)(2,1)S(1)}, u32[]{:S(2)}, u32[]{:S(2)}) async-start(bf16[32,2,128]{2,0,1:T(8,128)(2,1)} %copy.58), calls=%async_computation.3 | async-start | bytes 32768 | tf_op jit(solution)/shard_map/all_to_all | solution.py:123
  32.2 1.6 pad_maximum_fusion.1
  33.8 2.2 all-to-all-done.3
  36.0 3.4 %all-to-all-start = ((bf16[8,80,128]{2,1,0:T(8,128)(2,1)}), bf16[8,80,128]{2,1,0:T(8,128)(2,1)S(1)}, u32[]{:S(2)}, u32[]{:S(2)}) async-start(bf16[8,80,128]{2,1,0:T(8,128)(2,1)} %pad_maximum_fusion.1), calls=%async_computation | async-start | bytes 327680 | tf_op jit(solution)/shard_map/all_to_all | solution.py:106
  39.5 13.3 %all-to-all-done = bf16[8,80,128]{2,1,0:T(8,128)(2,1)S(1)} async-done(((bf16[8,80,128]{2,1,0:T(8,128)(2,1)}), bf16[8,80,128]{2,1,0:T(8,128)(2,1)S(1)}, u32[]{:S(2)}, u32[]{:S(2)}) %all-to-all-start) | async-done | bytes 163872 | tf_op jit(solution)/shard_map/all_to_all | solution.py:106
  52.8 3.5 %all-to-all-start.5 = ((bf16[8,4,7168]{2,1,0:T(4,128)(2,1)}), bf16[8,4,7168]{2,1,0:T(4,128)(2,1)S(1)}, u32[]{:S(2)}, u32[]{:S(2)}) async-start(bf16[8,4,7168]{2,1,0:T(4,128)(2,1)} %param.15), calls=%async_computation.5 | async-start | bytes 917504 | tf_op jit(solution)/shard_map/all_to_all | solution.py:157
  56.3 21.3 %all-to-all-done.5 = bf16[8,4,7168]{2,1,0:T(4,128)(2,1)S(1)} async-done(((bf16[8,4,7168]{2,1,0:T(4,128)(2,1)}), bf16[8,4,7168]{2,1,0:T(4,128)(2,1)S(1)}, u32[]{:S(2)}, u32[]{:S(2)}) %all-to-all-start.5) | async-done | bytes 458784 | tf_op jit(solution)/shard_map/all_to_all | solution.py:157
  77.6 1.3 broadcast_in_dim.17
  79.0 8.7 %all-to-all-start.1 = ((bf16[32,160,128]{2,1,0:T(8,128)(2,1)}), bf16[32,160,128]{2,1,0:T(8,128)(2,1)S(1)}, u32[]{:S(2)}, u32[]{:S(2)}) async-start(bf16[32,160,128]{2,1,0:T(8,128)(2,1)} %bitcast.19), calls=%async_computation.1 | async-start | bytes 2621440 | tf_op jit(solution)/shard_map/all_to_all | solution.py:36
  87.7 1.4 copy.62.refs_5_
  89.1 1.9 collective-permute-start.3
  91.1 18.5 %collective-permute-done.3 = bf16[128,576]{1,0:T(8,128)(2,1)S(1)} collective-permute-done((bf16[128,576]{1,0:T(8,128)(2,1)S(1)}, bf16[128,576]{1,0:T(8,128)(2,1)S(1)}, u32[]{:S(2)}, u32[]{:S(2)}) %collective-permute-start.3) | collective-permute-done | bytes 147488 | tf_op jit(solution)/shard_map/ppermute | solution.py:22
  109.6 3.4 %collective-permute-start.4 = (bf16[128,576]{1,0:T(8,128)(2,1)S(1)}, bf16[128,576]{1,0:T(8,128)(2,1)S(1)}, u32[]{:S(2)}, u32[]{:S(2)}) collective-permute-start(bf16[128,576]{1,0:T(8,128)(2,1)S(1)} %collective-permute-done.3), channel_id=1, source_target_pairs={{0,32},{32,0},{1,33},{33,1},{2,34},{34,2},{3,35},{35,3},{4,36},{36... | collective-permute-start | bytes 442376 | tf_op jit(solution)/shard_map/ppermute | solution.py:22
  113.0 3.8 %collective-permute-done.4 = bf16[128,576]{1,0:T(8,128)(2,1)S(1)} collective-permute-done((bf16[128,576]{1,0:T(8,128)(2,1)S(1)}, bf16[128,576]{1,0:T(8,128)(2,1)S(1)}, u32[]{:S(2)}, u32[]{:S(2)}) %collective-permute-start.4) | collective-permute-done | bytes 147488 | tf_op jit(solution)/shard_map/ppermute | solution.py:22
  116.8 4.8 %collective-permute-start.5 = (bf16[256,576]{1,0:T(8,128)(2,1)S(1)}, bf16[256,576]{1,0:T(8,128)(2,1)S(1)}, u32[]{:S(2)}, u32[]{:S(2)}) collective-permute-start(bf16[256,576]{1,0:T(8,128)(2,1)S(1)} %pad_maximum_fusion), channel_id=1, source_target_pairs={{0,2},{2,0},{1,3},{3,1},{4,6},{6,4},{5,7},{7,5},{8,10},{10,8},{9,1... | collective-permute-start | bytes 884744 | tf_op jit(solution)/shard_map/ppermute | solution.py:22
  121.6 3.6 %collective-permute-start.2 = (bf16[512,576]{0,1:T(8,128)(2,1)}, bf16[512,576]{0,1:T(8,128)(2,1)}, u32[]{:S(2)}, u32[]{:S(2)}) collective-permute-start(bf16[512,576]{0,1:T(8,128)(2,1)} %param.11), channel_id=1, source_target_pairs={{0,32},{32,0},{1,33},{33,1},{2,34},{34,2},{3,35},{35,3},{4,36},{36... | collective-permute-start | bytes 1769480 | tf_op jit(solution)/shard_map/ppermute | solution.py:22
  125.2 3.0 %collective-permute-start = (bf16[16,1536]{1,0:T(8,128)(2,1)S(1)}, bf16[16,1536]{1,0:T(8,128)(2,1)S(1)}, u32[]{:S(2)}, u32[]{:S(2)}) collective-permute-start(bf16[16,1536]{1,0:T(8,128)(2,1)S(1)} %copy-done.4), channel_id=1, source_target_pairs={{0,16},{16,0},{1,17},{17,1},{2,18},{18,2},{3,19},{19,3},{4,20},{20... | collective-permute-start | bytes 147464 | tf_op jit(solution)/shard_map/ppermute | solution.py:22
  128.3 1.1 copy.60
  129.4 1.9 collective-permute-start.6
  131.4 9.0 %collective-permute-done = bf16[16,1536]{1,0:T(8,128)(2,1)S(1)} collective-permute-done((bf16[16,1536]{1,0:T(8,128)(2,1)S(1)}, bf16[16,1536]{1,0:T(8,128)(2,1)S(1)}, u32[]{:S(2)}, u32[]{:S(2)}) %collective-permute-start) | collective-permute-done | bytes 49184 | tf_op jit(solution)/shard_map/ppermute | solution.py:22
  140.4 2.3 %collective-permute-start.1 = (bf16[32,1536]{1,0:T(8,128)(2,1)S(1)}, bf16[32,1536]{1,0:T(8,128)(2,1)S(1)}, u32[]{:S(2)}, u32[]{:S(2)}) collective-permute-start(bf16[32,1536]{1,0:T(8,128)(2,1)S(1)} %maximum_select_fusion.1), channel_id=1, source_target_pairs={{0,32},{32,0},{1,33},{33,1},{2,34},{34,2},{3,35},{35,3},{4,36},{36... | collective-permute-start | bytes 294920 | tf_op jit(solution)/shard_map/ppermute | solution.py:22
  142.7 1.0 copy.71
  143.7 1.6 reshape.45
  145.2 1.1 copy.66
  146.4 7.5 %all-to-all-start.6 = ((bf16[16,4,8,448]{3,2,1,0:T(8,128)(2,1)}), bf16[16,4,8,448]{3,2,1,0:T(8,128)(2,1)}, u32[]{:S(2)}, u32[]{:S(2)}) async-start(bf16[16,4,8,448]{3,2,1,0:T(8,128)(2,1)} %copy.66), calls=%async_computation.6 | async-start | bytes 1048576 | tf_op jit(solution)/shard_map/all_to_all | solution.py:36
  153.9 0.1 copy.61.refs_4_
  154.0 0.1 stack.67.refs_0_
  154.2 1.4 copy.63.refs_6_
  155.6 2.2 copy.64.refs_8_
  157.7 1.1 copy-done.1
  158.8 0.7 copy-done.3
  159.5 4.1 %attend.1 = bf16[64,256]{1,0:T(8,128)(2,1)S(1)} custom-call(s32[16]{0:T(128)S(1)} %stack.67.refs_0_, bf16[64,1536]{1,0:T(8,128)(2,1)S(1)} %maximum_select_fusion.refs_1_, bf16[16,2,2,80,128]{4,3,2,1,0:T(8,128)(2,1)S(1)} %bitcast.38, bf16[64,128]{1,0:T(8,128)(2,1)S(1)} %bitcast.42, s32[64,1]{1,0:T(8,128)S(1)} %copy.61.refs_4_, ...), custom_call_target="tpu_custom_call" | custom-call | flops 1000000000 | bytes 5000000 | tf_op jit(solution)/shard_map/attend/pallas_call | solution.py:143
  163.6 0.9 broadcast_in_dim.19
  164.5 7.2 %all-to-all-start.4 = ((bf16[16,64,256]{2,1,0:T(8,128)(2,1)}), bf16[16,64,256]{2,1,0:T(8,128)(2,1)S(1)}, u32[]{:S(2)}, u32[]{:S(2)}) async-start(bf16[16,64,256]{2,1,0:T(8,128)(2,1)} %broadcast_in_dim.19), calls=%async_computation.4 | async-start | bytes 1048576 | tf_op jit(solution)/shard_map/all_to_all | solution.py:36
  171.7 1.1 copy.67
  172.8 7.0 %all-to-all-done.4 = bf16[16,64,256]{2,1,0:T(8,128)(2,1)S(1)} async-done(((bf16[16,64,256]{2,1,0:T(8,128)(2,1)}), bf16[16,64,256]{2,1,0:T(8,128)(2,1)S(1)}, u32[]{:S(2)}, u32[]{:S(2)}) %all-to-all-start.4) | async-done | bytes 524320 | tf_op jit(solution)/shard_map/all_to_all | solution.py:36
  179.7 0.4 project.1
  180.2 0.2 copy.68
  180.4 4.1 %all_to_all.100 = bf16[2,256,448]{1,2,0:T(8,128)(2,1)S(1)} all-to-all(bf16[2,256,448]{1,2,0:T(8,128)(2,1)S(1)} %copy.68), channel_id=1, replica_groups=mesh['x'=4,'yh'=2,'yl'=2,'zh'=2,'zlh'=4,'zll'=2,'c'=2] {'c'}, dimensions={0} | all-to-all | bytes 917504 | tf_op jit(solution)/shard_map/all_to_all | solution.py:36
  184.5 0.1 reduce_sum.24
  184.6 0.1 copy.69
  184.8 29.4 %all_to_all.101 = bf16[16,16,448]{2,1,0:T(8,128)(2,1)S(1)} all-to-all(bf16[16,16,448]{2,1,0:T(8,128)(2,1)S(1)} %bitcast.46), channel_id=1, replica_groups=mesh['x'=4,'yh'=2,'yl'=2,'zh'=2,'zlh'=4,'zll'=2,'c'=2] {'zlh','zll','zh'}, dimensions={0} | all-to-all | bytes 458752 | tf_op jit(solution)/shard_map/all_to_all | solution.py:36
  214.2 5.5 %collective-permute-start.7 = (bf16[16,448]{1,0:T(8,128)(2,1)S(1)}, bf16[16,448]{1,0:T(8,128)(2,1)S(1)}, u32[]{:S(2)}, u32[]{:S(2)}) collective-permute-start(bf16[16,448]{1,0:T(8,128)(2,1)S(1)} %reduce_sum.25), channel_id=1, source_target_pairs={{0,0},{1,256},{2,32},{3,288},{4,64},{5,320},{6,96},{7,352},{8,128}... | collective-permute-start | bytes 43016 | tf_op jit(solution)/shard_map/ppermute | solution.py:189
  219.7 5.8 %collective-permute-done.7 = bf16[16,448]{1,0:T(8,128)(2,1)S(1)} collective-permute-done((bf16[16,448]{1,0:T(8,128)(2,1)S(1)}, bf16[16,448]{1,0:T(8,128)(2,1)S(1)}, u32[]{:S(2)}, u32[]{:S(2)}) %collective-permute-start.7) | collective-permute-done | bytes 14368 | tf_op jit(solution)/shard_map/ppermute | solution.py:189
  225.5 0.6 copy.75
  (26 shorter events, 0.4 us)
Async XLA Ops:
  0.0 153.9 %copy-start = (s32[512]{0:T(512)S(1)}, s32[512]{0:T(512)}, u32[]{:S(2)}) copy-start(s32[512]{0:T(512)} %param.10) | copy-start | bytes 6148
  29.0 7.1 %all-to-all-start.3 = ((bf16[32,2,128]{2,0,1:T(8,128)(2,1)}), bf16[32,2,128]{2,0,1:T(8,128)(2,1)S(1)}, u32[]{:S(2)}, u32[]{:S(2)}) async-start(bf16[32,2,128]{2,0,1:T(8,128)(2,1)} %copy.58), calls=%async_computation.3 | async-start | bytes 32768 | tf_op jit(solution)/shard_map/all_to_all | solution.py:123
  36.0 42.9 %copy-start.2 = (bf16[32,2,128]{2,0,1:T(8,128)(2,1)}, bf16[32,2,128]{2,0,1:T(8,128)(2,1)S(1)}, u32[]{:S(2)}) copy-start(bf16[32,2,128]{2,0,1:T(8,128)(2,1)S(1)} %all-to-all-done.3) | copy-start | bytes 49156
  36.0 16.8 %all-to-all-start = ((bf16[8,80,128]{2,1,0:T(8,128)(2,1)}), bf16[8,80,128]{2,1,0:T(8,128)(2,1)S(1)}, u32[]{:S(2)}, u32[]{:S(2)}) async-start(bf16[8,80,128]{2,1,0:T(8,128)(2,1)} %pad_maximum_fusion.1), calls=%async_computation | async-start | bytes 327680 | tf_op jit(solution)/shard_map/all_to_all | solution.py:106
  52.8 24.8 %all-to-all-start.5 = ((bf16[8,4,7168]{2,1,0:T(4,128)(2,1)}), bf16[8,4,7168]{2,1,0:T(4,128)(2,1)S(1)}, u32[]{:S(2)}, u32[]{:S(2)}) async-start(bf16[8,4,7168]{2,1,0:T(4,128)(2,1)} %param.15), calls=%async_computation.5 | async-start | bytes 917504 | tf_op jit(solution)/shard_map/all_to_all | solution.py:157
  79.0 67.4 %all-to-all-start.1 = ((bf16[32,160,128]{2,1,0:T(8,128)(2,1)}), bf16[32,160,128]{2,1,0:T(8,128)(2,1)S(1)}, u32[]{:S(2)}, u32[]{:S(2)}) async-start(bf16[32,160,128]{2,1,0:T(8,128)(2,1)} %bitcast.19), calls=%async_computation.1 | async-start | bytes 2621440 | tf_op jit(solution)/shard_map/all_to_all | solution.py:36
  87.7 37.5 %copy-start.4 = (bf16[16,1536]{1,0:T(8,128)(2,1)S(1)}, bf16[16,1536]{1,0:T(8,128)(2,1)}, u32[]{:S(2)}) copy-start(bf16[16,1536]{1,0:T(8,128)(2,1)} %param.8) | copy-start | bytes 147460
  89.1 20.5 %collective-permute-start.3 = (bf16[128,576]{1,0:T(8,128)(2,1)S(1)}, bf16[128,576]{1,0:T(8,128)(2,1)S(1)}, u32[]{:S(2)}, u32[]{:S(2)}) collective-permute-start(bf16[128,576]{1,0:T(8,128)(2,1)S(1)} %constant_dynamic-slice_fusion), channel_id=1, source_target_pairs={{0,16},{16,0},{1,17},{17,1},{2,18},{18,2},{3,19},{19,3},{4,20},{20... | collective-permute-start | bytes 442376 | tf_op jit(solution)/shard_map/ppermute | solution.py:22
  109.6 7.2 %collective-permute-start.4 = (bf16[128,576]{1,0:T(8,128)(2,1)S(1)}, bf16[128,576]{1,0:T(8,128)(2,1)S(1)}, u32[]{:S(2)}, u32[]{:S(2)}) collective-permute-start(bf16[128,576]{1,0:T(8,128)(2,1)S(1)} %collective-permute-done.3), channel_id=1, source_target_pairs={{0,32},{32,0},{1,33},{33,1},{2,34},{34,2},{3,35},{35,3},{4,36},{36... | collective-permute-start | bytes 442376 | tf_op jit(solution)/shard_map/ppermute | solution.py:22
  116.8 11.4 %collective-permute-start.5 = (bf16[256,576]{1,0:T(8,128)(2,1)S(1)}, bf16[256,576]{1,0:T(8,128)(2,1)S(1)}, u32[]{:S(2)}, u32[]{:S(2)}) collective-permute-start(bf16[256,576]{1,0:T(8,128)(2,1)S(1)} %pad_maximum_fusion), channel_id=1, source_target_pairs={{0,2},{2,0},{1,3},{3,1},{4,6},{6,4},{5,7},{7,5},{8,10},{10,8},{9,1... | collective-permute-start | bytes 884744 | tf_op jit(solution)/shard_map/ppermute | solution.py:22
  121.6 32.6 %collective-permute-start.2 = (bf16[512,576]{0,1:T(8,128)(2,1)}, bf16[512,576]{0,1:T(8,128)(2,1)}, u32[]{:S(2)}, u32[]{:S(2)}) collective-permute-start(bf16[512,576]{0,1:T(8,128)(2,1)} %param.11), channel_id=1, source_target_pairs={{0,32},{32,0},{1,33},{33,1},{2,34},{34,2},{3,35},{35,3},{4,36},{36... | collective-permute-start | bytes 1769480 | tf_op jit(solution)/shard_map/ppermute | solution.py:22
  125.2 15.2 %collective-permute-start = (bf16[16,1536]{1,0:T(8,128)(2,1)S(1)}, bf16[16,1536]{1,0:T(8,128)(2,1)S(1)}, u32[]{:S(2)}, u32[]{:S(2)}) collective-permute-start(bf16[16,1536]{1,0:T(8,128)(2,1)S(1)} %copy-done.4), channel_id=1, source_target_pairs={{0,16},{16,0},{1,17},{17,1},{2,18},{18,2},{3,19},{19,3},{4,20},{20... | collective-permute-start | bytes 147464 | tf_op jit(solution)/shard_map/ppermute | solution.py:22
  129.4 26.1 %collective-permute-start.6 = (bf16[512,576]{0,1:T(8,128)(2,1)}, bf16[512,576]{0,1:T(8,128)(2,1)}, u32[]{:S(2)}, u32[]{:S(2)}) collective-permute-start(bf16[512,576]{0,1:T(8,128)(2,1)} %copy.60), channel_id=1, source_target_pairs={{0,1},{1,0},{2,3},{3,2},{4,5},{5,4},{6,7},{7,6},{8,9},{9,8},{10,11... | collective-permute-start | bytes 1769480 | tf_op jit(solution)/shard_map/ppermute | solution.py:22
  140.4 13.8 %collective-permute-start.1 = (bf16[32,1536]{1,0:T(8,128)(2,1)S(1)}, bf16[32,1536]{1,0:T(8,128)(2,1)S(1)}, u32[]{:S(2)}, u32[]{:S(2)}) collective-permute-start(bf16[32,1536]{1,0:T(8,128)(2,1)S(1)} %maximum_select_fusion.1), channel_id=1, source_target_pairs={{0,32},{32,0},{1,33},{33,1},{2,34},{34,2},{3,35},{35,3},{4,36},{36... | collective-permute-start | bytes 294920 | tf_op jit(solution)/shard_map/ppermute | solution.py:22
  146.4 17.2 %all-to-all-start.6 = ((bf16[16,4,8,448]{3,2,1,0:T(8,128)(2,1)}), bf16[16,4,8,448]{3,2,1,0:T(8,128)(2,1)}, u32[]{:S(2)}, u32[]{:S(2)}) async-start(bf16[16,4,8,448]{3,2,1,0:T(8,128)(2,1)} %copy.66), calls=%async_computation.6 | async-start | bytes 1048576 | tf_op jit(solution)/shard_map/all_to_all | solution.py:36
  157.7 1.1 copy-start.1
  158.8 0.7 copy-start.3
  164.5 15.3 %all-to-all-start.4 = ((bf16[16,64,256]{2,1,0:T(8,128)(2,1)}), bf16[16,64,256]{2,1,0:T(8,128)(2,1)S(1)}, u32[]{:S(2)}, u32[]{:S(2)}) async-start(bf16[16,64,256]{2,1,0:T(8,128)(2,1)} %broadcast_in_dim.19), calls=%async_computation.4 | async-start | bytes 1048576 | tf_op jit(solution)/shard_map/all_to_all | solution.py:36
  214.2 11.2 %collective-permute-start.7 = (bf16[16,448]{1,0:T(8,128)(2,1)S(1)}, bf16[16,448]{1,0:T(8,128)(2,1)S(1)}, u32[]{:S(2)}, u32[]{:S(2)}) collective-permute-start(bf16[16,448]{1,0:T(8,128)(2,1)S(1)} %reduce_sum.25), channel_id=1, source_target_pairs={{0,0},{1,256},{2,32},{3,288},{4,64},{5,320},{6,96},{7,352},{8,128}... | collective-permute-start | bytes 43016 | tf_op jit(solution)/shard_map/ppermute | solution.py:189

commit v2 on v1

--- a/solution.py
+++ b/solution.py
@@ -22,14 +22,25 @@
     return lax.ppermute(block, axis, [(0, 1), (1, 0)])
 
 
-def pair(block, axis):
-    theirs = swap(block, axis)
-    upper = lax.axis_index(axis) == 1
+def ordered(ours, theirs, position, dim):
     return jnp.where(
-        upper,
-        jnp.concatenate([theirs, block], axis=0),
-        jnp.concatenate([block, theirs], axis=0),
-    )
+        position == 1,
+        jnp.concatenate([theirs, ours], axis=dim),
+        jnp.concatenate([ours, theirs], axis=dim),
+    )
+
+
+def pack(blocks):
+    return jnp.concatenate([block.reshape(-1, block.shape[-1]) for block in blocks], axis=0)
+
+
+def unpack(packed, shapes):
+    blocks, at = [], 0
+    for shape in shapes:
+        count = math.prod(shape[:-1])
+        blocks.append(packed[at : at + count].reshape(shape))
+        at += count
+    return blocks
 
 
 def exchange(blocks, axes):
@@ -49,9 +60,9 @@
 ):
     rows, heads, n_uq, n_uk, n_uv, width = sizes
     caches = (kv0, kv1, kv2, kv3)
-    per_block = kv0.shape[0]
+    per_block = kv0.shape[1]
     chunk = per_block * len(caches) // starts.shape[0]
-    query = latent[...]
+    query = jnp.concatenate([latent[i] for i in range(latent.shape[0])], axis=1)
     limit = lengths[...]
     lanes = lax.broadcasted_iota(jnp.int32, (rows, chunk), 1)
     for h in range(heads):
@@ -59,11 +70,11 @@
         w_uk = weights[:, h, :, n_uq : n_uq + n_uk, :].reshape(-1, weights.shape[-1])
         q_nope = dot(query, w_uq).astype(BF16)
         q_lat = dot_nt(q_nope, w_uk).astype(BF16)
-        rope_width = kv0.shape[1] - width
+        rope_width = kv0.shape[0] - width
         q_rope = rope[:, h * rope_width : (h + 1) * rope_width]
         top = jnp.full((rows, 1), -1e30, F32)
         for b, cache in enumerate(caches):
-            s = dot_nt(q_lat, cache[:, :width]) + dot_nt(q_rope, cache[:, width:])
+            s = dot(q_lat, cache[:width, :]) + dot(q_rope, cache[width:, :])
             s = s * temper
             for i in range(per_block // chunk):
                 k = b * (per_block // chunk) + i
@@ -76,7 +87,7 @@
         for b, cache in enumerate(caches):
             p = jnp.exp(scores[:, b * per_block : (b + 1) * per_block] - top)
             total = total + jnp.sum(p, axis=1, keepdims=True)
-            context = context + dot(p.astype(BF16), cache[:, :width])
+            context = context + dot_nt(p.astype(BF16), cache[:width, :])
         context = (context / total).astype(BF16)
         w_uv = weights[:, h, :, n_uq + n_uk :, :].reshape(-1, weights.shape[-1])
         vdim = w_uv.shape[1]
@@ -96,35 +107,68 @@
 def local(query_latent, query_rope, lengths, kv_cache, w_uq, w_uk, w_uv, w_out):
     yl, zh, zll, core = (lax.axis_index(a) for a in ("yl", "zh", "zll", "c"))
     plane = 16
-    tokens, kv_width = kv_cache.shape
+    cache = kv_cache.T
+    kv_width, tokens = cache.shape
     latent_width = w_uk.shape[1] * 32
     rope_width = kv_width - latent_width
-    temper = 1.0 / math.sqrt(w_uq.shape[2] + rope_width)
+    lanes = w_uq.shape[2]
+    temper = 1.0 / math.sqrt(lanes + rope_width)
     n_uq, n_uk, n_uv = w_uq.shape[1], w_uk.shape[1], w_uv.shape[1]
-
+    n_all = n_uq + n_uk + n_uv
+    own_rows = query_latent.shape[0]
+    heads_in = w_uq.shape[0]
+    four, heads = heads_in // 2, heads_in // 4
+
+    quarter = tokens // 4
+    piece = lax.dynamic_slice_in_dim(cache, (core * 2 + zll) * quarter, quarter, 1)
     stacked = jnp.concatenate([w_uq, w_uk, w_uv], axis=1)
-    stacked = lax.all_to_all(stacked, "zh", 0, 1, tiled=True)
-    quarter = tokens // 4
-    piece = lax.dynamic_slice_in_dim(kv_cache, (core * 2 + zll) * quarter, quarter, 0)
-    piece = swap(piece, "zh")
-    near = swap(kv_cache, "yl")
-    latent_rows = pair(query_latent, "zh")
-    rope_rows = query_rope.reshape(query_rope.shape[0], -1)
-    rope_rows = lax.all_to_all(rope_rows, "zh", 1, 0, tiled=True)
-
-    heads = stacked.shape[0] // 2
+    kept = lax.dynamic_slice_in_dim(stacked, zh * four, four, 0)
+    given = lax.dynamic_slice_in_dim(stacked, (1 - zh) * four, four, 0)
+    latent = jnp.transpose(query_latent.reshape(own_rows, -1, lanes), (1, 0, 2))
+    rope = jnp.transpose(query_rope.reshape(own_rows, -1, lanes), (1, 0, 2))
+    rope_kept = lax.dynamic_slice_in_dim(rope, zh * 2, 2, 0)
+    rope_given = lax.dynamic_slice_in_dim(rope, (1 - zh) * 2, 2, 0)
+    sent = [piece, given, latent, rope_given]
+    packed = pack(sent)
+    near = swap(cache, "yl")
+    far_piece, taken, latent_far, rope_far = unpack(
+        swap(packed, "zh"), [block.shape for block in sent]
+    )
+
+    vpart, width = w_out.shape[1:]
+    columns = width // plane
+    out_proj = w_out.reshape(heads_in * vpart, plane, columns)
+    out_proj = exchange(jnp.transpose(out_proj, (1, 0, 2)), PLANE)
+    out_proj = out_proj.reshape(plane, heads_in, vpart, columns)
+
+    far_piece, taken, latent_far, rope_far, near, out_proj = lax.optimization_barrier(
+        (far_piece, taken, latent_far, rope_far, near, out_proj)
+    )
+
+    proj_kept = lax.dynamic_slice_in_dim(out_proj, zh * four, four, 1)
+    proj_given = lax.dynamic_slice_in_dim(out_proj, (1 - zh) * four, four, 1)
+    proj_far = [swap(proj_given[a:b], "zh") for a, b in ((0, 4), (4, 8), (8, 16))]
+
+    stacked = ordered(kept, taken, zh, 1)
     weights = jnp.broadcast_to(
-        stacked.reshape((1, 2, heads) + stacked.shape[1:]),
-        (plane // 2, 2, heads) + stacked.shape[1:],
-    ).reshape((plane * heads,) + stacked.shape[1:])
-    weights = exchange(weights, PLANE).reshape(plane, heads, 2, n_uq + n_uk + n_uv, -1)
-
-    latent_rows = pair(latent_rows, "yl")
-    rope_rows = lax.all_to_all(rope_rows, "yl", 1, 0, tiled=True)
-
-    piece = jnp.concatenate([piece, swap(piece, "yl")], axis=0)
-    piece = jnp.concatenate([piece, swap(piece, "zll")], axis=0)
-    far = swap(piece, "c")
+        stacked.reshape((1, 2, heads, 2 * n_all, lanes)), (plane // 2, 2, heads, 2 * n_all, lanes)
+    ).reshape(plane * heads, 2 * n_all, lanes)
+    weights = exchange(weights, PLANE).reshape(plane, heads, 2, n_all, lanes)
+
+    latent = ordered(latent, latent_far, zh, 1)
+    rope = ordered(rope_kept, rope_far, zh, 1)
+    rope_kept = lax.dynamic_slice_in_dim(rope, yl, 1, 0)
+    rope_given = lax.dynamic_slice_in_dim(rope, 1 - yl, 1, 0)
+    sent = [far_piece, latent, rope_given]
+    piece_y, latent_y, rope_y = unpack(swap(pack(sent), "yl"), [block.shape for block in sent])
+    piece_z = swap(far_piece, "zll")
+    piece_yz = lax.ppermute(far_piece, ("yl", "zll"), [(0, 3), (1, 2), (2, 1), (3, 0)])
+    far = jnp.concatenate([far_piece, piece_y, piece_z, piece_yz], axis=1)
+    far, proj_far[0] = lax.optimization_barrier((far, proj_far[0]))
+    far_other = swap(far, "c")
+    latent = ordered(latent, latent_y, yl, 1)
+    rope = ordered(rope_kept[0], rope_y[0], yl, 0)
+
     starts = []
     for ylo in (yl, 1 - yl):
         for i in range(4):
@@ -135,35 +179,30 @@
                 starts.append((ylo * 2 + 1 - zh) * tokens + (co * 2 + zo) * quarter)
     starts = jnp.stack(starts).astype(jnp.int32)
 
-    rows = latent_rows.shape[0]
+    weights, proj_far[1] = lax.optimization_barrier((weights, proj_far[1]))
+    rows = latent.shape[1]
     sequence = lax.axis_index("x") * 2 + lax.axis_index("yh")
     row_lengths = lax.dynamic_slice_in_dim(lengths, sequence * rows, rows, 0)[:, None]
-    vdim = w_uv.shape[2]
     vmem = pl.BlockSpec(memory_space=pltpu.VMEM)
     values = pl.pallas_call(
         lambda *refs: attend_kernel(
             *refs, sizes=(rows, heads, n_uq, n_uk, n_uv, latent_width), temper=temper
         ),
-        out_shape=jax.ShapeDtypeStruct((rows, heads * vdim), BF16),
+        out_shape=jax.ShapeDtypeStruct((rows, heads * lanes), BF16),
         in_specs=[pl.BlockSpec(memory_space=pltpu.SMEM)] + [vmem] * 8,
         out_specs=vmem,
         scratch_shapes=[pltpu.VMEM((rows, 4 * tokens), F32)],
         compiler_params=pltpu.CompilerParams(vmem_limit_bytes=VMEM_LIMIT),
         cost_estimate=pl.CostEstimate(flops=10**9, bytes_accessed=5 * 10**6, transcendentals=0),
         name="attend",
-    )(starts, latent_rows, weights, rope_rows, row_lengths, kv_cache, near, piece, far)
-
-    w_out, _ = lax.optimization_barrier((w_out, stacked))
-    out_proj = lax.all_to_all(w_out, "zh", 0, 1, tiled=True)
-    four, vpart, width = out_proj.shape
-    columns = width // plane
-    out_proj = out_proj.reshape(four, vpart, plane, columns)
-    out_proj = exchange(jnp.transpose(out_proj, (2, 0, 1, 3)), PLANE)
-    out_proj = jnp.transpose(out_proj, (1, 0, 2, 3)).reshape(four * plane * vpart, columns)
-
+    )(starts, latent, weights, rope, row_lengths, cache, near, far, far_other)
+
+    values, proj_far[2] = lax.optimization_barrier((values, proj_far[2]))
+    out_proj = ordered(proj_kept, jnp.concatenate(proj_far, axis=0), zh, 2)
+    out_proj = jnp.transpose(out_proj, (1, 0, 2, 3)).reshape(-1, columns)
     gathered = exchange(
         jnp.broadcast_to(values[None], (plane,) + values.shape).reshape(-1, values.shape[1]), PLANE
-    ).reshape(plane // 2, 2, rows, heads * vdim)
+    ).reshape(plane // 2, 2, rows, heads * lanes)
     all_rows = plane // 2 * rows
     partial_out = pl.pallas_call(
         project_kernel,

time: 230 us -> 194 us (0.84)
  the two profiles are of different devices: /device:TPU:6 before, /device:TPU:38 now
where the time goes in v2:
time: 194 us; the launch traced here: 193 us
  starting transfers between devices  81.1 us (42%)
  waiting for transfers between devices  60.3 us (31%)
  blocking collectives  29.5 us (15%)
  local copies, waits for them, and re-layouts  13.2 us (7%)
  Pallas kernels  4.84 us (2%)
  other arithmetic  3.43 us (2%)
    ppermute x8, starting transfers between devices, swap(): return lax.ppermute(block, axis, [(0, 1), (1, 0)])  54.3 us
    ppermute x8, waiting for transfers between devices, swap(): return lax.ppermute(block, axis, [(0, 1), (1, 0)])  42.5 us
    all_to_all x2, blocking collectives, exchange(): return lax.all_to_all(blocks, axes, 0, 0, tiled=True)  29.5 us
    all_to_all x3, starting transfers between devices, exchange(): return lax.all_to_all(blocks, axes, 0, 0, tiled=True)  22 us
    ppermute x1, waiting for transfers between devices, local(): return lax.ppermute(total, AXES, route)  9.94 us
    all_to_all x3, waiting for transfers between devices, exchange(): return lax.all_to_all(blocks, axes, 0, 0, tiled=True)  7.87 us
    pallas_call x1, Pallas kernels, local(): pl.pallas_call(lambda *refs: attend_kernel(*refs, sizes=(rows, heads, n_u...  4.4 us
  transfers between devices with their start and end apart: 13, of which 7 were waited for; matrix products, arithmetic and copies ran while one was open for 6% of the time, Pallas kernels for 2%

profile of v2, /device:TPU:38, one launch (start us, length us, event | category | flops | bytes accessed | tf_op | source)
XLA Modules:
  0.0 192.9 jit_solution(8768082211374641469)
XLA Ops:
  0.0 3.6 %collective-permute-start.1 = (bf16[576,512]{1,0:T(8,128)(2,1)}, bf16[576,512]{1,0:T(8,128)(2,1)S(1)}, u32[]{:S(2)}, u32[]{:S(2)}) collective-permute-start(bf16[576,512]{1,0:T(8,128)(2,1)} %bitcast.64), channel_id=1, source_target_pairs={{0,32},{32,0},{1,33},{33,1},{2,34},{34,2},{3,35},{35,3},{4,36},{36... | collective-permute-start | bytes 1769480 | tf_op jit(solution)/shard_map/ppermute | solution.py:22
  3.6 1.6 reshape.105
  5.2 1.1 copy.42
  6.4 7.3 %all-to-all-start = ((bf16[16,32,448]{2,1,0:T(8,128)(2,1)}), bf16[16,32,448]{2,1,0:T(8,128)(2,1)S(1)}, u32[]{:S(2)}, u32[]{:S(2)}) async-start(bf16[16,32,448]{2,1,0:T(8,128)(2,1)} %copy.42), calls=%async_computation | async-start | bytes 1048576 | tf_op jit(solution)/shard_map/all_to_all | solution.py:47
  13.7 0.1 reshape.100
  14.0 14.8 %collective-permute-start = (bf16[1120,128]{1,0:T(8,128)(2,1)S(1)}, bf16[1120,128]{1,0:T(8,128)(2,1)S(1)}, u32[]{:S(2)}, u32[]{:S(2)}) collective-permute-start(bf16[1120,128]{1,0:T(8,128)(2,1)S(1)} %pad_maximum_fusion.1), channel_id=1, source_target_pairs={{0,16},{16,0},{1,17},{17,1},{2,18},{18,2},{3,19},{19,3},{4,20},{20... | collective-permute-start | bytes 860168 | tf_op jit(solution)/shard_map/ppermute | solution.py:22
  28.8 24.4 %collective-permute-done = bf16[1120,128]{1,0:T(8,128)(2,1)S(1)} collective-permute-done((bf16[1120,128]{1,0:T(8,128)(2,1)S(1)}, bf16[1120,128]{1,0:T(8,128)(2,1)S(1)}, u32[]{:S(2)}, u32[]{:S(2)}) %collective-permute-start) | collective-permute-done | bytes 286752 | tf_op jit(solution)/shard_map/ppermute | solution.py:22
  53.2 0.7 copy-done.4
  53.9 0.3 copy.43
  54.3 1.3 broadcast_in_dim.6
  55.7 7.4 %all-to-all-start.1 = ((bf16[32,160,128]{2,1,0:T(8,128)(2,1)}), bf16[32,160,128]{2,1,0:T(8,128)(2,1)S(1)}, u32[]{:S(2)}, u32[]{:S(2)}) async-start(bf16[32,160,128]{2,1,0:T(8,128)(2,1)} %bitcast.66), calls=%async_computation.1 | async-start | bytes 2621440 | tf_op jit(solution)/shard_map/all_to_all | solution.py:47
  63.1 0.7 pad_maximum_fusion.2
  63.8 3.4 %collective-permute-start.2 = (bf16[992,128]{1,0:T(8,128)(2,1)}, bf16[992,128]{1,0:T(8,128)(2,1)}, u32[]{:S(2)}, u32[]{:S(2)}) collective-permute-start(bf16[992,128]{1,0:T(8,128)(2,1)} %pad_maximum_fusion.2), channel_id=1, source_target_pairs={{0,32},{32,0},{1,33},{33,1},{2,34},{34,2},{3,35},{35,3},{4,36},{36... | collective-permute-start | bytes 761864 | tf_op jit(solution)/shard_map/ppermute | solution.py:22
  67.2 1.9 collective-permute-start.5
  69.1 3.9 %collective-permute-start.4 = (bf16[576,128]{1,0:T(8,128)(2,1)S(1)}, bf16[576,128]{1,0:T(8,128)(2,1)}, u32[]{:S(2)}, u32[]{:S(2)}) collective-permute-start(bf16[576,128]{1,0:T(8,128)(2,1)S(1)} %slice.40), channel_id=1, source_target_pairs={{0,2},{2,0},{1,3},{3,1},{4,6},{6,4},{5,7},{7,5},{8,10},{10,8},{9,1... | collective-permute-start | bytes 442376 | tf_op jit(solution)/shard_map/ppermute | solution.py:22
  73.1 0.1 constant_dynamic-slice_fusion
  73.1 12.2 %collective-permute-start.6 = (bf16[4,4,4,448]{3,0,2,1:T(4,128)(2,1)S(1)}, bf16[4,4,4,448]{3,0,2,1:T(4,128)(2,1)S(1)}, u32[]{:S(2)}, u32[]{:S(2)}) collective-permute-start(bf16[4,4,4,448]{3,0,2,1:T(4,128)(2,1)S(1)} %get-tuple-element.29), channel_id=1, source_target_pairs={{0,16},{16,0},{1,17},{17,1},{2,18},{18,2},{3,19},{19,3},{4,20},{20... | collective-permute-start | bytes 172040 | tf_op jit(solution)/shard_map/ppermute | solution.py:22
  85.3 1.2 collective-permute-done.2
  86.5 0.9 slice.46
  87.4 1.0 pad_maximum_fusion.refs_7_
  88.5 0.8 collective-permute-done.6
  89.3 0.6 copy-done.6
  89.9 1.9 collective-permute-start.7
  91.9 0.8 dynamic-slice_bitcast_fusion.3
  92.7 0.1 copy.45.refs_4_
  92.8 0.1 stack.67.refs_0_
  92.8 11.8 %collective-permute-start.3 = (bf16[4,4,4,448]{3,0,2,1:T(4,128)(2,1)S(1)}, bf16[4,4,4,448]{3,0,2,1:T(4,128)(2,1)}, u32[]{:S(2)}, u32[]{:S(2)}) collective-permute-start(bf16[4,4,4,448]{3,0,2,1:T(4,128)(2,1)S(1)} %get-tuple-element.30), channel_id=1, source_target_pairs={{0,16},{16,0},{1,17},{17,1},{2,18},{18,2},{3,19},{19,3},{4,20},{20... | collective-permute-start | bytes 172040 | tf_op jit(solution)/shard_map/ppermute | solution.py:22
  104.7 1.6 constant_dynamic-slice_fusion.3
  106.3 2.7 %collective-permute-start.8 = (bf16[8,4,4,448]{3,0,2,1:T(8,128)(2,1)}, bf16[8,4,4,448]{3,0,2,1:T(8,128)(2,1)}, u32[]{:S(2)}, u32[]{:S(2)}) collective-permute-start(bf16[8,4,4,448]{3,0,2,1:T(8,128)(2,1)} %constant_dynamic-slice_fusion.3), channel_id=1, source_target_pairs={{0,16},{16,0},{1,17},{17,1},{2,18},{18,2},{3,19},{19,3},{4,20},{20... | collective-permute-start | bytes 344072 | tf_op jit(solution)/shard_map/ppermute | solution.py:22
  109.0 0.9 slice.44
  109.9 0.7 slice.45
  110.7 0.4 collective-permute-done.3
  111.0 4.4 %attend.1 = bf16[64,256]{1,0:T(8,128)(2,1)S(1)} custom-call(s32[16]{0:T(128)S(1)} %stack.67.refs_0_, bf16[12,64,128]{2,1,0:T(8,128)(2,1)S(1)} %maximum_select_fusion.1.refs_1_, bf16[16,2,2,80,128]{4,3,2,1,0:T(8,128)(2,1)S(1)} %bitcast.60, bf16[64,128]{1,0:T(8,128)(2,1)S(1)} %maximum_select_fusion.5.refs_3_, s32[64,1]{1,0:T(8,128)S(1)} %copy.45.refs_4_, ...), custom_call_target="tpu_custom_call" | custom-call | flops 1000000000 | bytes 5000000 | tf_op jit(solution)/shard_map/attend/pallas_call | solution.py:187
  115.5 15.8 %collective-permute-done.8 = bf16[8,4,4,448]{3,0,2,1:T(8,128)(2,1)} collective-permute-done((bf16[8,4,4,448]{3,0,2,1:T(8,128)(2,1)}, bf16[8,4,4,448]{3,0,2,1:T(8,128)(2,1)}, u32[]{:S(2)}, u32[]{:S(2)}) %collective-permute-start.8) | collective-permute-done | bytes 114720 | tf_op jit(solution)/shard_map/ppermute | solution.py:22
  131.2 0.9 broadcast_in_dim.16
  132.1 7.4 %all-to-all-start.2 = ((bf16[16,64,256]{2,1,0:T(8,128)(2,1)}), bf16[16,64,256]{2,1,0:T(8,128)(2,1)S(1)}, u32[]{:S(2)}, u32[]{:S(2)}) async-start(bf16[16,64,256]{2,1,0:T(8,128)(2,1)} %broadcast_in_dim.16), calls=%async_computation.2 | async-start | bytes 1048576 | tf_op jit(solution)/shard_map/all_to_all | solution.py:47
  139.5 1.3 fusion
  140.8 0.3 copy.46
  141.2 7.9 %all-to-all-done.2 = bf16[16,64,256]{2,1,0:T(8,128)(2,1)S(1)} async-done(((bf16[16,64,256]{2,1,0:T(8,128)(2,1)}), bf16[16,64,256]{2,1,0:T(8,128)(2,1)S(1)}, u32[]{:S(2)}, u32[]{:S(2)}) %all-to-all-start.2) | async-done | bytes 524320 | tf_op jit(solution)/shard_map/all_to_all | solution.py:47
  149.0 0.4 project.1
  149.5 0.2 copy.47
  149.7 4.1 %all_to_all.34 = bf16[2,256,448]{1,2,0:T(8,128)(2,1)S(1)} all-to-all(bf16[2,256,448]{1,2,0:T(8,128)(2,1)S(1)} %copy.47), channel_id=1, replica_groups=mesh['x'=4,'yh'=2,'yl'=2,'zh'=2,'zlh'=4,'zll'=2,'c'=2] {'c'}, dimensions={0} | all-to-all | bytes 917504 | tf_op jit(solution)/shard_map/all_to_all | solution.py:47
  153.8 0.1 reduce_sum.24
  153.9 0.1 copy.48
  154.1 25.4 %all_to_all.35 = bf16[16,16,448]{2,1,0:T(8,128)(2,1)S(1)} all-to-all(bf16[16,16,448]{2,1,0:T(8,128)(2,1)S(1)} %bitcast.71), channel_id=1, replica_groups=mesh['x'=4,'yh'=2,'yl'=2,'zh'=2,'zlh'=4,'zll'=2,'c'=2] {'zlh','zll','zh'}, dimensions={0} | all-to-all | bytes 458752 | tf_op jit(solution)/shard_map/all_to_all | solution.py:47
  179.5 2.9 %collective-permute-start.9 = (bf16[16,448]{1,0:T(8,128)(2,1)S(1)}, bf16[16,448]{1,0:T(8,128)(2,1)S(1)}, u32[]{:S(2)}, u32[]{:S(2)}) collective-permute-start(bf16[16,448]{1,0:T(8,128)(2,1)S(1)} %reduce_sum.25), channel_id=1, source_target_pairs={{0,0},{1,256},{2,32},{3,288},{4,64},{5,320},{6,96},{7,352},{8,128}... | collective-permute-start | bytes 43016 | tf_op jit(solution)/shard_map/ppermute | solution.py:228
  182.4 9.9 %collective-permute-done.9 = bf16[16,448]{1,0:T(8,128)(2,1)S(1)} collective-permute-done((bf16[16,448]{1,0:T(8,128)(2,1)S(1)}, bf16[16,448]{1,0:T(8,128)(2,1)S(1)}, u32[]{:S(2)}, u32[]{:S(2)}) %collective-permute-start.9) | collective-permute-done | bytes 14368 | tf_op jit(solution)/shard_map/ppermute | solution.py:228
  192.3 0.6 copy.60
  (50 shorter events, 0.5 us)
Async XLA Ops:
  0.0 13.6 %copy-start = (bf16[16,1536]{1,0:T(8,128)(2,1)S(1)}, bf16[16,1536]{1,0:T(8,128)(2,1)}, u32[]{:S(2)}) copy-start(bf16[16,1536]{1,0:T(8,128)(2,1)} %param.8) | copy-start | bytes 147460
  0.0 54.2 %collective-permute-start.1 = (bf16[576,512]{1,0:T(8,128)(2,1)}, bf16[576,512]{1,0:T(8,128)(2,1)S(1)}, u32[]{:S(2)}, u32[]{:S(2)}) collective-permute-start(bf16[576,512]{1,0:T(8,128)(2,1)} %bitcast.64), channel_id=1, source_target_pairs={{0,32},{32,0},{1,33},{33,1},{2,34},{34,2},{3,35},{35,3},{4,36},{36... | collective-permute-start | bytes 1769480 | tf_op jit(solution)/shard_map/ppermute | solution.py:22
  5.2 8.5 %copy-start.8 = (bf16[16,8,64]{2,1,0:T(8,128)(2,1)S(1)}, bf16[16,8,64]{2,1,0:T(8,128)(2,1)}, u32[]{:S(2)}) copy-start(bf16[16,8,64]{2,1,0:T(8,128)(2,1)} %param.9) | copy-start | bytes 49156
  5.2 8.6 %copy-start.5 = (bf16[8,48,128]{2,1,0:T(8,128)(2,1)S(1)}, bf16[8,48,128]{2,1,0:T(8,128)(2,1)}, u32[]{:S(2)}) copy-start(bf16[8,48,128]{2,1,0:T(8,128)(2,1)} %param.12) | copy-start | bytes 294916
  5.2 8.6 %copy-start.9 = (bf16[8,16,128]{2,1,0:T(8,128)(2,1)S(1)}, bf16[8,16,128]{2,1,0:T(8,128)(2,1)}, u32[]{:S(2)}) copy-start(bf16[8,16,128]{2,1,0:T(8,128)(2,1)} %param.13) | copy-start | bytes 98308
  5.2 8.6 %copy-start.10 = (bf16[8,16,128]{2,1,0:T(8,128)(2,1)S(1)}, bf16[8,16,128]{2,1,0:T(8,128)(2,1)}, u32[]{:S(2)}) copy-start(bf16[8,16,128]{2,1,0:T(8,128)(2,1)} %param.14) | copy-start | bytes 98308
  6.4 7.6 %copy-start.1 = (bf16[512,576]{0,1:T(8,128)(2,1)S(1)}, bf16[512,576]{0,1:T(8,128)(2,1)}, u32[]{:S(2)}) copy-start(bf16[512,576]{0,1:T(8,128)(2,1)} %param.11) | copy-start | bytes 1769476
  6.4 47.6 %all-to-all-start = ((bf16[16,32,448]{2,1,0:T(8,128)(2,1)}), bf16[16,32,448]{2,1,0:T(8,128)(2,1)S(1)}, u32[]{:S(2)}, u32[]{:S(2)}) async-start(bf16[16,32,448]{2,1,0:T(8,128)(2,1)} %copy.42), calls=%async_computation | async-start | bytes 1048576 | tf_op jit(solution)/shard_map/all_to_all | solution.py:47
  14.0 39.2 %collective-permute-start = (bf16[1120,128]{1,0:T(8,128)(2,1)S(1)}, bf16[1120,128]{1,0:T(8,128)(2,1)S(1)}, u32[]{:S(2)}, u32[]{:S(2)}) collective-permute-start(bf16[1120,128]{1,0:T(8,128)(2,1)S(1)} %pad_maximum_fusion.1), channel_id=1, source_target_pairs={{0,16},{16,0},{1,17},{17,1},{2,18},{18,2},{3,19},{19,3},{4,20},{20... | collective-permute-start | bytes 860168 | tf_op jit(solution)/shard_map/ppermute | solution.py:22
  53.2 0.7 copy-start.4
  54.2 18.8 %copy-start.2 = (bf16[16,32,448]{2,0,1:T(8,128)(2,1)}, bf16[16,32,448]{2,0,1:T(8,128)(2,1)S(1)}, u32[]{:S(2)}) copy-start(bf16[16,32,448]{2,0,1:T(8,128)(2,1)S(1)} %copy.43) | copy-start | bytes 1376260
  55.6 7.4 %slice-start.1 = ((bf16[1120,128]{1,0:T(8,128)(2,1)}), bf16[32,128]{1,0:T(8,128)(2,1)S(1)}, s32[]{:S(2)}) async-start(bf16[1120,128]{1,0:T(8,128)(2,1)} %copy-done.4), calls=%async_computation.6 | async-start | bytes 16384 | tf_op jit(solution)/shard_map/slice | solution.py:41
  55.6 7.4 %slice-start = ((bf16[1120,128]{1,0:T(8,128)(2,1)}), bf16[192,128]{1,0:T(8,128)(2,1)S(1)}, s32[]{:S(2)}) async-start(bf16[1120,128]{1,0:T(8,128)(2,1)} %copy-done.4), calls=%async_computation.5 | async-start | bytes 98304 | tf_op jit(solution)/shard_map/slice | solution.py:41
  55.7 55.4 %all-to-all-start.1 = ((bf16[32,160,128]{2,1,0:T(8,128)(2,1)}), bf16[32,160,128]{2,1,0:T(8,128)(2,1)S(1)}, u32[]{:S(2)}, u32[]{:S(2)}) async-start(bf16[32,160,128]{2,1,0:T(8,128)(2,1)} %bitcast.66), calls=%async_computation.1 | async-start | bytes 2621440 | tf_op jit(solution)/shard_map/all_to_all | solution.py:47
  63.8 22.7 %collective-permute-start.2 = (bf16[992,128]{1,0:T(8,128)(2,1)}, bf16[992,128]{1,0:T(8,128)(2,1)}, u32[]{:S(2)}, u32[]{:S(2)}) collective-permute-start(bf16[992,128]{1,0:T(8,128)(2,1)} %pad_maximum_fusion.2), channel_id=1, source_target_pairs={{0,32},{32,0},{1,33},{33,1},{2,34},{34,2},{3,35},{35,3},{4,36},{36... | collective-permute-start | bytes 761864 | tf_op jit(solution)/shard_map/ppermute | solution.py:22
  67.2 20.2 %collective-permute-start.5 = (bf16[576,128]{1,0:T(8,128)(2,1)S(1)}, bf16[576,128]{1,0:T(8,128)(2,1)}, u32[]{:S(2)}, u32[]{:S(2)}) collective-permute-start(bf16[576,128]{1,0:T(8,128)(2,1)S(1)} %slice.40), channel_id=1, source_target_pairs={{0,34},{2,32},{32,2},{34,0},{1,35},{3,33},{33,3},{35,1},{4,38},{6,... | collective-permute-start | bytes 442376 | tf_op jit(solution)/shard_map/ppermute | solution.py:165
  69.1 18.3 %collective-permute-start.4 = (bf16[576,128]{1,0:T(8,128)(2,1)S(1)}, bf16[576,128]{1,0:T(8,128)(2,1)}, u32[]{:S(2)}, u32[]{:S(2)}) collective-permute-start(bf16[576,128]{1,0:T(8,128)(2,1)S(1)} %slice.40), channel_id=1, source_target_pairs={{0,2},{2,0},{1,3},{3,1},{4,6},{6,4},{5,7},{7,5},{8,10},{10,8},{9,1... | collective-permute-start | bytes 442376 | tf_op jit(solution)/shard_map/ppermute | solution.py:22
  73.1 16.2 %collective-permute-start.6 = (bf16[4,4,4,448]{3,0,2,1:T(4,128)(2,1)S(1)}, bf16[4,4,4,448]{3,0,2,1:T(4,128)(2,1)S(1)}, u32[]{:S(2)}, u32[]{:S(2)}) collective-permute-start(bf16[4,4,4,448]{3,0,2,1:T(4,128)(2,1)S(1)} %get-tuple-element.29), channel_id=1, source_target_pairs={{0,16},{16,0},{1,17},{17,1},{2,18},{18,2},{3,19},{19,3},{4,20},{20... | collective-permute-start | bytes 172040 | tf_op jit(solution)/shard_map/ppermute | solution.py:22
  89.3 0.6 copy-start.6
  89.9 21.1 %collective-permute-start.7 = (bf16[576,512]{1,0:T(8,128)(2,1)S(1)}, bf16[576,512]{1,0:T(8,128)(2,1)}, u32[]{:S(2)}, u32[]{:S(2)}) collective-permute-start(bf16[576,512]{1,0:T(8,128)(2,1)S(1)} %pad_maximum_fusion.refs_7_), channel_id=1, source_target_pairs={{0,1},{1,0},{2,3},{3,2},{4,5},{5,4},{6,7},{7,6},{8,9},{9,8},{10,11... | collective-permute-start | bytes 1769480 | tf_op jit(solution)/shard_map/ppermute | solution.py:22
  92.8 18.2 %collective-permute-start.3 = (bf16[4,4,4,448]{3,0,2,1:T(4,128)(2,1)S(1)}, bf16[4,4,4,448]{3,0,2,1:T(4,128)(2,1)}, u32[]{:S(2)}, u32[]{:S(2)}) collective-permute-start(bf16[4,4,4,448]{3,0,2,1:T(4,128)(2,1)S(1)} %get-tuple-element.30), channel_id=1, source_target_pairs={{0,16},{16,0},{1,17},{17,1},{2,18},{18,2},{3,19},{19,3},{4,20},{20... | collective-permute-start | bytes 172040 | tf_op jit(solution)/shard_map/ppermute | solution.py:22
  106.3 25.0 %collective-permute-start.8 = (bf16[8,4,4,448]{3,0,2,1:T(8,128)(2,1)}, bf16[8,4,4,448]{3,0,2,1:T(8,128)(2,1)}, u32[]{:S(2)}, u32[]{:S(2)}) collective-permute-start(bf16[8,4,4,448]{3,0,2,1:T(8,128)(2,1)} %constant_dynamic-slice_fusion.3), channel_id=1, source_target_pairs={{0,16},{16,0},{1,17},{17,1},{2,18},{18,2},{3,19},{19,3},{4,20},{20... | collective-permute-start | bytes 344072 | tf_op jit(solution)/shard_map/ppermute | solution.py:22
  115.4 24.1 %copy-start.3 = (bf16[16,32,448]{2,0,1:T(8,128)(2,1)S(1)}, bf16[16,32,448]{2,0,1:T(8,128)(2,1)}, u32[]{:S(2)}) copy-start(bf16[16,32,448]{2,0,1:T(8,128)(2,1)} %copy-done.2) | copy-start | bytes 1376260
  115.4 24.1 %copy-start.7 = (bf16[4,4,4,448]{3,0,2,1:T(4,128)(2,1)S(1)}, bf16[4,4,4,448]{3,0,2,1:T(4,128)(2,1)}, u32[]{:S(2)}) copy-start(bf16[4,4,4,448]{3,0,2,1:T(4,128)(2,1)} %copy-done.6) | copy-start | bytes 172036
  132.1 16.9 %all-to-all-start.2 = ((bf16[16,64,256]{2,1,0:T(8,128)(2,1)}), bf16[16,64,256]{2,1,0:T(8,128)(2,1)S(1)}, u32[]{:S(2)}, u32[]{:S(2)}) async-start(bf16[16,64,256]{2,1,0:T(8,128)(2,1)} %broadcast_in_dim.16), calls=%async_computation.2 | async-start | bytes 1048576 | tf_op jit(solution)/shard_map/all_to_all | solution.py:47
  179.5 12.8 %collective-permute-start.9 = (bf16[16,448]{1,0:T(8,128)(2,1)S(1)}, bf16[16,448]{1,0:T(8,128)(2,1)S(1)}, u32[]{:S(2)}, u32[]{:S(2)}) collective-permute-start(bf16[16,448]{1,0:T(8,128)(2,1)S(1)} %reduce_sum.25), channel_id=1, source_target_pairs={{0,0},{1,256},{2,32},{3,288},{4,64},{5,320},{6,96},{7,352},{8,128}... | collective-permute-start | bytes 43016 | tf_op jit(solution)/shard_map/ppermute | solution.py:228

commit v3 on v2

--- a/solution.py
+++ b/solution.py
@@ -16,6 +16,7 @@
 BF16 = jnp.bfloat16
 F32 = jnp.float32
 VMEM_LIMIT = 40 * 1024 * 1024
+UNPACK_FLOPS = 2 * 10**10
 
 
 def swap(block, axis):
@@ -55,16 +56,82 @@
     return lax.dot_general(a, b, (((1,), (1,)), ((), ())), preferred_element_type=F32)
 
 
+def unpack_kernel(place, received, kept, latent, rope, sent, packed, piece, rope_out, *, sizes):
+    n_piece, n_all, own_rows, copies = sizes
+    zh, yl = place[0], place[1]
+    four = kept.shape[0]
+    ours = pl.ds(pl.multiple_of(zh * n_all, 16), n_all)
+    theirs = pl.ds(pl.multiple_of((1 - zh) * n_all, 16), n_all)
+    at = n_piece
+    for h in range(four):
+        mine, other = kept[h], received[at : at + n_all]
+        for copy in range(copies):
+            sent[copy, h, ours] = mine
+            sent[copy, h, theirs] = other
+        at += n_all
+    ours = pl.ds(pl.multiple_of(zh * own_rows, 16), own_rows)
+    theirs = pl.ds(pl.multiple_of((1 - zh) * own_rows, 16), own_rows)
+    to = n_piece
+    for i in range(latent.shape[0]):
+        packed[pl.ds(pl.multiple_of(to + zh * own_rows, 16), own_rows)] = latent[i]
+        packed[pl.ds(pl.multiple_of(to + (1 - zh) * own_rows, 16), own_rows)] = received[
+            at : at + own_rows
+        ]
+        to += 2 * own_rows
+        at += own_rows
+    lower = [rope[0], received[at : at + own_rows]]
+    upper = [rope[1], received[at + own_rows : at + 2 * own_rows]]
+    stay = [jnp.where(yl == 0, x, y) for x, y in zip(lower, upper)]
+    go = [jnp.where(yl == 0, y, x) for x, y in zip(lower, upper)]
+    rope_out[ours] = stay[0]
+    rope_out[theirs] = stay[1]
+    packed[pl.ds(pl.multiple_of(to + zh * own_rows, 16), own_rows)] = go[0]
+    packed[pl.ds(pl.multiple_of(to + (1 - zh) * own_rows, 16), own_rows)] = go[1]
+    packed[:n_piece] = received[:n_piece]
+    piece[...] = received[:n_piece]
+
+
 def attend_kernel(
-    starts, latent, weights, rope, lengths, kv0, kv1, kv2, kv3, value_out, scores, *, sizes, temper
+    place,
+    ours,
+    theirs,
+    weights,
+    rope_ours,
+    lengths,
+    kv0,
+    kv1,
+    kv2,
+    kv3,
+    keep_out,
+    give_out,
+    query_rows,
+    rope,
+    scores,
+    *,
+    sizes,
+    temper,
 ):
-    rows, heads, n_uq, n_uk, n_uv, width = sizes
+    rows, heads, n_uq, n_uk, n_uv, width, n_starts = sizes
     caches = (kv0, kv1, kv2, kv3)
+    zh, yl, starts = place[0], place[1], [place[2 + i] for i in range(n_starts)]
     per_block = kv0.shape[1]
-    chunk = per_block * len(caches) // starts.shape[0]
-    query = jnp.concatenate([latent[i] for i in range(latent.shape[0])], axis=1)
+    chunk = per_block * len(caches) // n_starts
+    half = rows // 2
+    mine = pl.ds(pl.multiple_of(yl * half, 16), half)
+    other = pl.ds(pl.multiple_of((1 - yl) * half, 16), half)
+    at = kv0.shape[0]
+    lane_count = ours.shape[1]
+    for i in range(query_rows.shape[1] // lane_count):
+        lanes_here = slice(i * lane_count, (i + 1) * lane_count)
+        query_rows[mine, lanes_here] = ours[at : at + half]
+        query_rows[other, lanes_here] = theirs[at : at + half]
+        at += half
+    rope[mine, :] = rope_ours[...]
+    rope[other, :] = theirs[at : at + half]
+    query = query_rows[...]
     limit = lengths[...]
     lanes = lax.broadcasted_iota(jnp.int32, (rows, chunk), 1)
+    values = []
     for h in range(heads):
         w_uq = weights[:, h, :, 0:n_uq, :].reshape(-1, weights.shape[-1])
         w_uk = weights[:, h, :, n_uq : n_uq + n_uk, :].reshape(-1, weights.shape[-1])
@@ -90,8 +157,19 @@
             context = context + dot_nt(p.astype(BF16), cache[:width, :])
         context = (context / total).astype(BF16)
         w_uv = weights[:, h, :, n_uq + n_uk :, :].reshape(-1, weights.shape[-1])
-        vdim = w_uv.shape[1]
-        value_out[:, h * vdim : (h + 1) * vdim] = dot(context, w_uv).astype(BF16)
+        values.append(dot(context, w_uv).astype(BF16))
+    vdim = values[0].shape[1]
+    wide = heads * vdim
+    to = lax.broadcasted_iota(jnp.int32, (wide, wide), 1)
+    source = lax.broadcasted_iota(jnp.int32, (wide, wide), 0)
+    side = to // (wide // 2)
+    head = to % (wide // 2) // (vdim // 2)
+    item = to % (vdim // 2)
+    wanted = head * vdim + item // 4 * 8 + jnp.where(side == 0, zh, 1 - zh) * 4 + item % 4
+    move = jnp.where(source == wanted, 1.0, 0.0).astype(BF16)
+    moved = dot(jnp.concatenate(values, axis=1), move).astype(BF16)
+    keep_out[...] = moved[:, : wide // 2]
+    give_out[...] = moved[:, wide // 2 :]
 
 
 def project_kernel(values, weights, out):
@@ -131,43 +209,44 @@
     sent = [piece, given, latent, rope_given]
     packed = pack(sent)
     near = swap(cache, "yl")
-    far_piece, taken, latent_far, rope_far = unpack(
-        swap(packed, "zh"), [block.shape for block in sent]
-    )
+    received = swap(pack(sent), "zh")
+    place = jnp.stack([zh, yl]).astype(jnp.int32)
+    vmem = pl.BlockSpec(memory_space=pltpu.VMEM)
+    smem = pl.BlockSpec(memory_space=pltpu.SMEM)
+    n_pack = kv_width + (2 * latent.shape[0] + 2) * own_rows
+    sent, packed, far_piece, rope_kept = pl.pallas_call(
+        lambda *refs: unpack_kernel(*refs, sizes=(kv_width, n_all, own_rows, plane // 2)),
+        out_shape=(
+            jax.ShapeDtypeStruct((plane // 2, four, 2 * n_all, lanes), BF16),
+            jax.ShapeDtypeStruct((n_pack, lanes), BF16),
+            jax.ShapeDtypeStruct((kv_width, quarter), BF16),
+            jax.ShapeDtypeStruct((2 * own_rows, lanes), BF16),
+        ),
+        in_specs=[smem] + [vmem] * 4,
+        out_specs=(vmem,) * 4,
+        compiler_params=pltpu.CompilerParams(vmem_limit_bytes=VMEM_LIMIT),
+        cost_estimate=pl.CostEstimate(
+            flops=UNPACK_FLOPS, bytes_accessed=3 * 10**6, transcendentals=0
+        ),
+        name="unpack",
+    )(place, received, kept, latent, rope_kept)
 
     vpart, width = w_out.shape[1:]
     columns = width // plane
     out_proj = w_out.reshape(heads_in * vpart, plane, columns)
     out_proj = exchange(jnp.transpose(out_proj, (1, 0, 2)), PLANE)
-    out_proj = out_proj.reshape(plane, heads_in, vpart, columns)
-
-    far_piece, taken, latent_far, rope_far, near, out_proj = lax.optimization_barrier(
-        (far_piece, taken, latent_far, rope_far, near, out_proj)
+    sent, packed, far_piece, near, out_proj = lax.optimization_barrier(
+        (sent, packed, far_piece, near, out_proj)
     )
 
-    proj_kept = lax.dynamic_slice_in_dim(out_proj, zh * four, four, 1)
-    proj_given = lax.dynamic_slice_in_dim(out_proj, (1 - zh) * four, four, 1)
-    proj_far = [swap(proj_given[a:b], "zh") for a, b in ((0, 4), (4, 8), (8, 16))]
-
-    stacked = ordered(kept, taken, zh, 1)
-    weights = jnp.broadcast_to(
-        stacked.reshape((1, 2, heads, 2 * n_all, lanes)), (plane // 2, 2, heads, 2 * n_all, lanes)
-    ).reshape(plane * heads, 2 * n_all, lanes)
-    weights = exchange(weights, PLANE).reshape(plane, heads, 2, n_all, lanes)
-
-    latent = ordered(latent, latent_far, zh, 1)
-    rope = ordered(rope_kept, rope_far, zh, 1)
-    rope_kept = lax.dynamic_slice_in_dim(rope, yl, 1, 0)
-    rope_given = lax.dynamic_slice_in_dim(rope, 1 - yl, 1, 0)
-    sent = [far_piece, latent, rope_given]
-    piece_y, latent_y, rope_y = unpack(swap(pack(sent), "yl"), [block.shape for block in sent])
+    weights = exchange(sent.reshape(plane * heads, 2 * n_all, lanes), PLANE)
+    weights = weights.reshape(plane, heads, 2, n_all, lanes)
+
+    packed_y = swap(packed, "yl")
     piece_z = swap(far_piece, "zll")
     piece_yz = lax.ppermute(far_piece, ("yl", "zll"), [(0, 3), (1, 2), (2, 1), (3, 0)])
-    far = jnp.concatenate([far_piece, piece_y, piece_z, piece_yz], axis=1)
-    far, proj_far[0] = lax.optimization_barrier((far, proj_far[0]))
+    far = jnp.concatenate([far_piece, packed_y[:kv_width], piece_z, piece_yz], axis=1)
     far_other = swap(far, "c")
-    latent = ordered(latent, latent_y, yl, 1)
-    rope = ordered(rope_kept[0], rope_y[0], yl, 0)
 
     starts = []
     for ylo in (yl, 1 - yl):
@@ -177,32 +256,36 @@
         for zo in (zll, 1 - zll):
             for ylo in (yl, 1 - yl):
                 starts.append((ylo * 2 + 1 - zh) * tokens + (co * 2 + zo) * quarter)
-    starts = jnp.stack(starts).astype(jnp.int32)
-
-    weights, proj_far[1] = lax.optimization_barrier((weights, proj_far[1]))
-    rows = latent.shape[1]
+    place = jnp.stack([zh, yl] + starts).astype(jnp.int32)
+
+    rows = 4 * own_rows
     sequence = lax.axis_index("x") * 2 + lax.axis_index("yh")
     row_lengths = lax.dynamic_slice_in_dim(lengths, sequence * rows, rows, 0)[:, None]
-    vmem = pl.BlockSpec(memory_space=pltpu.VMEM)
-    values = pl.pallas_call(
+    keep, give = pl.pallas_call(
         lambda *refs: attend_kernel(
-            *refs, sizes=(rows, heads, n_uq, n_uk, n_uv, latent_width), temper=temper
+            *refs,
+            sizes=(rows, heads, n_uq, n_uk, n_uv, latent_width, len(starts)),
+            temper=temper,
         ),
-        out_shape=jax.ShapeDtypeStruct((rows, heads * lanes), BF16),
-        in_specs=[pl.BlockSpec(memory_space=pltpu.SMEM)] + [vmem] * 8,
-        out_specs=vmem,
-        scratch_shapes=[pltpu.VMEM((rows, 4 * tokens), F32)],
+        out_shape=(jax.ShapeDtypeStruct((rows, lanes), BF16),) * 2,
+        in_specs=[smem] + [vmem] * 9,
+        out_specs=(vmem,) * 2,
+        scratch_shapes=[
+            pltpu.VMEM((rows, query_latent.shape[1]), BF16),
+            pltpu.VMEM((rows, lanes), BF16),
+            pltpu.VMEM((rows, 4 * tokens), F32),
+        ],
         compiler_params=pltpu.CompilerParams(vmem_limit_bytes=VMEM_LIMIT),
         cost_estimate=pl.CostEstimate(flops=10**9, bytes_accessed=5 * 10**6, transcendentals=0),
         name="attend",
-    )(starts, latent, weights, rope, row_lengths, cache, near, far, far_other)
-
-    values, proj_far[2] = lax.optimization_barrier((values, proj_far[2]))
-    out_proj = ordered(proj_kept, jnp.concatenate(proj_far, axis=0), zh, 2)
-    out_proj = jnp.transpose(out_proj, (1, 0, 2, 3)).reshape(-1, columns)
+    )(place, packed, packed_y, weights, rope_kept, row_lengths, cache, near, far, far_other)
+
+    values = ordered(keep, swap(give, "zh"), zh, 1)
     gathered = exchange(
         jnp.broadcast_to(values[None], (plane,) + values.shape).reshape(-1, values.shape[1]), PLANE
     ).reshape(plane // 2, 2, rows, heads * lanes)
+    out_proj = out_proj.reshape(plane, 2, 2, heads, vpart, columns)
+    out_proj = jnp.transpose(out_proj, (2, 1, 3, 0, 4, 5)).reshape(-1, columns)
     all_rows = plane // 2 * rows
     partial_out = pl.pallas_call(
         project_kernel,

time: 194 us -> 171 us (0.88)
  starting transfers between devices: 81.1 us -> 64.9 us
  waiting for transfers between devices: 60.3 us -> 51.4 us
  blocking collectives: 29.5 us -> 35.9 us
  other arithmetic: 3.43 us -> 0.37 us
  local copies, waits for them, and re-layouts: 13.2 us -> 10.6 us
  Pallas kernels: 4.84 us -> 6.79 us
    ppermute x8 -> x6, starting transfers between devices: 54.3 us -> 37.5 us  [swap(): return lax.ppermute(block, axis, [(0, 1), (1, 0)])]
    ppermute x8 -> x6, waiting for transfers between devices: 42.5 us -> 33.9 us  [swap(): return lax.ppermute(block, axis, [(0, 1), (1, 0)])]
    all_to_all x2, blocking collectives: 29.5 us -> 35.9 us  [exchange(): return lax.all_to_all(blocks, axes, 0, 0, tiled=True)]
    slice x11 -> x1, local copies, waits for them, and re-layouts: 4.18 us -> 0.01 us  [local(): packed_y[:kv_width]]
  transfers between devices with their start and end apart: 13 -> 11, of which waited for: 7 -> 7; matrix products, arithmetic and copies ran while one was open for 6% -> 2% of each run, Pallas kernels for 2% -> 1%
where the time goes in v3:
time: 171 us; the launch traced here: 170 us
  starting transfers between devices  64.9 us (38%)
  waiting for transfers between devices  51.4 us (30%)
  blocking collectives  35.9 us (21%)
  local copies, waits for them, and re-layouts  10.6 us (6%)
  Pallas kernels  6.79 us (4%)
    ppermute x6, starting transfers between devices, swap(): return lax.ppermute(block, axis, [(0, 1), (1, 0)])  37.5 us
    all_to_all x2, blocking collectives, exchange(): return lax.all_to_all(blocks, axes, 0, 0, tiled=True)  35.9 us
    ppermute x6, waiting for transfers between devices, swap(): return lax.ppermute(block, axis, [(0, 1), (1, 0)])  33.9 us
    all_to_all x3, starting transfers between devices, exchange(): return lax.all_to_all(blocks, axes, 0, 0, tiled=True)  21.7 us
    ppermute x1, waiting for transfers between devices, local(): return lax.ppermute(total, AXES, route)  9.94 us
    all_to_all x3, waiting for transfers between devices, exchange(): return lax.all_to_all(blocks, axes, 0, 0, tiled=True)  7.57 us
    pallas_call x1, Pallas kernels, local(): pl.pallas_call(lambda *refs: attend_kernel(*refs, sizes=(rows, heads, n_u...  4.53 us
  transfers between devices with their start and end apart: 11, of which 7 were waited for; matrix products, arithmetic and copies ran while one was open for 2% of the time, Pallas kernels for 1%

profile of v3, /device:TPU:38, one launch (start us, length us, event | category | flops | bytes accessed | tf_op | source)
XLA Modules:
  0.0 170.4 jit_solution(7050660372749896856)
XLA Ops:
  0.0 0.9 reshape.78
  1.0 0.9 constant_dynamic-update-slice_fusion.2
  1.9 0.9 dynamic-slice_bitcast_fusion
  2.8 0.8 constant_dynamic-update-slice_fusion.1
  3.6 0.8 constant_dynamic-update-slice_fusion
  4.4 14.8 %collective-permute-start = (bf16[1120,128]{1,0:T(8,128)(2,1)S(1)}, bf16[1120,128]{1,0:T(8,128)(2,1)S(1)}, u32[]{:S(2)}, u32[]{:S(2)}) collective-permute-start(bf16[1120,128]{1,0:T(8,128)(2,1)S(1)} %pad_maximum_fusion.1), channel_id=1, source_target_pairs={{0,16},{16,0},{1,17},{17,1},{2,18},{18,2},{3,19},{19,3},{4,20},{20... | collective-permute-start | bytes 860168 | tf_op jit(solution)/shard_map/ppermute | solution.py:23
  19.2 0.5 reshape.80
  19.8 0.0 copy-start.1
  19.8 1.1 copy.41
  20.9 7.4 %all-to-all-start = ((bf16[16,32,448]{2,1,0:T(8,128)(2,1)}), bf16[16,32,448]{2,1,0:T(8,128)(2,1)S(1)}, u32[]{:S(2)}, u32[]{:S(2)}) async-start(bf16[16,32,448]{2,1,0:T(8,128)(2,1)} %copy.41), calls=%async_computation | async-start | bytes 1048576 | tf_op jit(solution)/shard_map/all_to_all | solution.py:48
  28.3 3.4 %collective-permute-start.1 = (bf16[576,512]{1,0:T(8,128)(2,1)S(1)}, bf16[576,512]{1,0:T(8,128)(2,1)S(1)}, u32[]{:S(2)}, u32[]{:S(2)}) collective-permute-start(bf16[576,512]{1,0:T(8,128)(2,1)S(1)} %bitcast.53), channel_id=1, source_target_pairs={{0,32},{32,0},{1,33},{33,1},{2,34},{34,2},{3,35},{35,3},{4,36},{36... | collective-permute-start | bytes 1769480 | tf_op jit(solution)/shard_map/ppermute | solution.py:23
  31.7 0.1 pad_add_fusion.refs_0_
  31.8 12.7 %collective-permute-done.refs_1_ = bf16[1120,128]{1,0:T(8,128)(2,1)S(1)} collective-permute-done((bf16[1120,128]{1,0:T(8,128)(2,1)S(1)}, bf16[1120,128]{1,0:T(8,128)(2,1)S(1)}, u32[]{:S(2)}, u32[]{:S(2)}) %collective-permute-start) | collective-permute-done | bytes 286752 | tf_op jit(solution)/shard_map/ppermute | solution.py:23
  44.5 1.8 %unpack.1 = (bf16[8,4,160,128]{3,2,1,0:T(8,128)(2,1)}, bf16[992,128]{1,0:T(8,128)(2,1)S(1)}, bf16[576,128]{1,0:T(8,128)(2,1)S(1)}, bf16[32,128]{1,0:T(8,128)(2,1)S(1)}) custom-call(s32[2]{0:T(128)S(1)} %pad_add_fusion.refs_0_, bf16[1120,128]{1,0:T(8,128)(2,1)S(1)} %collective-permute-done.refs_1_, bf16[4,80,128]{2,1,0:T(8,128)(2,1)S(1)} %get-tuple-element.27.refs_2_, ...), custom_call_target="tpu_custom_call" | custom-call | flops 20000000000 | bytes 3000000 | tf_op jit(solution)/shard_map/unpack/pallas_call | solution.py:217
  46.3 1.8 %collective-permute-done.1.refs_7_ = bf16[576,512]{1,0:T(8,128)(2,1)S(1)} collective-permute-done((bf16[576,512]{1,0:T(8,128)(2,1)S(1)}, bf16[576,512]{1,0:T(8,128)(2,1)S(1)}, u32[]{:S(2)}, u32[]{:S(2)}) %collective-permute-start.1) | collective-permute-done | bytes 589856 | tf_op jit(solution)/shard_map/ppermute | solution.py:23
  48.1 7.2 %all-to-all-start.1 = ((bf16[32,160,128]{2,1,0:T(8,128)(2,1)}), bf16[32,160,128]{2,1,0:T(8,128)(2,1)S(1)}, u32[]{:S(2)}, u32[]{:S(2)}) async-start(bf16[32,160,128]{2,1,0:T(8,128)(2,1)} %bitcast.27), calls=%async_computation.1 | async-start | bytes 2621440 | tf_op jit(solution)/shard_map/all_to_all | solution.py:48
  55.3 3.4 %collective-permute-start.2 = (bf16[992,128]{1,0:T(8,128)(2,1)S(1)}, bf16[992,128]{1,0:T(8,128)(2,1)S(1)}, u32[]{:S(2)}, u32[]{:S(2)}) collective-permute-start(bf16[992,128]{1,0:T(8,128)(2,1)S(1)} %get-tuple-element.19.refs_1_), channel_id=1, source_target_pairs={{0,32},{32,0},{1,33},{33,1},{2,34},{34,2},{3,35},{35,3},{4,36},{36... | collective-permute-start | bytes 761864 | tf_op jit(solution)/shard_map/ppermute | solution.py:23
  58.6 2.9 %collective-permute-start.4 = (bf16[576,128]{1,0:T(8,128)(2,1)S(1)}, bf16[576,128]{1,0:T(8,128)(2,1)S(1)}, u32[]{:S(2)}, u32[]{:S(2)}) collective-permute-start(bf16[576,128]{1,0:T(8,128)(2,1)S(1)} %get-tuple-element.23), channel_id=1, source_target_pairs={{0,34},{2,32},{32,2},{34,0},{1,35},{3,33},{33,3},{35,1},{4,38},{6,... | collective-permute-start | bytes 442376 | tf_op jit(solution)/shard_map/ppermute | solution.py:247
  61.6 2.9 %collective-permute-start.3 = (bf16[576,128]{1,0:T(8,128)(2,1)S(1)}, bf16[576,128]{1,0:T(8,128)(2,1)S(1)}, u32[]{:S(2)}, u32[]{:S(2)}) collective-permute-start(bf16[576,128]{1,0:T(8,128)(2,1)S(1)} %get-tuple-element.23), channel_id=1, source_target_pairs={{0,2},{2,0},{1,3},{3,1},{4,6},{6,4},{5,7},{7,5},{8,10},{10,8},{9,1... | collective-permute-start | bytes 442376 | tf_op jit(solution)/shard_map/ppermute | solution.py:23
  64.5 14.9 %collective-permute-done.2.refs_2_ = bf16[992,128]{1,0:T(8,128)(2,1)S(1)} collective-permute-done((bf16[992,128]{1,0:T(8,128)(2,1)S(1)}, bf16[992,128]{1,0:T(8,128)(2,1)S(1)}, u32[]{:S(2)}, u32[]{:S(2)}) %collective-permute-start.2) | collective-permute-done | bytes 253984 | tf_op jit(solution)/shard_map/ppermute | solution.py:23
  79.5 0.0 collective-permute-done.4
  79.5 0.0 collective-permute-done.3
  79.5 0.1 pad_maximum_fusion.refs_8_
  79.6 1.9 %collective-permute-start.5 = (bf16[576,512]{1,0:T(8,128)(2,1)S(1)}, bf16[576,512]{1,0:T(8,128)(2,1)}, u32[]{:S(2)}, u32[]{:S(2)}) collective-permute-start(bf16[576,512]{1,0:T(8,128)(2,1)S(1)} %pad_maximum_fusion.refs_8_), channel_id=1, source_target_pairs={{0,1},{1,0},{2,3},{3,2},{4,5},{5,4},{6,7},{7,6},{8,9},{9,8},{10,11... | collective-permute-start | bytes 1769480 | tf_op jit(solution)/shard_map/ppermute | solution.py:23
  81.5 0.8 dynamic-slice_bitcast_fusion.2
  82.3 0.1 copy.42.refs_5_
  82.4 0.1 stack.80.refs_0_
  82.5 1.1 collective-permute-done.5.refs_9_
  83.6 0.9 copy-done.3
  84.5 4.5 %attend.1 = (bf16[64,128]{1,0:T(8,128)(2,1)S(1)}, bf16[64,128]{1,0:T(8,128)(2,1)S(1)}) custom-call(s32[18]{0:T(128)S(1)} %stack.80.refs_0_, bf16[992,128]{1,0:T(8,128)(2,1)S(1)} %copy-done.3, bf16[992,128]{1,0:T(8,128)(2,1)S(1)} %collective-permute-done.2.refs_2_, bf16[16,2,2,80,128]{4,3,2,1,0:T(8,128)(2,1)S(1)} %bitcast.50, ...), custom_call_target="tpu_custom_call" | custom-call | flops 1000000000 | bytes 5000000 | tf_op jit(solution)/shard_map/attend/pallas_call | solution.py:264
  89.1 11.0 %collective-permute-start.6 = (bf16[64,128]{1,0:T(8,128)(2,1)S(1)}, bf16[64,128]{1,0:T(8,128)(2,1)S(1)}, u32[]{:S(2)}, u32[]{:S(2)}) collective-permute-start(bf16[64,128]{1,0:T(8,128)(2,1)S(1)} %get-tuple-element.24), channel_id=1, source_target_pairs={{0,16},{16,0},{1,17},{17,1},{2,18},{18,2},{3,19},{19,3},{4,20},{20... | collective-permute-start | bytes 49160 | tf_op jit(solution)/shard_map/ppermute | solution.py:23
  100.1 3.4 %collective-permute-done.6 = bf16[64,128]{1,0:T(8,128)(2,1)S(1)} collective-permute-done((bf16[64,128]{1,0:T(8,128)(2,1)S(1)}, bf16[64,128]{1,0:T(8,128)(2,1)S(1)}, u32[]{:S(2)}, u32[]{:S(2)}) %collective-permute-start.6) | collective-permute-done | bytes 16416 | tf_op jit(solution)/shard_map/ppermute | solution.py:23
  103.6 0.8 broadcast_in_dim.10
  104.4 7.1 %all-to-all-start.2 = ((bf16[16,64,256]{2,1,0:T(8,128)(2,1)}), bf16[16,64,256]{2,1,0:T(8,128)(2,1)S(1)}, u32[]{:S(2)}, u32[]{:S(2)}) async-start(bf16[16,64,256]{2,1,0:T(8,128)(2,1)} %broadcast_in_dim.10), calls=%async_computation.2 | async-start | bytes 1048576 | tf_op jit(solution)/shard_map/all_to_all | solution.py:48
  111.5 0.3 copy.43
  111.8 0.4 copy.44
  112.2 0.3 reshape.85.weights
  112.5 7.6 %all-to-all-done.2 = bf16[16,64,256]{2,1,0:T(8,128)(2,1)S(1)} async-done(((bf16[16,64,256]{2,1,0:T(8,128)(2,1)}), bf16[16,64,256]{2,1,0:T(8,128)(2,1)S(1)}, u32[]{:S(2)}, u32[]{:S(2)}) %all-to-all-start.2) | async-done | bytes 524320 | tf_op jit(solution)/shard_map/all_to_all | solution.py:48
  120.1 0.4 project.1
  120.5 0.2 copy.45
  120.7 4.1 %all_to_all.34 = bf16[2,256,448]{1,2,0:T(8,128)(2,1)S(1)} all-to-all(bf16[2,256,448]{1,2,0:T(8,128)(2,1)S(1)} %copy.45), channel_id=1, replica_groups=mesh['x'=4,'yh'=2,'yl'=2,'zh'=2,'zlh'=4,'zll'=2,'c'=2] {'c'}, dimensions={0} | all-to-all | bytes 917504 | tf_op jit(solution)/shard_map/all_to_all | solution.py:48
  124.8 0.1 reduce_sum.24
  125.0 0.1 copy.46
  125.1 31.8 %all_to_all.35 = bf16[16,16,448]{2,1,0:T(8,128)(2,1)S(1)} all-to-all(bf16[16,16,448]{2,1,0:T(8,128)(2,1)S(1)} %bitcast.58), channel_id=1, replica_groups=mesh['x'=4,'yh'=2,'yl'=2,'zh'=2,'zlh'=4,'zll'=2,'c'=2] {'zlh','zll','zh'}, dimensions={0} | all-to-all | bytes 458752 | tf_op jit(solution)/shard_map/all_to_all | solution.py:48
  156.9 0.1 reduce_sum.25
  156.9 2.9 %collective-permute-start.7 = (bf16[16,448]{1,0:T(8,128)(2,1)S(1)}, bf16[16,448]{1,0:T(8,128)(2,1)S(1)}, u32[]{:S(2)}, u32[]{:S(2)}) collective-permute-start(bf16[16,448]{1,0:T(8,128)(2,1)S(1)} %reduce_sum.25), channel_id=1, source_target_pairs={{0,0},{1,256},{2,32},{3,288},{4,64},{5,320},{6,96},{7,352},{8,128}... | collective-permute-start | bytes 43016 | tf_op jit(solution)/shard_map/ppermute | solution.py:311
  159.8 9.9 %collective-permute-done.7 = bf16[16,448]{1,0:T(8,128)(2,1)S(1)} collective-permute-done((bf16[16,448]{1,0:T(8,128)(2,1)S(1)}, bf16[16,448]{1,0:T(8,128)(2,1)S(1)}, u32[]{:S(2)}, u32[]{:S(2)}) %collective-permute-start.7) | collective-permute-done | bytes 14368 | tf_op jit(solution)/shard_map/ppermute | solution.py:311
  169.8 0.6 copy.57
  (22 shorter events, 0.1 us)
Async XLA Ops:
  0.0 1.0 copy-start
  0.0 19.2 %copy-start.6 = (bf16[8,4,7168]{2,1,0:T(4,128)(2,1)S(1)}, bf16[8,4,7168]{2,1,0:T(4,128)(2,1)}, u32[]{:S(2)}) copy-start(bf16[8,4,7168]{2,1,0:T(4,128)(2,1)} %param.15) | copy-start | bytes 1376260
  4.4 40.1 %collective-permute-start = (bf16[1120,128]{1,0:T(8,128)(2,1)S(1)}, bf16[1120,128]{1,0:T(8,128)(2,1)S(1)}, u32[]{:S(2)}, u32[]{:S(2)}) collective-permute-start(bf16[1120,128]{1,0:T(8,128)(2,1)S(1)} %pad_maximum_fusion.1), channel_id=1, source_target_pairs={{0,16},{16,0},{1,17},{17,1},{2,18},{18,2},{3,19},{19,3},{4,20},{20... | collective-permute-start | bytes 860168 | tf_op jit(solution)/shard_map/ppermute | solution.py:23
  19.8 8.5 %copy-start.1 = (bf16[512,576]{0,1:T(8,128)(2,1)S(1)}, bf16[512,576]{0,1:T(8,128)(2,1)}, u32[]{:S(2)}) copy-start(bf16[512,576]{0,1:T(8,128)(2,1)} %param.11) | copy-start | bytes 1769476
  20.9 25.4 %all-to-all-start = ((bf16[16,32,448]{2,1,0:T(8,128)(2,1)}), bf16[16,32,448]{2,1,0:T(8,128)(2,1)S(1)}, u32[]{:S(2)}, u32[]{:S(2)}) async-start(bf16[16,32,448]{2,1,0:T(8,128)(2,1)} %copy.41), calls=%async_computation | async-start | bytes 1048576 | tf_op jit(solution)/shard_map/all_to_all | solution.py:48
  28.3 19.8 %collective-permute-start.1 = (bf16[576,512]{1,0:T(8,128)(2,1)S(1)}, bf16[576,512]{1,0:T(8,128)(2,1)S(1)}, u32[]{:S(2)}, u32[]{:S(2)}) collective-permute-start(bf16[576,512]{1,0:T(8,128)(2,1)S(1)} %bitcast.53), channel_id=1, source_target_pairs={{0,32},{32,0},{1,33},{33,1},{2,34},{34,2},{3,35},{35,3},{4,36},{36... | collective-permute-start | bytes 1769480 | tf_op jit(solution)/shard_map/ppermute | solution.py:23
  46.3 9.0 %copy-start.2 = (bf16[992,128]{1,0:T(8,128)(2,1)}, bf16[992,128]{1,0:T(8,128)(2,1)S(1)}, u32[]{:S(2)}) copy-start(bf16[992,128]{1,0:T(8,128)(2,1)S(1)} %get-tuple-element.19.refs_1_) | copy-start | bytes 761860
  46.3 1.8 %copy-start.4 = (bf16[16,32,448]{2,1,0:T(8,128)(2,1)}, bf16[16,32,448]{2,1,0:T(8,128)(2,1)S(1)}, u32[]{:S(2)}) copy-start(bf16[16,32,448]{2,1,0:T(8,128)(2,1)S(1)} %all-to-all-done) | copy-start | bytes 1376260
  48.1 35.5 %all-to-all-start.1 = ((bf16[32,160,128]{2,1,0:T(8,128)(2,1)}), bf16[32,160,128]{2,1,0:T(8,128)(2,1)S(1)}, u32[]{:S(2)}, u32[]{:S(2)}) async-start(bf16[32,160,128]{2,1,0:T(8,128)(2,1)} %bitcast.27), calls=%async_computation.1 | async-start | bytes 2621440 | tf_op jit(solution)/shard_map/all_to_all | solution.py:48
  55.3 24.2 %collective-permute-start.2 = (bf16[992,128]{1,0:T(8,128)(2,1)S(1)}, bf16[992,128]{1,0:T(8,128)(2,1)S(1)}, u32[]{:S(2)}, u32[]{:S(2)}) collective-permute-start(bf16[992,128]{1,0:T(8,128)(2,1)S(1)} %get-tuple-element.19.refs_1_), channel_id=1, source_target_pairs={{0,32},{32,0},{1,33},{33,1},{2,34},{34,2},{3,35},{35,3},{4,36},{36... | collective-permute-start | bytes 761864 | tf_op jit(solution)/shard_map/ppermute | solution.py:23
  58.6 20.8 %collective-permute-start.4 = (bf16[576,128]{1,0:T(8,128)(2,1)S(1)}, bf16[576,128]{1,0:T(8,128)(2,1)S(1)}, u32[]{:S(2)}, u32[]{:S(2)}) collective-permute-start(bf16[576,128]{1,0:T(8,128)(2,1)S(1)} %get-tuple-element.23), channel_id=1, source_target_pairs={{0,34},{2,32},{32,2},{34,0},{1,35},{3,33},{33,3},{35,1},{4,38},{6,... | collective-permute-start | bytes 442376 | tf_op jit(solution)/shard_map/ppermute | solution.py:247
  61.6 17.9 %collective-permute-start.3 = (bf16[576,128]{1,0:T(8,128)(2,1)S(1)}, bf16[576,128]{1,0:T(8,128)(2,1)S(1)}, u32[]{:S(2)}, u32[]{:S(2)}) collective-permute-start(bf16[576,128]{1,0:T(8,128)(2,1)S(1)} %get-tuple-element.23), channel_id=1, source_target_pairs={{0,2},{2,0},{1,3},{3,1},{4,6},{6,4},{5,7},{7,5},{8,10},{10,8},{9,1... | collective-permute-start | bytes 442376 | tf_op jit(solution)/shard_map/ppermute | solution.py:23
  79.6 4.0 %collective-permute-start.5 = (bf16[576,512]{1,0:T(8,128)(2,1)S(1)}, bf16[576,512]{1,0:T(8,128)(2,1)}, u32[]{:S(2)}, u32[]{:S(2)}) collective-permute-start(bf16[576,512]{1,0:T(8,128)(2,1)S(1)} %pad_maximum_fusion.refs_8_), channel_id=1, source_target_pairs={{0,1},{1,0},{2,3},{3,2},{4,5},{5,4},{6,7},{7,6},{8,9},{9,8},{10,11... | collective-permute-start | bytes 1769480 | tf_op jit(solution)/shard_map/ppermute | solution.py:23
  83.6 0.9 copy-start.3
  89.1 22.4 %copy-start.5 = (bf16[16,32,448]{2,1,0:T(8,128)(2,1)S(1)}, bf16[16,32,448]{2,1,0:T(8,128)(2,1)}, u32[]{:S(2)}) copy-start(bf16[16,32,448]{2,1,0:T(8,128)(2,1)} %copy-done.4) | copy-start | bytes 1376260
  89.1 14.5 %collective-permute-start.6 = (bf16[64,128]{1,0:T(8,128)(2,1)S(1)}, bf16[64,128]{1,0:T(8,128)(2,1)S(1)}, u32[]{:S(2)}, u32[]{:S(2)}) collective-permute-start(bf16[64,128]{1,0:T(8,128)(2,1)S(1)} %get-tuple-element.24), channel_id=1, source_target_pairs={{0,16},{16,0},{1,17},{17,1},{2,18},{18,2},{3,19},{19,3},{4,20},{20... | collective-permute-start | bytes 49160 | tf_op jit(solution)/shard_map/ppermute | solution.py:23
  104.4 15.6 %all-to-all-start.2 = ((bf16[16,64,256]{2,1,0:T(8,128)(2,1)}), bf16[16,64,256]{2,1,0:T(8,128)(2,1)S(1)}, u32[]{:S(2)}, u32[]{:S(2)}) async-start(bf16[16,64,256]{2,1,0:T(8,128)(2,1)} %broadcast_in_dim.10), calls=%async_computation.2 | async-start | bytes 1048576 | tf_op jit(solution)/shard_map/all_to_all | solution.py:48
  156.9 12.8 %collective-permute-start.7 = (bf16[16,448]{1,0:T(8,128)(2,1)S(1)}, bf16[16,448]{1,0:T(8,128)(2,1)S(1)}, u32[]{:S(2)}, u32[]{:S(2)}) collective-permute-start(bf16[16,448]{1,0:T(8,128)(2,1)S(1)} %reduce_sum.25), channel_id=1, source_target_pairs={{0,0},{1,256},{2,32},{3,288},{4,64},{5,320},{6,96},{7,352},{8,128}... | collective-permute-start | bytes 43016 | tf_op jit(solution)/shard_map/ppermute | solution.py:311

commit v4 on v3

v4 whole, which is shorter than its diff:
```python
import math

import jax
import jax.numpy as jnp
from jax import lax
from jax.experimental import pallas as pl
from jax.experimental.pallas import tpu as pltpu
from jax.sharding import Mesh, PartitionSpec as P

AXES = ("x", "yh", "yl", "zh", "zlh", "zll", "c")
SIZES = (4, 2, 2, 2, 4, 2, 2)
FSDP = ("x", "yh", "yl", "zh")
HEAD = ("zlh", "zll", "c")
PLANE = ("x", "yh", "yl")
COLUMN = ("zlh", "zll", "zh")
BF16 = jnp.bfloat16
F32 = jnp.float32
VMEM_LIMIT = 40 * 1024 * 1024
PACK_LIMIT = 60 * 1024 * 1024
UNPACK_FLOPS = 2 * 10**10


def swap(block, axis):
    return lax.ppermute(block, axis, [(0, 1), (1, 0)])


def exchange(blocks, axes):
    return lax.all_to_all(blocks, axes, 0, 0, tiled=True)


def dot(a, b):
    return jnp.dot(a, b, preferred_element_type=F32)


def dot_nt(a, b):
    return lax.dot_general(a, b, (((1,), (1,)), ((), ())), preferred_element_type=F32)


def head_pairs(rope):
    return [
        jnp.concatenate([rope[:, 2 * p, :], rope[:, 2 * p + 1, :]], axis=1)
        for p in range(rope.shape[1] // 2)
    ]


def pack_kernel(
    place, cache, w_uq, w_uk, w_uv, latent, rope, out, half_out, uq, uk, uv, latent_in, rope_in, sems
):
    zh, quarter = place[0], place[2]
    lanes, wide = out.shape[1], half_out.shape[1]
    width = cache.shape[0]
    four = uq.shape[0]
    given = pl.ds((1 - zh) * four, four)
    copies = [
        (cache.at[:, pl.ds(pl.multiple_of(quarter * lanes, lanes), lanes)], out.at[pl.ds(0, width)]),
        (w_uq.at[given], uq),
        (w_uk.at[given], uk),
        (w_uv.at[given], uv),
        (latent, latent_in),
        (rope, rope_in),
        (cache.at[:, pl.ds(pl.multiple_of(place[3] * wide, wide), wide)], half_out),
    ]
    copies = [pltpu.make_async_copy(x, y, sems.at[i]) for i, (x, y) in enumerate(copies)]
    for copy in copies:
        copy.start()
    for copy in copies:
        copy.wait()
    at = width
    for h in range(four):
        for w in (uq, uk, uv):
            out[at : at + w.shape[1]] = w[h]
            at += w.shape[1]
    rows = latent_in.shape[0]
    for i in range(latent_in.shape[1] // lanes):
        out[at : at + rows] = latent_in[:, i * lanes : (i + 1) * lanes]
        at += rows
    pairs = head_pairs(rope_in)
    for p in range(len(pairs) // 2):
        out[at : at + rows] = jnp.where(zh == 0, pairs[p + len(pairs) // 2], pairs[p])
        at += rows


def unpack_kernel(
    place, received, w_uq, w_uk, w_uv, latent, rope, sent, packed, piece, rope_out, *, sizes
):
    n_piece, copies = sizes
    zh, yl = place[0], place[1]
    four = w_uq.shape[0] // 2
    n_all = w_uq.shape[1] + w_uk.shape[1] + w_uv.shape[1]
    own_rows = latent.shape[0]
    lanes = packed.shape[1]
    theirs = pl.ds(pl.multiple_of((1 - zh) * n_all, 16), n_all)
    at = n_piece
    for h in range(four):
        other = received[at : at + n_all]
        for copy in range(copies):
            sent[copy, h, theirs] = other
        at += n_all
        to = zh * n_all
        for w in (w_uq, w_uk, w_uv):
            mine = w[zh * four + h]
            for copy in range(copies):
                sent[copy, h, pl.ds(pl.multiple_of(to, 16), w.shape[1])] = mine
            to += w.shape[1]
    ours = pl.ds(pl.multiple_of(zh * own_rows, 16), own_rows)
    theirs = pl.ds(pl.multiple_of((1 - zh) * own_rows, 16), own_rows)
    to = n_piece
    for i in range(latent.shape[1] // lanes):
        packed[pl.ds(pl.multiple_of(to + zh * own_rows, 16), own_rows)] = latent[
            :, i * lanes : (i + 1) * lanes
        ]
        packed[pl.ds(pl.multiple_of(to + (1 - zh) * own_rows, 16), own_rows)] = received[
            at : at + own_rows
        ]
        to += 2 * own_rows
        at += own_rows
    pairs = head_pairs(rope)
    lower = [jnp.where(zh == 0, pairs[0], pairs[2]), received[at : at + own_rows]]
    upper = [jnp.where(zh == 0, pairs[1], pairs[3]), received[at + own_rows : at + 2 * own_rows]]
    stay = [jnp.where(yl == 0, x, y) for x, y in zip(lower, upper)]
    go = [jnp.where(yl == 0, y, x) for x, y in zip(lower, upper)]
    rope_out[ours] = stay[0]
    rope_out[theirs] = stay[1]
    packed[pl.ds(pl.multiple_of(to + zh * own_rows, 16), own_rows)] = go[0]
    packed[pl.ds(pl.multiple_of(to + (1 - zh) * own_rows, 16), own_rows)] = go[1]
    packed[:n_piece] = received[:n_piece]
    piece[...] = received[:n_piece]


def attend_kernel(
    place,
    ours,
    theirs,
    weights,
    rope_ours,
    lengths,
    kv0,
    kv1,
    kv2,
    kv3,
    kv4,
    value_out,
    query_rows,
    rope,
    scores,
    *,
    sizes,
    temper,
):
    rows, heads, n_uq, n_uk, n_uv, width, n_starts = sizes
    caches = (kv0, kv1, kv2, kv3, kv4)
    yl, starts = place[1], [place[3 + i] for i in range(n_starts)]
    spans, tokens = [], 0
    for cache in caches:
        spans.append((tokens, tokens + cache.shape[1]))
        tokens += cache.shape[1]
    chunk = tokens // n_starts
    half = rows // 2
    mine = pl.ds(pl.multiple_of(yl * half, 16), half)
    other = pl.ds(pl.multiple_of((1 - yl) * half, 16), half)
    at = kv0.shape[0]
    lane_count = ours.shape[1]
    for i in range(query_rows.shape[1] // lane_count):
        lanes_here = slice(i * lane_count, (i + 1) * lane_count)
        query_rows[mine, lanes_here] = ours[at : at + half]
        query_rows[other, lanes_here] = theirs[at : at + half]
        at += half
    rope[mine, :] = rope_ours[...]
    rope[other, :] = theirs[at : at + half]
    query = query_rows[...]
    limit = lengths[...]
    lanes = lax.broadcasted_iota(jnp.int32, (rows, chunk), 1)
    values = []
    for h in range(heads):
        w_uq = weights[:, h, :, 0:n_uq, :].reshape(-1, weights.shape[-1])
        w_uk = weights[:, h, :, n_uq : n_uq + n_uk, :].reshape(-1, weights.shape[-1])
        q_nope = dot(query, w_uq).astype(BF16)
        q_lat = dot_nt(q_nope, w_uk).astype(BF16)
        rope_width = kv0.shape[0] - width
        q_rope = rope[:, h * rope_width : (h + 1) * rope_width]
        top = jnp.full((rows, 1), -1e30, F32)
        for (begin, end), cache in zip(spans, caches):
            s = dot(q_lat, cache[:width, :]) + dot(q_rope, cache[width:, :])
            s = s * temper
            for k in range(begin // chunk, end // chunk):
                piece = s[:, k * chunk - begin : (k + 1) * chunk - begin]
                piece = jnp.where(lanes + starts[k] < limit, piece, -1e30)
                top = jnp.maximum(top, jnp.max(piece, axis=1, keepdims=True))
                scores[:, k * chunk : (k + 1) * chunk] = piece
        total = jnp.zeros((rows, 1), F32)
        context = jnp.zeros((rows, width), F32)
        for (begin, end), cache in zip(spans, caches):
            p = jnp.exp(scores[:, begin:end] - top)
            total = total + jnp.sum(p, axis=1, keepdims=True)
            context = context + dot_nt(p.astype(BF16), cache[:width, :])
        context = (context / total).astype(BF16)
        w_uv = weights[:, h, :, n_uq + n_uk :, :].reshape(-1, weights.shape[-1])
        values.append(dot(context, w_uv).astype(BF16))
    vdim = values[0].shape[1]
    wide = heads * vdim
    to = lax.broadcasted_iota(jnp.int32, (wide, wide), 1)
    source = lax.broadcasted_iota(jnp.int32, (wide, wide), 0)
    head = to % (wide // 2) // (vdim // 2)
    item = to % (vdim // 2)
    wanted = head * vdim + item // 4 * 8 + to // (wide // 2) * 4 + item % 4
    move = jnp.where(source == wanted, 1.0, 0.0).astype(BF16)
    moved = dot(jnp.concatenate(values, axis=1), move).astype(BF16)
    for z in range(2):
        for c in range(2):
            value_out[z * 2 + c] = moved[
                c * half : (c + 1) * half, z * wide // 2 : (z + 1) * wide // 2
            ]


def project_kernel(place, values, ours, theirs, out):
    core = place[3]
    lanes = values.shape[-1]
    total = None
    for y in range(values.shape[1]):
        for z in range(2):
            for weights, c in ((ours, core), (theirs, 1 - core)):
                rows = values[:, y, z * 2 + c].reshape(-1, lanes)
                part = dot(rows, weights[y, z])
                total = part if total is None else total + part
    out[...] = total.astype(BF16)


def local(query_latent, query_rope, lengths, kv_cache, w_uq, w_uk, w_uv, w_out):
    yl, zh, zll, core = (lax.axis_index(a) for a in ("yl", "zh", "zll", "c"))
    plane = 16
    cache = kv_cache.T
    kv_width, tokens = cache.shape
    latent_width = w_uk.shape[1] * 32
    rope_width = kv_width - latent_width
    lanes = w_uq.shape[2]
    temper = 1.0 / math.sqrt(lanes + rope_width)
    n_uq, n_uk, n_uv = w_uq.shape[1], w_uk.shape[1], w_uv.shape[1]
    n_all = n_uq + n_uk + n_uv
    own_rows = query_latent.shape[0]
    heads_in = w_uq.shape[0]
    four, heads = heads_in // 2, heads_in // 4

    quarter = tokens // 4
    starts = []
    for i in range(4):
        starts.append((yl * 2 + zh) * tokens + i * quarter)
    for co in (core, 1 - core):
        for i in range(2):
            starts.append(((1 - yl) * 2 + zh) * tokens + (co * 2 + i) * quarter)
    for co in (core, 1 - core):
        for zo in (zll, 1 - zll):
            for ylo in (yl, 1 - yl):
                starts.append((ylo * 2 + 1 - zh) * tokens + (co * 2 + zo) * quarter)
    place = jnp.stack([zh, yl, core * 2 + zll, core]).astype(jnp.int32)
    vmem = pl.BlockSpec(memory_space=pltpu.VMEM)
    smem = pl.BlockSpec(memory_space=pltpu.SMEM)
    raw = (w_uq, w_uk, w_uv, query_latent, query_rope)
    latent_chunks = query_latent.shape[1] // lanes
    n_sent = kv_width + four * n_all + (latent_chunks + 2) * own_rows
    packed, near = pl.pallas_call(
        pack_kernel,
        out_shape=(
            jax.ShapeDtypeStruct((n_sent, lanes), BF16),
            jax.ShapeDtypeStruct((kv_width, tokens // 2), BF16),
        ),
        in_specs=[smem] + [pl.BlockSpec(memory_space=pltpu.HBM)] * 6,
        out_specs=(vmem,) * 2,
        scratch_shapes=[pltpu.VMEM((four,) + w.shape[1:], BF16) for w in raw[:3]]
        + [pltpu.VMEM(x.shape, BF16) for x in raw[3:]]
        + [pltpu.SemaphoreType.DMA((7,))],
        compiler_params=pltpu.CompilerParams(vmem_limit_bytes=PACK_LIMIT),
        cost_estimate=pl.CostEstimate(flops=10**6, bytes_accessed=10**6, transcendentals=0),
        name="pack",
    )(place, cache, *raw)
    near = swap(near, "yl")
    received = swap(packed, "zh")
    n_pack = kv_width + (2 * latent_chunks + 2) * own_rows
    sent, packed, far_piece, rope_kept = pl.pallas_call(
        lambda *refs: unpack_kernel(*refs, sizes=(kv_width, plane // 2)),
        out_shape=(
            jax.ShapeDtypeStruct((plane // 2, four, 2 * n_all, lanes), BF16),
            jax.ShapeDtypeStruct((n_pack, lanes), BF16),
            jax.ShapeDtypeStruct((kv_width, quarter), BF16),
            jax.ShapeDtypeStruct((2 * own_rows, lanes), BF16),
        ),
        in_specs=[smem] + [vmem] * 6,
        out_specs=(vmem,) * 4,
        compiler_params=pltpu.CompilerParams(vmem_limit_bytes=VMEM_LIMIT),
        cost_estimate=pl.CostEstimate(
            flops=UNPACK_FLOPS, bytes_accessed=3 * 10**6, transcendentals=0
        ),
        name="unpack",
    )(place, received, *raw)

    vpart, width = w_out.shape[1:]
    columns = width // plane
    out_proj = w_out.reshape(heads_in * vpart, plane, columns)
    out_proj = exchange(jnp.transpose(out_proj, (1, 0, 2)), PLANE)
    sent, packed, far_piece, near, out_proj = lax.optimization_barrier(
        (sent, packed, far_piece, near, out_proj)
    )
    out_proj = out_proj.reshape(plane, 2, 2, heads, vpart, columns)
    out_proj = jnp.transpose(out_proj, (2, 1, 3, 0, 4, 5)).reshape(2, 2, -1, columns)

    weights = exchange(sent.reshape(plane * heads, 2 * n_all, lanes), PLANE)
    weights = weights.reshape(plane, heads, 2, n_all, lanes)

    packed_y = swap(packed, "yl")
    piece_z = swap(far_piece, "zll")
    piece_yz = lax.ppermute(far_piece, ("yl", "zll"), [(0, 3), (1, 2), (2, 1), (3, 0)])
    far = jnp.concatenate([far_piece, packed_y[:kv_width], piece_z, piece_yz], axis=1)
    near_other = swap(near, "c")
    far, near_other, out_proj = lax.optimization_barrier((far, near_other, out_proj))
    far_other = swap(far, "c")
    out_proj_other = swap(out_proj, "c")

    rows = 4 * own_rows
    sequence = lax.axis_index("x") * 2 + lax.axis_index("yh")
    row_lengths = lax.dynamic_slice_in_dim(lengths, sequence * rows, rows, 0)[:, None]
    weights, out_proj_other = lax.optimization_barrier((weights, out_proj_other))
    place_all = jnp.stack([zh, yl, core] + starts).astype(jnp.int32)
    values = pl.pallas_call(
        lambda *refs: attend_kernel(
            *refs,
            sizes=(rows, heads, n_uq, n_uk, n_uv, latent_width, len(starts)),
            temper=temper,
        ),
        out_shape=jax.ShapeDtypeStruct((4, rows // 2, lanes), BF16),
        in_specs=[smem] + [vmem] * 10,
        out_specs=vmem,
        scratch_shapes=[
            pltpu.VMEM((rows, query_latent.shape[1]), BF16),
            pltpu.VMEM((rows, lanes), BF16),
            pltpu.VMEM((rows, 4 * tokens), F32),
        ],
        compiler_params=pltpu.CompilerParams(vmem_limit_bytes=VMEM_LIMIT),
        cost_estimate=pl.CostEstimate(flops=10**9, bytes_accessed=5 * 10**6, transcendentals=0),
        name="attend",
    )(place_all, packed, packed_y, weights, rope_kept, row_lengths, cache, near, near_other, far, far_other)

    values = exchange(values, ("zh", "c"))
    gathered = exchange(
        jnp.broadcast_to(values[None], (plane,) + values.shape).reshape((-1,) + values.shape[1:]),
        PLANE,
    ).reshape((plane // 2, 2) + values.shape)
    half_rows = plane // 2 * rows // 2
    partial_out = pl.pallas_call(
        project_kernel,
        out_shape=jax.ShapeDtypeStruct((half_rows, columns), BF16),
        in_specs=[smem] + [vmem] * 3,
        out_specs=vmem,
        compiler_params=pltpu.CompilerParams(vmem_limit_bytes=VMEM_LIMIT),
        cost_estimate=pl.CostEstimate(flops=2 * 10**8, bytes_accessed=2 * 10**6, transcendentals=0),
        name="project",
    )(place, gathered, out_proj, out_proj_other)

    total = exchange(partial_out, COLUMN).reshape(16, half_rows // 16, columns)
    total = jnp.sum(total.astype(F32), axis=0).astype(BF16)
    route = []
    for xy in range(16):
        for z_hi in range(2):
            for z_lo in range(8):
                for c in range(2):
                    source = ((xy * 2 + z_hi) * 8 + z_lo) * 2 + c
                    route.append((source, (z_lo * 4 + c * 2 + z_hi) * 16 + xy))
    return lax.ppermute(total, AXES, route)


def solution(mesh):
    fine = Mesh(mesh.devices.reshape(SIZES), AXES)
    placed = (
        P(FSDP, None),
        P(FSDP, HEAD, None),
        P(),
        P(FSDP, None),
        P(HEAD, FSDP, None),
        P(HEAD, FSDP, None),
        P(HEAD, FSDP, None),
        P(HEAD, FSDP, None),
    )
    return jax.shard_map(
        local, mesh=fine, in_specs=placed, out_specs=P(FSDP, HEAD), check_vma=False
    )
```

time: 171 us -> 174 us (1.018)
  the two profiles are of different devices: /device:TPU:38 before, /device:TPU:6 now
where the time goes in v4:
time: 174 us; the launch traced here: 171 us
  blocking collectives  67.9 us (39%)
  starting transfers between devices  58.6 us (34%)
  waiting for transfers between devices  25 us (14%)
  Pallas kernels  10.8 us (6%)
  local copies, waits for them, and re-layouts  7.54 us (4%)
    all_to_all x3, blocking collectives, exchange(): return lax.all_to_all(blocks, axes, 0, 0, tiled=True)  67.9 us
    ppermute x7, starting transfers between devices, swap(): return lax.ppermute(block, axis, [(0, 1), (1, 0)])  30.6 us
    ppermute x7, waiting for transfers between devices, swap(): return lax.ppermute(block, axis, [(0, 1), (1, 0)])  17.1 us
    all_to_all x2, starting transfers between devices, exchange(): return lax.all_to_all(blocks, axes, 0, 0, tiled=True)  14.6 us
    ppermute x1, waiting for transfers between devices, local(): return lax.ppermute(total, AXES, route)  7.94 us
    ppermute x1, starting transfers between devices, local(): lax.ppermute(far_piece, ('yl', 'zll'), [(0, 3), (1, 2), (2, 1), (3, 0)])  7.89 us
    ppermute x1, starting transfers between devices, local(): return lax.ppermute(total, AXES, route)  5.5 us
    pallas_call x1, Pallas kernels, local(): pl.pallas_call(lambda *refs: attend_kernel(*refs, sizes=(rows, heads, n_u...  4.56 us
  transfers between devices with their start and end apart: 11, of which 4 were waited for; matrix products, arithmetic and copies ran while one was open for 2% of the time, Pallas kernels for 1%

profile of v4, /device:TPU:6, one launch (start us, length us, event | category | flops | bytes accessed | tf_op | source)
XLA Modules:
  0.0 171.1 jit_solution(12261559474704616940)
XLA Ops:
  0.0 0.7 pad_add_fusion.place.refs_0_
  0.7 2.7 %pack.1 = (bf16[1120,128]{1,0:T(8,128)(2,1)}, bf16[576,256]{1,0:T(8,128)(2,1)}) custom-call(s32[4]{0:T(128)} %pad_add_fusion.place.refs_0_, bf16[576,512]{1,0:T(8,128)(2,1)} %bitcast.34, bf16[8,48,128]{2,1,0:T(8,128)(2,1)} %refs_2_.1, bf16[8,16,128]{2,1,0:T(8,128)(2,1)} %refs_3_.1, bf16[8,16,128]{2,1,0:T(8,128)(2,1)} %refs_4_.1, bf16[16,1536]{1,0:T(8,128)(2,1)} %refs_5_.1, ...), custom_call_target="tpu_custom_call" | custom-call | flops 1000000 | bytes 1000000 | tf_op jit(solution)/shard_map/pack/pallas_call | solution.py:260
  3.4 15.7 %collective-permute-start = (bf16[1120,128]{1,0:T(8,128)(2,1)}, bf16[1120,128]{1,0:T(8,128)(2,1)S(1)}, u32[]{:S(2)}, u32[]{:S(2)}) collective-permute-start(bf16[1120,128]{1,0:T(8,128)(2,1)} %get-tuple-element.21), channel_id=1, source_target_pairs={{0,16},{16,0},{1,17},{17,1},{2,18},{18,2},{3,19},{19,3},{4,20},{20... | collective-permute-start | bytes 860168 | tf_op jit(solution)/shard_map/ppermute | solution.py:24
  19.1 0.5 reshape.26
  19.7 0.0 copy-start.7
  19.7 0.0 copy-start.8
  19.7 0.0 copy-start.9
  19.7 0.0 copy-start.10
  19.8 0.0 copy-start.11
  19.8 1.1 copy.19
  20.9 7.4 %all-to-all-start = ((bf16[16,32,448]{2,1,0:T(8,128)(2,1)}), bf16[16,32,448]{2,1,0:T(8,128)(2,1)S(1)}, u32[]{:S(2)}, u32[]{:S(2)}) async-start(bf16[16,32,448]{2,1,0:T(8,128)(2,1)} %copy.19), calls=%async_computation | async-start | bytes 1048576 | tf_op jit(solution)/shard_map/all_to_all | solution.py:28
  28.3 3.4 %collective-permute-start.1 = (bf16[576,256]{1,0:T(8,128)(2,1)S(1)}, bf16[576,256]{1,0:T(8,128)(2,1)S(1)}, u32[]{:S(2)}, u32[]{:S(2)}) collective-permute-start(bf16[576,256]{1,0:T(8,128)(2,1)S(1)} %copy-done.14), channel_id=1, source_target_pairs={{0,32},{32,0},{1,33},{33,1},{2,34},{34,2},{3,35},{35,3},{4,36},{36... | collective-permute-start | bytes 884744 | tf_op jit(solution)/shard_map/ppermute | solution.py:24
  31.7 0.0 collective-permute-done.refs_1_
  31.8 1.8 %unpack.1 = (bf16[8,4,160,128]{3,2,1,0:T(8,128)(2,1)}, bf16[992,128]{1,0:T(8,128)(2,1)S(1)}, bf16[576,128]{1,0:T(8,128)(2,1)S(1)}, bf16[32,128]{1,0:T(8,128)(2,1)S(1)}) custom-call(s32[4]{0:T(128)S(1)} %copy-done.12, bf16[1120,128]{1,0:T(8,128)(2,1)S(1)} %collective-permute-done.refs_1_, bf16[8,48,128]{2,1,0:T(8,128)(2,1)S(1)} %copy-done.7, ...), custom_call_target="tpu_custom_call" | custom-call | flops 20000000000 | bytes 3000000 | tf_op jit(solution)/shard_map/unpack/pallas_call | solution.py:278
  33.6 8.2 %collective-permute-done.1.refs_7_ = bf16[576,256]{1,0:T(8,128)(2,1)S(1)} collective-permute-done((bf16[576,256]{1,0:T(8,128)(2,1)S(1)}, bf16[576,256]{1,0:T(8,128)(2,1)S(1)}, u32[]{:S(2)}, u32[]{:S(2)}) %collective-permute-start.1) | collective-permute-done | bytes 294944 | tf_op jit(solution)/shard_map/ppermute | solution.py:24
  41.8 7.2 %all-to-all-start.1 = ((bf16[32,160,128]{2,1,0:T(8,128)(2,1)}), bf16[32,160,128]{2,1,0:T(8,128)(2,1)S(1)}, u32[]{:S(2)}, u32[]{:S(2)}) async-start(bf16[32,160,128]{2,1,0:T(8,128)(2,1)} %bitcast.22), calls=%async_computation.1 | async-start | bytes 2621440 | tf_op jit(solution)/shard_map/all_to_all | solution.py:28
  48.9 3.4 %collective-permute-start.2 = (bf16[992,128]{1,0:T(8,128)(2,1)S(1)}, bf16[992,128]{1,0:T(8,128)(2,1)S(1)}, u32[]{:S(2)}, u32[]{:S(2)}) collective-permute-start(bf16[992,128]{1,0:T(8,128)(2,1)S(1)} %get-tuple-element.26.refs_1_), channel_id=1, source_target_pairs={{0,32},{32,0},{1,33},{33,1},{2,34},{34,2},{3,35},{35,3},{4,36},{36... | collective-permute-start | bytes 761864 | tf_op jit(solution)/shard_map/ppermute | solution.py:24
  52.3 1.9 %collective-permute-start.5 = (bf16[576,256]{1,0:T(8,128)(2,1)S(1)}, bf16[576,256]{1,0:T(8,128)(2,1)S(1)}, u32[]{:S(2)}, u32[]{:S(2)}) collective-permute-start(bf16[576,256]{1,0:T(8,128)(2,1)S(1)} %collective-permute-done.1.refs_7_), channel_id=1, source_target_pairs={{0,1},{1,0},{2,3},{3,2},{4,5},{5,4},{6,7},{7,6},{8,9},{9,8},{10,11... | collective-permute-start | bytes 884744 | tf_op jit(solution)/shard_map/ppermute | solution.py:24
  54.2 7.9 %collective-permute-start.4 = (bf16[576,128]{1,0:T(8,128)(2,1)S(1)}, bf16[576,128]{1,0:T(8,128)(2,1)S(1)}, u32[]{:S(2)}, u32[]{:S(2)}) collective-permute-start(bf16[576,128]{1,0:T(8,128)(2,1)S(1)} %get-tuple-element.28), channel_id=1, source_target_pairs={{0,34},{2,32},{32,2},{34,0},{1,35},{3,33},{33,3},{35,1},{4,38},{6,... | collective-permute-start | bytes 442376 | tf_op jit(solution)/shard_map/ppermute | solution.py:310
  62.1 1.9 %collective-permute-start.3 = (bf16[576,128]{1,0:T(8,128)(2,1)S(1)}, bf16[576,128]{1,0:T(8,128)(2,1)S(1)}, u32[]{:S(2)}, u32[]{:S(2)}) collective-permute-start(bf16[576,128]{1,0:T(8,128)(2,1)S(1)} %get-tuple-element.28), channel_id=1, source_target_pairs={{0,2},{2,0},{1,3},{3,1},{4,6},{6,4},{5,7},{7,5},{8,10},{10,8},{9,1... | collective-permute-start | bytes 442376 | tf_op jit(solution)/shard_map/ppermute | solution.py:24
  64.1 0.3 copy.20
  64.4 0.5 copy.21
  64.9 8.2 %collective-permute-done.2.refs_2_ = bf16[992,128]{1,0:T(8,128)(2,1)S(1)} collective-permute-done((bf16[992,128]{1,0:T(8,128)(2,1)S(1)}, bf16[992,128]{1,0:T(8,128)(2,1)S(1)}, u32[]{:S(2)}, u32[]{:S(2)}) %collective-permute-start.2) | collective-permute-done | bytes 253984 | tf_op jit(solution)/shard_map/ppermute | solution.py:24
  73.1 0.0 copy-start.1
  73.2 0.0 collective-permute-done.3
  73.2 0.1 pad_maximum_fusion.refs_9_
  73.2 0.0 collective-permute-done.5.refs_8_
  73.3 0.7 copy-done.4
  74.0 1.9 %collective-permute-start.7 = (bf16[576,512]{1,0:T(8,128)(2,1)S(1)}, bf16[576,512]{1,0:T(8,128)(2,1)}, u32[]{:S(2)}, u32[]{:S(2)}) collective-permute-start(bf16[576,512]{1,0:T(8,128)(2,1)S(1)} %pad_maximum_fusion.refs_9_), channel_id=1, source_target_pairs={{0,1},{1,0},{2,3},{3,2},{4,5},{5,4},{6,7},{7,6},{8,9},{9,8},{10,11... | collective-permute-start | bytes 1769480 | tf_op jit(solution)/shard_map/ppermute | solution.py:24
  75.9 0.1 copy.22.ours
  75.9 2.4 %collective-permute-start.6 = (bf16[2,2,128,448]{3,2,1,0:T(8,128)(2,1)S(1)}, bf16[2,2,128,448]{3,2,1,0:T(8,128)(2,1)}, u32[]{:S(2)}, u32[]{:S(2)}) collective-permute-start(bf16[2,2,128,448]{3,2,1,0:T(8,128)(2,1)S(1)} %copy.22.ours), channel_id=1, source_target_pairs={{0,1},{1,0},{2,3},{3,2},{4,5},{5,4},{6,7},{7,6},{8,9},{9,8},{10,11... | collective-permute-start | bytes 1376264 | tf_op jit(solution)/shard_map/ppermute | solution.py:24
  78.4 0.1 dynamic-slice_bitcast_fusion
  78.5 0.7 copy.23.refs_5_
  79.2 0.1 stack.90.refs_0_
  79.3 0.7 collective-permute-done.6.theirs
  80.0 1.0 copy-done.3
  81.0 1.0 copy-done.5
  81.9 0.8 copy-done.6
  82.7 4.6 %attend.1 = bf16[4,32,128]{2,1,0:T(8,128)(2,1)S(1)} custom-call(s32[19]{0:T(128)S(1)} %stack.90.refs_0_, bf16[992,128]{1,0:T(8,128)(2,1)S(1)} %get-tuple-element.26.refs_1_, bf16[992,128]{1,0:T(8,128)(2,1)S(1)} %collective-permute-done.2.refs_2_, bf16[16,2,2,80,128]{4,3,2,1,0:T(8,128)(2,1)S(1)} %bitcast.33, bf16[32,128]{1,0:T(8,128)(2,1)S(1)} %get-tuple-element.33.refs_4_, ...), custom_call_target="tpu_custom_call" | custom-call | flops 1000000000 | bytes 5000000 | tf_op jit(solution)/shard_map/attend/pallas_call | solution.py:322
  87.3 22.0 %all_to_all.29 = bf16[4,32,128]{2,1,0:T(8,128)(2,1)S(1)} all-to-all(bf16[4,32,128]{2,1,0:T(8,128)(2,1)S(1)} %attend.1), channel_id=1, replica_groups=mesh['x'=4,'yh'=2,'yl'=2,'zh'=2,'zlh'=4,'zll'=2,'c'=2] {'zh','c'}, dimensions={0} | all-to-all | bytes 65536 | tf_op jit(solution)/shard_map/all_to_all | solution.py:28
  109.3 0.1 broadcast_in_dim.10
  109.4 17.9 %all_to_all.30 = bf16[64,32,128]{2,1,0:T(8,128)(2,1)S(1)} all-to-all(bf16[64,32,128]{2,1,0:T(8,128)(2,1)S(1)} %bitcast.40), channel_id=1, replica_groups=mesh['x'=4,'yh'=2,'yl'=2,'zh'=2,'zlh'=4,'zll'=2,'c'=2] {'x','yh','yl'}, dimensions={0} | all-to-all | bytes 1048576 | tf_op jit(solution)/shard_map/all_to_all | solution.py:28
  127.3 1.7 %project.1 = bf16[256,448]{1,0:T(8,128)(2,1)S(1)} custom-call(s32[4]{0:T(128)S(1)} %copy-done.12, bf16[8,2,4,32,128]{4,3,2,1,0:T(8,128)(2,1)S(1)} %bitcast.36, bf16[2,2,128,448]{3,2,1,0:T(8,128)(2,1)S(1)} %copy.22.ours, bf16[2,2,128,448]{3,2,1,0:T(8,128)(2,1)} %collective-permute-done.6.theirs), custom_call_target="tpu_custom_call" | custom-call | flops 200000000 | bytes 2000000 | tf_op jit(solution)/shard_map/project/pallas_call | solution.py:347
  129.1 28.0 %all_to_all.31 = bf16[16,16,448]{2,1,0:T(8,128)(2,1)S(1)} all-to-all(bf16[16,16,448]{2,1,0:T(8,128)(2,1)S(1)} %bitcast.37), channel_id=1, replica_groups=mesh['x'=4,'yh'=2,'yl'=2,'zh'=2,'zlh'=4,'zll'=2,'c'=2] {'zlh','zll','zh'}, dimensions={0} | all-to-all | bytes 458752 | tf_op jit(solution)/shard_map/all_to_all | solution.py:28
  157.0 0.1 reduce_sum.12
  157.1 5.5 %collective-permute-start.8 = (bf16[16,448]{1,0:T(8,128)(2,1)S(1)}, bf16[16,448]{1,0:T(8,128)(2,1)S(1)}, u32[]{:S(2)}, u32[]{:S(2)}) collective-permute-start(bf16[16,448]{1,0:T(8,128)(2,1)S(1)} %reduce_sum.12), channel_id=1, source_target_pairs={{0,0},{1,32},{2,64},{3,96},{4,128},{5,160},{6,192},{7,224},{8,256}... | collective-permute-start | bytes 43016 | tf_op jit(solution)/shard_map/ppermute | solution.py:366
  162.6 7.9 %collective-permute-done.8 = bf16[16,448]{1,0:T(8,128)(2,1)S(1)} collective-permute-done((bf16[16,448]{1,0:T(8,128)(2,1)S(1)}, bf16[16,448]{1,0:T(8,128)(2,1)S(1)}, u32[]{:S(2)}, u32[]{:S(2)}) %collective-permute-start.8) | collective-permute-done | bytes 14368 | tf_op jit(solution)/shard_map/ppermute | solution.py:366
  170.5 0.6 copy.26
  (25 shorter events, 0.1 us)
Async XLA Ops:
  0.0 78.4 %copy-start = (s32[512]{0:T(512)S(1)}, s32[512]{0:T(512)}, u32[]{:S(2)}) copy-start(s32[512]{0:T(512)} %param.10) | copy-start | bytes 6148
  0.0 19.1 %copy-start.13 = (bf16[8,4,7168]{2,1,0:T(4,128)(2,1)S(1)}, bf16[8,4,7168]{2,1,0:T(4,128)(2,1)}, u32[]{:S(2)}) copy-start(bf16[8,4,7168]{2,1,0:T(4,128)(2,1)} %param.15) | copy-start | bytes 1376260
  3.4 28.3 %collective-permute-start = (bf16[1120,128]{1,0:T(8,128)(2,1)}, bf16[1120,128]{1,0:T(8,128)(2,1)S(1)}, u32[]{:S(2)}, u32[]{:S(2)}) collective-permute-start(bf16[1120,128]{1,0:T(8,128)(2,1)} %get-tuple-element.21), channel_id=1, source_target_pairs={{0,16},{16,0},{1,17},{17,1},{2,18},{18,2},{3,19},{19,3},{4,20},{20... | collective-permute-start | bytes 860168 | tf_op jit(solution)/shard_map/ppermute | solution.py:24
  19.7 8.6 %copy-start.14 = (bf16[576,256]{1,0:T(8,128)(2,1)S(1)}, bf16[576,256]{1,0:T(8,128)(2,1)}, u32[]{:S(2)}) copy-start(bf16[576,256]{1,0:T(8,128)(2,1)} %get-tuple-element.25) | copy-start | bytes 884740
  19.7 12.0 %copy-start.7 = (bf16[8,48,128]{2,1,0:T(8,128)(2,1)S(1)}, bf16[8,48,128]{2,1,0:T(8,128)(2,1)}, u32[]{:S(2)}) copy-start(bf16[8,48,128]{2,1,0:T(8,128)(2,1)} %refs_2_.1) | copy-start | bytes 294916
  19.7 12.0 %copy-start.8 = (bf16[16,1536]{1,0:T(8,128)(2,1)S(1)}, bf16[16,1536]{1,0:T(8,128)(2,1)}, u32[]{:S(2)}) copy-start(bf16[16,1536]{1,0:T(8,128)(2,1)} %refs_5_.1) | copy-start | bytes 147460
  19.7 12.0 %copy-start.9 = (bf16[8,16,128]{2,1,0:T(8,128)(2,1)S(1)}, bf16[8,16,128]{2,1,0:T(8,128)(2,1)}, u32[]{:S(2)}) copy-start(bf16[8,16,128]{2,1,0:T(8,128)(2,1)} %refs_3_.1) | copy-start | bytes 98308
  19.7 12.0 %copy-start.10 = (bf16[8,16,128]{2,1,0:T(8,128)(2,1)S(1)}, bf16[8,16,128]{2,1,0:T(8,128)(2,1)}, u32[]{:S(2)}) copy-start(bf16[8,16,128]{2,1,0:T(8,128)(2,1)} %refs_4_.1) | copy-start | bytes 98308
  19.8 12.0 %copy-start.11 = (bf16[16,8,64]{2,1,0:T(8,128)(2,1)S(1)}, bf16[16,8,64]{2,1,0:T(8,128)(2,1)}, u32[]{:S(2)}) copy-start(bf16[16,8,64]{2,1,0:T(8,128)(2,1)} %refs_6_.1) | copy-start | bytes 49156
  19.8 12.0 %copy-start.12 = (s32[4]{0:T(128)S(1)}, s32[4]{0:T(128)}, u32[]{:S(2)}) copy-start(s32[4]{0:T(128)} %pad_add_fusion.place.refs_0_) | copy-start | bytes 52
  20.9 20.9 %all-to-all-start = ((bf16[16,32,448]{2,1,0:T(8,128)(2,1)}), bf16[16,32,448]{2,1,0:T(8,128)(2,1)S(1)}, u32[]{:S(2)}, u32[]{:S(2)}) async-start(bf16[16,32,448]{2,1,0:T(8,128)(2,1)} %copy.19), calls=%async_computation | async-start | bytes 1048576 | tf_op jit(solution)/shard_map/all_to_all | solution.py:28
  28.3 13.4 %collective-permute-start.1 = (bf16[576,256]{1,0:T(8,128)(2,1)S(1)}, bf16[576,256]{1,0:T(8,128)(2,1)S(1)}, u32[]{:S(2)}, u32[]{:S(2)}) collective-permute-start(bf16[576,256]{1,0:T(8,128)(2,1)S(1)} %copy-done.14), channel_id=1, source_target_pairs={{0,32},{32,0},{1,33},{33,1},{2,34},{34,2},{3,35},{35,3},{4,36},{36... | collective-permute-start | bytes 884744 | tf_op jit(solution)/shard_map/ppermute | solution.py:24
  41.7 10.6 %copy-start.2 = (bf16[576,256]{1,0:T(8,128)(2,1)}, bf16[576,256]{1,0:T(8,128)(2,1)S(1)}, u32[]{:S(2)}) copy-start(bf16[576,256]{1,0:T(8,128)(2,1)S(1)} %collective-permute-done.1.refs_7_) | copy-start | bytes 884740
  41.8 38.3 %all-to-all-start.1 = ((bf16[32,160,128]{2,1,0:T(8,128)(2,1)}), bf16[32,160,128]{2,1,0:T(8,128)(2,1)S(1)}, u32[]{:S(2)}, u32[]{:S(2)}) async-start(bf16[32,160,128]{2,1,0:T(8,128)(2,1)} %bitcast.22), calls=%async_computation.1 | async-start | bytes 2621440 | tf_op jit(solution)/shard_map/all_to_all | solution.py:28
  48.9 24.2 %collective-permute-start.2 = (bf16[992,128]{1,0:T(8,128)(2,1)S(1)}, bf16[992,128]{1,0:T(8,128)(2,1)S(1)}, u32[]{:S(2)}, u32[]{:S(2)}) collective-permute-start(bf16[992,128]{1,0:T(8,128)(2,1)S(1)} %get-tuple-element.26.refs_1_), channel_id=1, source_target_pairs={{0,32},{32,0},{1,33},{33,1},{2,34},{34,2},{3,35},{35,3},{4,36},{36... | collective-permute-start | bytes 761864 | tf_op jit(solution)/shard_map/ppermute | solution.py:24
  52.3 20.9 %collective-permute-start.5 = (bf16[576,256]{1,0:T(8,128)(2,1)S(1)}, bf16[576,256]{1,0:T(8,128)(2,1)S(1)}, u32[]{:S(2)}, u32[]{:S(2)}) collective-permute-start(bf16[576,256]{1,0:T(8,128)(2,1)S(1)} %collective-permute-done.1.refs_7_), channel_id=1, source_target_pairs={{0,1},{1,0},{2,3},{3,2},{4,5},{5,4},{6,7},{7,6},{8,9},{9,8},{10,11... | collective-permute-start | bytes 884744 | tf_op jit(solution)/shard_map/ppermute | solution.py:24
  54.2 18.9 %collective-permute-start.4 = (bf16[576,128]{1,0:T(8,128)(2,1)S(1)}, bf16[576,128]{1,0:T(8,128)(2,1)S(1)}, u32[]{:S(2)}, u32[]{:S(2)}) collective-permute-start(bf16[576,128]{1,0:T(8,128)(2,1)S(1)} %get-tuple-element.28), channel_id=1, source_target_pairs={{0,34},{2,32},{32,2},{34,0},{1,35},{3,33},{33,3},{35,1},{4,38},{6,... | collective-permute-start | bytes 442376 | tf_op jit(solution)/shard_map/ppermute | solution.py:310
  62.1 11.0 %collective-permute-start.3 = (bf16[576,128]{1,0:T(8,128)(2,1)S(1)}, bf16[576,128]{1,0:T(8,128)(2,1)S(1)}, u32[]{:S(2)}, u32[]{:S(2)}) collective-permute-start(bf16[576,128]{1,0:T(8,128)(2,1)S(1)} %get-tuple-element.28), channel_id=1, source_target_pairs={{0,2},{2,0},{1,3},{3,1},{4,6},{6,4},{5,7},{7,5},{8,10},{10,8},{9,1... | collective-permute-start | bytes 442376 | tf_op jit(solution)/shard_map/ppermute | solution.py:24
  73.1 6.9 %copy-start.1 = (bf16[512,576]{0,1:T(8,128)(2,1)S(1)}, bf16[512,576]{0,1:T(8,128)(2,1)}, u32[]{:S(2)}) copy-start(bf16[512,576]{0,1:T(8,128)(2,1)} %param.11) | copy-start | bytes 1769476
  73.3 0.7 copy-start.4
  74.0 6.0 %collective-permute-start.7 = (bf16[576,512]{1,0:T(8,128)(2,1)S(1)}, bf16[576,512]{1,0:T(8,128)(2,1)}, u32[]{:S(2)}, u32[]{:S(2)}) collective-permute-start(bf16[576,512]{1,0:T(8,128)(2,1)S(1)} %pad_maximum_fusion.refs_9_), channel_id=1, source_target_pairs={{0,1},{1,0},{2,3},{3,2},{4,5},{5,4},{6,7},{7,6},{8,9},{9,8},{10,11... | collective-permute-start | bytes 1769480 | tf_op jit(solution)/shard_map/ppermute | solution.py:24
  75.9 4.1 %collective-permute-start.6 = (bf16[2,2,128,448]{3,2,1,0:T(8,128)(2,1)S(1)}, bf16[2,2,128,448]{3,2,1,0:T(8,128)(2,1)}, u32[]{:S(2)}, u32[]{:S(2)}) collective-permute-start(bf16[2,2,128,448]{3,2,1,0:T(8,128)(2,1)S(1)} %copy.22.ours), channel_id=1, source_target_pairs={{0,1},{1,0},{2,3},{3,2},{4,5},{5,4},{6,7},{7,6},{8,9},{9,8},{10,11... | collective-permute-start | bytes 1376264 | tf_op jit(solution)/shard_map/ppermute | solution.py:24
  80.0 1.0 copy-start.3
  81.0 1.0 copy-start.5
  81.9 0.8 copy-start.6
  157.1 13.4 %collective-permute-start.8 = (bf16[16,448]{1,0:T(8,128)(2,1)S(1)}, bf16[16,448]{1,0:T(8,128)(2,1)S(1)}, u32[]{:S(2)}, u32[]{:S(2)}) collective-permute-start(bf16[16,448]{1,0:T(8,128)(2,1)S(1)} %reduce_sum.12), channel_id=1, source_target_pairs={{0,0},{1,32},{2,64},{3,96},{4,128},{5,160},{6,192},{7,224},{8,256}... | collective-permute-start | bytes 43016 | tf_op jit(solution)/shard_map/ppermute | solution.py:366

commit v5 on v3

--- a/solution.py
+++ b/solution.py
@@ -15,7 +15,8 @@
 COLUMN = ("zlh", "zll", "zh")
 BF16 = jnp.bfloat16
 F32 = jnp.float32
-VMEM_LIMIT = 40 * 1024 * 1024
+VMEM_LIMIT = 16 * 1024 * 1024
+PACK_LIMIT = 60 * 1024 * 1024
 UNPACK_FLOPS = 2 * 10**10
 
 
@@ -31,19 +32,6 @@
     )
 
 
-def pack(blocks):
-    return jnp.concatenate([block.reshape(-1, block.shape[-1]) for block in blocks], axis=0)
-
-
-def unpack(packed, shapes):
-    blocks, at = [], 0
-    for shape in shapes:
-        count = math.prod(shape[:-1])
-        blocks.append(packed[at : at + count].reshape(shape))
-        at += count
-    return blocks
-
-
 def exchange(blocks, axes):
     return lax.all_to_all(blocks, axes, 0, 0, tiled=True)
 
@@ -56,31 +44,118 @@
     return lax.dot_general(a, b, (((1,), (1,)), ((), ())), preferred_element_type=F32)
 
 
-def unpack_kernel(place, received, kept, latent, rope, sent, packed, piece, rope_out, *, sizes):
-    n_piece, n_all, own_rows, copies = sizes
+def head_pairs(rope):
+    return [
+        jnp.concatenate([rope[:, 2 * p, :], rope[:, 2 * p + 1, :]], axis=1)
+        for p in range(rope.shape[1] // 2)
+    ]
+
+
+def pack_kernel(
+    place, cache, w_uq, w_uk, w_uv, latent, rope, out, uq, uk, uv, latent_in, rope_in, sems
+):
+    zh, quarter = place[0], place[2]
+    lanes = out.shape[1]
+    width = cache.shape[0]
+    four = uq.shape[0]
+    given = pl.ds((1 - zh) * four, four)
+    copies = [
+        (cache.at[:, pl.ds(pl.multiple_of(quarter * lanes, lanes), lanes)], out.at[pl.ds(0, width)]),
+        (w_uq.at[given], uq),
+        (w_uk.at[given], uk),
+        (w_uv.at[given], uv),
+        (latent, latent_in),
+        (rope, rope_in),
+    ]
+    copies = [pltpu.make_async_copy(x, y, sems.at[i]) for i, (x, y) in enumerate(copies)]
+    for copy in copies:
+        copy.start()
+    for copy in copies:
+        copy.wait()
+    at = width
+    for h in range(four):
+        for w in (uq, uk, uv):
+            out[at : at + w.shape[1]] = w[h]
+            at += w.shape[1]
+    rows = latent_in.shape[0]
+    for i in range(latent_in.shape[1] // lanes):
+        out[at : at + rows] = latent_in[:, i * lanes : (i + 1) * lanes]
+        at += rows
+    pairs = head_pairs(rope_in)
+    for p in range(len(pairs) // 2):
+        out[at : at + rows] = jnp.where(zh == 0, pairs[p + len(pairs) // 2], pairs[p])
+        at += rows
+
+
+def spread_kernel(place, w_uq, w_uk, w_uv, w_out, out):
+    zh = place[0]
+    copies, lanes = out.shape[0], out.shape[2]
+    four = w_uq.shape[0] // 2
+    for h in range(four):
+        at = h % (four // 2) * (w_uq.shape[1] + w_uk.shape[1] + w_uv.shape[1])
+        for w in (w_uq, w_uk, w_uv):
+            block = w[zh * four + h]
+            for copy in range(h // (four // 2), copies, 2):
+                out[copy, at : at + w.shape[1]] = block
+            at += w.shape[1]
+    rows, columns = w_out.shape[0], w_out.shape[1] // copies
+    for copy in range(copies):
+        to = at
+        for begin in range(0, columns, lanes):
+            width = min(lanes, columns - begin)
+            block = w_out[:, copy * columns + begin : copy * columns + begin + width]
+            if width < lanes:
+                block = jnp.concatenate([block, jnp.zeros((rows, lanes - width), BF16)], axis=1)
+            out[copy, to : to + rows] = block
+            to += rows
+
+
+def order_kernel(received, out):
+    rows, columns = out.shape
+    copies, lanes = received.shape[0], received.shape[2]
+    each = rows // copies
+    count = -(-columns // lanes)
+    first = received.shape[1] - count * each
+    blocks = [
+        received[:, first + i * each : first + (i + 1) * each].reshape(rows, lanes)
+        for i in range(count)
+    ]
+    weights = jnp.concatenate(blocks, axis=1)[:, :columns]
+    to = lax.broadcasted_iota(jnp.int32, (rows, rows), 0)
+    source = lax.broadcasted_iota(jnp.int32, (rows, rows), 1)
+    y, z, j, xy, v = to // 256, to // 128 % 2, to // 64 % 2, to // 4 % 16, to % 4
+    move = jnp.where(source == xy * 32 + (z * 4 + y * 2 + j) * 4 + v, 1.0, 0.0).astype(BF16)
+    out[...] = dot(move, weights).astype(BF16)
+
+
+def unpack_kernel(
+    place, received, latent, rope, sent, packed, piece, rope_out, *, sizes
+):
+    n_piece, n_all, copies = sizes
     zh, yl = place[0], place[1]
-    four = kept.shape[0]
-    ours = pl.ds(pl.multiple_of(zh * n_all, 16), n_all)
-    theirs = pl.ds(pl.multiple_of((1 - zh) * n_all, 16), n_all)
+    own_rows = latent.shape[0]
+    lanes = packed.shape[1]
     at = n_piece
-    for h in range(four):
-        mine, other = kept[h], received[at : at + n_all]
+    for h in range(sent.shape[1]):
+        other = received[at : at + n_all]
         for copy in range(copies):
-            sent[copy, h, ours] = mine
-            sent[copy, h, theirs] = other
+            sent[copy, h] = other
         at += n_all
     ours = pl.ds(pl.multiple_of(zh * own_rows, 16), own_rows)
     theirs = pl.ds(pl.multiple_of((1 - zh) * own_rows, 16), own_rows)
     to = n_piece
-    for i in range(latent.shape[0]):
-        packed[pl.ds(pl.multiple_of(to + zh * own_rows, 16), own_rows)] = latent[i]
+    for i in range(latent.shape[1] // lanes):
+        packed[pl.ds(pl.multiple_of(to + zh * own_rows, 16), own_rows)] = latent[
+            :, i * lanes : (i + 1) * lanes
+        ]
         packed[pl.ds(pl.multiple_of(to + (1 - zh) * own_rows, 16), own_rows)] = received[
             at : at + own_rows
         ]
         to += 2 * own_rows
         at += own_rows
-    lower = [rope[0], received[at : at + own_rows]]
-    upper = [rope[1], received[at + own_rows : at + 2 * own_rows]]
+    pairs = head_pairs(rope)
+    lower = [jnp.where(zh == 0, pairs[0], pairs[2]), received[at : at + own_rows]]
+    upper = [jnp.where(zh == 0, pairs[1], pairs[3]), received[at + own_rows : at + 2 * own_rows]]
     stay = [jnp.where(yl == 0, x, y) for x, y in zip(lower, upper)]
     go = [jnp.where(yl == 0, y, x) for x, y in zip(lower, upper)]
     rope_out[ours] = stay[0]
@@ -95,7 +170,8 @@
     place,
     ours,
     theirs,
-    weights,
+    weights_ours,
+    weights_theirs,
     rope_ours,
     lengths,
     kv0,
@@ -107,6 +183,7 @@
     query_rows,
     rope,
     scores,
+    weights,
     *,
     sizes,
     temper,
@@ -114,6 +191,10 @@
     rows, heads, n_uq, n_uk, n_uv, width, n_starts = sizes
     caches = (kv0, kv1, kv2, kv3)
     zh, yl, starts = place[0], place[1], [place[2 + i] for i in range(n_starts)]
+    n_all = n_uq + n_uk + n_uv
+    for h in range(heads):
+        weights[:, h, zh] = weights_ours[:, h * n_all : (h + 1) * n_all]
+        weights[:, h, 1 - zh] = weights_theirs[:, h]
     per_block = kv0.shape[1]
     chunk = per_block * len(caches) // n_starts
     half = rows // 2
@@ -198,49 +279,65 @@
     four, heads = heads_in // 2, heads_in // 4
 
     quarter = tokens // 4
-    piece = lax.dynamic_slice_in_dim(cache, (core * 2 + zll) * quarter, quarter, 1)
-    stacked = jnp.concatenate([w_uq, w_uk, w_uv], axis=1)
-    kept = lax.dynamic_slice_in_dim(stacked, zh * four, four, 0)
-    given = lax.dynamic_slice_in_dim(stacked, (1 - zh) * four, four, 0)
-    latent = jnp.transpose(query_latent.reshape(own_rows, -1, lanes), (1, 0, 2))
-    rope = jnp.transpose(query_rope.reshape(own_rows, -1, lanes), (1, 0, 2))
-    rope_kept = lax.dynamic_slice_in_dim(rope, zh * 2, 2, 0)
-    rope_given = lax.dynamic_slice_in_dim(rope, (1 - zh) * 2, 2, 0)
-    sent = [piece, given, latent, rope_given]
-    packed = pack(sent)
-    near = swap(cache, "yl")
-    received = swap(pack(sent), "zh")
-    place = jnp.stack([zh, yl]).astype(jnp.int32)
+    place = jnp.stack([zh, yl, core * 2 + zll]).astype(jnp.int32)
     vmem = pl.BlockSpec(memory_space=pltpu.VMEM)
     smem = pl.BlockSpec(memory_space=pltpu.SMEM)
-    n_pack = kv_width + (2 * latent.shape[0] + 2) * own_rows
+    weights = (w_uq, w_uk, w_uv)
+    queries = (query_latent, query_rope)
+    latent_chunks = query_latent.shape[1] // lanes
+    n_sent = kv_width + four * n_all + (latent_chunks + 2) * own_rows
+    packed = pl.pallas_call(
+        pack_kernel,
+        out_shape=jax.ShapeDtypeStruct((n_sent, lanes), BF16),
+        in_specs=[smem] + [pl.BlockSpec(memory_space=pltpu.HBM)] * 6,
+        out_specs=vmem,
+        scratch_shapes=[pltpu.VMEM((four,) + w.shape[1:], BF16) for w in weights]
+        + [pltpu.VMEM(x.shape, BF16) for x in queries]
+        + [pltpu.SemaphoreType.DMA((6,))],
+        compiler_params=pltpu.CompilerParams(vmem_limit_bytes=PACK_LIMIT),
+        cost_estimate=pl.CostEstimate(flops=10**6, bytes_accessed=10**6, transcendentals=0),
+        name="pack",
+    )(place, cache, *weights, *queries)
+    near = swap(cache, "yl")
+    received = swap(packed, "zh")
+
+    vpart, width = w_out.shape[1:]
+    columns = width // plane
+    w_rows = heads_in * vpart
+    n_spread = heads * n_all + -(-columns // lanes) * w_rows
+    spread = pl.pallas_call(
+        spread_kernel,
+        out_shape=jax.ShapeDtypeStruct((plane, n_spread, lanes), BF16),
+        in_specs=[smem] + [vmem] * 4,
+        out_specs=vmem,
+        compiler_params=pltpu.CompilerParams(vmem_limit_bytes=VMEM_LIMIT),
+        cost_estimate=pl.CostEstimate(flops=10**6, bytes_accessed=10**6, transcendentals=0),
+        name="spread",
+    )(place, *weights, w_out.reshape(w_rows, width))
+    spread = exchange(spread, PLANE)
+
+    n_pack = kv_width + (2 * latent_chunks + 2) * own_rows
+    received, near = lax.optimization_barrier((received, near))
     sent, packed, far_piece, rope_kept = pl.pallas_call(
-        lambda *refs: unpack_kernel(*refs, sizes=(kv_width, n_all, own_rows, plane // 2)),
+        lambda *refs: unpack_kernel(*refs, sizes=(kv_width, n_all, plane // 2)),
         out_shape=(
-            jax.ShapeDtypeStruct((plane // 2, four, 2 * n_all, lanes), BF16),
+            jax.ShapeDtypeStruct((plane // 2, four, n_all, lanes), BF16),
             jax.ShapeDtypeStruct((n_pack, lanes), BF16),
             jax.ShapeDtypeStruct((kv_width, quarter), BF16),
             jax.ShapeDtypeStruct((2 * own_rows, lanes), BF16),
         ),
-        in_specs=[smem] + [vmem] * 4,
+        in_specs=[smem] + [vmem] * 3,
         out_specs=(vmem,) * 4,
         compiler_params=pltpu.CompilerParams(vmem_limit_bytes=VMEM_LIMIT),
         cost_estimate=pl.CostEstimate(
             flops=UNPACK_FLOPS, bytes_accessed=3 * 10**6, transcendentals=0
         ),
         name="unpack",
-    )(place, received, kept, latent, rope_kept)
-
-    vpart, width = w_out.shape[1:]
-    columns = width // plane
-    out_proj = w_out.reshape(heads_in * vpart, plane, columns)
-    out_proj = exchange(jnp.transpose(out_proj, (1, 0, 2)), PLANE)
-    sent, packed, far_piece, near, out_proj = lax.optimization_barrier(
-        (sent, packed, far_piece, near, out_proj)
-    )
-
-    weights = exchange(sent.reshape(plane * heads, 2 * n_all, lanes), PLANE)
-    weights = weights.reshape(plane, heads, 2, n_all, lanes)
+    )(place, received, *queries)
+    sent, packed, far_piece, spread = lax.optimization_barrier((sent, packed, far_piece, spread))
+
+    weights_far = exchange(sent.reshape(plane * heads, n_all, lanes), PLANE)
+    weights_far = weights_far.reshape(plane, heads, n_all, lanes)
 
     packed_y = swap(packed, "yl")
     piece_z = swap(far_piece, "zll")
@@ -268,24 +365,32 @@
             temper=temper,
         ),
         out_shape=(jax.ShapeDtypeStruct((rows, lanes), BF16),) * 2,
-        in_specs=[smem] + [vmem] * 9,
+        in_specs=[smem] + [vmem] * 10,
         out_specs=(vmem,) * 2,
         scratch_shapes=[
             pltpu.VMEM((rows, query_latent.shape[1]), BF16),
             pltpu.VMEM((rows, lanes), BF16),
             pltpu.VMEM((rows, 4 * tokens), F32),
+            pltpu.VMEM((plane, heads, 2, n_all, lanes), BF16),
         ],
         compiler_params=pltpu.CompilerParams(vmem_limit_bytes=VMEM_LIMIT),
         cost_estimate=pl.CostEstimate(flops=10**9, bytes_accessed=5 * 10**6, transcendentals=0),
         name="attend",
-    )(place, packed, packed_y, weights, rope_kept, row_lengths, cache, near, far, far_other)
+    )(place, packed, packed_y, spread, weights_far, rope_kept, row_lengths, cache, near, far, far_other)
 
     values = ordered(keep, swap(give, "zh"), zh, 1)
     gathered = exchange(
         jnp.broadcast_to(values[None], (plane,) + values.shape).reshape(-1, values.shape[1]), PLANE
     ).reshape(plane // 2, 2, rows, heads * lanes)
-    out_proj = out_proj.reshape(plane, 2, 2, heads, vpart, columns)
-    out_proj = jnp.transpose(out_proj, (2, 1, 3, 0, 4, 5)).reshape(-1, columns)
+    out_proj = pl.pallas_call(
+        order_kernel,
+        out_shape=jax.ShapeDtypeStruct((plane * w_rows, columns), BF16),
+        in_specs=[vmem],
+        out_specs=vmem,
+        compiler_params=pltpu.CompilerParams(vmem_limit_bytes=VMEM_LIMIT),
+        cost_estimate=pl.CostEstimate(flops=2 * 10**8, bytes_accessed=2 * 10**6, transcendentals=0),
+        name="order",
+    )(spread)
     all_rows = plane // 2 * rows
     partial_out = pl.pallas_call(
         project_kernel,

time: 171 us -> 163 us (0.953)
  waiting for transfers between devices: 51.4 us -> 39.8 us
  Pallas kernels: 6.79 us -> 12.1 us
  local copies, waits for them, and re-layouts: 10.6 us -> 5.31 us
    ppermute x6, waiting for transfers between devices: 33.9 us -> 18.2 us  [swap(): return lax.ppermute(block, axis, [(0, 1), (1, 0)])]
    pallas_call x0 -> x3, Pallas kernels: none -> 4.88 us  [the longest x1 2.58 us: local(): pl.pallas_call(pack_kernel, out_shape=jax.ShapeDtypeStruct((n_sent, lanes...]
    all_to_all x3, waiting for transfers between devices: 7.57 us -> 11.7 us  [exchange(): return lax.all_to_all(blocks, axes, 0, 0, tiled=True)]
    ppermute x6, starting transfers between devices: 37.5 us -> 39.3 us  [swap(): return lax.ppermute(block, axis, [(0, 1), (1, 0)])]
  transfers between devices with their start and end apart: 11 -> 11, of which waited for: 7 -> 5; matrix products, arithmetic and copies ran while one was open for 2% -> 2% of each run, Pallas kernels for 1% -> 4%
where the time goes in v5:
time: 163 us; the launch traced here: 162 us
  starting transfers between devices  65 us (40%)
  waiting for transfers between devices  39.8 us (24%)
  blocking collectives  37.4 us (23%)
  Pallas kernels  12.1 us (7%)
  local copies, waits for them, and re-layouts  5.31 us (3%)
  other arithmetic  1.99 us (1%)
    ppermute x6, starting transfers between devices, swap(): return lax.ppermute(block, axis, [(0, 1), (1, 0)])  39.3 us
    all_to_all x2, blocking collectives, exchange(): return lax.all_to_all(blocks, axes, 0, 0, tiled=True)  37.4 us
    all_to_all x3, starting transfers between devices, exchange(): return lax.all_to_all(blocks, axes, 0, 0, tiled=True)  20.2 us
    ppermute x6, waiting for transfers between devices, swap(): return lax.ppermute(block, axis, [(0, 1), (1, 0)])  18.2 us
    all_to_all x3, waiting for transfers between devices, exchange(): return lax.all_to_all(blocks, axes, 0, 0, tiled=True)  11.7 us
    ppermute x1, waiting for transfers between devices, local(): return lax.ppermute(total, AXES, route)  9.91 us
    pallas_call x1, Pallas kernels, local(): pl.pallas_call(lambda *refs: attend_kernel(*refs, sizes=(rows, heads, n_u...  5.24 us
  transfers between devices with their start and end apart: 11, of which 5 were waited for; matrix products, arithmetic and copies ran while one was open for 2% of the time, Pallas kernels for 4%

profile of v5, /device:TPU:38, one launch (start us, length us, event | category | flops | bytes accessed | tf_op | source)
XLA Modules:
  0.0 161.9 jit_solution(12493111936713958682)
XLA Ops:
  0.0 0.0 copy-start
  0.0 0.0 copy-start.7
  0.0 3.6 %collective-permute-start.1 = (bf16[576,512]{1,0:T(8,128)(2,1)}, bf16[576,512]{1,0:T(8,128)(2,1)S(1)}, u32[]{:S(2)}, u32[]{:S(2)}) collective-permute-start(bf16[576,512]{1,0:T(8,128)(2,1)} %bitcast.28), channel_id=1, source_target_pairs={{0,32},{32,0},{1,33},{33,1},{2,34},{34,2},{3,35},{35,3},{4,36},{36... | collective-permute-start | bytes 1769480 | tf_op jit(solution)/shard_map/ppermute | solution.py:24
  3.7 0.6 pad_add_fusion.place.refs_0_
  4.3 2.6 %pack.1 = bf16[1120,128]{1,0:T(8,128)(2,1)} custom-call(s32[3]{0:T(128)} %pad_add_fusion.place.refs_0_, bf16[576,512]{1,0:T(8,128)(2,1)} %bitcast.29, bf16[8,48,128]{2,1,0:T(8,128)(2,1)} %w_uq.3, bf16[8,16,128]{2,1,0:T(8,128)(2,1)} %w_uk.3, bf16[8,16,128]{2,1,0:T(8,128)(2,1)} %w_uv.3, bf16[16,1536]{1,0:T(8,128)(2,1)} %refs_2_.1, bf16[16,8,64]{2,1,0:T(8,128)(2,1)} %refs_3_.1), custom_call_target="tpu_custom_call" | custom-call | flops 1000000 | bytes 1000000 | tf_op jit(solution)/shard_map/pack/pallas_call | solution.py:289
  6.9 14.8 %collective-permute-start = (bf16[1120,128]{1,0:T(8,128)(2,1)}, bf16[1120,128]{1,0:T(8,128)(2,1)S(1)}, u32[]{:S(2)}, u32[]{:S(2)}) collective-permute-start(bf16[1120,128]{1,0:T(8,128)(2,1)} %pack.1), channel_id=1, source_target_pairs={{0,16},{16,0},{1,17},{17,1},{2,18},{18,2},{3,19},{19,3},{4,20},{20... | collective-permute-start | bytes 860168 | tf_op jit(solution)/shard_map/ppermute | solution.py:24
  21.8 0.1 reshape.54.w_out
  21.9 1.8 %spread.1 = bf16[16,288,128]{2,1,0:T(8,128)(2,1)} custom-call(s32[3]{0:T(128)S(1)} %copy-done.11, bf16[8,48,128]{2,1,0:T(8,128)(2,1)S(1)} %copy-done.4, bf16[8,16,128]{2,1,0:T(8,128)(2,1)S(1)} %copy-done.6, bf16[8,16,128]{2,1,0:T(8,128)(2,1)S(1)} %copy-done.7, bf16[32,7168]{1,0:T(8,128)(2,1)S(1)} %reshape.54.w_out), custom_call_target="tpu_custom_call" | custom-call | flops 1000000 | bytes 1000000 | tf_op jit(solution)/shard_map/spread/pallas_call | solution.py:308
  23.7 7.3 %all-to-all-start = ((bf16[16,288,128]{2,1,0:T(8,128)(2,1)}), bf16[16,288,128]{2,1,0:T(8,128)(2,1)S(1)}, u32[]{:S(2)}, u32[]{:S(2)}) async-start(bf16[16,288,128]{2,1,0:T(8,128)(2,1)} %spread.1), calls=%async_computation | async-start | bytes 2359296 | tf_op jit(solution)/shard_map/all_to_all | solution.py:36
  31.0 15.9 %collective-permute-done.refs_1_ = bf16[1120,128]{1,0:T(8,128)(2,1)S(1)} collective-permute-done((bf16[1120,128]{1,0:T(8,128)(2,1)}, bf16[1120,128]{1,0:T(8,128)(2,1)S(1)}, u32[]{:S(2)}, u32[]{:S(2)}) %collective-permute-start) | collective-permute-done | bytes 286752 | tf_op jit(solution)/shard_map/ppermute | solution.py:24
  46.9 0.0 collective-permute-done.1.refs_8_
  46.9 1.5 unpack.1
  48.5 0.0 all-to-all-done.refs_3_.received
  48.5 2.4 %collective-permute-start.2 = (bf16[992,128]{1,0:T(8,128)(2,1)S(1)}, bf16[992,128]{1,0:T(8,128)(2,1)S(1)}, u32[]{:S(2)}, u32[]{:S(2)}) collective-permute-start(bf16[992,128]{1,0:T(8,128)(2,1)S(1)} %get-tuple-element.21.refs_1_), channel_id=1, source_target_pairs={{0,32},{32,0},{1,33},{33,1},{2,34},{34,2},{3,35},{35,3},{4,36},{36... | collective-permute-start | bytes 761864 | tf_op jit(solution)/shard_map/ppermute | solution.py:24
  50.8 2.6 %collective-permute-start.4 = (bf16[576,128]{1,0:T(8,128)(2,1)S(1)}, bf16[576,128]{1,0:T(8,128)(2,1)S(1)}, u32[]{:S(2)}, u32[]{:S(2)}) collective-permute-start(bf16[576,128]{1,0:T(8,128)(2,1)S(1)} %get-tuple-element.26), channel_id=1, source_target_pairs={{0,34},{2,32},{32,2},{34,0},{1,35},{3,33},{33,3},{35,1},{4,38},{6,... | collective-permute-start | bytes 442376 | tf_op jit(solution)/shard_map/ppermute | solution.py:344
  53.5 4.2 %collective-permute-start.3 = (bf16[576,128]{1,0:T(8,128)(2,1)S(1)}, bf16[576,128]{1,0:T(8,128)(2,1)}, u32[]{:S(2)}, u32[]{:S(2)}) collective-permute-start(bf16[576,128]{1,0:T(8,128)(2,1)S(1)} %get-tuple-element.26), channel_id=1, source_target_pairs={{0,2},{2,0},{1,3},{3,1},{4,6},{6,4},{5,7},{7,5},{8,10},{10,8},{9,1... | collective-permute-start | bytes 442376 | tf_op jit(solution)/shard_map/ppermute | solution.py:24
  57.7 0.0 copy-start.1
  57.7 7.3 %all-to-all-start.1 = ((bf16[32,80,128]{2,1,0:T(8,128)(2,1)}), bf16[32,80,128]{2,1,0:T(8,128)(2,1)S(1)}, u32[]{:S(2)}, u32[]{:S(2)}) async-start(bf16[32,80,128]{2,1,0:T(8,128)(2,1)} %bitcast.20), calls=%async_computation.1 | async-start | bytes 1310720 | tf_op jit(solution)/shard_map/all_to_all | solution.py:36
  65.0 0.0 collective-permute-done.2.refs_2_
  65.0 0.0 collective-permute-done.4
  65.1 0.6 copy-done.13
  65.7 0.0 collective-permute-done.3
  65.7 1.1 pad_maximum_fusion.refs_9_
  66.8 1.9 %collective-permute-start.5 = (bf16[576,512]{1,0:T(8,128)(2,1)S(1)}, bf16[576,512]{1,0:T(8,128)(2,1)}, u32[]{:S(2)}, u32[]{:S(2)}) collective-permute-start(bf16[576,512]{1,0:T(8,128)(2,1)S(1)} %pad_maximum_fusion.refs_9_), channel_id=1, source_target_pairs={{0,1},{1,0},{2,3},{3,2},{4,5},{5,4},{6,7},{7,6},{8,9},{9,8},{10,11... | collective-permute-start | bytes 1769480 | tf_op jit(solution)/shard_map/ppermute | solution.py:24
  68.8 0.1 dynamic-slice_bitcast_fusion
  68.9 0.7 copy.14.refs_6_
  69.6 0.1 stack.83.refs_0_
  69.7 4.2 %all-to-all-done.1 = bf16[32,80,128]{2,1,0:T(8,128)(2,1)S(1)} async-done(((bf16[32,80,128]{2,1,0:T(8,128)(2,1)}), bf16[32,80,128]{2,1,0:T(8,128)(2,1)S(1)}, u32[]{:S(2)}, u32[]{:S(2)}) %all-to-all-start.1) | async-done | bytes 655392 | tf_op jit(solution)/shard_map/all_to_all | solution.py:36
  73.9 0.0 collective-permute-done.5.refs_10_
  73.9 1.1 copy-done.3
  75.0 0.8 copy-done.8
  75.7 5.2 %attend.1 = (bf16[64,128]{1,0:T(8,128)(2,1)S(1)}, bf16[64,128]{1,0:T(8,128)(2,1)}) custom-call(s32[18]{0:T(128)S(1)} %stack.83.refs_0_, bf16[992,128]{1,0:T(8,128)(2,1)S(1)} %get-tuple-element.21.refs_1_, bf16[992,128]{1,0:T(8,128)(2,1)S(1)} %collective-permute-done.2.refs_2_, bf16[16,288,128]{2,1,0:T(8,128)(2,1)S(1)} %all-to-all-done.refs_3_.received, ...), custom_call_target="tpu_custom_call" | custom-call | flops 1000000000 | bytes 5000000 | tf_op jit(solution)/shard_map/attend/pallas_call | solution.py:361
  81.0 12.3 %collective-permute-start.6 = (bf16[64,128]{1,0:T(8,128)(2,1)}, bf16[64,128]{1,0:T(8,128)(2,1)S(1)}, u32[]{:S(2)}, u32[]{:S(2)}) collective-permute-start(bf16[64,128]{1,0:T(8,128)(2,1)} %get-tuple-element.27), channel_id=1, source_target_pairs={{0,16},{16,0},{1,17},{17,1},{2,18},{18,2},{3,19},{19,3},{4,20},{20... | collective-permute-start | bytes 49160 | tf_op jit(solution)/shard_map/ppermute | solution.py:24
  93.3 2.2 %collective-permute-done.6 = bf16[64,128]{1,0:T(8,128)(2,1)S(1)} collective-permute-done((bf16[64,128]{1,0:T(8,128)(2,1)}, bf16[64,128]{1,0:T(8,128)(2,1)S(1)}, u32[]{:S(2)}, u32[]{:S(2)}) %collective-permute-start.6) | collective-permute-done | bytes 16416 | tf_op jit(solution)/shard_map/ppermute | solution.py:24
  95.5 0.9 broadcast_in_dim.10
  96.4 5.7 %all-to-all-start.2 = ((bf16[16,64,256]{2,1,0:T(8,128)(2,1)}), bf16[16,64,256]{2,1,0:T(8,128)(2,1)S(1)}, u32[]{:S(2)}, u32[]{:S(2)}) async-start(bf16[16,64,256]{2,1,0:T(8,128)(2,1)} %broadcast_in_dim.10), calls=%async_computation.2 | async-start | bytes 1048576 | tf_op jit(solution)/shard_map/all_to_all | solution.py:36
  102.0 0.5 order.1.weights
  102.5 7.6 %all-to-all-done.2 = bf16[16,64,256]{2,1,0:T(8,128)(2,1)S(1)} async-done(((bf16[16,64,256]{2,1,0:T(8,128)(2,1)}), bf16[16,64,256]{2,1,0:T(8,128)(2,1)S(1)}, u32[]{:S(2)}, u32[]{:S(2)}) %all-to-all-start.2) | async-done | bytes 524320 | tf_op jit(solution)/shard_map/all_to_all | solution.py:36
  110.1 0.4 project.1
  110.5 0.2 copy.15
  110.7 4.1 %all_to_all.34 = bf16[2,256,448]{1,2,0:T(8,128)(2,1)S(1)} all-to-all(bf16[2,256,448]{1,2,0:T(8,128)(2,1)S(1)} %copy.15), channel_id=1, replica_groups=mesh['x'=4,'yh'=2,'yl'=2,'zh'=2,'zlh'=4,'zll'=2,'c'=2] {'c'}, dimensions={0} | all-to-all | bytes 917504 | tf_op jit(solution)/shard_map/all_to_all | solution.py:36
  114.8 0.1 reduce_sum.24
  115.0 0.1 copy.16
  115.1 33.3 %all_to_all.35 = bf16[16,16,448]{2,1,0:T(8,128)(2,1)S(1)} all-to-all(bf16[16,16,448]{2,1,0:T(8,128)(2,1)S(1)} %bitcast.33), channel_id=1, replica_groups=mesh['x'=4,'yh'=2,'yl'=2,'zh'=2,'zlh'=4,'zll'=2,'c'=2] {'zlh','zll','zh'}, dimensions={0} | all-to-all | bytes 458752 | tf_op jit(solution)/shard_map/all_to_all | solution.py:36
  148.4 0.1 reduce_sum.25
  148.5 2.9 %collective-permute-start.7 = (bf16[16,448]{1,0:T(8,128)(2,1)S(1)}, bf16[16,448]{1,0:T(8,128)(2,1)S(1)}, u32[]{:S(2)}, u32[]{:S(2)}) collective-permute-start(bf16[16,448]{1,0:T(8,128)(2,1)S(1)} %reduce_sum.25), channel_id=1, source_target_pairs={{0,0},{1,256},{2,32},{3,288},{4,64},{5,320},{6,96},{7,352},{8,128}... | collective-permute-start | bytes 43016 | tf_op jit(solution)/shard_map/ppermute | solution.py:416
  151.4 9.9 %collective-permute-done.7 = bf16[16,448]{1,0:T(8,128)(2,1)S(1)} collective-permute-done((bf16[16,448]{1,0:T(8,128)(2,1)S(1)}, bf16[16,448]{1,0:T(8,128)(2,1)S(1)}, u32[]{:S(2)}, u32[]{:S(2)}) %collective-permute-start.7) | collective-permute-done | bytes 14368 | tf_op jit(solution)/shard_map/ppermute | solution.py:416
  161.3 0.6 copy.18
  (24 shorter events, 0.1 us)
Async XLA Ops:
  0.0 68.8 %copy-start = (s32[512]{0:T(512)S(1)}, s32[512]{0:T(512)}, u32[]{:S(2)}) copy-start(s32[512]{0:T(512)} %param.10) | copy-start | bytes 6148
  0.0 21.9 %copy-start.4 = (bf16[8,48,128]{2,1,0:T(8,128)(2,1)S(1)}, bf16[8,48,128]{2,1,0:T(8,128)(2,1)}, u32[]{:S(2)}) copy-start(bf16[8,48,128]{2,1,0:T(8,128)(2,1)} %w_uq.3) | copy-start | bytes 294916
  0.0 21.9 %copy-start.6 = (bf16[8,16,128]{2,1,0:T(8,128)(2,1)S(1)}, bf16[8,16,128]{2,1,0:T(8,128)(2,1)}, u32[]{:S(2)}) copy-start(bf16[8,16,128]{2,1,0:T(8,128)(2,1)} %w_uk.3) | copy-start | bytes 98308
  0.0 21.9 %copy-start.7 = (bf16[8,16,128]{2,1,0:T(8,128)(2,1)S(1)}, bf16[8,16,128]{2,1,0:T(8,128)(2,1)}, u32[]{:S(2)}) copy-start(bf16[8,16,128]{2,1,0:T(8,128)(2,1)} %w_uv.3) | copy-start | bytes 98308
  0.0 21.7 %copy-start.12 = (bf16[8,4,7168]{2,1,0:T(4,128)(2,1)S(1)}, bf16[8,4,7168]{2,1,0:T(4,128)(2,1)}, u32[]{:S(2)}) copy-start(bf16[8,4,7168]{2,1,0:T(4,128)(2,1)} %param.15) | copy-start | bytes 1376260
  0.0 46.9 %collective-permute-start.1 = (bf16[576,512]{1,0:T(8,128)(2,1)}, bf16[576,512]{1,0:T(8,128)(2,1)S(1)}, u32[]{:S(2)}, u32[]{:S(2)}) collective-permute-start(bf16[576,512]{1,0:T(8,128)(2,1)} %bitcast.28), channel_id=1, source_target_pairs={{0,32},{32,0},{1,33},{33,1},{2,34},{34,2},{3,35},{35,3},{4,36},{36... | collective-permute-start | bytes 1769480 | tf_op jit(solution)/shard_map/ppermute | solution.py:24
  4.3 17.6 %copy-start.11 = (s32[3]{0:T(128)S(1)}, s32[3]{0:T(128)}, u32[]{:S(2)}) copy-start(s32[3]{0:T(128)} %pad_add_fusion.place.refs_0_) | copy-start | bytes 40
  6.9 40.0 %collective-permute-start = (bf16[1120,128]{1,0:T(8,128)(2,1)}, bf16[1120,128]{1,0:T(8,128)(2,1)S(1)}, u32[]{:S(2)}, u32[]{:S(2)}) collective-permute-start(bf16[1120,128]{1,0:T(8,128)(2,1)} %pack.1), channel_id=1, source_target_pairs={{0,16},{16,0},{1,17},{17,1},{2,18},{18,2},{3,19},{19,3},{4,20},{20... | collective-permute-start | bytes 860168 | tf_op jit(solution)/shard_map/ppermute | solution.py:24
  23.7 23.2 %copy-start.9 = (bf16[16,1536]{1,0:T(8,128)(2,1)S(1)}, bf16[16,1536]{1,0:T(8,128)(2,1)}, u32[]{:S(2)}) copy-start(bf16[16,1536]{1,0:T(8,128)(2,1)} %refs_2_.1) | copy-start | bytes 147460
  23.7 23.2 %copy-start.10 = (bf16[16,8,64]{2,1,0:T(8,128)(2,1)S(1)}, bf16[16,8,64]{2,1,0:T(8,128)(2,1)}, u32[]{:S(2)}) copy-start(bf16[16,8,64]{2,1,0:T(8,128)(2,1)} %refs_3_.1) | copy-start | bytes 49156
  23.7 24.7 %all-to-all-start = ((bf16[16,288,128]{2,1,0:T(8,128)(2,1)}), bf16[16,288,128]{2,1,0:T(8,128)(2,1)S(1)}, u32[]{:S(2)}, u32[]{:S(2)}) async-start(bf16[16,288,128]{2,1,0:T(8,128)(2,1)} %spread.1), calls=%async_computation | async-start | bytes 2359296 | tf_op jit(solution)/shard_map/all_to_all | solution.py:36
  46.9 1.6 copy-start.2
  48.5 16.6 %copy-start.5 = (bf16[576,128]{1,0:T(8,128)(2,1)}, bf16[576,128]{1,0:T(8,128)(2,1)S(1)}, u32[]{:S(2)}) copy-start(bf16[576,128]{1,0:T(8,128)(2,1)S(1)} %get-tuple-element.26) | copy-start | bytes 442372
  48.5 16.5 %collective-permute-start.2 = (bf16[992,128]{1,0:T(8,128)(2,1)S(1)}, bf16[992,128]{1,0:T(8,128)(2,1)S(1)}, u32[]{:S(2)}, u32[]{:S(2)}) collective-permute-start(bf16[992,128]{1,0:T(8,128)(2,1)S(1)} %get-tuple-element.21.refs_1_), channel_id=1, source_target_pairs={{0,32},{32,0},{1,33},{33,1},{2,34},{34,2},{3,35},{35,3},{4,36},{36... | collective-permute-start | bytes 761864 | tf_op jit(solution)/shard_map/ppermute | solution.py:24
  50.8 14.2 %collective-permute-start.4 = (bf16[576,128]{1,0:T(8,128)(2,1)S(1)}, bf16[576,128]{1,0:T(8,128)(2,1)S(1)}, u32[]{:S(2)}, u32[]{:S(2)}) collective-permute-start(bf16[576,128]{1,0:T(8,128)(2,1)S(1)} %get-tuple-element.26), channel_id=1, source_target_pairs={{0,34},{2,32},{32,2},{34,0},{1,35},{3,33},{33,3},{35,1},{4,38},{6,... | collective-permute-start | bytes 442376 | tf_op jit(solution)/shard_map/ppermute | solution.py:344
  53.5 12.2 %collective-permute-start.3 = (bf16[576,128]{1,0:T(8,128)(2,1)S(1)}, bf16[576,128]{1,0:T(8,128)(2,1)}, u32[]{:S(2)}, u32[]{:S(2)}) collective-permute-start(bf16[576,128]{1,0:T(8,128)(2,1)S(1)} %get-tuple-element.26), channel_id=1, source_target_pairs={{0,2},{2,0},{1,3},{3,1},{4,6},{6,4},{5,7},{7,5},{8,10},{10,8},{9,1... | collective-permute-start | bytes 442376 | tf_op jit(solution)/shard_map/ppermute | solution.py:24
  57.7 16.2 %copy-start.1 = (bf16[512,576]{0,1:T(8,128)(2,1)S(1)}, bf16[512,576]{0,1:T(8,128)(2,1)}, u32[]{:S(2)}) copy-start(bf16[512,576]{0,1:T(8,128)(2,1)} %param.11) | copy-start | bytes 1769476
  57.7 16.2 %all-to-all-start.1 = ((bf16[32,80,128]{2,1,0:T(8,128)(2,1)}), bf16[32,80,128]{2,1,0:T(8,128)(2,1)S(1)}, u32[]{:S(2)}, u32[]{:S(2)}) async-start(bf16[32,80,128]{2,1,0:T(8,128)(2,1)} %bitcast.20), calls=%async_computation.1 | async-start | bytes 1310720 | tf_op jit(solution)/shard_map/all_to_all | solution.py:36
  65.0 0.6 copy-start.13
  66.8 7.1 %collective-permute-start.5 = (bf16[576,512]{1,0:T(8,128)(2,1)S(1)}, bf16[576,512]{1,0:T(8,128)(2,1)}, u32[]{:S(2)}, u32[]{:S(2)}) collective-permute-start(bf16[576,512]{1,0:T(8,128)(2,1)S(1)} %pad_maximum_fusion.refs_9_), channel_id=1, source_target_pairs={{0,1},{1,0},{2,3},{3,2},{4,5},{5,4},{6,7},{7,6},{8,9},{9,8},{10,11... | collective-permute-start | bytes 1769480 | tf_op jit(solution)/shard_map/ppermute | solution.py:24
  73.9 1.1 copy-start.3
  75.0 0.8 copy-start.8
  81.0 14.5 %collective-permute-start.6 = (bf16[64,128]{1,0:T(8,128)(2,1)}, bf16[64,128]{1,0:T(8,128)(2,1)S(1)}, u32[]{:S(2)}, u32[]{:S(2)}) collective-permute-start(bf16[64,128]{1,0:T(8,128)(2,1)} %get-tuple-element.27), channel_id=1, source_target_pairs={{0,16},{16,0},{1,17},{17,1},{2,18},{18,2},{3,19},{19,3},{4,20},{20... | collective-permute-start | bytes 49160 | tf_op jit(solution)/shard_map/ppermute | solution.py:24
  96.4 13.7 %all-to-all-start.2 = ((bf16[16,64,256]{2,1,0:T(8,128)(2,1)}), bf16[16,64,256]{2,1,0:T(8,128)(2,1)S(1)}, u32[]{:S(2)}, u32[]{:S(2)}) async-start(bf16[16,64,256]{2,1,0:T(8,128)(2,1)} %broadcast_in_dim.10), calls=%async_computation.2 | async-start | bytes 1048576 | tf_op jit(solution)/shard_map/all_to_all | solution.py:36
  148.5 12.9 %collective-permute-start.7 = (bf16[16,448]{1,0:T(8,128)(2,1)S(1)}, bf16[16,448]{1,0:T(8,128)(2,1)S(1)}, u32[]{:S(2)}, u32[]{:S(2)}) collective-permute-start(bf16[16,448]{1,0:T(8,128)(2,1)S(1)} %reduce_sum.25), channel_id=1, source_target_pairs={{0,0},{1,256},{2,32},{3,288},{4,64},{5,320},{6,96},{7,352},{8,128}... | collective-permute-start | bytes 43016 | tf_op jit(solution)/shard_map/ppermute | solution.py:416

commit v6 on v5

--- a/solution.py
+++ b/solution.py
@@ -12,7 +12,7 @@
 FSDP = ("x", "yh", "yl", "zh")
 HEAD = ("zlh", "zll", "c")
 PLANE = ("x", "yh", "yl")
-COLUMN = ("zlh", "zll", "zh")
+COLUMN = ("zh", "zlh", "zll")
 BF16 = jnp.bfloat16
 F32 = jnp.float32
 VMEM_LIMIT = 16 * 1024 * 1024
@@ -188,15 +188,25 @@
     sizes,
     temper,
 ):
-    rows, heads, n_uq, n_uk, n_uv, width, n_starts = sizes
+    rows, heads, n_uq, n_uk, n_uv, width = sizes
     caches = (kv0, kv1, kv2, kv3)
-    zh, yl, starts = place[0], place[1], [place[2 + i] for i in range(n_starts)]
+    zh, yl, core = place[0], place[1], place[3]
+    zll = place[2] - core * 2
+    quarter = kv0.shape[1] // 4
+    starts = []
+    for ylo in (yl, 1 - yl):
+        for i in range(4):
+            starts.append((ylo * 2 + zh) * kv0.shape[1] + i * quarter)
+    for co in (core, 1 - core):
+        for zo in (zll, 1 - zll):
+            for ylo in (yl, 1 - yl):
+                starts.append((ylo * 2 + 1 - zh) * kv0.shape[1] + (co * 2 + zo) * quarter)
     n_all = n_uq + n_uk + n_uv
     for h in range(heads):
         weights[:, h, zh] = weights_ours[:, h * n_all : (h + 1) * n_all]
         weights[:, h, 1 - zh] = weights_theirs[:, h]
     per_block = kv0.shape[1]
-    chunk = per_block * len(caches) // n_starts
+    chunk = quarter
     half = rows // 2
     mine = pl.ds(pl.multiple_of(yl * half, 16), half)
     other = pl.ds(pl.multiple_of((1 - yl) * half, 16), half)
@@ -210,35 +220,47 @@
     rope[mine, :] = rope_ours[...]
     rope[other, :] = theirs[at : at + half]
     query = query_rows[...]
-    limit = lengths[...]
-    lanes = lax.broadcasted_iota(jnp.int32, (rows, chunk), 1)
-    values = []
+    diagonal = lax.broadcasted_iota(jnp.int32, (rows, rows), 0) == lax.broadcasted_iota(
+        jnp.int32, (rows, rows), 1
+    )
+    limit = jnp.sum(
+        jnp.where(diagonal, lengths[pl.ds(place[4], 1), :], 0), axis=1, keepdims=True
+    )
+    limit = jnp.concatenate([limit] * heads, axis=0)
+    all_rows = heads * rows
+    lanes = lax.broadcasted_iota(jnp.int32, (all_rows, chunk), 1)
+    rope_width = kv0.shape[0] - width
+    q_lat = []
     for h in range(heads):
         w_uq = weights[:, h, :, 0:n_uq, :].reshape(-1, weights.shape[-1])
         w_uk = weights[:, h, :, n_uq : n_uq + n_uk, :].reshape(-1, weights.shape[-1])
         q_nope = dot(query, w_uq).astype(BF16)
-        q_lat = dot_nt(q_nope, w_uk).astype(BF16)
-        rope_width = kv0.shape[0] - width
-        q_rope = rope[:, h * rope_width : (h + 1) * rope_width]
-        top = jnp.full((rows, 1), -1e30, F32)
-        for b, cache in enumerate(caches):
-            s = dot(q_lat, cache[:width, :]) + dot(q_rope, cache[width:, :])
-            s = s * temper
-            for i in range(per_block // chunk):
-                k = b * (per_block // chunk) + i
-                piece = s[:, i * chunk : (i + 1) * chunk]
-                piece = jnp.where(lanes + starts[k] < limit, piece, -1e30)
-                top = jnp.maximum(top, jnp.max(piece, axis=1, keepdims=True))
-                scores[:, k * chunk : (k + 1) * chunk] = piece
-        total = jnp.zeros((rows, 1), F32)
-        context = jnp.zeros((rows, width), F32)
-        for b, cache in enumerate(caches):
-            p = jnp.exp(scores[:, b * per_block : (b + 1) * per_block] - top)
-            total = total + jnp.sum(p, axis=1, keepdims=True)
-            context = context + dot_nt(p.astype(BF16), cache[:width, :])
-        context = (context / total).astype(BF16)
+        q_lat.append(dot_nt(q_nope, w_uk).astype(BF16))
+    q_lat = jnp.concatenate(q_lat, axis=0)
+    q_rope = jnp.concatenate(
+        [rope[:, h * rope_width : (h + 1) * rope_width] for h in range(heads)], axis=0
+    )
+    top = jnp.full((all_rows, 1), -1e30, F32)
+    for b, cache in enumerate(caches):
+        s = dot(q_lat, cache[:width, :]) + dot(q_rope, cache[width:, :])
+        s = s * temper
+        for i in range(per_block // chunk):
+            k = b * (per_block // chunk) + i
+            piece = s[:, i * chunk : (i + 1) * chunk]
+            piece = jnp.where(lanes + starts[k] < limit, piece, -1e30)
+            top = jnp.maximum(top, jnp.max(piece, axis=1, keepdims=True))
+            scores[:, k * chunk : (k + 1) * chunk] = piece
+    total = jnp.zeros((all_rows, 1), F32)
+    context = jnp.zeros((all_rows, width), F32)
+    for b, cache in enumerate(caches):
+        p = jnp.exp(scores[:, b * per_block : (b + 1) * per_block] - top)
+        total = total + jnp.sum(p, axis=1, keepdims=True)
+        context = context + dot_nt(p.astype(BF16), cache[:width, :])
+    context = (context / total).astype(BF16)
+    values = []
+    for h in range(heads):
         w_uv = weights[:, h, :, n_uq + n_uk :, :].reshape(-1, weights.shape[-1])
-        values.append(dot(context, w_uv).astype(BF16))
+        values.append(dot(context[h * rows : (h + 1) * rows], w_uv).astype(BF16))
     vdim = values[0].shape[1]
     wide = heads * vdim
     to = lax.broadcasted_iota(jnp.int32, (wide, wide), 1)
@@ -253,14 +275,22 @@
     give_out[...] = moved[:, wide // 2 :]
 
 
-def project_kernel(values, weights, out):
-    total = None
+def project_kernel(place, values, weights, keep_out, give_out, total):
+    core = place[3]
     half = values.shape[3]
     for y in range(values.shape[1]):
         rows = values[:, y].reshape(-1, half)
         part = dot(rows, weights[y * half : (y + 1) * half, :])
-        total = part if total is None else total + part
-    out[...] = total.astype(BF16)
+        if y == 0:
+            total[...] = part
+        else:
+            total[...] += part
+    high, low, rows, columns = keep_out.shape
+    for c, out in ((core, keep_out), (1 - core, give_out)):
+        mine = total[pl.ds(pl.multiple_of(c * high * low * rows, rows), high * low * rows)]
+        mine = mine.astype(BF16).reshape(low, high, rows, columns)
+        for z in range(high):
+            out[z] = mine[:, z]
 
 
 def local(query_latent, query_rope, lengths, kv_cache, w_uq, w_uk, w_uv, w_out):
@@ -279,7 +309,8 @@
     four, heads = heads_in // 2, heads_in // 4
 
     quarter = tokens // 4
-    place = jnp.stack([zh, yl, core * 2 + zll]).astype(jnp.int32)
+    sequence = lax.axis_index("x") * 2 + lax.axis_index("yh")
+    place = jnp.stack([zh, yl, core * 2 + zll, core, sequence]).astype(jnp.int32)
     vmem = pl.BlockSpec(memory_space=pltpu.VMEM)
     smem = pl.BlockSpec(memory_space=pltpu.SMEM)
     weights = (w_uq, w_uk, w_uv)
@@ -317,7 +348,6 @@
     spread = exchange(spread, PLANE)
 
     n_pack = kv_width + (2 * latent_chunks + 2) * own_rows
-    received, near = lax.optimization_barrier((received, near))
     sent, packed, far_piece, rope_kept = pl.pallas_call(
         lambda *refs: unpack_kernel(*refs, sizes=(kv_width, n_all, plane // 2)),
         out_shape=(
@@ -334,7 +364,11 @@
         ),
         name="unpack",
     )(place, received, *queries)
-    sent, packed, far_piece, spread = lax.optimization_barrier((sent, packed, far_piece, spread))
+    rows = 4 * own_rows
+    row_lengths = lengths.reshape(-1, rows)
+    sent, packed, far_piece, spread, near, row_lengths = lax.optimization_barrier(
+        (sent, packed, far_piece, spread, near, row_lengths)
+    )
 
     weights_far = exchange(sent.reshape(plane * heads, n_all, lanes), PLANE)
     weights_far = weights_far.reshape(plane, heads, n_all, lanes)
@@ -345,23 +379,10 @@
     far = jnp.concatenate([far_piece, packed_y[:kv_width], piece_z, piece_yz], axis=1)
     far_other = swap(far, "c")
 
-    starts = []
-    for ylo in (yl, 1 - yl):
-        for i in range(4):
-            starts.append((ylo * 2 + zh) * tokens + i * quarter)
-    for co in (core, 1 - core):
-        for zo in (zll, 1 - zll):
-            for ylo in (yl, 1 - yl):
-                starts.append((ylo * 2 + 1 - zh) * tokens + (co * 2 + zo) * quarter)
-    place = jnp.stack([zh, yl] + starts).astype(jnp.int32)
-
-    rows = 4 * own_rows
-    sequence = lax.axis_index("x") * 2 + lax.axis_index("yh")
-    row_lengths = lax.dynamic_slice_in_dim(lengths, sequence * rows, rows, 0)[:, None]
     keep, give = pl.pallas_call(
         lambda *refs: attend_kernel(
             *refs,
-            sizes=(rows, heads, n_uq, n_uk, n_uv, latent_width, len(starts)),
+            sizes=(rows, heads, n_uq, n_uk, n_uv, latent_width),
             temper=temper,
         ),
         out_shape=(jax.ShapeDtypeStruct((rows, lanes), BF16),) * 2,
@@ -370,7 +391,7 @@
         scratch_shapes=[
             pltpu.VMEM((rows, query_latent.shape[1]), BF16),
             pltpu.VMEM((rows, lanes), BF16),
-            pltpu.VMEM((rows, 4 * tokens), F32),
+            pltpu.VMEM((heads * rows, 4 * tokens), F32),
             pltpu.VMEM((plane, heads, 2, n_all, lanes), BF16),
         ],
         compiler_params=pltpu.CompilerParams(vmem_limit_bytes=VMEM_LIMIT),
@@ -392,19 +413,19 @@
         name="order",
     )(spread)
     all_rows = plane // 2 * rows
-    partial_out = pl.pallas_call(
+    keep, give = pl.pallas_call(
         project_kernel,
-        out_shape=jax.ShapeDtypeStruct((all_rows, columns), BF16),
-        in_specs=[vmem, vmem],
-        out_specs=vmem,
+        out_shape=(jax.ShapeDtypeStruct((2, 8, all_rows // 32, columns), BF16),) * 2,
+        in_specs=[smem] + [vmem] * 2,
+        out_specs=(vmem,) * 2,
+        scratch_shapes=[pltpu.VMEM((all_rows, columns), F32)],
         compiler_params=pltpu.CompilerParams(vmem_limit_bytes=VMEM_LIMIT),
         cost_estimate=pl.CostEstimate(flops=2 * 10**8, bytes_accessed=2 * 10**6, transcendentals=0),
         name="project",
-    )(gathered, out_proj)
-
-    total = exchange(partial_out, "c").reshape(2, all_rows // 2, columns)
-    total = jnp.sum(total.astype(F32), axis=0).astype(BF16)
-    total = exchange(total, COLUMN).reshape(16, all_rows // 32, columns)
+    )(place, gathered, out_proj)
+
+    total = (keep.astype(F32) + swap(give, "c").astype(F32)).astype(BF16)
+    total = exchange(total.reshape((16,) + total.shape[2:]), COLUMN)
     total = jnp.sum(total.astype(F32), axis=0).astype(BF16)
     route = []
     for xy in range(16):

time: 163 us -> 156 us (0.957)
  the two profiles are of different devices: /device:TPU:38 before, /device:TPU:30 now
where the time goes in v6:
time: 156 us; the launch traced here: 155 us
  starting transfers between devices  73.7 us (47%)
  waiting for transfers between devices  34.7 us (22%)
  blocking collectives  28.4 us (18%)
  Pallas kernels  11.4 us (7%)
  local copies, waits for them, and re-layouts  5.16 us (3%)
    ppermute x7, starting transfers between devices, swap(): return lax.ppermute(block, axis, [(0, 1), (1, 0)])  38.2 us
    all_to_all x1, blocking collectives, exchange(): return lax.all_to_all(blocks, axes, 0, 0, tiled=True)  28.4 us
    all_to_all x3, starting transfers between devices, exchange(): return lax.all_to_all(blocks, axes, 0, 0, tiled=True)  22.4 us
    ppermute x7, waiting for transfers between devices, swap(): return lax.ppermute(block, axis, [(0, 1), (1, 0)])  18.3 us
    all_to_all x3, waiting for transfers between devices, exchange(): return lax.all_to_all(blocks, axes, 0, 0, tiled=True)  10 us
    ppermute x1, starting transfers between devices, local(): return lax.ppermute(total, AXES, route)  9.58 us
    ppermute x1, waiting for transfers between devices, local(): return lax.ppermute(total, AXES, route)  6.29 us
    pallas_call x1, Pallas kernels, local(): pl.pallas_call(lambda *refs: attend_kernel(*refs, sizes=(rows, heads, n_u...  3.91 us
  transfers between devices with their start and end apart: 12, of which 7 were waited for; matrix products, arithmetic and copies ran while one was open for 2% of the time, Pallas kernels for 2%

profile of v6, /device:TPU:30, one launch (start us, length us, event | category | flops | bytes accessed | tf_op | source)
XLA Modules:
  0.0 154.9 jit_solution(1248493587806544403)
XLA Ops:
  0.0 0.0 copy-start.6
  0.0 0.6 stack.23.place.refs_0_
  0.6 2.6 %pack.1 = bf16[1120,128]{1,0:T(8,128)(2,1)} custom-call(s32[5]{0:T(128)} %stack.23.place.refs_0_, bf16[576,512]{1,0:T(8,128)(2,1)} %bitcast.11, bf16[8,48,128]{2,1,0:T(8,128)(2,1)} %w_uq.3, bf16[8,16,128]{2,1,0:T(8,128)(2,1)} %w_uk.3, bf16[8,16,128]{2,1,0:T(8,128)(2,1)} %w_uv.3, bf16[16,1536]{1,0:T(8,128)(2,1)} %refs_2_.1, bf16[16,8,64]{2,1,0:T(8,128)(2,1)} %refs_3_.1), custom_call_target="tpu_custom_call" | custom-call | flops 1000000 | bytes 1000000 | tf_op jit(solution)/shard_map/pack/pallas_call | solution.py:320
  3.2 15.7 %collective-permute-start = (bf16[1120,128]{1,0:T(8,128)(2,1)}, bf16[1120,128]{1,0:T(8,128)(2,1)S(1)}, u32[]{:S(2)}, u32[]{:S(2)}) collective-permute-start(bf16[1120,128]{1,0:T(8,128)(2,1)} %pack.1), channel_id=1, source_target_pairs={{0,16},{16,0},{1,17},{17,1},{2,18},{18,2},{3,19},{19,3},{4,20},{20... | collective-permute-start | bytes 860168 | tf_op jit(solution)/shard_map/ppermute | solution.py:24
  18.9 0.0 copy-done
  18.9 2.7 %collective-permute-start.1 = (bf16[576,512]{1,0:T(8,128)(2,1)S(1)}, bf16[576,512]{1,0:T(8,128)(2,1)S(1)}, u32[]{:S(2)}, u32[]{:S(2)}) collective-permute-start(bf16[576,512]{1,0:T(8,128)(2,1)S(1)} %bitcast.12), channel_id=1, source_target_pairs={{0,32},{32,0},{1,33},{33,1},{2,34},{34,2},{3,35},{35,3},{4,36},{36... | collective-permute-start | bytes 1769480 | tf_op jit(solution)/shard_map/ppermute | solution.py:24
  21.6 1.1 reshape.52.w_out
  22.7 0.0 copy-done.3
  22.7 0.0 copy-done.5
  22.8 0.0 copy-done.6
  22.8 0.0 copy-done.9
  22.8 1.9 %spread.1 = bf16[16,288,128]{2,1,0:T(8,128)(2,1)} custom-call(s32[5]{0:T(128)S(1)} %copy-done.9, bf16[8,48,128]{2,1,0:T(8,128)(2,1)S(1)} %copy-done.3, bf16[8,16,128]{2,1,0:T(8,128)(2,1)S(1)} %copy-done.5, bf16[8,16,128]{2,1,0:T(8,128)(2,1)S(1)} %copy-done.6, bf16[32,7168]{1,0:T(8,128)(2,1)S(1)} %reshape.52.w_out), custom_call_target="tpu_custom_call" | custom-call | flops 1000000 | bytes 1000000 | tf_op jit(solution)/shard_map/spread/pallas_call | solution.py:339
  24.6 7.8 %all-to-all-start = ((bf16[16,288,128]{2,1,0:T(8,128)(2,1)}), bf16[16,288,128]{2,1,0:T(8,128)(2,1)S(1)}, u32[]{:S(2)}, u32[]{:S(2)}) async-start(bf16[16,288,128]{2,1,0:T(8,128)(2,1)} %spread.1), calls=%async_computation | async-start | bytes 2359296 | tf_op jit(solution)/shard_map/all_to_all | solution.py:36
  32.4 0.1 reshape.53.refs_6_
  32.5 0.0 collective-permute-done.refs_1_
  32.5 0.0 copy-done.7
  32.5 1.5 unpack.1
  34.0 12.6 %collective-permute-done.1.refs_8_ = bf16[576,512]{1,0:T(8,128)(2,1)S(1)} collective-permute-done((bf16[576,512]{1,0:T(8,128)(2,1)S(1)}, bf16[576,512]{1,0:T(8,128)(2,1)S(1)}, u32[]{:S(2)}, u32[]{:S(2)}) %collective-permute-start.1) | collective-permute-done | bytes 589856 | tf_op jit(solution)/shard_map/ppermute | solution.py:24
  46.6 0.8 copy-done.1
  47.4 0.9 all-to-all-done.refs_3_.received
  48.3 2.7 %collective-permute-start.2 = (bf16[992,128]{1,0:T(8,128)(2,1)S(1)}, bf16[992,128]{1,0:T(8,128)(2,1)S(1)}, u32[]{:S(2)}, u32[]{:S(2)}) collective-permute-start(bf16[992,128]{1,0:T(8,128)(2,1)S(1)} %get-tuple-element.22.refs_1_), channel_id=1, source_target_pairs={{0,32},{32,0},{1,33},{33,1},{2,34},{34,2},{3,35},{35,3},{4,36},{36... | collective-permute-start | bytes 761864 | tf_op jit(solution)/shard_map/ppermute | solution.py:24
  51.0 3.6 %collective-permute-start.4 = (bf16[576,128]{1,0:T(8,128)(2,1)S(1)}, bf16[576,128]{1,0:T(8,128)(2,1)}, u32[]{:S(2)}, u32[]{:S(2)}) collective-permute-start(bf16[576,128]{1,0:T(8,128)(2,1)S(1)} %get-tuple-element.28), channel_id=1, source_target_pairs={{0,34},{2,32},{32,2},{34,0},{1,35},{3,33},{33,3},{35,1},{4,38},{6,... | collective-permute-start | bytes 442376 | tf_op jit(solution)/shard_map/ppermute | solution.py:378
  54.6 2.9 %collective-permute-start.3 = (bf16[576,128]{1,0:T(8,128)(2,1)S(1)}, bf16[576,128]{1,0:T(8,128)(2,1)}, u32[]{:S(2)}, u32[]{:S(2)}) collective-permute-start(bf16[576,128]{1,0:T(8,128)(2,1)S(1)} %get-tuple-element.28), channel_id=1, source_target_pairs={{0,2},{2,0},{1,3},{3,1},{4,6},{6,4},{5,7},{7,5},{8,10},{10,8},{9,1... | collective-permute-start | bytes 442376 | tf_op jit(solution)/shard_map/ppermute | solution.py:24
  57.5 7.0 %all-to-all-start.1 = ((bf16[32,80,128]{2,1,0:T(8,128)(2,1)}), bf16[32,80,128]{2,1,0:T(8,128)(2,1)S(1)}, u32[]{:S(2)}, u32[]{:S(2)}) async-start(bf16[32,80,128]{2,1,0:T(8,128)(2,1)} %bitcast.6), calls=%async_computation.1 | async-start | bytes 1310720 | tf_op jit(solution)/shard_map/all_to_all | solution.py:36
  64.6 0.0 collective-permute-done.2.refs_2_
  64.6 0.0 collective-permute-done.4
  64.6 0.0 collective-permute-done.3
  64.6 1.1 pad_maximum_fusion.refs_9_
  65.8 1.9 %collective-permute-start.5 = (bf16[576,512]{1,0:T(8,128)(2,1)S(1)}, bf16[576,512]{1,0:T(8,128)(2,1)}, u32[]{:S(2)}, u32[]{:S(2)}) collective-permute-start(bf16[576,512]{1,0:T(8,128)(2,1)S(1)} %pad_maximum_fusion.refs_9_), channel_id=1, source_target_pairs={{0,1},{1,0},{2,3},{3,2},{4,5},{5,4},{6,7},{7,6},{8,9},{9,8},{10,11... | collective-permute-start | bytes 1769480 | tf_op jit(solution)/shard_map/ppermute | solution.py:24
  67.7 3.6 %all-to-all-done.1 = bf16[32,80,128]{2,1,0:T(8,128)(2,1)S(1)} async-done(((bf16[32,80,128]{2,1,0:T(8,128)(2,1)}), bf16[32,80,128]{2,1,0:T(8,128)(2,1)S(1)}, u32[]{:S(2)}, u32[]{:S(2)}) %all-to-all-start.1) | async-done | bytes 655392 | tf_op jit(solution)/shard_map/all_to_all | solution.py:36
  71.3 0.0 collective-permute-done.5.refs_10_
  71.3 1.1 copy-done.2
  72.4 3.9 %attend.1 = (bf16[64,128]{1,0:T(8,128)(2,1)S(1)}, bf16[64,128]{1,0:T(8,128)(2,1)}) custom-call(s32[5]{0:T(128)S(1)} %copy-done.9, bf16[992,128]{1,0:T(8,128)(2,1)S(1)} %get-tuple-element.22.refs_1_, bf16[992,128]{1,0:T(8,128)(2,1)S(1)} %collective-permute-done.2.refs_2_, bf16[16,288,128]{2,1,0:T(8,128)(2,1)S(1)} %all-to-all-done.refs_3_.received, ...), custom_call_target="tpu_custom_call" | custom-call | flops 1000000000 | bytes 5000000 | tf_op jit(solution)/shard_map/attend/pallas_call | solution.py:382
  76.3 10.3 %collective-permute-start.6 = (bf16[64,128]{1,0:T(8,128)(2,1)}, bf16[64,128]{1,0:T(8,128)(2,1)S(1)}, u32[]{:S(2)}, u32[]{:S(2)}) collective-permute-start(bf16[64,128]{1,0:T(8,128)(2,1)} %get-tuple-element.29), channel_id=1, source_target_pairs={{0,16},{16,0},{1,17},{17,1},{2,18},{18,2},{3,19},{19,3},{4,20},{20... | collective-permute-start | bytes 49160 | tf_op jit(solution)/shard_map/ppermute | solution.py:24
  86.7 4.2 %collective-permute-done.6 = bf16[64,128]{1,0:T(8,128)(2,1)S(1)} collective-permute-done((bf16[64,128]{1,0:T(8,128)(2,1)}, bf16[64,128]{1,0:T(8,128)(2,1)S(1)}, u32[]{:S(2)}, u32[]{:S(2)}) %collective-permute-start.6) | collective-permute-done | bytes 16416 | tf_op jit(solution)/shard_map/ppermute | solution.py:24
  90.9 0.9 broadcast_in_dim.2
  91.7 7.6 %all-to-all-start.2 = ((bf16[16,64,256]{2,1,0:T(8,128)(2,1)}), bf16[16,64,256]{2,1,0:T(8,128)(2,1)S(1)}, u32[]{:S(2)}, u32[]{:S(2)}) async-start(bf16[16,64,256]{2,1,0:T(8,128)(2,1)} %broadcast_in_dim.2), calls=%async_computation.2 | async-start | bytes 1048576 | tf_op jit(solution)/shard_map/all_to_all | solution.py:36
  99.3 0.5 order.1.weights
  99.8 5.5 %all-to-all-done.2 = bf16[16,64,256]{2,1,0:T(8,128)(2,1)S(1)} async-done(((bf16[16,64,256]{2,1,0:T(8,128)(2,1)}), bf16[16,64,256]{2,1,0:T(8,128)(2,1)S(1)}, u32[]{:S(2)}, u32[]{:S(2)}) %all-to-all-start.2) | async-done | bytes 524320 | tf_op jit(solution)/shard_map/all_to_all | solution.py:36
  105.3 1.0 project.1
  106.4 1.9 %collective-permute-start.7 = (bf16[2,8,16,448]{3,2,1,0:T(8,128)(2,1)S(1)}, bf16[2,8,16,448]{3,2,1,0:T(8,128)(2,1)S(1)}, u32[]{:S(2)}, u32[]{:S(2)}) collective-permute-start(bf16[2,8,16,448]{3,2,1,0:T(8,128)(2,1)S(1)} %get-tuple-element.32), channel_id=1, source_target_pairs={{0,1},{1,0},{2,3},{3,2},{4,5},{5,4},{6,7},{7,6},{8,9},{9,8},{10,11... | collective-permute-start | bytes 688136 | tf_op jit(solution)/shard_map/ppermute | solution.py:24
  108.3 1.5 collective-permute-done.7
  109.8 0.1 add_convert_fusion
  109.9 28.4 %all_to_all.21 = bf16[16,16,448]{2,1,0:T(8,128)(2,1)S(1)} all-to-all(bf16[16,16,448]{2,1,0:T(8,128)(2,1)S(1)} %bitcast.15), channel_id=1, replica_groups=mesh['x'=4,'yh'=2,'yl'=2,'zh'=2,'zlh'=4,'zll'=2,'c'=2] {'zh','zlh','zll'}, dimensions={0} | all-to-all | bytes 458752 | tf_op jit(solution)/shard_map/all_to_all | solution.py:36
  138.3 0.1 reduce_sum.12
  138.4 9.6 %collective-permute-start.8 = (bf16[16,448]{1,0:T(8,128)(2,1)S(1)}, bf16[16,448]{1,0:T(8,128)(2,1)S(1)}, u32[]{:S(2)}, u32[]{:S(2)}) collective-permute-start(bf16[16,448]{1,0:T(8,128)(2,1)S(1)} %reduce_sum.12), channel_id=1, source_target_pairs={{0,0},{1,256},{2,32},{3,288},{4,64},{5,320},{6,96},{7,352},{8,128}... | collective-permute-start | bytes 43016 | tf_op jit(solution)/shard_map/ppermute | solution.py:437
  148.0 6.3 %collective-permute-done.8 = bf16[16,448]{1,0:T(8,128)(2,1)S(1)} collective-permute-done((bf16[16,448]{1,0:T(8,128)(2,1)S(1)}, bf16[16,448]{1,0:T(8,128)(2,1)S(1)}, u32[]{:S(2)}, u32[]{:S(2)}) %collective-permute-start.8) | collective-permute-done | bytes 14368 | tf_op jit(solution)/shard_map/ppermute | solution.py:437
  154.3 0.6 copy.10
  (15 shorter events, 0.0 us)
Async XLA Ops:
  0.0 18.9 %copy-start = (bf16[512,576]{0,1:T(8,128)(2,1)S(1)}, bf16[512,576]{0,1:T(8,128)(2,1)}, u32[]{:S(2)}) copy-start(bf16[512,576]{0,1:T(8,128)(2,1)} %param.11) | copy-start | bytes 1769476
  0.0 22.7 %copy-start.3 = (bf16[8,48,128]{2,1,0:T(8,128)(2,1)S(1)}, bf16[8,48,128]{2,1,0:T(8,128)(2,1)}, u32[]{:S(2)}) copy-start(bf16[8,48,128]{2,1,0:T(8,128)(2,1)} %w_uq.3) | copy-start | bytes 294916
  0.0 22.7 %copy-start.5 = (bf16[8,16,128]{2,1,0:T(8,128)(2,1)S(1)}, bf16[8,16,128]{2,1,0:T(8,128)(2,1)}, u32[]{:S(2)}) copy-start(bf16[8,16,128]{2,1,0:T(8,128)(2,1)} %w_uk.3) | copy-start | bytes 98308
  0.0 22.7 %copy-start.6 = (bf16[8,16,128]{2,1,0:T(8,128)(2,1)S(1)}, bf16[8,16,128]{2,1,0:T(8,128)(2,1)}, u32[]{:S(2)}) copy-start(bf16[8,16,128]{2,1,0:T(8,128)(2,1)} %w_uv.3) | copy-start | bytes 98308
  0.6 22.2 %copy-start.9 = (s32[5]{0:T(128)S(1)}, s32[5]{0:T(128)}, u32[]{:S(2)}) copy-start(s32[5]{0:T(128)} %stack.23.place.refs_0_) | copy-start | bytes 64
  3.2 29.3 %collective-permute-start = (bf16[1120,128]{1,0:T(8,128)(2,1)}, bf16[1120,128]{1,0:T(8,128)(2,1)S(1)}, u32[]{:S(2)}, u32[]{:S(2)}) collective-permute-start(bf16[1120,128]{1,0:T(8,128)(2,1)} %pack.1), channel_id=1, source_target_pairs={{0,16},{16,0},{1,17},{17,1},{2,18},{18,2},{3,19},{19,3},{4,20},{20... | collective-permute-start | bytes 860168 | tf_op jit(solution)/shard_map/ppermute | solution.py:24
  18.9 27.7 %collective-permute-start.1 = (bf16[576,512]{1,0:T(8,128)(2,1)S(1)}, bf16[576,512]{1,0:T(8,128)(2,1)S(1)}, u32[]{:S(2)}, u32[]{:S(2)}) collective-permute-start(bf16[576,512]{1,0:T(8,128)(2,1)S(1)} %bitcast.12), channel_id=1, source_target_pairs={{0,32},{32,0},{1,33},{33,1},{2,34},{34,2},{3,35},{35,3},{4,36},{36... | collective-permute-start | bytes 1769480 | tf_op jit(solution)/shard_map/ppermute | solution.py:24
  24.6 7.8 %copy-start.10 = (s32[512]{0:T(512)S(1)}, s32[512]{0:T(512)}, u32[]{:S(2)}) copy-start(s32[512]{0:T(512)} %param.10) | copy-start | bytes 6148
  24.6 7.8 %copy-start.7 = (bf16[16,1536]{1,0:T(8,128)(2,1)S(1)}, bf16[16,1536]{1,0:T(8,128)(2,1)}, u32[]{:S(2)}) copy-start(bf16[16,1536]{1,0:T(8,128)(2,1)} %refs_2_.1) | copy-start | bytes 147460
  24.6 7.8 %copy-start.8 = (bf16[16,8,64]{2,1,0:T(8,128)(2,1)S(1)}, bf16[16,8,64]{2,1,0:T(8,128)(2,1)}, u32[]{:S(2)}) copy-start(bf16[16,8,64]{2,1,0:T(8,128)(2,1)} %refs_3_.1) | copy-start | bytes 49156
  24.6 23.7 %all-to-all-start = ((bf16[16,288,128]{2,1,0:T(8,128)(2,1)}), bf16[16,288,128]{2,1,0:T(8,128)(2,1)S(1)}, u32[]{:S(2)}, u32[]{:S(2)}) async-start(bf16[16,288,128]{2,1,0:T(8,128)(2,1)} %spread.1), calls=%async_computation | async-start | bytes 2359296 | tf_op jit(solution)/shard_map/all_to_all | solution.py:36
  34.0 30.6 %copy-start.4 = (bf16[576,128]{1,0:T(8,128)(2,1)}, bf16[576,128]{1,0:T(8,128)(2,1)S(1)}, u32[]{:S(2)}) copy-start(bf16[576,128]{1,0:T(8,128)(2,1)S(1)} %get-tuple-element.28) | copy-start | bytes 442372
  46.6 0.8 copy-start.1
  48.3 16.3 %collective-permute-start.2 = (bf16[992,128]{1,0:T(8,128)(2,1)S(1)}, bf16[992,128]{1,0:T(8,128)(2,1)S(1)}, u32[]{:S(2)}, u32[]{:S(2)}) collective-permute-start(bf16[992,128]{1,0:T(8,128)(2,1)S(1)} %get-tuple-element.22.refs_1_), channel_id=1, source_target_pairs={{0,32},{32,0},{1,33},{33,1},{2,34},{34,2},{3,35},{35,3},{4,36},{36... | collective-permute-start | bytes 761864 | tf_op jit(solution)/shard_map/ppermute | solution.py:24
  51.0 13.6 %collective-permute-start.4 = (bf16[576,128]{1,0:T(8,128)(2,1)S(1)}, bf16[576,128]{1,0:T(8,128)(2,1)}, u32[]{:S(2)}, u32[]{:S(2)}) collective-permute-start(bf16[576,128]{1,0:T(8,128)(2,1)S(1)} %get-tuple-element.28), channel_id=1, source_target_pairs={{0,34},{2,32},{32,2},{34,0},{1,35},{3,33},{33,3},{35,1},{4,38},{6,... | collective-permute-start | bytes 442376 | tf_op jit(solution)/shard_map/ppermute | solution.py:378
  54.6 10.0 %collective-permute-start.3 = (bf16[576,128]{1,0:T(8,128)(2,1)S(1)}, bf16[576,128]{1,0:T(8,128)(2,1)}, u32[]{:S(2)}, u32[]{:S(2)}) collective-permute-start(bf16[576,128]{1,0:T(8,128)(2,1)S(1)} %get-tuple-element.28), channel_id=1, source_target_pairs={{0,2},{2,0},{1,3},{3,1},{4,6},{6,4},{5,7},{7,5},{8,10},{10,8},{9,1... | collective-permute-start | bytes 442376 | tf_op jit(solution)/shard_map/ppermute | solution.py:24
  57.5 13.8 %all-to-all-start.1 = ((bf16[32,80,128]{2,1,0:T(8,128)(2,1)}), bf16[32,80,128]{2,1,0:T(8,128)(2,1)S(1)}, u32[]{:S(2)}, u32[]{:S(2)}) async-start(bf16[32,80,128]{2,1,0:T(8,128)(2,1)} %bitcast.6), calls=%async_computation.1 | async-start | bytes 1310720 | tf_op jit(solution)/shard_map/all_to_all | solution.py:36
  65.8 5.6 %collective-permute-start.5 = (bf16[576,512]{1,0:T(8,128)(2,1)S(1)}, bf16[576,512]{1,0:T(8,128)(2,1)}, u32[]{:S(2)}, u32[]{:S(2)}) collective-permute-start(bf16[576,512]{1,0:T(8,128)(2,1)S(1)} %pad_maximum_fusion.refs_9_), channel_id=1, source_target_pairs={{0,1},{1,0},{2,3},{3,2},{4,5},{5,4},{6,7},{7,6},{8,9},{9,8},{10,11... | collective-permute-start | bytes 1769480 | tf_op jit(solution)/shard_map/ppermute | solution.py:24
  71.3 1.1 copy-start.2
  76.3 14.5 %collective-permute-start.6 = (bf16[64,128]{1,0:T(8,128)(2,1)}, bf16[64,128]{1,0:T(8,128)(2,1)S(1)}, u32[]{:S(2)}, u32[]{:S(2)}) collective-permute-start(bf16[64,128]{1,0:T(8,128)(2,1)} %get-tuple-element.29), channel_id=1, source_target_pairs={{0,16},{16,0},{1,17},{17,1},{2,18},{18,2},{3,19},{19,3},{4,20},{20... | collective-permute-start | bytes 49160 | tf_op jit(solution)/shard_map/ppermute | solution.py:24
  91.7 13.6 %all-to-all-start.2 = ((bf16[16,64,256]{2,1,0:T(8,128)(2,1)}), bf16[16,64,256]{2,1,0:T(8,128)(2,1)S(1)}, u32[]{:S(2)}, u32[]{:S(2)}) async-start(bf16[16,64,256]{2,1,0:T(8,128)(2,1)} %broadcast_in_dim.2), calls=%async_computation.2 | async-start | bytes 1048576 | tf_op jit(solution)/shard_map/all_to_all | solution.py:36
  106.4 3.4 %collective-permute-start.7 = (bf16[2,8,16,448]{3,2,1,0:T(8,128)(2,1)S(1)}, bf16[2,8,16,448]{3,2,1,0:T(8,128)(2,1)S(1)}, u32[]{:S(2)}, u32[]{:S(2)}) collective-permute-start(bf16[2,8,16,448]{3,2,1,0:T(8,128)(2,1)S(1)} %get-tuple-element.32), channel_id=1, source_target_pairs={{0,1},{1,0},{2,3},{3,2},{4,5},{5,4},{6,7},{7,6},{8,9},{9,8},{10,11... | collective-permute-start | bytes 688136 | tf_op jit(solution)/shard_map/ppermute | solution.py:24
  138.4 15.9 %collective-permute-start.8 = (bf16[16,448]{1,0:T(8,128)(2,1)S(1)}, bf16[16,448]{1,0:T(8,128)(2,1)S(1)}, u32[]{:S(2)}, u32[]{:S(2)}) collective-permute-start(bf16[16,448]{1,0:T(8,128)(2,1)S(1)} %reduce_sum.12), channel_id=1, source_target_pairs={{0,0},{1,256},{2,32},{3,288},{4,64},{5,320},{6,96},{7,352},{8,128}... | collective-permute-start | bytes 43016 | tf_op jit(solution)/shard_map/ppermute | solution.py:437

commit v7 on v6

--- a/solution.py
+++ b/solution.py
@@ -2,6 +2,7 @@
 
 import jax
 import jax.numpy as jnp
+import numpy as np
 from jax import lax
 from jax.experimental import pallas as pl
 from jax.experimental.pallas import tpu as pltpu
@@ -12,6 +13,7 @@
 FSDP = ("x", "yh", "yl", "zh")
 HEAD = ("zlh", "zll", "c")
 PLANE = ("x", "yh", "yl")
+RING = ("yh", "yl")
 COLUMN = ("zh", "zlh", "zll")
 BF16 = jnp.bfloat16
 F32 = jnp.float32
@@ -98,49 +100,28 @@
             for copy in range(h // (four // 2), copies, 2):
                 out[copy, at : at + w.shape[1]] = block
             at += w.shape[1]
-    rows, columns = w_out.shape[0], w_out.shape[1] // copies
+    rows, columns = w_out.shape[0], (out.shape[1] - at) // w_out.shape[0] * lanes
+    parts = w_out.shape[1] // columns
     for copy in range(copies):
-        to = at
-        for begin in range(0, columns, lanes):
-            width = min(lanes, columns - begin)
-            block = w_out[:, copy * columns + begin : copy * columns + begin + width]
-            if width < lanes:
-                block = jnp.concatenate([block, jnp.zeros((rows, lanes - width), BF16)], axis=1)
-            out[copy, to : to + rows] = block
-            to += rows
-
-
-def order_kernel(received, out):
-    rows, columns = out.shape
-    copies, lanes = received.shape[0], received.shape[2]
-    each = rows // copies
-    count = -(-columns // lanes)
-    first = received.shape[1] - count * each
-    blocks = [
-        received[:, first + i * each : first + (i + 1) * each].reshape(rows, lanes)
-        for i in range(count)
-    ]
-    weights = jnp.concatenate(blocks, axis=1)[:, :columns]
-    to = lax.broadcasted_iota(jnp.int32, (rows, rows), 0)
-    source = lax.broadcasted_iota(jnp.int32, (rows, rows), 1)
-    y, z, j, xy, v = to // 256, to // 128 % 2, to // 64 % 2, to // 4 % 16, to % 4
-    move = jnp.where(source == xy * 32 + (z * 4 + y * 2 + j) * 4 + v, 1.0, 0.0).astype(BF16)
-    out[...] = dot(move, weights).astype(BF16)
-
-
-def unpack_kernel(
-    place, received, latent, rope, sent, packed, piece, rope_out, *, sizes
-):
-    n_piece, n_all, copies = sizes
+        begin = copy % parts * columns
+        for i in range(columns // lanes):
+            block = w_out[:, begin + i * lanes : begin + (i + 1) * lanes]
+            out[copy, at + i * rows : at + (i + 1) * rows] = block
+
+
+def repeat_kernel(received, sent, *, first):
+    copies, heads, rows = sent.shape[:3]
+    for h in range(heads):
+        block = received[first + h * rows : first + (h + 1) * rows]
+        for copy in range(copies):
+            sent[copy, h] = block
+
+
+def unpack_kernel(place, received, latent, rope, packed, piece, rope_out, *, sizes):
+    n_piece, at = sizes
     zh, yl = place[0], place[1]
     own_rows = latent.shape[0]
     lanes = packed.shape[1]
-    at = n_piece
-    for h in range(sent.shape[1]):
-        other = received[at : at + n_all]
-        for copy in range(copies):
-            sent[copy, h] = other
-        at += n_all
     ours = pl.ds(pl.multiple_of(zh * own_rows, 16), own_rows)
     theirs = pl.ds(pl.multiple_of((1 - zh) * own_rows, 16), own_rows)
     to = n_piece
@@ -275,22 +256,35 @@
     give_out[...] = moved[:, wide // 2 :]
 
 
-def project_kernel(place, values, weights, keep_out, give_out, total):
+def feature_order(heads, plane, items):
+    count = 4 * heads * plane * items
+    to = np.arange(count).reshape(plane, 2, 2, heads, items).transpose(2, 1, 3, 0, 4).reshape(-1)
+    return np.equal(to[:, None], np.arange(count)[None, :]).astype(np.float32)
+
+
+def project_kernel(place, values, received, order, keep_out, give_out):
     core = place[3]
-    half = values.shape[3]
-    for y in range(values.shape[1]):
-        rows = values[:, y].reshape(-1, half)
-        part = dot(rows, weights[y * half : (y + 1) * half, :])
-        if y == 0:
-            total[...] = part
-        else:
-            total[...] += part
-    high, low, rows, columns = keep_out.shape
-    for c, out in ((core, keep_out), (1 - core, give_out)):
-        mine = total[pl.ds(pl.multiple_of(c * high * low * rows, rows), high * low * rows)]
-        mine = mine.astype(BF16).reshape(low, high, rows, columns)
-        for z in range(high):
-            out[z] = mine[:, z]
+    lanes = received.shape[2]
+    rows = [jnp.concatenate([values[2 * i], values[2 * i + 1]], axis=1) for i in range(2)]
+    rows = dot(jnp.concatenate(rows, axis=0), order[...]).astype(BF16)
+    depth = rows.shape[1]
+    each = depth // received.shape[0]
+    blocks, _, low, _, columns = keep_out.shape
+    count = 2 * columns // lanes
+    first = received.shape[1] - low * count * each
+    for z in range(low):
+        weights = jnp.concatenate(
+            [
+                received[:, at : at + each].reshape(depth, lanes)
+                for at in range(first + z * count * each, first + (z + 1) * count * each, each)
+            ],
+            axis=1,
+        )
+        part = dot(rows, weights)
+        even, odd = part[:, :columns], part[:, columns:]
+        shape = keep_out.shape[:2] + keep_out.shape[3:]
+        keep_out[:, :, z] = jnp.where(core == 0, even, odd).astype(BF16).reshape(shape)
+        give_out[:, :, z] = jnp.where(core == 0, odd, even).astype(BF16).reshape(shape)
 
 
 def local(query_latent, query_rope, lengths, kv_cache, w_uq, w_uk, w_uv, w_out):
@@ -333,9 +327,9 @@
     received = swap(packed, "zh")
 
     vpart, width = w_out.shape[1:]
-    columns = width // plane
+    columns = width // 4
     w_rows = heads_in * vpart
-    n_spread = heads * n_all + -(-columns // lanes) * w_rows
+    n_spread = heads * n_all + columns // lanes * w_rows
     spread = pl.pallas_call(
         spread_kernel,
         out_shape=jax.ShapeDtypeStruct((plane, n_spread, lanes), BF16),
@@ -348,16 +342,15 @@
     spread = exchange(spread, PLANE)
 
     n_pack = kv_width + (2 * latent_chunks + 2) * own_rows
-    sent, packed, far_piece, rope_kept = pl.pallas_call(
-        lambda *refs: unpack_kernel(*refs, sizes=(kv_width, n_all, plane // 2)),
+    packed, far_piece, rope_kept = pl.pallas_call(
+        lambda *refs: unpack_kernel(*refs, sizes=(kv_width, kv_width + four * n_all)),
         out_shape=(
-            jax.ShapeDtypeStruct((plane // 2, four, n_all, lanes), BF16),
             jax.ShapeDtypeStruct((n_pack, lanes), BF16),
             jax.ShapeDtypeStruct((kv_width, quarter), BF16),
             jax.ShapeDtypeStruct((2 * own_rows, lanes), BF16),
         ),
         in_specs=[smem] + [vmem] * 3,
-        out_specs=(vmem,) * 4,
+        out_specs=(vmem,) * 3,
         compiler_params=pltpu.CompilerParams(vmem_limit_bytes=VMEM_LIMIT),
         cost_estimate=pl.CostEstimate(
             flops=UNPACK_FLOPS, bytes_accessed=3 * 10**6, transcendentals=0
@@ -366,9 +359,22 @@
     )(place, received, *queries)
     rows = 4 * own_rows
     row_lengths = lengths.reshape(-1, rows)
-    sent, packed, far_piece, spread, near, row_lengths = lax.optimization_barrier(
-        (sent, packed, far_piece, spread, near, row_lengths)
-    )
+    packed, far_piece, received, row_lengths = lax.optimization_barrier(
+        (packed, far_piece, received, row_lengths)
+    )
+    received, near = lax.optimization_barrier((received, near))
+    sent = pl.pallas_call(
+        lambda *refs: repeat_kernel(*refs, first=kv_width),
+        out_shape=jax.ShapeDtypeStruct((plane // 2, four, n_all, lanes), BF16),
+        in_specs=[vmem],
+        out_specs=vmem,
+        compiler_params=pltpu.CompilerParams(vmem_limit_bytes=VMEM_LIMIT),
+        cost_estimate=pl.CostEstimate(
+            flops=UNPACK_FLOPS, bytes_accessed=3 * 10**6, transcendentals=0
+        ),
+        name="repeat",
+    )(received)
+    sent, spread = lax.optimization_barrier((sent, spread))
 
     weights_far = exchange(sent.reshape(plane * heads, n_all, lanes), PLANE)
     weights_far = weights_far.reshape(plane, heads, n_all, lanes)
@@ -401,40 +407,24 @@
 
     values = ordered(keep, swap(give, "zh"), zh, 1)
     gathered = exchange(
-        jnp.broadcast_to(values[None], (plane,) + values.shape).reshape(-1, values.shape[1]), PLANE
-    ).reshape(plane // 2, 2, rows, heads * lanes)
-    out_proj = pl.pallas_call(
-        order_kernel,
-        out_shape=jax.ShapeDtypeStruct((plane * w_rows, columns), BF16),
-        in_specs=[vmem],
-        out_specs=vmem,
-        compiler_params=pltpu.CompilerParams(vmem_limit_bytes=VMEM_LIMIT),
-        cost_estimate=pl.CostEstimate(flops=2 * 10**8, bytes_accessed=2 * 10**6, transcendentals=0),
-        name="order",
-    )(spread)
-    all_rows = plane // 2 * rows
+        jnp.broadcast_to(values[None], (4,) + values.shape).reshape(-1, values.shape[1]), RING
+    ).reshape((4,) + values.shape)
+    order = jnp.asarray(feature_order(heads, plane, vpart), BF16)
+    shape = (4, 2, 2, own_rows, columns // 4)
     keep, give = pl.pallas_call(
         project_kernel,
-        out_shape=(jax.ShapeDtypeStruct((2, 8, all_rows // 32, columns), BF16),) * 2,
-        in_specs=[smem] + [vmem] * 2,
+        out_shape=(jax.ShapeDtypeStruct(shape, BF16),) * 2,
+        in_specs=[smem] + [vmem] * 3,
         out_specs=(vmem,) * 2,
-        scratch_shapes=[pltpu.VMEM((all_rows, columns), F32)],
         compiler_params=pltpu.CompilerParams(vmem_limit_bytes=VMEM_LIMIT),
         cost_estimate=pl.CostEstimate(flops=2 * 10**8, bytes_accessed=2 * 10**6, transcendentals=0),
         name="project",
-    )(place, gathered, out_proj)
+    )(place, gathered, spread, order)
 
     total = (keep.astype(F32) + swap(give, "c").astype(F32)).astype(BF16)
-    total = exchange(total.reshape((16,) + total.shape[2:]), COLUMN)
-    total = jnp.sum(total.astype(F32), axis=0).astype(BF16)
-    route = []
-    for xy in range(16):
-        for z_hi in range(2):
-            for z_lo in range(8):
-                for c in range(2):
-                    source = ((xy * 2 + z_hi) * 8 + z_lo) * 2 + c
-                    route.append((source, (c * 16 + z_lo * 2 + z_hi) * 16 + xy))
-    return lax.ppermute(total, AXES, route)
+    total = jnp.transpose(exchange(total, RING), (1, 0, 2, 3, 4))
+    total = exchange(total.reshape((16,) + total.shape[3:]), COLUMN)
+    return jnp.sum(total.astype(F32), axis=0).astype(BF16)
 
 
 def solution(mesh):

time: 156 us -> 163 us (1.045)
  the two profiles are of different devices: /device:TPU:30 before, /device:TPU:6 now
where the time goes in v7:
time: 163 us; the launch traced here: 161 us
  starting transfers between devices  60.3 us (37%)
  blocking collectives  41.8 us (26%)
  waiting for transfers between devices  34.1 us (21%)
  local copies, waits for them, and re-layouts  13.5 us (8%)
  Pallas kernels  9.48 us (6%)
  other arithmetic  1.87 us (1%)
    all_to_all x3, blocking collectives, exchange(): return lax.all_to_all(blocks, axes, 0, 0, tiled=True)  41.8 us
    ppermute x7, starting transfers between devices, swap(): return lax.ppermute(block, axis, [(0, 1), (1, 0)])  31.4 us
    ppermute x7, waiting for transfers between devices, swap(): return lax.ppermute(block, axis, [(0, 1), (1, 0)])  30.5 us
    all_to_all x2, starting transfers between devices, exchange(): return lax.all_to_all(blocks, axes, 0, 0, tiled=True)  14.9 us
    ppermute x1, starting transfers between devices, local(): lax.ppermute(far_piece, ('yl', 'zll'), [(0, 3), (1, 2), (2, 1), (3, 0)])  14 us
    unnamed x48, local copies, waits for them, and re-layouts  11.5 us
    all_to_all x2, waiting for transfers between devices, exchange(): return lax.all_to_all(blocks, axes, 0, 0, tiled=True)  3.66 us
    pallas_call x1, Pallas kernels, local(): pl.pallas_call(lambda *refs: attend_kernel(*refs, sizes=(rows, heads, n_u...  3.29 us
  transfers between devices with their start and end apart: 10, of which 5 were waited for; matrix products, arithmetic and copies ran while one was open for 1% of the time, Pallas kernels for 1%

profile of v7, /device:TPU:6, one launch (start us, length us, event | category | flops | bytes accessed | tf_op | source)
XLA Modules:
  0.0 161.3 jit_solution(3976601216025821963)
XLA Ops:
  0.0 0.0 copy-start.15
  0.0 0.7 stack.23.place.refs_0_
  0.7 2.6 %pack.1 = bf16[1120,128]{1,0:T(8,128)(2,1)} custom-call(s32[5]{0:T(128)} %stack.23.place.refs_0_, bf16[576,512]{1,0:T(8,128)(2,1)} %bitcast.11, bf16[8,48,128]{2,1,0:T(8,128)(2,1)} %w_uq.3, bf16[8,16,128]{2,1,0:T(8,128)(2,1)} %w_uk.3, bf16[8,16,128]{2,1,0:T(8,128)(2,1)} %w_uv.3, bf16[16,1536]{1,0:T(8,128)(2,1)} %refs_2_.1, bf16[16,8,64]{2,1,0:T(8,128)(2,1)} %refs_3_.1), custom_call_target="tpu_custom_call" | custom-call | flops 1000000 | bytes 1000000 | tf_op jit(solution)/shard_map/pack/pallas_call | solution.py:314
  3.3 15.7 %collective-permute-start = (bf16[1120,128]{1,0:T(8,128)(2,1)}, bf16[1120,128]{1,0:T(8,128)(2,1)S(1)}, u32[]{:S(2)}, u32[]{:S(2)}) collective-permute-start(bf16[1120,128]{1,0:T(8,128)(2,1)} %pack.1), channel_id=1, source_target_pairs={{0,16},{16,0},{1,17},{17,1},{2,18},{18,2},{3,19},{19,3},{4,20},{20... | collective-permute-start | bytes 860168 | tf_op jit(solution)/shard_map/ppermute | solution.py:26
  19.1 3.5 %collective-permute-start.2 = (bf16[576,512]{1,0:T(8,128)(2,1)S(1)}, bf16[576,512]{1,0:T(8,128)(2,1)}, u32[]{:S(2)}, u32[]{:S(2)}) collective-permute-start(bf16[576,512]{1,0:T(8,128)(2,1)S(1)} %bitcast.12), channel_id=1, source_target_pairs={{0,32},{32,0},{1,33},{33,1},{2,34},{34,2},{3,35},{35,3},{4,36},{36... | collective-permute-start | bytes 1769480 | tf_op jit(solution)/shard_map/ppermute | solution.py:26
  22.6 1.1 reshape.51.w_out
  23.7 0.9 spread.1
  24.6 1.5 copy-done
  26.1 7.3 %all-to-all-start = ((bf16[16,608,128]{2,1,0:T(8,128)(2,1)}), bf16[16,608,128]{2,1,0:T(8,128)(2,1)S(1)}, u32[]{:S(2)}, u32[]{:S(2)}) async-start(bf16[16,608,128]{2,1,0:T(8,128)(2,1)} %copy-done), calls=%async_computation | async-start | bytes 4980736 | tf_op jit(solution)/shard_map/all_to_all | solution.py:38
  33.4 0.1 reshape.50.refs_6_
  33.5 0.0 collective-permute-done.refs_1_.refs_0_
  33.5 1.3 unpack.1
  34.8 0.6 copy-done.19
  35.4 3.4 %collective-permute-start.1 = (bf16[992,128]{1,0:T(8,128)(2,1)S(1)}, bf16[992,128]{1,0:T(8,128)(2,1)S(1)}, u32[]{:S(2)}, u32[]{:S(2)}) collective-permute-start(bf16[992,128]{1,0:T(8,128)(2,1)S(1)} %get-tuple-element.22.refs_1_), channel_id=1, source_target_pairs={{0,32},{32,0},{1,33},{33,1},{2,34},{34,2},{3,35},{35,3},{4,36},{36... | collective-permute-start | bytes 761864 | tf_op jit(solution)/shard_map/ppermute | solution.py:26
  38.7 14.0 %collective-permute-start.4 = (bf16[576,128]{1,0:T(8,128)(2,1)}, bf16[576,128]{1,0:T(8,128)(2,1)}, u32[]{:S(2)}, u32[]{:S(2)}) collective-permute-start(bf16[576,128]{1,0:T(8,128)(2,1)} %get-tuple-element.30), channel_id=1, source_target_pairs={{0,34},{2,32},{32,2},{34,0},{1,35},{3,33},{33,3},{35,1},{4,38},{6,... | collective-permute-start | bytes 442376 | tf_op jit(solution)/shard_map/ppermute | solution.py:384
  52.7 2.0 %collective-permute-start.3 = (bf16[576,128]{1,0:T(8,128)(2,1)}, bf16[576,128]{1,0:T(8,128)(2,1)}, u32[]{:S(2)}, u32[]{:S(2)}) collective-permute-start(bf16[576,128]{1,0:T(8,128)(2,1)} %get-tuple-element.30), channel_id=1, source_target_pairs={{0,2},{2,0},{1,3},{3,1},{4,6},{6,4},{5,7},{7,5},{8,10},{10,8},{9,1... | collective-permute-start | bytes 442376 | tf_op jit(solution)/shard_map/ppermute | solution.py:26
  54.8 16.3 %collective-permute-done.1.refs_2_ = bf16[992,128]{1,0:T(8,128)(2,1)S(1)} collective-permute-done((bf16[992,128]{1,0:T(8,128)(2,1)S(1)}, bf16[992,128]{1,0:T(8,128)(2,1)S(1)}, u32[]{:S(2)}, u32[]{:S(2)}) %collective-permute-start.1) | collective-permute-done | bytes 253984 | tf_op jit(solution)/shard_map/ppermute | solution.py:26
  71.1 0.0 collective-permute-done.2.refs_8_
  71.1 1.0 copy-done.22
  72.1 0.1 repeat.1
  72.2 0.8 copy-done.5
  73.1 0.0 all-to-all-done.refs_3_.received
  73.1 7.7 %all-to-all-start.1 = ((bf16[32,80,128]{2,1,0:T(8,128)(2,1)}), bf16[32,80,128]{2,1,0:T(8,128)(2,1)S(1)}, u32[]{:S(2)}, u32[]{:S(2)}) async-start(bf16[32,80,128]{2,1,0:T(8,128)(2,1)} %bitcast.14), calls=%async_computation.1 | async-start | bytes 1310720 | tf_op jit(solution)/shard_map/all_to_all | solution.py:38
  80.7 0.0 collective-permute-done.4
  80.7 0.0 collective-permute-done.3
  80.8 1.1 pad_maximum_fusion.refs_9_
  81.9 1.9 %collective-permute-start.5 = (bf16[576,512]{1,0:T(8,128)(2,1)S(1)}, bf16[576,512]{1,0:T(8,128)(2,1)S(1)}, u32[]{:S(2)}, u32[]{:S(2)}) collective-permute-start(bf16[576,512]{1,0:T(8,128)(2,1)S(1)} %pad_maximum_fusion.refs_9_), channel_id=1, source_target_pairs={{0,1},{1,0},{2,3},{3,2},{4,5},{5,4},{6,7},{7,6},{8,9},{9,8},{10,11... | collective-permute-start | bytes 1769480 | tf_op jit(solution)/shard_map/ppermute | solution.py:26
  83.8 0.8 copy-done.1
  84.6 1.2 collective-permute-done.5.refs_10_
  85.8 0.9 copy-done.8
  86.7 3.7 %all-to-all-done.1 = bf16[32,80,128]{2,1,0:T(8,128)(2,1)S(1)} async-done(((bf16[32,80,128]{2,1,0:T(8,128)(2,1)}), bf16[32,80,128]{2,1,0:T(8,128)(2,1)S(1)}, u32[]{:S(2)}, u32[]{:S(2)}) %all-to-all-start.1) | async-done | bytes 655392 | tf_op jit(solution)/shard_map/all_to_all | solution.py:38
  90.3 1.1 copy-done.2
  91.4 1.1 copy-done.4
  92.4 1.1 copy-done.9
  93.5 0.9 copy-done.13
  94.5 0.7 copy-done.20
  95.2 3.3 %attend.1 = (bf16[64,128]{1,0:T(8,128)(2,1)S(1)}, bf16[64,128]{1,0:T(8,128)(2,1)S(1)}) custom-call(s32[5]{0:T(128)S(1)} %copy-done.18, bf16[992,128]{1,0:T(8,128)(2,1)S(1)} %copy-done.13, bf16[992,128]{1,0:T(8,128)(2,1)S(1)} %copy-done.7, bf16[16,608,128]{2,1,0:T(8,128)(2,1)S(1)} %all-to-all-done.refs_3_.received, bf16[16,2,80,128]{3,2,1,0:T(8,128)(2,1)S(1)} %bitcast.10, ...), custom_call_target="tpu_custom_call" | custom-call | flops 1000000000 | bytes 5000000 | tf_op jit(solution)/shard_map/attend/pallas_call | solution.py:388
  98.5 3.0 %collective-permute-start.6 = (bf16[64,128]{1,0:T(8,128)(2,1)S(1)}, bf16[64,128]{1,0:T(8,128)(2,1)S(1)}, u32[]{:S(2)}, u32[]{:S(2)}) collective-permute-start(bf16[64,128]{1,0:T(8,128)(2,1)S(1)} %get-tuple-element.31), channel_id=1, source_target_pairs={{0,16},{16,0},{1,17},{17,1},{2,18},{18,2},{3,19},{19,3},{4,20},{20... | collective-permute-start | bytes 49160 | tf_op jit(solution)/shard_map/ppermute | solution.py:26
  101.4 11.5 %collective-permute-done.6 = bf16[64,128]{1,0:T(8,128)(2,1)S(1)} collective-permute-done((bf16[64,128]{1,0:T(8,128)(2,1)S(1)}, bf16[64,128]{1,0:T(8,128)(2,1)S(1)}, u32[]{:S(2)}, u32[]{:S(2)}) %collective-permute-start.6) | collective-permute-done | bytes 16416 | tf_op jit(solution)/shard_map/ppermute | solution.py:26
  113.0 8.4 %all_to_all.26.values = bf16[4,64,256]{2,1,0:T(8,128)(2,1)S(1)} all-to-all(bf16[4,64,256]{2,1,0:T(8,128)(2,1)S(1)} %broadcast_in_dim.2), channel_id=1, replica_groups=mesh['x'=4,'yh'=2,'yl'=2,'zh'=2,'zlh'=4,'zll'=2,'c'=2] {'yh','yl'}, dimensions={0} | all-to-all | bytes 262144 | tf_op jit(solution)/shard_map/all_to_all | solution.py:38
  121.3 1.0 copy-done.10
  122.4 1.3 project.1
  123.7 1.9 %collective-permute-start.7 = (bf16[4,2,2,16,448]{4,3,2,1,0:T(8,128)(2,1)S(1)}, bf16[4,2,2,16,448]{4,3,2,1,0:T(8,128)(2,1)S(1)}, u32[]{:S(2)}, u32[]{:S(2)}) collective-permute-start(bf16[4,2,2,16,448]{4,3,2,1,0:T(8,128)(2,1)S(1)} %get-tuple-element.34), channel_id=1, source_target_pairs={{0,1},{1,0},{2,3},{3,2},{4,5},{5,4},{6,7},{7,6},{8,9},{9,8},{10,11... | collective-permute-start | bytes 688136 | tf_op jit(solution)/shard_map/ppermute | solution.py:26
  125.6 1.5 collective-permute-done.7
  127.1 0.1 add_convert_fusion
  127.2 9.6 %all_to_all.27 = bf16[4,2,2,16,448]{4,3,2,1,0:T(8,128)(2,1)S(1)} all-to-all(bf16[4,2,2,16,448]{4,3,2,1,0:T(8,128)(2,1)S(1)} %add_convert_fusion), channel_id=1, replica_groups=mesh['x'=4,'yh'=2,'yl'=2,'zh'=2,'zlh'=4,'zll'=2,'c'=2] {'yh','yl'}, dimensions={0} | all-to-all | bytes 458752 | tf_op jit(solution)/shard_map/all_to_all | solution.py:38
  136.9 23.8 %all_to_all.28 = bf16[16,16,448]{2,1,0:T(8,128)(2,1)S(1)} all-to-all(bf16[16,16,448]{2,1,0:T(8,128)(2,1)S(1)} %bitcast.16), channel_id=1, replica_groups=mesh['x'=4,'yh'=2,'yl'=2,'zh'=2,'zlh'=4,'zll'=2,'c'=2] {'zh','zlh','zll'}, dimensions={0} | all-to-all | bytes 458752 | tf_op jit(solution)/shard_map/all_to_all | solution.py:38
  160.6 0.7 reduce_sum.12
  (40 shorter events, 0.1 us)
Async XLA Ops:
  0.0 19.1 %copy-start.3 = (bf16[512,576]{0,1:T(8,128)(2,1)S(1)}, bf16[512,576]{0,1:T(8,128)(2,1)}, u32[]{:S(2)}) copy-start(bf16[512,576]{0,1:T(8,128)(2,1)} %param.12) | copy-start | bytes 1769476
  0.0 23.7 %copy-start.11 = (bf16[8,48,128]{2,1,0:T(8,128)(2,1)S(1)}, bf16[8,48,128]{2,1,0:T(8,128)(2,1)}, u32[]{:S(2)}) copy-start(bf16[8,48,128]{2,1,0:T(8,128)(2,1)} %w_uq.3) | copy-start | bytes 294916
  0.0 23.7 %copy-start.14 = (bf16[8,16,128]{2,1,0:T(8,128)(2,1)S(1)}, bf16[8,16,128]{2,1,0:T(8,128)(2,1)}, u32[]{:S(2)}) copy-start(bf16[8,16,128]{2,1,0:T(8,128)(2,1)} %w_uk.3) | copy-start | bytes 98308
  0.0 23.7 %copy-start.15 = (bf16[8,16,128]{2,1,0:T(8,128)(2,1)S(1)}, bf16[8,16,128]{2,1,0:T(8,128)(2,1)}, u32[]{:S(2)}) copy-start(bf16[8,16,128]{2,1,0:T(8,128)(2,1)} %w_uv.3) | copy-start | bytes 98308
  0.7 23.0 %copy-start.18 = (s32[5]{0:T(128)S(1)}, s32[5]{0:T(128)}, u32[]{:S(2)}) copy-start(s32[5]{0:T(128)} %stack.23.place.refs_0_) | copy-start | bytes 64
  3.3 30.1 %collective-permute-start = (bf16[1120,128]{1,0:T(8,128)(2,1)}, bf16[1120,128]{1,0:T(8,128)(2,1)S(1)}, u32[]{:S(2)}, u32[]{:S(2)}) collective-permute-start(bf16[1120,128]{1,0:T(8,128)(2,1)} %pack.1), channel_id=1, source_target_pairs={{0,16},{16,0},{1,17},{17,1},{2,18},{18,2},{3,19},{19,3},{4,20},{20... | collective-permute-start | bytes 860168 | tf_op jit(solution)/shard_map/ppermute | solution.py:26
  19.1 52.0 %collective-permute-start.2 = (bf16[576,512]{1,0:T(8,128)(2,1)S(1)}, bf16[576,512]{1,0:T(8,128)(2,1)}, u32[]{:S(2)}, u32[]{:S(2)}) collective-permute-start(bf16[576,512]{1,0:T(8,128)(2,1)S(1)} %bitcast.12), channel_id=1, source_target_pairs={{0,32},{32,0},{1,33},{33,1},{2,34},{34,2},{3,35},{35,3},{4,36},{36... | collective-permute-start | bytes 1769480 | tf_op jit(solution)/shard_map/ppermute | solution.py:26
  24.6 1.5 copy-start
  26.1 7.3 %copy-start.23 = (s32[512]{0:T(512)S(1)}, s32[512]{0:T(512)}, u32[]{:S(2)}) copy-start(s32[512]{0:T(512)} %param.11) | copy-start | bytes 6148
  26.1 7.4 %copy-start.16 = (bf16[16,1536]{1,0:T(8,128)(2,1)S(1)}, bf16[16,1536]{1,0:T(8,128)(2,1)}, u32[]{:S(2)}) copy-start(bf16[16,1536]{1,0:T(8,128)(2,1)} %refs_2_.1) | copy-start | bytes 147460
  26.1 7.4 %copy-start.17 = (bf16[16,8,64]{2,1,0:T(8,128)(2,1)S(1)}, bf16[16,8,64]{2,1,0:T(8,128)(2,1)}, u32[]{:S(2)}) copy-start(bf16[16,8,64]{2,1,0:T(8,128)(2,1)} %refs_3_.1) | copy-start | bytes 49156
  26.1 46.9 %all-to-all-start = ((bf16[16,608,128]{2,1,0:T(8,128)(2,1)}), bf16[16,608,128]{2,1,0:T(8,128)(2,1)S(1)}, u32[]{:S(2)}, u32[]{:S(2)}) async-start(bf16[16,608,128]{2,1,0:T(8,128)(2,1)} %copy-done), calls=%async_computation | async-start | bytes 4980736 | tf_op jit(solution)/shard_map/all_to_all | solution.py:38
  33.5 1.3 copy-start.21
  34.8 0.6 copy-start.19
  35.4 35.7 %copy-start.12 = (bf16[992,128]{1,0:T(8,128)(2,1)}, bf16[992,128]{1,0:T(8,128)(2,1)S(1)}, u32[]{:S(2)}) copy-start(bf16[992,128]{1,0:T(8,128)(2,1)S(1)} %get-tuple-element.22.refs_1_) | copy-start | bytes 761860
  35.4 35.7 %collective-permute-start.1 = (bf16[992,128]{1,0:T(8,128)(2,1)S(1)}, bf16[992,128]{1,0:T(8,128)(2,1)S(1)}, u32[]{:S(2)}, u32[]{:S(2)}) collective-permute-start(bf16[992,128]{1,0:T(8,128)(2,1)S(1)} %get-tuple-element.22.refs_1_), channel_id=1, source_target_pairs={{0,32},{32,0},{1,33},{33,1},{2,34},{34,2},{3,35},{35,3},{4,36},{36... | collective-permute-start | bytes 761864 | tf_op jit(solution)/shard_map/ppermute | solution.py:26
  38.7 42.0 %collective-permute-start.4 = (bf16[576,128]{1,0:T(8,128)(2,1)}, bf16[576,128]{1,0:T(8,128)(2,1)}, u32[]{:S(2)}, u32[]{:S(2)}) collective-permute-start(bf16[576,128]{1,0:T(8,128)(2,1)} %get-tuple-element.30), channel_id=1, source_target_pairs={{0,34},{2,32},{32,2},{34,0},{1,35},{3,33},{33,3},{35,1},{4,38},{6,... | collective-permute-start | bytes 442376 | tf_op jit(solution)/shard_map/ppermute | solution.py:384
  52.7 28.0 %collective-permute-start.3 = (bf16[576,128]{1,0:T(8,128)(2,1)}, bf16[576,128]{1,0:T(8,128)(2,1)}, u32[]{:S(2)}, u32[]{:S(2)}) collective-permute-start(bf16[576,128]{1,0:T(8,128)(2,1)} %get-tuple-element.30), channel_id=1, source_target_pairs={{0,2},{2,0},{1,3},{3,1},{4,6},{6,4},{5,7},{7,5},{8,10},{10,8},{9,1... | collective-permute-start | bytes 442376 | tf_op jit(solution)/shard_map/ppermute | solution.py:26
  71.0 1.2 copy-start.6
  71.1 1.1 copy-start.22
  72.2 0.8 copy-start.5
  73.1 7.7 %slice-start = ((bf16[992,128]{1,0:T(8,128)(2,1)}), bf16[576,128]{1,0:T(8,128)(2,1)S(1)}, s32[]{:S(2)}) async-start(bf16[992,128]{1,0:T(8,128)(2,1)} %copy-done.6), calls=%async_computation.5 | async-start | bytes 294912 | tf_op jit(solution)/shard_map/slice | solution.py:385
  73.1 17.3 %copy-start.7 = (bf16[992,128]{1,0:T(8,128)(2,1)S(1)}, bf16[992,128]{1,0:T(8,128)(2,1)}, u32[]{:S(2)}) copy-start(bf16[992,128]{1,0:T(8,128)(2,1)} %copy-done.6) | copy-start | bytes 761860
  73.1 17.2 %all-to-all-start.1 = ((bf16[32,80,128]{2,1,0:T(8,128)(2,1)}), bf16[32,80,128]{2,1,0:T(8,128)(2,1)S(1)}, u32[]{:S(2)}, u32[]{:S(2)}) async-start(bf16[32,80,128]{2,1,0:T(8,128)(2,1)} %bitcast.14), calls=%async_computation.1 | async-start | bytes 1310720 | tf_op jit(solution)/shard_map/all_to_all | solution.py:38
  81.9 3.9 %collective-permute-start.5 = (bf16[576,512]{1,0:T(8,128)(2,1)S(1)}, bf16[576,512]{1,0:T(8,128)(2,1)S(1)}, u32[]{:S(2)}, u32[]{:S(2)}) collective-permute-start(bf16[576,512]{1,0:T(8,128)(2,1)S(1)} %pad_maximum_fusion.refs_9_), channel_id=1, source_target_pairs={{0,1},{1,0},{2,3},{3,2},{4,5},{5,4},{6,7},{7,6},{8,9},{9,8},{10,11... | collective-permute-start | bytes 1769480 | tf_op jit(solution)/shard_map/ppermute | solution.py:26
  83.8 0.8 copy-start.1
  85.8 0.9 copy-start.8
  90.3 1.1 copy-start.2
  91.4 1.1 copy-start.4
  92.4 1.1 copy-start.9
  93.5 0.9 copy-start.13
  94.5 0.7 copy-start.20
  98.5 14.5 %collective-permute-start.6 = (bf16[64,128]{1,0:T(8,128)(2,1)S(1)}, bf16[64,128]{1,0:T(8,128)(2,1)S(1)}, u32[]{:S(2)}, u32[]{:S(2)}) collective-permute-start(bf16[64,128]{1,0:T(8,128)(2,1)S(1)} %get-tuple-element.31), channel_id=1, source_target_pairs={{0,16},{16,0},{1,17},{17,1},{2,18},{18,2},{3,19},{19,3},{4,20},{20... | collective-permute-start | bytes 49160 | tf_op jit(solution)/shard_map/ppermute | solution.py:26
  121.3 1.0 copy-start.10
  123.7 3.4 %collective-permute-start.7 = (bf16[4,2,2,16,448]{4,3,2,1,0:T(8,128)(2,1)S(1)}, bf16[4,2,2,16,448]{4,3,2,1,0:T(8,128)(2,1)S(1)}, u32[]{:S(2)}, u32[]{:S(2)}) collective-permute-start(bf16[4,2,2,16,448]{4,3,2,1,0:T(8,128)(2,1)S(1)} %get-tuple-element.34), channel_id=1, source_target_pairs={{0,1},{1,0},{2,3},{3,2},{4,5},{5,4},{6,7},{7,6},{8,9},{9,8},{10,11... | collective-permute-start | bytes 688136 | tf_op jit(solution)/shard_map/ppermute | solution.py:26

commit v8 on v7

--- a/solution.py
+++ b/solution.py
@@ -8,17 +8,17 @@
 from jax.experimental.pallas import tpu as pltpu
 from jax.sharding import Mesh, PartitionSpec as P
 
-AXES = ("x", "yh", "yl", "zh", "zlh", "zll", "c")
-SIZES = (4, 2, 2, 2, 4, 2, 2)
-FSDP = ("x", "yh", "yl", "zh")
+AXES = ("xh", "xl", "yh", "yl", "zh", "zlh", "zll", "c")
+SIZES = (2, 2, 2, 2, 2, 4, 2, 2)
+FSDP = ("xh", "xl", "yh", "yl", "zh")
 HEAD = ("zlh", "zll", "c")
-PLANE = ("x", "yh", "yl")
-RING = ("yh", "yl")
+PLANE = ("xh", "xl", "yh", "yl")
+PART = ("xl", "yh", "yl")
 COLUMN = ("zh", "zlh", "zll")
 BF16 = jnp.bfloat16
 F32 = jnp.float32
-VMEM_LIMIT = 16 * 1024 * 1024
-PACK_LIMIT = 60 * 1024 * 1024
+VMEM_LIMIT = 63 * 1024 * 1024
+PACK_LIMIT = 63 * 1024 * 1024
 UNPACK_FLOPS = 2 * 10**10
 
 
@@ -109,19 +109,19 @@
             out[copy, at + i * rows : at + (i + 1) * rows] = block
 
 
-def repeat_kernel(received, sent, *, first):
-    copies, heads, rows = sent.shape[:3]
-    for h in range(heads):
-        block = received[first + h * rows : first + (h + 1) * rows]
-        for copy in range(copies):
-            sent[copy, h] = block
-
-
-def unpack_kernel(place, received, latent, rope, packed, piece, rope_out, *, sizes):
-    n_piece, at = sizes
+def unpack_kernel(
+    place, received, latent, rope, sent, packed, piece, rope_out, *, sizes
+):
+    n_piece, n_all, copies = sizes
     zh, yl = place[0], place[1]
     own_rows = latent.shape[0]
     lanes = packed.shape[1]
+    at = n_piece
+    for h in range(sent.shape[1]):
+        other = received[at : at + n_all]
+        for copy in range(copies):
+            sent[copy, h] = other
+        at += n_all
     ours = pl.ds(pl.multiple_of(zh * own_rows, 16), own_rows)
     theirs = pl.ds(pl.multiple_of((1 - zh) * own_rows, 16), own_rows)
     to = n_piece
@@ -265,26 +265,26 @@
 def project_kernel(place, values, received, order, keep_out, give_out):
     core = place[3]
     lanes = received.shape[2]
-    rows = [jnp.concatenate([values[2 * i], values[2 * i + 1]], axis=1) for i in range(2)]
+    rows = [
+        jnp.concatenate([values[i], values[i + 1]], axis=1) for i in range(0, values.shape[0], 2)
+    ]
     rows = dot(jnp.concatenate(rows, axis=0), order[...]).astype(BF16)
     depth = rows.shape[1]
     each = depth // received.shape[0]
-    blocks, _, low, _, columns = keep_out.shape
+    columns = keep_out.shape[-1]
     count = 2 * columns // lanes
-    first = received.shape[1] - low * count * each
-    for z in range(low):
-        weights = jnp.concatenate(
-            [
-                received[:, at : at + each].reshape(depth, lanes)
-                for at in range(first + z * count * each, first + (z + 1) * count * each, each)
-            ],
-            axis=1,
-        )
-        part = dot(rows, weights)
-        even, odd = part[:, :columns], part[:, columns:]
-        shape = keep_out.shape[:2] + keep_out.shape[3:]
-        keep_out[:, :, z] = jnp.where(core == 0, even, odd).astype(BF16).reshape(shape)
-        give_out[:, :, z] = jnp.where(core == 0, odd, even).astype(BF16).reshape(shape)
+    first = received.shape[1] - count * each
+    weights = jnp.concatenate(
+        [
+            received[:, at : at + each].reshape(depth, lanes)
+            for at in range(first, received.shape[1], each)
+        ],
+        axis=1,
+    )
+    part = dot(rows, weights)
+    even, odd = part[:, :columns], part[:, columns:]
+    keep_out[...] = jnp.where(core == 0, even, odd).astype(BF16).reshape(keep_out.shape)
+    give_out[...] = jnp.where(core == 0, odd, even).astype(BF16).reshape(give_out.shape)
 
 
 def local(query_latent, query_rope, lengths, kv_cache, w_uq, w_uk, w_uv, w_out):
@@ -303,7 +303,7 @@
     four, heads = heads_in // 2, heads_in // 4
 
     quarter = tokens // 4
-    sequence = lax.axis_index("x") * 2 + lax.axis_index("yh")
+    sequence = lax.axis_index("xh") * 4 + lax.axis_index("xl") * 2 + lax.axis_index("yh")
     place = jnp.stack([zh, yl, core * 2 + zll, core, sequence]).astype(jnp.int32)
     vmem = pl.BlockSpec(memory_space=pltpu.VMEM)
     smem = pl.BlockSpec(memory_space=pltpu.SMEM)
@@ -327,7 +327,7 @@
     received = swap(packed, "zh")
 
     vpart, width = w_out.shape[1:]
-    columns = width // 4
+    columns = width // 8
     w_rows = heads_in * vpart
     n_spread = heads * n_all + columns // lanes * w_rows
     spread = pl.pallas_call(
@@ -342,15 +342,16 @@
     spread = exchange(spread, PLANE)
 
     n_pack = kv_width + (2 * latent_chunks + 2) * own_rows
-    packed, far_piece, rope_kept = pl.pallas_call(
-        lambda *refs: unpack_kernel(*refs, sizes=(kv_width, kv_width + four * n_all)),
+    sent, packed, far_piece, rope_kept = pl.pallas_call(
+        lambda *refs: unpack_kernel(*refs, sizes=(kv_width, n_all, plane // 2)),
         out_shape=(
+            jax.ShapeDtypeStruct((plane // 2, four, n_all, lanes), BF16),
             jax.ShapeDtypeStruct((n_pack, lanes), BF16),
             jax.ShapeDtypeStruct((kv_width, quarter), BF16),
             jax.ShapeDtypeStruct((2 * own_rows, lanes), BF16),
         ),
         in_specs=[smem] + [vmem] * 3,
-        out_specs=(vmem,) * 3,
+        out_specs=(vmem,) * 4,
         compiler_params=pltpu.CompilerParams(vmem_limit_bytes=VMEM_LIMIT),
         cost_estimate=pl.CostEstimate(
             flops=UNPACK_FLOPS, bytes_accessed=3 * 10**6, transcendentals=0
@@ -359,21 +360,9 @@
     )(place, received, *queries)
     rows = 4 * own_rows
     row_lengths = lengths.reshape(-1, rows)
-    packed, far_piece, received, row_lengths = lax.optimization_barrier(
-        (packed, far_piece, received, row_lengths)
-    )
-    received, near = lax.optimization_barrier((received, near))
-    sent = pl.pallas_call(
-        lambda *refs: repeat_kernel(*refs, first=kv_width),
-        out_shape=jax.ShapeDtypeStruct((plane // 2, four, n_all, lanes), BF16),
-        in_specs=[vmem],
-        out_specs=vmem,
-        compiler_params=pltpu.CompilerParams(vmem_limit_bytes=VMEM_LIMIT),
-        cost_estimate=pl.CostEstimate(
-            flops=UNPACK_FLOPS, bytes_accessed=3 * 10**6, transcendentals=0
-        ),
-        name="repeat",
-    )(received)
+    sent, packed, far_piece, near, row_lengths = lax.optimization_barrier(
+        (sent, packed, far_piece, near, row_lengths)
+    )
     sent, spread = lax.optimization_barrier((sent, spread))
 
     weights_far = exchange(sent.reshape(plane * heads, n_all, lanes), PLANE)
@@ -407,10 +396,10 @@
 
     values = ordered(keep, swap(give, "zh"), zh, 1)
     gathered = exchange(
-        jnp.broadcast_to(values[None], (4,) + values.shape).reshape(-1, values.shape[1]), RING
-    ).reshape((4,) + values.shape)
+        jnp.broadcast_to(values[None], (8,) + values.shape).reshape(-1, values.shape[1]), PART
+    ).reshape((8,) + values.shape)
     order = jnp.asarray(feature_order(heads, plane, vpart), BF16)
-    shape = (4, 2, 2, own_rows, columns // 4)
+    shape = (8, 2, own_rows, columns // 2)
     keep, give = pl.pallas_call(
         project_kernel,
         out_shape=(jax.ShapeDtypeStruct(shape, BF16),) * 2,
@@ -422,8 +411,8 @@
     )(place, gathered, spread, order)
 
     total = (keep.astype(F32) + swap(give, "c").astype(F32)).astype(BF16)
-    total = jnp.transpose(exchange(total, RING), (1, 0, 2, 3, 4))
-    total = exchange(total.reshape((16,) + total.shape[3:]), COLUMN)
+    total = jnp.transpose(exchange(total, PART), (1, 0, 2, 3))
+    total = exchange(total.reshape((16,) + total.shape[2:]), COLUMN)
     return jnp.sum(total.astype(F32), axis=0).astype(BF16)
 
 

time: 163 us -> 157 us (0.963)
  the two profiles are of different devices: /device:TPU:6 before, /device:TPU:32 now
where the time goes in v8:
time: 157 us
  starting transfers between devices  52.9 us (34%)
  blocking collectives  45.3 us (29%)
  waiting for transfers between devices  35.1 us (22%)
  Pallas kernels  15.7 us (10%)
  local copies, waits for them, and re-layouts  4.87 us (3%)
  other arithmetic  2.56 us (2%)
    all_to_all x3, blocking collectives, exchange(): return lax.all_to_all(blocks, axes, 0, 0, tiled=True)  45.3 us
    ppermute x7, starting transfers between devices, swap(): return lax.ppermute(block, axis, [(0, 1), (1, 0)])  37 us
    ppermute x7, waiting for transfers between devices, swap(): return lax.ppermute(block, axis, [(0, 1), (1, 0)])  26.1 us
    all_to_all x2, starting transfers between devices, exchange(): return lax.all_to_all(blocks, axes, 0, 0, tiled=True)  13.9 us
    all_to_all x2, waiting for transfers between devices, exchange(): return lax.all_to_all(blocks, axes, 0, 0, tiled=True)  9.02 us
    pallas_call x1, Pallas kernels, local(): pl.pallas_call(lambda *refs: attend_kernel(*refs, sizes=(rows, heads, n_u...  5.34 us
    pallas_call x1, Pallas kernels, local(): pl.pallas_call(project_kernel, out_shape=(jax.ShapeDtypeStruct(shape, BF1...  3.26 us
  transfers between devices with their start and end apart: 10, of which 6 were waited for; matrix products, arithmetic and copies ran while one was open for 2% of the time, Pallas kernels for 3%

profile of v8, /device:TPU:32, one launch (start us, length us, event | category | flops | bytes accessed | tf_op | source)
XLA Modules:
  0.0 156.6 jit_solution(8686368931853802052)
XLA Ops:
  0.0 0.7 stack.23.place.refs_0_
  0.7 2.5 %pack.1 = bf16[1120,128]{1,0:T(8,128)(2,1)} custom-call(s32[5]{0:T(128)} %stack.23.place.refs_0_, bf16[576,512]{1,0:T(8,128)(2,1)} %bitcast.11, bf16[8,48,128]{2,1,0:T(8,128)(2,1)} %w_uq.3, bf16[8,16,128]{2,1,0:T(8,128)(2,1)} %w_uk.3, bf16[8,16,128]{2,1,0:T(8,128)(2,1)} %w_uv.3, bf16[16,1536]{1,0:T(8,128)(2,1)} %refs_2_.1, bf16[16,8,64]{2,1,0:T(8,128)(2,1)} %refs_3_.1), custom_call_target="tpu_custom_call" | custom-call | flops 1000000 | bytes 1000000 | tf_op jit(solution)/shard_map/pack/pallas_call | solution.py:314
  3.1 14.8 %collective-permute-start = (bf16[1120,128]{1,0:T(8,128)(2,1)}, bf16[1120,128]{1,0:T(8,128)(2,1)S(1)}, u32[]{:S(2)}, u32[]{:S(2)}) collective-permute-start(bf16[1120,128]{1,0:T(8,128)(2,1)} %pack.1), channel_id=1, source_target_pairs={{0,16},{16,0},{1,17},{17,1},{2,18},{18,2},{3,19},{19,3},{4,20},{20... | collective-permute-start | bytes 860168 | tf_op jit(solution)/shard_map/ppermute | solution.py:26
  18.0 0.0 copy-done.1
  18.0 3.5 %collective-permute-start.1 = (bf16[576,512]{1,0:T(8,128)(2,1)S(1)}, bf16[576,512]{1,0:T(8,128)(2,1)}, u32[]{:S(2)}, u32[]{:S(2)}) collective-permute-start(bf16[576,512]{1,0:T(8,128)(2,1)S(1)} %bitcast.13), channel_id=1, source_target_pairs={{0,32},{32,0},{1,33},{33,1},{2,34},{34,2},{3,35},{35,3},{4,36},{36... | collective-permute-start | bytes 1769480 | tf_op jit(solution)/shard_map/ppermute | solution.py:26
  21.5 1.9 %reshape.51.w_out = bf16[32,7168]{1,0:T(8,128)(2,1)} reshape(bf16[8,4,7168]{2,1,0:T(4,128)(2,1)} %param.16) | data formatting | bytes 917504 | tf_op jit(solution)/shard_map/reshape | solution.py:341
  23.4 2.5 %spread.1 = bf16[16,384,128]{2,1,0:T(8,128)(2,1)} custom-call(s32[5]{0:T(128)} %stack.23.place.refs_0_, bf16[8,48,128]{2,1,0:T(8,128)(2,1)} %w_uq.3, bf16[8,16,128]{2,1,0:T(8,128)(2,1)} %w_uk.3, bf16[8,16,128]{2,1,0:T(8,128)(2,1)} %w_uv.3, bf16[32,7168]{1,0:T(8,128)(2,1)} %reshape.51.w_out), custom_call_target="tpu_custom_call" | custom-call | flops 1000000 | bytes 1000000 | tf_op jit(solution)/shard_map/spread/pallas_call | solution.py:333
  25.9 0.0 copy-start.5
  25.9 6.9 %all-to-all-start = ((bf16[16,384,128]{2,1,0:T(8,128)(2,1)}), bf16[16,384,128]{2,1,0:T(8,128)(2,1)}, u32[]{:S(2)}, u32[]{:S(2)}) async-start(bf16[16,384,128]{2,1,0:T(8,128)(2,1)} %spread.1), calls=%async_computation | async-start | bytes 3145728 | tf_op jit(solution)/shard_map/all_to_all | solution.py:38
  32.8 0.0 copy-done.5
  32.8 0.7 reshape.50.refs_6_
  33.5 9.9 %collective-permute-done.refs_1_ = bf16[1120,128]{1,0:T(8,128)(2,1)S(1)} collective-permute-done((bf16[1120,128]{1,0:T(8,128)(2,1)}, bf16[1120,128]{1,0:T(8,128)(2,1)S(1)}, u32[]{:S(2)}, u32[]{:S(2)}) %collective-permute-start) | collective-permute-done | bytes 286752 | tf_op jit(solution)/shard_map/ppermute | solution.py:26
  43.4 0.0 copy-start.6
  43.4 0.7 copy-done.6
  44.1 2.1 %unpack.1 = (bf16[8,4,80,128]{3,2,1,0:T(8,128)(2,1)}, bf16[992,128]{1,0:T(8,128)(2,1)}, bf16[576,128]{1,0:T(8,128)(2,1)}, bf16[32,128]{1,0:T(8,128)(2,1)}) custom-call(s32[5]{0:T(128)} %stack.23.place.refs_0_, bf16[1120,128]{1,0:T(8,128)(2,1)} %copy-done.6, bf16[16,1536]{1,0:T(8,128)(2,1)} %refs_2_.1, bf16[16,8,64]{2,1,0:T(8,128)(2,1)} %refs_3_.1), custom_call_target="tpu_custom_call" | custom-call | flops 20000000000 | bytes 3000000 | tf_op jit(solution)/shard_map/unpack/pallas_call | solution.py:345
  46.2 0.0 copy-start.4
  46.2 0.0 collective-permute-done.1.refs_8_
  46.2 3.6 %collective-permute-start.2 = (bf16[992,128]{1,0:T(8,128)(2,1)}, bf16[992,128]{1,0:T(8,128)(2,1)S(1)}, u32[]{:S(2)}, u32[]{:S(2)}) collective-permute-start(bf16[992,128]{1,0:T(8,128)(2,1)} %get-tuple-element.23.refs_1_), channel_id=1, source_target_pairs={{0,32},{32,0},{1,33},{33,1},{2,34},{34,2},{3,35},{35,3},{4,36},{36... | collective-permute-start | bytes 761864 | tf_op jit(solution)/shard_map/ppermute | solution.py:26
  49.9 1.9 %collective-permute-start.4 = (bf16[576,128]{1,0:T(8,128)(2,1)}, bf16[576,128]{1,0:T(8,128)(2,1)S(1)}, u32[]{:S(2)}, u32[]{:S(2)}) collective-permute-start(bf16[576,128]{1,0:T(8,128)(2,1)} %get-tuple-element.30), channel_id=1, source_target_pairs={{0,34},{2,32},{32,2},{34,0},{1,35},{3,33},{33,3},{35,1},{4,38},{6,... | collective-permute-start | bytes 442376 | tf_op jit(solution)/shard_map/ppermute | solution.py:373
  51.8 3.8 %collective-permute-start.3 = (bf16[576,128]{1,0:T(8,128)(2,1)}, bf16[576,128]{1,0:T(8,128)(2,1)S(1)}, u32[]{:S(2)}, u32[]{:S(2)}) collective-permute-start(bf16[576,128]{1,0:T(8,128)(2,1)} %get-tuple-element.30), channel_id=1, source_target_pairs={{0,2},{2,0},{1,3},{3,1},{4,6},{6,4},{5,7},{7,5},{8,10},{10,8},{9,1... | collective-permute-start | bytes 442376 | tf_op jit(solution)/shard_map/ppermute | solution.py:26
  55.6 5.2 %collective-permute-done.2.refs_2_ = bf16[992,128]{1,0:T(8,128)(2,1)S(1)} collective-permute-done((bf16[992,128]{1,0:T(8,128)(2,1)}, bf16[992,128]{1,0:T(8,128)(2,1)S(1)}, u32[]{:S(2)}, u32[]{:S(2)}) %collective-permute-start.2) | collective-permute-done | bytes 253984 | tf_op jit(solution)/shard_map/ppermute | solution.py:26
  60.8 0.0 copy-start.3
  60.8 0.0 all-to-all-done.refs_3_.received
  60.9 7.0 %all-to-all-start.1 = ((bf16[32,80,128]{2,1,0:T(8,128)(2,1)}), bf16[32,80,128]{2,1,0:T(8,128)(2,1)S(1)}, u32[]{:S(2)}, u32[]{:S(2)}) async-start(bf16[32,80,128]{2,1,0:T(8,128)(2,1)} %bitcast.16), calls=%async_computation.1 | async-start | bytes 1310720 | tf_op jit(solution)/shard_map/all_to_all | solution.py:38
  67.9 0.0 collective-permute-done.4
  67.9 0.0 collective-permute-done.3
  67.9 0.0 copy-done.4
  67.9 0.1 pad_maximum_fusion.refs_9_
  68.0 0.0 copy-done.3
  68.0 0.0 copy-start.2
  68.0 1.9 %collective-permute-start.5 = (bf16[576,512]{1,0:T(8,128)(2,1)S(1)}, bf16[576,512]{1,0:T(8,128)(2,1)}, u32[]{:S(2)}, u32[]{:S(2)}) collective-permute-start(bf16[576,512]{1,0:T(8,128)(2,1)S(1)} %pad_maximum_fusion.refs_9_), channel_id=1, source_target_pairs={{0,1},{1,0},{2,3},{3,2},{4,5},{5,4},{6,7},{7,6},{8,9},{9,8},{10,11... | collective-permute-start | bytes 1769480 | tf_op jit(solution)/shard_map/ppermute | solution.py:26
  69.9 0.0 copy-done.2
  69.9 2.1 %collective-permute-done.5.refs_10_ = bf16[576,512]{1,0:T(8,128)(2,1)} collective-permute-done((bf16[576,512]{1,0:T(8,128)(2,1)S(1)}, bf16[576,512]{1,0:T(8,128)(2,1)}, u32[]{:S(2)}, u32[]{:S(2)}) %collective-permute-start.5) | collective-permute-done | bytes 589856 | tf_op jit(solution)/shard_map/ppermute | solution.py:26
  72.0 9.0 %all-to-all-done.1 = bf16[32,80,128]{2,1,0:T(8,128)(2,1)S(1)} async-done(((bf16[32,80,128]{2,1,0:T(8,128)(2,1)}), bf16[32,80,128]{2,1,0:T(8,128)(2,1)S(1)}, u32[]{:S(2)}, u32[]{:S(2)}) %all-to-all-start.1) | async-done | bytes 655392 | tf_op jit(solution)/shard_map/all_to_all | solution.py:38
  81.1 0.0 copy-start
  81.1 0.9 copy-done
  81.9 5.3 %attend.1 = (bf16[64,128]{1,0:T(8,128)(2,1)}, bf16[64,128]{1,0:T(8,128)(2,1)}) custom-call(s32[5]{0:T(128)} %stack.23.place.refs_0_, bf16[992,128]{1,0:T(8,128)(2,1)} %get-tuple-element.23.refs_1_, bf16[992,128]{1,0:T(8,128)(2,1)} %copy-done.3, bf16[16,384,128]{2,1,0:T(8,128)(2,1)} %all-to-all-done.refs_3_.received, bf16[16,2,80,128]{3,2,1,0:T(8,128)(2,1)} %bitcast.10, ...), custom_call_target="tpu_custom_call" | custom-call | flops 1000000000 | bytes 5000000 | tf_op jit(solution)/shard_map/attend/pallas_call | solution.py:377
  87.3 7.5 %collective-permute-start.6 = (bf16[64,128]{1,0:T(8,128)(2,1)}, bf16[64,128]{1,0:T(8,128)(2,1)S(1)}, u32[]{:S(2)}, u32[]{:S(2)}) collective-permute-start(bf16[64,128]{1,0:T(8,128)(2,1)} %get-tuple-element.31), channel_id=1, source_target_pairs={{0,16},{16,0},{1,17},{17,1},{2,18},{18,2},{3,19},{19,3},{4,20},{20... | collective-permute-start | bytes 49160 | tf_op jit(solution)/shard_map/ppermute | solution.py:26
  94.7 7.1 %collective-permute-done.6 = bf16[64,128]{1,0:T(8,128)(2,1)S(1)} collective-permute-done((bf16[64,128]{1,0:T(8,128)(2,1)}, bf16[64,128]{1,0:T(8,128)(2,1)S(1)}, u32[]{:S(2)}, u32[]{:S(2)}) %collective-permute-start.6) | collective-permute-done | bytes 16416 | tf_op jit(solution)/shard_map/ppermute | solution.py:26
  101.9 0.8 maximum_select_fusion
  102.7 10.3 %all_to_all.26.values = bf16[8,64,256]{2,1,0:T(8,128)(2,1)} all-to-all(bf16[8,64,256]{2,1,0:T(8,128)(2,1)S(1)} %broadcast_in_dim.2), channel_id=1, replica_groups=mesh['xh'=2,'xl'=2,'yh'=2,'yl'=2,'zh'=2,'zlh'=4,'zll'=2,'c'=2] {'xl','yh..., dimensions={0} | all-to-all | bytes 524288 | tf_op jit(solution)/shard_map/all_to_all | solution.py:38
  113.0 3.3 %project.1 = (bf16[8,2,16,448]{3,2,1,0:T(8,128)(2,1)}, bf16[8,2,16,448]{3,2,1,0:T(8,128)(2,1)}) custom-call(s32[5]{0:T(128)} %stack.23.place.refs_0_, bf16[8,64,256]{2,1,0:T(8,128)(2,1)} %all_to_all.26.values, bf16[16,384,128]{2,1,0:T(8,128)(2,1)} %all-to-all-done.refs_3_.received, bf16[512,512]{1,0:T(8,128)(2,1)} %constant.37.clone.order), custom_call_target="tpu_custom_call" | custom-call | flops 200000000 | bytes 2000000 | tf_op jit(solution)/shard_map/project/pallas_call | solution.py:403
  116.2 1.9 %collective-permute-start.7 = (bf16[8,2,16,448]{3,2,1,0:T(8,128)(2,1)}, bf16[8,2,16,448]{3,2,1,0:T(8,128)(2,1)S(1)}, u32[]{:S(2)}, u32[]{:S(2)}) collective-permute-start(bf16[8,2,16,448]{3,2,1,0:T(8,128)(2,1)} %get-tuple-element.34), channel_id=1, source_target_pairs={{0,1},{1,0},{2,3},{3,2},{4,5},{5,4},{6,7},{7,6},{8,9},{9,8},{10,11... | collective-permute-start | bytes 688136 | tf_op jit(solution)/shard_map/ppermute | solution.py:26
  118.2 1.7 %collective-permute-done.7 = bf16[8,2,16,448]{3,2,1,0:T(8,128)(2,1)S(1)} collective-permute-done((bf16[8,2,16,448]{3,2,1,0:T(8,128)(2,1)}, bf16[8,2,16,448]{3,2,1,0:T(8,128)(2,1)S(1)}, u32[]{:S(2)}, u32[]{:S(2)}) %collective-permute-start.7) | collective-permute-done | bytes 229408 | tf_op jit(solution)/shard_map/ppermute | solution.py:26
  119.9 1.0 add_convert_fusion
  120.9 10.2 %all_to_all.27 = bf16[8,2,16,448]{3,2,1,0:T(8,128)(2,1)S(1)} all-to-all(bf16[8,2,16,448]{3,2,1,0:T(8,128)(2,1)S(1)} %add_convert_fusion), channel_id=1, replica_groups=mesh['xh'=2,'xl'=2,'yh'=2,'yl'=2,'zh'=2,'zlh'=4,'zll'=2,'c'=2] {'xl','yh..., dimensions={0} | all-to-all | bytes 458752 | tf_op jit(solution)/shard_map/all_to_all | solution.py:38
  131.1 24.8 %all_to_all.28 = bf16[16,16,448]{2,1,0:T(8,128)(2,1)S(1)} all-to-all(bf16[16,16,448]{2,1,0:T(8,128)(2,1)S(1)} %bitcast.15), channel_id=1, replica_groups=mesh['xh'=2,'xl'=2,'yh'=2,'yl'=2,'zh'=2,'zlh'=4,'zll'=2,'c'=2] {'zh','zl..., dimensions={0} | all-to-all | bytes 458752 | tf_op jit(solution)/shard_map/all_to_all | solution.py:38
  155.9 0.7 reduce_sum.12
  (4 shorter events, 0.0 us)
Async XLA Ops:
  0.0 18.0 %copy-start.1 = (bf16[512,576]{0,1:T(8,128)(2,1)S(1)}, bf16[512,576]{0,1:T(8,128)(2,1)}, u32[]{:S(2)}) copy-start(bf16[512,576]{0,1:T(8,128)(2,1)} %param.12) | copy-start | bytes 1769476
  3.1 40.3 %collective-permute-start = (bf16[1120,128]{1,0:T(8,128)(2,1)}, bf16[1120,128]{1,0:T(8,128)(2,1)S(1)}, u32[]{:S(2)}, u32[]{:S(2)}) collective-permute-start(bf16[1120,128]{1,0:T(8,128)(2,1)} %pack.1), channel_id=1, source_target_pairs={{0,16},{16,0},{1,17},{17,1},{2,18},{18,2},{3,19},{19,3},{4,20},{20... | collective-permute-start | bytes 860168 | tf_op jit(solution)/shard_map/ppermute | solution.py:26
  18.0 28.3 %collective-permute-start.1 = (bf16[576,512]{1,0:T(8,128)(2,1)S(1)}, bf16[576,512]{1,0:T(8,128)(2,1)}, u32[]{:S(2)}, u32[]{:S(2)}) collective-permute-start(bf16[576,512]{1,0:T(8,128)(2,1)S(1)} %bitcast.13), channel_id=1, source_target_pairs={{0,32},{32,0},{1,33},{33,1},{2,34},{34,2},{3,35},{35,3},{4,36},{36... | collective-permute-start | bytes 1769480 | tf_op jit(solution)/shard_map/ppermute | solution.py:26
  25.9 6.9 %copy-start.5 = (s32[512]{0:T(512)S(1)}, s32[512]{0:T(512)}, u32[]{:S(2)}) copy-start(s32[512]{0:T(512)} %param.11) | copy-start | bytes 6148
  25.9 35.0 %all-to-all-start = ((bf16[16,384,128]{2,1,0:T(8,128)(2,1)}), bf16[16,384,128]{2,1,0:T(8,128)(2,1)}, u32[]{:S(2)}, u32[]{:S(2)}) async-start(bf16[16,384,128]{2,1,0:T(8,128)(2,1)} %spread.1), calls=%async_computation | async-start | bytes 3145728 | tf_op jit(solution)/shard_map/all_to_all | solution.py:38
  43.4 0.7 copy-start.6
  46.2 21.7 %copy-start.4 = (bf16[576,128]{1,0:T(8,128)(2,1)S(1)}, bf16[576,128]{1,0:T(8,128)(2,1)}, u32[]{:S(2)}) copy-start(bf16[576,128]{1,0:T(8,128)(2,1)} %get-tuple-element.30) | copy-start | bytes 442372
  46.2 14.6 %collective-permute-start.2 = (bf16[992,128]{1,0:T(8,128)(2,1)}, bf16[992,128]{1,0:T(8,128)(2,1)S(1)}, u32[]{:S(2)}, u32[]{:S(2)}) collective-permute-start(bf16[992,128]{1,0:T(8,128)(2,1)} %get-tuple-element.23.refs_1_), channel_id=1, source_target_pairs={{0,32},{32,0},{1,33},{33,1},{2,34},{34,2},{3,35},{35,3},{4,36},{36... | collective-permute-start | bytes 761864 | tf_op jit(solution)/shard_map/ppermute | solution.py:26
  49.9 18.0 %collective-permute-start.4 = (bf16[576,128]{1,0:T(8,128)(2,1)}, bf16[576,128]{1,0:T(8,128)(2,1)S(1)}, u32[]{:S(2)}, u32[]{:S(2)}) collective-permute-start(bf16[576,128]{1,0:T(8,128)(2,1)} %get-tuple-element.30), channel_id=1, source_target_pairs={{0,34},{2,32},{32,2},{34,0},{1,35},{3,33},{33,3},{35,1},{4,38},{6,... | collective-permute-start | bytes 442376 | tf_op jit(solution)/shard_map/ppermute | solution.py:373
  51.8 16.1 %collective-permute-start.3 = (bf16[576,128]{1,0:T(8,128)(2,1)}, bf16[576,128]{1,0:T(8,128)(2,1)S(1)}, u32[]{:S(2)}, u32[]{:S(2)}) collective-permute-start(bf16[576,128]{1,0:T(8,128)(2,1)} %get-tuple-element.30), channel_id=1, source_target_pairs={{0,2},{2,0},{1,3},{3,1},{4,6},{6,4},{5,7},{7,5},{8,10},{10,8},{9,1... | collective-permute-start | bytes 442376 | tf_op jit(solution)/shard_map/ppermute | solution.py:26
  60.8 7.2 %copy-start.3 = (bf16[992,128]{1,0:T(8,128)(2,1)}, bf16[992,128]{1,0:T(8,128)(2,1)S(1)}, u32[]{:S(2)}) copy-start(bf16[992,128]{1,0:T(8,128)(2,1)S(1)} %collective-permute-done.2.refs_2_) | copy-start | bytes 761860
  60.9 20.2 %all-to-all-start.1 = ((bf16[32,80,128]{2,1,0:T(8,128)(2,1)}), bf16[32,80,128]{2,1,0:T(8,128)(2,1)S(1)}, u32[]{:S(2)}, u32[]{:S(2)}) async-start(bf16[32,80,128]{2,1,0:T(8,128)(2,1)} %bitcast.16), calls=%async_computation.1 | async-start | bytes 1310720 | tf_op jit(solution)/shard_map/all_to_all | solution.py:38
  68.0 1.9 %copy-start.2 = (bf16[576,512]{1,0:T(8,128)(2,1)}, bf16[576,512]{1,0:T(8,128)(2,1)S(1)}, u32[]{:S(2)}) copy-start(bf16[576,512]{1,0:T(8,128)(2,1)S(1)} %pad_maximum_fusion.refs_9_) | copy-start | bytes 1769476
  68.0 4.0 %collective-permute-start.5 = (bf16[576,512]{1,0:T(8,128)(2,1)S(1)}, bf16[576,512]{1,0:T(8,128)(2,1)}, u32[]{:S(2)}, u32[]{:S(2)}) collective-permute-start(bf16[576,512]{1,0:T(8,128)(2,1)S(1)} %pad_maximum_fusion.refs_9_), channel_id=1, source_target_pairs={{0,1},{1,0},{2,3},{3,2},{4,5},{5,4},{6,7},{7,6},{8,9},{9,8},{10,11... | collective-permute-start | bytes 1769480 | tf_op jit(solution)/shard_map/ppermute | solution.py:26
  81.1 0.9 copy-start
  87.3 14.6 %collective-permute-start.6 = (bf16[64,128]{1,0:T(8,128)(2,1)}, bf16[64,128]{1,0:T(8,128)(2,1)S(1)}, u32[]{:S(2)}, u32[]{:S(2)}) collective-permute-start(bf16[64,128]{1,0:T(8,128)(2,1)} %get-tuple-element.31), channel_id=1, source_target_pairs={{0,16},{16,0},{1,17},{17,1},{2,18},{18,2},{3,19},{19,3},{4,20},{20... | collective-permute-start | bytes 49160 | tf_op jit(solution)/shard_map/ppermute | solution.py:26
  116.2 3.6 %collective-permute-start.7 = (bf16[8,2,16,448]{3,2,1,0:T(8,128)(2,1)}, bf16[8,2,16,448]{3,2,1,0:T(8,128)(2,1)S(1)}, u32[]{:S(2)}, u32[]{:S(2)}) collective-permute-start(bf16[8,2,16,448]{3,2,1,0:T(8,128)(2,1)} %get-tuple-element.34), channel_id=1, source_target_pairs={{0,1},{1,0},{2,3},{3,2},{4,5},{5,4},{6,7},{7,6},{8,9},{9,8},{10,11... | collective-permute-start | bytes 688136 | tf_op jit(solution)/shard_map/ppermute | solution.py:26

commit v9 on v8

--- a/solution.py
+++ b/solution.py
@@ -2,7 +2,6 @@
 
 import jax
 import jax.numpy as jnp
-import numpy as np
 from jax import lax
 from jax.experimental import pallas as pl
 from jax.experimental.pallas import tpu as pltpu
@@ -17,8 +16,7 @@
 COLUMN = ("zh", "zlh", "zll")
 BF16 = jnp.bfloat16
 F32 = jnp.float32
-VMEM_LIMIT = 63 * 1024 * 1024
-PACK_LIMIT = 63 * 1024 * 1024
+VMEM_LIMIT = 12 * 1024 * 1024
 UNPACK_FLOPS = 2 * 10**10
 
 
@@ -53,37 +51,21 @@
     ]
 
 
-def pack_kernel(
-    place, cache, w_uq, w_uk, w_uv, latent, rope, out, uq, uk, uv, latent_in, rope_in, sems
-):
+def pack_kernel(place, cache, w_uq, w_uk, w_uv, latent, rope, out):
     zh, quarter = place[0], place[2]
     lanes = out.shape[1]
-    width = cache.shape[0]
-    four = uq.shape[0]
-    given = pl.ds((1 - zh) * four, four)
-    copies = [
-        (cache.at[:, pl.ds(pl.multiple_of(quarter * lanes, lanes), lanes)], out.at[pl.ds(0, width)]),
-        (w_uq.at[given], uq),
-        (w_uk.at[given], uk),
-        (w_uv.at[given], uv),
-        (latent, latent_in),
-        (rope, rope_in),
-    ]
-    copies = [pltpu.make_async_copy(x, y, sems.at[i]) for i, (x, y) in enumerate(copies)]
-    for copy in copies:
-        copy.start()
-    for copy in copies:
-        copy.wait()
-    at = width
+    at = cache.shape[0]
+    out[:at] = cache[:, pl.ds(pl.multiple_of(quarter * lanes, lanes), lanes)]
+    four = w_uq.shape[0] // 2
     for h in range(four):
-        for w in (uq, uk, uv):
-            out[at : at + w.shape[1]] = w[h]
+        for w in (w_uq, w_uk, w_uv):
+            out[at : at + w.shape[1]] = w[(1 - zh) * four + h]
             at += w.shape[1]
-    rows = latent_in.shape[0]
-    for i in range(latent_in.shape[1] // lanes):
-        out[at : at + rows] = latent_in[:, i * lanes : (i + 1) * lanes]
+    rows = latent.shape[0]
+    for i in range(latent.shape[1] // lanes):
+        out[at : at + rows] = latent[:, i * lanes : (i + 1) * lanes]
         at += rows
-    pairs = head_pairs(rope_in)
+    pairs = head_pairs(rope)
     for p in range(len(pairs) // 2):
         out[at : at + rows] = jnp.where(zh == 0, pairs[p + len(pairs) // 2], pairs[p])
         at += rows
@@ -124,7 +106,7 @@
         at += n_all
     ours = pl.ds(pl.multiple_of(zh * own_rows, 16), own_rows)
     theirs = pl.ds(pl.multiple_of((1 - zh) * own_rows, 16), own_rows)
-    to = n_piece
+    to = 0
     for i in range(latent.shape[1] // lanes):
         packed[pl.ds(pl.multiple_of(to + zh * own_rows, 16), own_rows)] = latent[
             :, i * lanes : (i + 1) * lanes
@@ -143,7 +125,6 @@
     rope_out[theirs] = stay[1]
     packed[pl.ds(pl.multiple_of(to + zh * own_rows, 16), own_rows)] = go[0]
     packed[pl.ds(pl.multiple_of(to + (1 - zh) * own_rows, 16), own_rows)] = go[1]
-    packed[:n_piece] = received[:n_piece]
     piece[...] = received[:n_piece]
 
 
@@ -170,7 +151,11 @@
     temper,
 ):
     rows, heads, n_uq, n_uk, n_uv, width = sizes
-    caches = (kv0, kv1, kv2, kv3)
+    caches = [kv0, kv1] + [kv.at[c] for kv in (kv2, kv3) for c in range(2)]
+    spans, tokens = [], 0
+    for cache in caches:
+        spans.append((tokens, tokens + cache.shape[1]))
+        tokens += cache.shape[1]
     zh, yl, core = place[0], place[1], place[3]
     zll = place[2] - core * 2
     quarter = kv0.shape[1] // 4
@@ -178,20 +163,19 @@
     for ylo in (yl, 1 - yl):
         for i in range(4):
             starts.append((ylo * 2 + zh) * kv0.shape[1] + i * quarter)
-    for co in (core, 1 - core):
-        for zo in (zll, 1 - zll):
+    for zo in (zll, 1 - zll):
+        for co in (0, 1):
             for ylo in (yl, 1 - yl):
                 starts.append((ylo * 2 + 1 - zh) * kv0.shape[1] + (co * 2 + zo) * quarter)
     n_all = n_uq + n_uk + n_uv
     for h in range(heads):
         weights[:, h, zh] = weights_ours[:, h * n_all : (h + 1) * n_all]
         weights[:, h, 1 - zh] = weights_theirs[:, h]
-    per_block = kv0.shape[1]
     chunk = quarter
     half = rows // 2
     mine = pl.ds(pl.multiple_of(yl * half, 16), half)
     other = pl.ds(pl.multiple_of((1 - yl) * half, 16), half)
-    at = kv0.shape[0]
+    at = 0
     lane_count = ours.shape[1]
     for i in range(query_rows.shape[1] // lane_count):
         lanes_here = slice(i * lane_count, (i + 1) * lane_count)
@@ -222,19 +206,18 @@
         [rope[:, h * rope_width : (h + 1) * rope_width] for h in range(heads)], axis=0
     )
     top = jnp.full((all_rows, 1), -1e30, F32)
-    for b, cache in enumerate(caches):
+    for (begin, end), cache in zip(spans, caches):
         s = dot(q_lat, cache[:width, :]) + dot(q_rope, cache[width:, :])
         s = s * temper
-        for i in range(per_block // chunk):
-            k = b * (per_block // chunk) + i
-            piece = s[:, i * chunk : (i + 1) * chunk]
+        for k in range(begin // chunk, end // chunk):
+            piece = s[:, k * chunk - begin : (k + 1) * chunk - begin]
             piece = jnp.where(lanes + starts[k] < limit, piece, -1e30)
             top = jnp.maximum(top, jnp.max(piece, axis=1, keepdims=True))
             scores[:, k * chunk : (k + 1) * chunk] = piece
     total = jnp.zeros((all_rows, 1), F32)
     context = jnp.zeros((all_rows, width), F32)
-    for b, cache in enumerate(caches):
-        p = jnp.exp(scores[:, b * per_block : (b + 1) * per_block] - top)
+    for (begin, end), cache in zip(spans, caches):
+        p = jnp.exp(scores[:, begin:end] - top)
         total = total + jnp.sum(p, axis=1, keepdims=True)
         context = context + dot_nt(p.astype(BF16), cache[:width, :])
     context = (context / total).astype(BF16)
@@ -256,20 +239,20 @@
     give_out[...] = moved[:, wide // 2 :]
 
 
-def feature_order(heads, plane, items):
-    count = 4 * heads * plane * items
-    to = np.arange(count).reshape(plane, 2, 2, heads, items).transpose(2, 1, 3, 0, 4).reshape(-1)
-    return np.equal(to[:, None], np.arange(count)[None, :]).astype(np.float32)
-
-
-def project_kernel(place, values, received, order, keep_out, give_out):
+def project_kernel(place, values, received, keep_out, give_out):
     core = place[3]
     lanes = received.shape[2]
     rows = [
         jnp.concatenate([values[i], values[i + 1]], axis=1) for i in range(0, values.shape[0], 2)
     ]
-    rows = dot(jnp.concatenate(rows, axis=0), order[...]).astype(BF16)
+    rows = jnp.concatenate(rows, axis=0)
     depth = rows.shape[1]
+    source = lax.broadcasted_iota(jnp.int32, (depth, depth), 0)
+    to = lax.broadcasted_iota(jnp.int32, (depth, depth), 1)
+    y, z, j = source // 256, source // 128 % 2, source // 64 % 2
+    wanted = source // 4 % 16 * 32 + (z * 4 + y * 2 + j) * 4 + source % 4
+    order = jnp.where(to == wanted, 1.0, 0.0).astype(BF16)
+    rows = dot(rows, order).astype(BF16)
     each = depth // received.shape[0]
     columns = keep_out.shape[-1]
     count = 2 * columns // lanes
@@ -314,12 +297,9 @@
     packed = pl.pallas_call(
         pack_kernel,
         out_shape=jax.ShapeDtypeStruct((n_sent, lanes), BF16),
-        in_specs=[smem] + [pl.BlockSpec(memory_space=pltpu.HBM)] * 6,
+        in_specs=[smem] + [vmem] * 6,
         out_specs=vmem,
-        scratch_shapes=[pltpu.VMEM((four,) + w.shape[1:], BF16) for w in weights]
-        + [pltpu.VMEM(x.shape, BF16) for x in queries]
-        + [pltpu.SemaphoreType.DMA((6,))],
-        compiler_params=pltpu.CompilerParams(vmem_limit_bytes=PACK_LIMIT),
+        compiler_params=pltpu.CompilerParams(vmem_limit_bytes=VMEM_LIMIT),
         cost_estimate=pl.CostEstimate(flops=10**6, bytes_accessed=10**6, transcendentals=0),
         name="pack",
     )(place, cache, *weights, *queries)
@@ -341,7 +321,7 @@
     )(place, *weights, w_out.reshape(w_rows, width))
     spread = exchange(spread, PLANE)
 
-    n_pack = kv_width + (2 * latent_chunks + 2) * own_rows
+    n_pack = (2 * latent_chunks + 2) * own_rows
     sent, packed, far_piece, rope_kept = pl.pallas_call(
         lambda *refs: unpack_kernel(*refs, sizes=(kv_width, n_all, plane // 2)),
         out_shape=(
@@ -371,8 +351,9 @@
     packed_y = swap(packed, "yl")
     piece_z = swap(far_piece, "zll")
     piece_yz = lax.ppermute(far_piece, ("yl", "zll"), [(0, 3), (1, 2), (2, 1), (3, 0)])
-    far = jnp.concatenate([far_piece, packed_y[:kv_width], piece_z, piece_yz], axis=1)
-    far_other = swap(far, "c")
+    piece_y = swap(far_piece, "yl")
+    far = lax.all_gather(jnp.concatenate([far_piece, piece_y], axis=1), "c", axis=0)
+    far_z = lax.all_gather(jnp.concatenate([piece_z, piece_yz], axis=1), "c", axis=0)
 
     keep, give = pl.pallas_call(
         lambda *refs: attend_kernel(
@@ -392,23 +373,22 @@
         compiler_params=pltpu.CompilerParams(vmem_limit_bytes=VMEM_LIMIT),
         cost_estimate=pl.CostEstimate(flops=10**9, bytes_accessed=5 * 10**6, transcendentals=0),
         name="attend",
-    )(place, packed, packed_y, spread, weights_far, rope_kept, row_lengths, cache, near, far, far_other)
+    )(place, packed, packed_y, spread, weights_far, rope_kept, row_lengths, cache, near, far, far_z)
 
     values = ordered(keep, swap(give, "zh"), zh, 1)
     gathered = exchange(
         jnp.broadcast_to(values[None], (8,) + values.shape).reshape(-1, values.shape[1]), PART
     ).reshape((8,) + values.shape)
-    order = jnp.asarray(feature_order(heads, plane, vpart), BF16)
     shape = (8, 2, own_rows, columns // 2)
     keep, give = pl.pallas_call(
         project_kernel,
         out_shape=(jax.ShapeDtypeStruct(shape, BF16),) * 2,
-        in_specs=[smem] + [vmem] * 3,
+        in_specs=[smem] + [vmem] * 2,
         out_specs=(vmem,) * 2,
         compiler_params=pltpu.CompilerParams(vmem_limit_bytes=VMEM_LIMIT),
         cost_estimate=pl.CostEstimate(flops=2 * 10**8, bytes_accessed=2 * 10**6, transcendentals=0),
         name="project",
-    )(place, gathered, spread, order)
+    )(place, gathered, spread)
 
     total = (keep.astype(F32) + swap(give, "c").astype(F32)).astype(BF16)
     total = jnp.transpose(exchange(total, PART), (1, 0, 2, 3))

time: 157 us -> 154 us (0.981)
  the two profiles are of different devices: /device:TPU:32 before, /device:TPU:6 now
where the time goes in v9:
time: 154 us; the launch traced here: 152 us
  starting transfers between devices  56 us (36%)
  blocking collectives  50.3 us (33%)
  waiting for transfers between devices  25.6 us (17%)
  Pallas kernels  10 us (6%)
  local copies, waits for them, and re-layouts  8.74 us (6%)
    all_to_all x3, blocking collectives, exchange(): return lax.all_to_all(blocks, axes, 0, 0, tiled=True)  45.9 us
    ppermute x7, starting transfers between devices, swap(): return lax.ppermute(block, axis, [(0, 1), (1, 0)])  37.8 us
    ppermute x7, waiting for transfers between devices, swap(): return lax.ppermute(block, axis, [(0, 1), (1, 0)])  25.4 us
    all_to_all x2, starting transfers between devices, exchange(): return lax.all_to_all(blocks, axes, 0, 0, tiled=True)  14.4 us
    unnamed x30, local copies, waits for them, and re-layouts  7.42 us
    pallas_call x1, Pallas kernels, local(): pl.pallas_call(lambda *refs: attend_kernel(*refs, sizes=(rows, heads, n_u...  3.87 us
    ppermute x1, starting transfers between devices, local(): lax.ppermute(far_piece, ('yl', 'zll'), [(0, 3), (1, 2), (2, 1), (3, 0)])  3.81 us
  transfers between devices with their start and end apart: 10, of which 5 were waited for; matrix products, arithmetic and copies ran while one was open for 1% of the time, Pallas kernels for 2%

profile of v9, /device:TPU:6, one launch (start us, length us, event | category | flops | bytes accessed | tf_op | source)
XLA Modules:
  0.0 151.7 jit_solution(10761432177512510720)
XLA Ops:
  0.0 0.1 stack.23.place.refs_0_
  0.1 0.9 copy-done.2
  1.0 0.8 copy-done.4
  1.7 0.8 copy-done.6
  2.5 0.8 copy-done.10
  3.3 0.8 copy-done.12
  4.1 1.2 pack.1
  5.3 15.7 %collective-permute-start = (bf16[1120,128]{1,0:T(8,128)(2,1)S(1)}, bf16[1120,128]{1,0:T(8,128)(2,1)S(1)}, u32[]{:S(2)}, u32[]{:S(2)}) collective-permute-start(bf16[1120,128]{1,0:T(8,128)(2,1)S(1)} %pack.1), channel_id=1, source_target_pairs={{0,16},{16,0},{1,17},{17,1},{2,18},{18,2},{3,19},{19,3},{4,20},{20... | collective-permute-start | bytes 860168 | tf_op jit(solution)/shard_map/ppermute | solution.py:24
  21.0 3.5 %collective-permute-start.1 = (bf16[576,512]{1,0:T(8,128)(2,1)}, bf16[576,512]{1,0:T(8,128)(2,1)S(1)}, u32[]{:S(2)}, u32[]{:S(2)}) collective-permute-start(bf16[576,512]{1,0:T(8,128)(2,1)} %bitcast.5.cache.refs_7_), channel_id=1, source_target_pairs={{0,32},{32,0},{1,33},{33,1},{2,34},{34,2},{3,35},{35,3},{4,36},{36... | collective-permute-start | bytes 1769480 | tf_op jit(solution)/shard_map/ppermute | solution.py:24
  24.5 1.1 reshape.51.w_out
  25.6 0.0 copy-done.5
  25.6 0.0 copy-done.7
  25.6 0.0 copy-done.3
  25.7 1.9 %spread.1 = bf16[16,384,128]{2,1,0:T(8,128)(2,1)} custom-call(s32[5]{0:T(128)S(1)} %stack.23.place.refs_0_, bf16[8,48,128]{2,1,0:T(8,128)(2,1)S(1)} %copy-done.3, bf16[8,16,128]{2,1,0:T(8,128)(2,1)S(1)} %copy-done.5, bf16[8,16,128]{2,1,0:T(8,128)(2,1)S(1)} %copy-done.7, bf16[32,7168]{1,0:T(8,128)(2,1)S(1)} %reshape.51.w_out), custom_call_target="tpu_custom_call" | custom-call | flops 1000000 | bytes 1000000 | tf_op jit(solution)/shard_map/spread/pallas_call | solution.py:313
  27.6 7.3 %all-to-all-start = ((bf16[16,384,128]{2,1,0:T(8,128)(2,1)}), bf16[16,384,128]{2,1,0:T(8,128)(2,1)S(1)}, u32[]{:S(2)}, u32[]{:S(2)}) async-start(bf16[16,384,128]{2,1,0:T(8,128)(2,1)} %spread.1), calls=%async_computation | async-start | bytes 3145728 | tf_op jit(solution)/shard_map/all_to_all | solution.py:36
  34.9 0.0 copy-done.14
  34.9 0.1 reshape.50.refs_6_
  35.0 0.0 collective-permute-done.refs_1_
  35.0 1.5 unpack.1
  36.5 15.4 %collective-permute-done.1.refs_8_ = bf16[576,512]{1,0:T(8,128)(2,1)S(1)} collective-permute-done((bf16[576,512]{1,0:T(8,128)(2,1)}, bf16[576,512]{1,0:T(8,128)(2,1)S(1)}, u32[]{:S(2)}, u32[]{:S(2)}) %collective-permute-start.1) | collective-permute-done | bytes 589856 | tf_op jit(solution)/shard_map/ppermute | solution.py:24
  51.9 0.8 copy-done
  52.7 3.6 %collective-permute-start.3 = (bf16[576,128]{1,0:T(8,128)(2,1)S(1)}, bf16[576,128]{1,0:T(8,128)(2,1)S(1)}, u32[]{:S(2)}, u32[]{:S(2)}) collective-permute-start(bf16[576,128]{1,0:T(8,128)(2,1)S(1)} %get-tuple-element.30), channel_id=1, source_target_pairs={{0,32},{32,0},{1,33},{33,1},{2,34},{34,2},{3,35},{35,3},{4,36},{36... | collective-permute-start | bytes 442376 | tf_op jit(solution)/shard_map/ppermute | solution.py:24
  56.3 0.2 all-to-all-done.refs_3_.received
  56.6 7.1 %all-to-all-start.1 = ((bf16[32,80,128]{2,1,0:T(8,128)(2,1)}), bf16[32,80,128]{2,1,0:T(8,128)(2,1)S(1)}, u32[]{:S(2)}, u32[]{:S(2)}) async-start(bf16[32,80,128]{2,1,0:T(8,128)(2,1)} %bitcast.6), calls=%async_computation.1 | async-start | bytes 1310720 | tf_op jit(solution)/shard_map/all_to_all | solution.py:36
  63.7 3.8 %collective-permute-start.5 = (bf16[576,128]{1,0:T(8,128)(2,1)S(1)}, bf16[576,128]{1,0:T(8,128)(2,1)S(1)}, u32[]{:S(2)}, u32[]{:S(2)}) collective-permute-start(bf16[576,128]{1,0:T(8,128)(2,1)S(1)} %get-tuple-element.30), channel_id=1, source_target_pairs={{0,34},{2,32},{32,2},{34,0},{1,35},{3,33},{33,3},{35,1},{4,38},{6,... | collective-permute-start | bytes 442376 | tf_op jit(solution)/shard_map/ppermute | solution.py:353
  67.5 2.9 %collective-permute-start.4 = (bf16[576,128]{1,0:T(8,128)(2,1)S(1)}, bf16[576,128]{1,0:T(8,128)(2,1)S(1)}, u32[]{:S(2)}, u32[]{:S(2)}) collective-permute-start(bf16[576,128]{1,0:T(8,128)(2,1)S(1)} %get-tuple-element.30), channel_id=1, source_target_pairs={{0,2},{2,0},{1,3},{3,1},{4,6},{6,4},{5,7},{7,5},{8,10},{10,8},{9,1... | collective-permute-start | bytes 442376 | tf_op jit(solution)/shard_map/ppermute | solution.py:24
  70.4 2.5 %collective-permute-start.2 = (bf16[416,128]{1,0:T(8,128)(2,1)S(1)}, bf16[416,128]{1,0:T(8,128)(2,1)S(1)}, u32[]{:S(2)}, u32[]{:S(2)}) collective-permute-start(bf16[416,128]{1,0:T(8,128)(2,1)S(1)} %get-tuple-element.23.refs_1_), channel_id=1, source_target_pairs={{0,32},{32,0},{1,33},{33,1},{2,34},{34,2},{3,35},{35,3},{4,36},{36... | collective-permute-start | bytes 319496 | tf_op jit(solution)/shard_map/ppermute | solution.py:24
  72.9 0.0 collective-permute-done.3
  73.0 0.0 collective-permute-done.5
  73.0 1.6 %collective-permute-done.4 = bf16[576,128]{1,0:T(8,128)(2,1)S(1)} collective-permute-done((bf16[576,128]{1,0:T(8,128)(2,1)S(1)}, bf16[576,128]{1,0:T(8,128)(2,1)S(1)}, u32[]{:S(2)}, u32[]{:S(2)}) %collective-permute-start.4) | collective-permute-done | bytes 147488 | tf_op jit(solution)/shard_map/ppermute | solution.py:24
  74.6 2.2 %all-gather = bf16[1152,256]{1,0:T(8,128)(2,1)S(1)} all-gather(bf16[576,256]{1,0:T(8,128)(2,1)S(1)} %pad_maximum_fusion), channel_id=2, replica_groups=mesh['xh'=2,'xl'=2,'yh'=2,'yl'=2,'zh'=2,'zlh'=4,'zll'=2,'c'=2] {'c'}, dimensions={0}, use_global_device_ids=true | all-gather | bytes 884736 | tf_op jit(solution)/shard_map/all_gather | solution.py:355
  76.8 2.2 %all-gather.1 = bf16[1152,256]{1,0:T(8,128)(2,1)S(1)} all-gather(bf16[576,256]{1,0:T(8,128)(2,1)S(1)} %pad_maximum_fusion.1), channel_id=3, replica_groups=mesh['xh'=2,'xl'=2,'yh'=2,'yl'=2,'zh'=2,'zlh'=4,'zll'=2,'c'=2] {'c'}, dimensions={0}, use_global_device_ids=true | all-gather | bytes 884736 | tf_op jit(solution)/shard_map/all_gather | solution.py:356
  79.0 0.0 collective-permute-done.2.refs_2_
  79.0 0.6 copy-done.8
  79.7 0.0 all-to-all-done.1
  79.7 1.1 copy-done.1
  80.8 0.9 copy-done.9
  81.7 3.9 %attend.1 = (bf16[64,128]{1,0:T(8,128)(2,1)S(1)}, bf16[64,128]{1,0:T(8,128)(2,1)}) custom-call(s32[5]{0:T(128)S(1)} %stack.23.place.refs_0_, bf16[416,128]{1,0:T(8,128)(2,1)S(1)} %get-tuple-element.23.refs_1_, bf16[416,128]{1,0:T(8,128)(2,1)S(1)} %copy-done.9, bf16[16,384,128]{2,1,0:T(8,128)(2,1)S(1)} %all-to-all-done.refs_3_.received, ...), custom_call_target="tpu_custom_call" | custom-call | flops 1000000000 | bytes 5000000 | tf_op jit(solution)/shard_map/attend/pallas_call | solution.py:358
  85.5 7.7 %collective-permute-start.6 = (bf16[64,128]{1,0:T(8,128)(2,1)}, bf16[64,128]{1,0:T(8,128)(2,1)S(1)}, u32[]{:S(2)}, u32[]{:S(2)}) collective-permute-start(bf16[64,128]{1,0:T(8,128)(2,1)} %get-tuple-element.31), channel_id=1, source_target_pairs={{0,16},{16,0},{1,17},{17,1},{2,18},{18,2},{3,19},{19,3},{4,20},{20... | collective-permute-start | bytes 49160 | tf_op jit(solution)/shard_map/ppermute | solution.py:24
  93.2 6.9 %collective-permute-done.6 = bf16[64,128]{1,0:T(8,128)(2,1)S(1)} collective-permute-done((bf16[64,128]{1,0:T(8,128)(2,1)}, bf16[64,128]{1,0:T(8,128)(2,1)S(1)}, u32[]{:S(2)}, u32[]{:S(2)}) %collective-permute-start.6) | collective-permute-done | bytes 16416 | tf_op jit(solution)/shard_map/ppermute | solution.py:24
  100.1 11.0 %all_to_all.26.values = bf16[8,64,256]{2,1,0:T(8,128)(2,1)S(1)} all-to-all(bf16[8,64,256]{2,1,0:T(8,128)(2,1)S(1)} %broadcast_in_dim.2), channel_id=1, replica_groups=mesh['xh'=2,'xl'=2,'yh'=2,'yl'=2,'zh'=2,'zlh'=4,'zll'=2,'c'=2] {'xl','yh..., dimensions={0} | all-to-all | bytes 524288 | tf_op jit(solution)/shard_map/all_to_all | solution.py:36
  111.1 1.5 project.1
  112.6 1.9 %collective-permute-start.7 = (bf16[8,2,16,448]{3,2,1,0:T(8,128)(2,1)S(1)}, bf16[8,2,16,448]{3,2,1,0:T(8,128)(2,1)S(1)}, u32[]{:S(2)}, u32[]{:S(2)}) collective-permute-start(bf16[8,2,16,448]{3,2,1,0:T(8,128)(2,1)S(1)} %get-tuple-element.34), channel_id=1, source_target_pairs={{0,1},{1,0},{2,3},{3,2},{4,5},{5,4},{6,7},{7,6},{8,9},{9,8},{10,11... | collective-permute-start | bytes 688136 | tf_op jit(solution)/shard_map/ppermute | solution.py:24
  114.6 1.5 collective-permute-done.7
  116.1 0.1 add_convert_fusion
  116.2 10.2 %all_to_all.27 = bf16[8,2,16,448]{3,2,1,0:T(8,128)(2,1)S(1)} all-to-all(bf16[8,2,16,448]{3,2,1,0:T(8,128)(2,1)S(1)} %add_convert_fusion), channel_id=1, replica_groups=mesh['xh'=2,'xl'=2,'yh'=2,'yl'=2,'zh'=2,'zlh'=4,'zll'=2,'c'=2] {'xl','yh..., dimensions={0} | all-to-all | bytes 458752 | tf_op jit(solution)/shard_map/all_to_all | solution.py:36
  126.4 24.6 %all_to_all.28 = bf16[16,16,448]{2,1,0:T(8,128)(2,1)S(1)} all-to-all(bf16[16,16,448]{2,1,0:T(8,128)(2,1)S(1)} %bitcast.16), channel_id=1, replica_groups=mesh['xh'=2,'xl'=2,'yh'=2,'yl'=2,'zh'=2,'zlh'=4,'zll'=2,'c'=2] {'zh','zl..., dimensions={0} | all-to-all | bytes 458752 | tf_op jit(solution)/shard_map/all_to_all | solution.py:36
  151.0 0.7 reduce_sum.12
  (22 shorter events, 0.1 us)
Async XLA Ops:
  0.0 25.6 %copy-start.5 = (bf16[8,16,128]{2,1,0:T(8,128)(2,1)S(1)}, bf16[8,16,128]{2,1,0:T(8,128)(2,1)}, u32[]{:S(2)}) copy-start(bf16[8,16,128]{2,1,0:T(8,128)(2,1)} %w_uk.3) | copy-start | bytes 98308
  0.0 25.6 %copy-start.7 = (bf16[8,16,128]{2,1,0:T(8,128)(2,1)S(1)}, bf16[8,16,128]{2,1,0:T(8,128)(2,1)}, u32[]{:S(2)}) copy-start(bf16[8,16,128]{2,1,0:T(8,128)(2,1)} %w_uv.3) | copy-start | bytes 98308
  0.1 0.9 copy-start.2
  1.0 0.8 copy-start.4
  1.7 0.8 copy-start.6
  2.5 0.8 copy-start.10
  3.3 0.8 copy-start.12
  4.1 21.6 %copy-start.3 = (bf16[8,48,128]{2,1,0:T(8,128)(2,1)S(1)}, bf16[8,48,128]{2,1,0:T(8,128)(2,1)}, u32[]{:S(2)}) copy-start(bf16[8,48,128]{2,1,0:T(8,128)(2,1)} %w_uq.3) | copy-start | bytes 294916
  5.3 29.7 %collective-permute-start = (bf16[1120,128]{1,0:T(8,128)(2,1)S(1)}, bf16[1120,128]{1,0:T(8,128)(2,1)S(1)}, u32[]{:S(2)}, u32[]{:S(2)}) collective-permute-start(bf16[1120,128]{1,0:T(8,128)(2,1)S(1)} %pack.1), channel_id=1, source_target_pairs={{0,16},{16,0},{1,17},{17,1},{2,18},{18,2},{3,19},{19,3},{4,20},{20... | collective-permute-start | bytes 860168 | tf_op jit(solution)/shard_map/ppermute | solution.py:24
  21.0 30.9 %collective-permute-start.1 = (bf16[576,512]{1,0:T(8,128)(2,1)}, bf16[576,512]{1,0:T(8,128)(2,1)S(1)}, u32[]{:S(2)}, u32[]{:S(2)}) collective-permute-start(bf16[576,512]{1,0:T(8,128)(2,1)} %bitcast.5.cache.refs_7_), channel_id=1, source_target_pairs={{0,32},{32,0},{1,33},{33,1},{2,34},{34,2},{3,35},{35,3},{4,36},{36... | collective-permute-start | bytes 1769480 | tf_op jit(solution)/shard_map/ppermute | solution.py:24
  27.6 7.3 %copy-start.14 = (s32[512]{0:T(512)S(1)}, s32[512]{0:T(512)}, u32[]{:S(2)}) copy-start(s32[512]{0:T(512)} %param.10) | copy-start | bytes 6148
  27.6 7.4 %copy-start.11 = (bf16[16,1536]{1,0:T(8,128)(2,1)S(1)}, bf16[16,1536]{1,0:T(8,128)(2,1)}, u32[]{:S(2)}) copy-start(bf16[16,1536]{1,0:T(8,128)(2,1)} %refs_2_.1) | copy-start | bytes 147460
  27.6 7.4 %copy-start.13 = (bf16[16,8,64]{2,1,0:T(8,128)(2,1)S(1)}, bf16[16,8,64]{2,1,0:T(8,128)(2,1)}, u32[]{:S(2)}) copy-start(bf16[16,8,64]{2,1,0:T(8,128)(2,1)} %refs_3_.1) | copy-start | bytes 49156
  27.6 28.9 %all-to-all-start = ((bf16[16,384,128]{2,1,0:T(8,128)(2,1)}), bf16[16,384,128]{2,1,0:T(8,128)(2,1)S(1)}, u32[]{:S(2)}, u32[]{:S(2)}) async-start(bf16[16,384,128]{2,1,0:T(8,128)(2,1)} %spread.1), calls=%async_computation | async-start | bytes 3145728 | tf_op jit(solution)/shard_map/all_to_all | solution.py:36
  51.9 0.8 copy-start
  52.7 20.2 %collective-permute-start.3 = (bf16[576,128]{1,0:T(8,128)(2,1)S(1)}, bf16[576,128]{1,0:T(8,128)(2,1)S(1)}, u32[]{:S(2)}, u32[]{:S(2)}) collective-permute-start(bf16[576,128]{1,0:T(8,128)(2,1)S(1)} %get-tuple-element.30), channel_id=1, source_target_pairs={{0,32},{32,0},{1,33},{33,1},{2,34},{34,2},{3,35},{35,3},{4,36},{36... | collective-permute-start | bytes 442376 | tf_op jit(solution)/shard_map/ppermute | solution.py:24
  56.6 23.1 %all-to-all-start.1 = ((bf16[32,80,128]{2,1,0:T(8,128)(2,1)}), bf16[32,80,128]{2,1,0:T(8,128)(2,1)S(1)}, u32[]{:S(2)}, u32[]{:S(2)}) async-start(bf16[32,80,128]{2,1,0:T(8,128)(2,1)} %bitcast.6), calls=%async_computation.1 | async-start | bytes 1310720 | tf_op jit(solution)/shard_map/all_to_all | solution.py:36
  63.7 9.3 %collective-permute-start.5 = (bf16[576,128]{1,0:T(8,128)(2,1)S(1)}, bf16[576,128]{1,0:T(8,128)(2,1)S(1)}, u32[]{:S(2)}, u32[]{:S(2)}) collective-permute-start(bf16[576,128]{1,0:T(8,128)(2,1)S(1)} %get-tuple-element.30), channel_id=1, source_target_pairs={{0,34},{2,32},{32,2},{34,0},{1,35},{3,33},{33,3},{35,1},{4,38},{6,... | collective-permute-start | bytes 442376 | tf_op jit(solution)/shard_map/ppermute | solution.py:353
  67.5 7.0 %collective-permute-start.4 = (bf16[576,128]{1,0:T(8,128)(2,1)S(1)}, bf16[576,128]{1,0:T(8,128)(2,1)S(1)}, u32[]{:S(2)}, u32[]{:S(2)}) collective-permute-start(bf16[576,128]{1,0:T(8,128)(2,1)S(1)} %get-tuple-element.30), channel_id=1, source_target_pairs={{0,2},{2,0},{1,3},{3,1},{4,6},{6,4},{5,7},{7,5},{8,10},{10,8},{9,1... | collective-permute-start | bytes 442376 | tf_op jit(solution)/shard_map/ppermute | solution.py:24
  70.4 8.6 %collective-permute-start.2 = (bf16[416,128]{1,0:T(8,128)(2,1)S(1)}, bf16[416,128]{1,0:T(8,128)(2,1)S(1)}, u32[]{:S(2)}, u32[]{:S(2)}) collective-permute-start(bf16[416,128]{1,0:T(8,128)(2,1)S(1)} %get-tuple-element.23.refs_1_), channel_id=1, source_target_pairs={{0,32},{32,0},{1,33},{33,1},{2,34},{34,2},{3,35},{35,3},{4,36},{36... | collective-permute-start | bytes 319496 | tf_op jit(solution)/shard_map/ppermute | solution.py:24
  79.0 0.6 copy-start.8
  79.7 1.1 copy-start.1
  80.8 0.9 copy-start.9
  85.5 14.5 %collective-permute-start.6 = (bf16[64,128]{1,0:T(8,128)(2,1)}, bf16[64,128]{1,0:T(8,128)(2,1)S(1)}, u32[]{:S(2)}, u32[]{:S(2)}) collective-permute-start(bf16[64,128]{1,0:T(8,128)(2,1)} %get-tuple-element.31), channel_id=1, source_target_pairs={{0,16},{16,0},{1,17},{17,1},{2,18},{18,2},{3,19},{19,3},{4,20},{20... | collective-permute-start | bytes 49160 | tf_op jit(solution)/shard_map/ppermute | solution.py:24
  112.6 3.4 %collective-permute-start.7 = (bf16[8,2,16,448]{3,2,1,0:T(8,128)(2,1)S(1)}, bf16[8,2,16,448]{3,2,1,0:T(8,128)(2,1)S(1)}, u32[]{:S(2)}, u32[]{:S(2)}) collective-permute-start(bf16[8,2,16,448]{3,2,1,0:T(8,128)(2,1)S(1)} %get-tuple-element.34), channel_id=1, source_target_pairs={{0,1},{1,0},{2,3},{3,2},{4,5},{5,4},{6,7},{7,6},{8,9},{9,8},{10,11... | collective-permute-start | bytes 688136 | tf_op jit(solution)/shard_map/ppermute | solution.py:24

commit v10 on v9

--- a/solution.py
+++ b/solution.py
@@ -51,11 +51,10 @@
     ]
 
 
-def pack_kernel(place, cache, w_uq, w_uk, w_uv, latent, rope, out):
-    zh, quarter = place[0], place[2]
+def pack_kernel(place, w_uq, w_uk, w_uv, latent, rope, out):
+    zh = place[0]
     lanes = out.shape[1]
-    at = cache.shape[0]
-    out[:at] = cache[:, pl.ds(pl.multiple_of(quarter * lanes, lanes), lanes)]
+    at = 0
     four = w_uq.shape[0] // 2
     for h in range(four):
         for w in (w_uq, w_uk, w_uv):
@@ -92,13 +91,13 @@
 
 
 def unpack_kernel(
-    place, received, latent, rope, sent, packed, piece, rope_out, *, sizes
+    place, received, latent, rope, sent, packed, rope_out, *, sizes
 ):
-    n_piece, n_all, copies = sizes
+    n_all, copies = sizes
     zh, yl = place[0], place[1]
     own_rows = latent.shape[0]
     lanes = packed.shape[1]
-    at = n_piece
+    at = 0
     for h in range(sent.shape[1]):
         other = received[at : at + n_all]
         for copy in range(copies):
@@ -125,7 +124,6 @@
     rope_out[theirs] = stay[1]
     packed[pl.ds(pl.multiple_of(to + zh * own_rows, 16), own_rows)] = go[0]
     packed[pl.ds(pl.multiple_of(to + (1 - zh) * own_rows, 16), own_rows)] = go[1]
-    piece[...] = received[:n_piece]
 
 
 def attend_kernel(
@@ -293,16 +291,18 @@
     weights = (w_uq, w_uk, w_uv)
     queries = (query_latent, query_rope)
     latent_chunks = query_latent.shape[1] // lanes
-    n_sent = kv_width + four * n_all + (latent_chunks + 2) * own_rows
+    n_sent = four * n_all + (latent_chunks + 2) * own_rows
     packed = pl.pallas_call(
         pack_kernel,
         out_shape=jax.ShapeDtypeStruct((n_sent, lanes), BF16),
-        in_specs=[smem] + [vmem] * 6,
+        in_specs=[smem] + [vmem] * 5,
         out_specs=vmem,
         compiler_params=pltpu.CompilerParams(vmem_limit_bytes=VMEM_LIMIT),
         cost_estimate=pl.CostEstimate(flops=10**6, bytes_accessed=10**6, transcendentals=0),
         name="pack",
-    )(place, cache, *weights, *queries)
+    )(place, *weights, *queries)
+    piece = lax.dynamic_slice_in_dim(cache, (core * 2 + zll) * quarter, quarter, 1)
+    far_piece = swap(piece, "zh")
     near = swap(cache, "yl")
     received = swap(packed, "zh")
 
@@ -322,16 +322,15 @@
     spread = exchange(spread, PLANE)
 
     n_pack = (2 * latent_chunks + 2) * own_rows
-    sent, packed, far_piece, rope_kept = pl.pallas_call(
-        lambda *refs: unpack_kernel(*refs, sizes=(kv_width, n_all, plane // 2)),
+    sent, packed, rope_kept = pl.pallas_call(
+        lambda *refs: unpack_kernel(*refs, sizes=(n_all, plane // 2)),
         out_shape=(
             jax.ShapeDtypeStruct((plane // 2, four, n_all, lanes), BF16),
             jax.ShapeDtypeStruct((n_pack, lanes), BF16),
-            jax.ShapeDtypeStruct((kv_width, quarter), BF16),
             jax.ShapeDtypeStruct((2 * own_rows, lanes), BF16),
         ),
         in_specs=[smem] + [vmem] * 3,
-        out_specs=(vmem,) * 4,
+        out_specs=(vmem,) * 3,
         compiler_params=pltpu.CompilerParams(vmem_limit_bytes=VMEM_LIMIT),
         cost_estimate=pl.CostEstimate(
             flops=UNPACK_FLOPS, bytes_accessed=3 * 10**6, transcendentals=0
@@ -340,20 +339,20 @@
     )(place, received, *queries)
     rows = 4 * own_rows
     row_lengths = lengths.reshape(-1, rows)
-    sent, packed, far_piece, near, row_lengths = lax.optimization_barrier(
-        (sent, packed, far_piece, near, row_lengths)
-    )
-    sent, spread = lax.optimization_barrier((sent, spread))
+
+    piece_y = swap(far_piece, "yl")
+    piece_z = swap(far_piece, "zll")
+    piece_yz = lax.ppermute(far_piece, ("yl", "zll"), [(0, 3), (1, 2), (2, 1), (3, 0)])
+    far = lax.all_gather(jnp.concatenate([far_piece, piece_y], axis=1), "c", axis=0)
+    far_z = lax.all_gather(jnp.concatenate([piece_z, piece_yz], axis=1), "c", axis=0)
+    sent, spread, far, far_z, near, row_lengths = lax.optimization_barrier(
+        (sent, spread, far, far_z, near, row_lengths)
+    )
 
     weights_far = exchange(sent.reshape(plane * heads, n_all, lanes), PLANE)
     weights_far = weights_far.reshape(plane, heads, n_all, lanes)
 
     packed_y = swap(packed, "yl")
-    piece_z = swap(far_piece, "zll")
-    piece_yz = lax.ppermute(far_piece, ("yl", "zll"), [(0, 3), (1, 2), (2, 1), (3, 0)])
-    piece_y = swap(far_piece, "yl")
-    far = lax.all_gather(jnp.concatenate([far_piece, piece_y], axis=1), "c", axis=0)
-    far_z = lax.all_gather(jnp.concatenate([piece_z, piece_yz], axis=1), "c", axis=0)
 
     keep, give = pl.pallas_call(
         lambda *refs: attend_kernel(

time: 154 us -> 174 us (1.13)
  waiting for transfers between devices: 25.6 us -> 35.6 us
  starting transfers between devices: 56 us -> 62.6 us
  blocking collectives: 50.3 us -> 54.8 us
    ppermute x7 -> x8, waiting for transfers between devices: 25.4 us -> 35.6 us  [swap(): return lax.ppermute(block, axis, [(0, 1), (1, 0)])]
    ppermute x7 -> x8, starting transfers between devices: 37.8 us -> 44.1 us  [swap(): return lax.ppermute(block, axis, [(0, 1), (1, 0)])]
    all_to_all x3, blocking collectives: 45.9 us -> 50.3 us  [exchange(): return lax.all_to_all(blocks, axes, 0, 0, tiled=True)]
    unnamed x30 -> x32, local copies, waits for them, and re-layouts: 7.42 us -> 6.6 us
  transfers between devices with their start and end apart: 10 -> 11, of which waited for: 5 -> 4; matrix products, arithmetic and copies ran while one was open for 1% -> 1% of each run, Pallas kernels for 2% -> 2%
where the time goes in v10:
time: 174 us; the launch traced here: 172 us
  starting transfers between devices  62.6 us (36%)
  blocking collectives  54.8 us (31%)
  waiting for transfers between devices  35.6 us (20%)
  local copies, waits for them, and re-layouts  8.88 us (5%)
  Pallas kernels  8.65 us (5%)
    all_to_all x3, blocking collectives, exchange(): return lax.all_to_all(blocks, axes, 0, 0, tiled=True)  50.3 us
    ppermute x8, starting transfers between devices, swap(): return lax.ppermute(block, axis, [(0, 1), (1, 0)])  44.1 us
    ppermute x8, waiting for transfers between devices, swap(): return lax.ppermute(block, axis, [(0, 1), (1, 0)])  35.6 us
    all_to_all x2, starting transfers between devices, exchange(): return lax.all_to_all(blocks, axes, 0, 0, tiled=True)  14.6 us
    unnamed x32, local copies, waits for them, and re-layouts  6.6 us
    pallas_call x1, Pallas kernels, local(): pl.pallas_call(lambda *refs: attend_kernel(*refs, sizes=(rows, heads, n_u...  3.87 us
    ppermute x1, starting transfers between devices, local(): lax.ppermute(far_piece, ('yl', 'zll'), [(0, 3), (1, 2), (2, 1), (3, 0)])  3.83 us
  transfers between devices with their start and end apart: 11, of which 4 were waited for; matrix products, arithmetic and copies ran while one was open for 1% of the time, Pallas kernels for 2%

profile of v10, /device:TPU:6, one launch (start us, length us, event | category | flops | bytes accessed | tf_op | source)
XLA Modules:
  0.0 171.6 jit_solution(872385093722337126)
XLA Ops:
  0.0 1.0 dynamic-slice_bitcast_fusion
  1.0 15.7 %collective-permute-start.2 = (bf16[576,128]{1,0:T(8,128)(2,1)S(1)}, bf16[576,128]{1,0:T(8,128)(2,1)S(1)}, u32[]{:S(2)}, u32[]{:S(2)}) collective-permute-start(bf16[576,128]{1,0:T(8,128)(2,1)S(1)} %dynamic-slice_bitcast_fusion), channel_id=1, source_target_pairs={{0,16},{16,0},{1,17},{17,1},{2,18},{18,2},{3,19},{19,3},{4,20},{20... | collective-permute-start | bytes 442376 | tf_op jit(solution)/shard_map/ppermute | solution.py:24
  16.7 0.1 stack.23.place.refs_0_
  16.8 0.9 copy-done.3
  17.7 0.8 copy-done.5
  18.5 0.8 copy-done.7
  19.2 0.8 copy-done.11
  20.0 0.8 copy-done.13
  20.8 0.6 pack.1
  21.4 1.9 %collective-permute-start = (bf16[544,128]{1,0:T(8,128)(2,1)S(1)}, bf16[544,128]{1,0:T(8,128)(2,1)S(1)}, u32[]{:S(2)}, u32[]{:S(2)}) collective-permute-start(bf16[544,128]{1,0:T(8,128)(2,1)S(1)} %pack.1), channel_id=1, source_target_pairs={{0,16},{16,0},{1,17},{17,1},{2,18},{18,2},{3,19},{19,3},{4,20},{20... | collective-permute-start | bytes 417800 | tf_op jit(solution)/shard_map/ppermute | solution.py:24
  23.3 1.1 reshape.50.w_out
  24.5 2.0 %spread.1 = bf16[16,384,128]{2,1,0:T(8,128)(2,1)} custom-call(s32[5]{0:T(128)S(1)} %stack.23.place.refs_0_, bf16[8,48,128]{2,1,0:T(8,128)(2,1)S(1)} %copy-done.4, bf16[8,16,128]{2,1,0:T(8,128)(2,1)S(1)} %copy-done.6, bf16[8,16,128]{2,1,0:T(8,128)(2,1)S(1)} %copy-done.8, bf16[32,7168]{1,0:T(8,128)(2,1)S(1)} %reshape.50.w_out), custom_call_target="tpu_custom_call" | custom-call | flops 1000000 | bytes 1000000 | tf_op jit(solution)/shard_map/spread/pallas_call | solution.py:313
  26.5 7.6 %all-to-all-start = ((bf16[16,384,128]{2,1,0:T(8,128)(2,1)}), bf16[16,384,128]{2,1,0:T(8,128)(2,1)S(1)}, u32[]{:S(2)}, u32[]{:S(2)}) async-start(bf16[16,384,128]{2,1,0:T(8,128)(2,1)} %spread.1), calls=%async_computation | async-start | bytes 3145728 | tf_op jit(solution)/shard_map/all_to_all | solution.py:36
  34.0 3.4 %collective-permute-start.6 = (bf16[576,512]{1,0:T(8,128)(2,1)S(1)}, bf16[576,512]{1,0:T(8,128)(2,1)}, u32[]{:S(2)}, u32[]{:S(2)}) collective-permute-start(bf16[576,512]{1,0:T(8,128)(2,1)S(1)} %bitcast.17), channel_id=1, source_target_pairs={{0,32},{32,0},{1,33},{33,1},{2,34},{34,2},{3,35},{35,3},{4,36},{36... | collective-permute-start | bytes 1769480 | tf_op jit(solution)/shard_map/ppermute | solution.py:24
  37.4 0.0 copy-done.15
  37.4 0.1 reshape.51.refs_6_
  37.5 0.0 collective-permute-done.2
  37.5 2.5 %collective-permute-start.3 = (bf16[576,128]{1,0:T(8,128)(2,1)S(1)}, bf16[576,128]{1,0:T(8,128)(2,1)S(1)}, u32[]{:S(2)}, u32[]{:S(2)}) collective-permute-start(bf16[576,128]{1,0:T(8,128)(2,1)S(1)} %collective-permute-done.2), channel_id=1, source_target_pairs={{0,32},{32,0},{1,33},{33,1},{2,34},{34,2},{3,35},{35,3},{4,36},{36... | collective-permute-start | bytes 442376 | tf_op jit(solution)/shard_map/ppermute | solution.py:24
  40.0 3.8 %collective-permute-start.5 = (bf16[576,128]{1,0:T(8,128)(2,1)S(1)}, bf16[576,128]{1,0:T(8,128)(2,1)S(1)}, u32[]{:S(2)}, u32[]{:S(2)}) collective-permute-start(bf16[576,128]{1,0:T(8,128)(2,1)S(1)} %collective-permute-done.2), channel_id=1, source_target_pairs={{0,34},{2,32},{32,2},{34,0},{1,35},{3,33},{33,3},{35,1},{4,38},{6,... | collective-permute-start | bytes 442376 | tf_op jit(solution)/shard_map/ppermute | solution.py:345
  43.8 2.9 %collective-permute-start.4 = (bf16[576,128]{1,0:T(8,128)(2,1)S(1)}, bf16[576,128]{1,0:T(8,128)(2,1)S(1)}, u32[]{:S(2)}, u32[]{:S(2)}) collective-permute-start(bf16[576,128]{1,0:T(8,128)(2,1)S(1)} %collective-permute-done.2), channel_id=1, source_target_pairs={{0,2},{2,0},{1,3},{3,1},{4,6},{6,4},{5,7},{7,5},{8,10},{10,8},{9,1... | collective-permute-start | bytes 442376 | tf_op jit(solution)/shard_map/ppermute | solution.py:24
  46.7 0.0 collective-permute-done.refs_1_
  46.8 0.0 copy-done.12
  46.8 0.7 unpack.1
  47.5 23.9 %collective-permute-done.3 = bf16[576,128]{1,0:T(8,128)(2,1)S(1)} collective-permute-done((bf16[576,128]{1,0:T(8,128)(2,1)S(1)}, bf16[576,128]{1,0:T(8,128)(2,1)S(1)}, u32[]{:S(2)}, u32[]{:S(2)}) %collective-permute-start.3) | collective-permute-done | bytes 147488 | tf_op jit(solution)/shard_map/ppermute | solution.py:24
  71.5 0.0 collective-permute-done.5
  71.5 0.0 collective-permute-done.4
  71.5 2.2 %all-gather = bf16[1152,256]{1,0:T(8,128)(2,1)S(1)} all-gather(bf16[576,256]{1,0:T(8,128)(2,1)S(1)} %pad_maximum_fusion), channel_id=2, replica_groups=mesh['xh'=2,'xl'=2,'yh'=2,'yl'=2,'zh'=2,'zlh'=4,'zll'=2,'c'=2] {'c'}, dimensions={0}, use_global_device_ids=true | all-gather | bytes 884736 | tf_op jit(solution)/shard_map/all_gather | solution.py:346
  73.7 2.2 %all-gather.1 = bf16[1152,256]{1,0:T(8,128)(2,1)S(1)} all-gather(bf16[576,256]{1,0:T(8,128)(2,1)S(1)} %pad_maximum_fusion.1), channel_id=3, replica_groups=mesh['xh'=2,'xl'=2,'yh'=2,'yl'=2,'zh'=2,'zlh'=4,'zll'=2,'c'=2] {'c'}, dimensions={0}, use_global_device_ids=true | all-gather | bytes 884736 | tf_op jit(solution)/shard_map/all_gather | solution.py:347
  76.0 0.0 collective-permute-done.6.refs_8_
  76.0 0.0 all-to-all-done.refs_3_.received
  76.0 7.1 %all-to-all-start.1 = ((bf16[32,80,128]{2,1,0:T(8,128)(2,1)}), bf16[32,80,128]{2,1,0:T(8,128)(2,1)S(1)}, u32[]{:S(2)}, u32[]{:S(2)}) async-start(bf16[32,80,128]{2,1,0:T(8,128)(2,1)} %bitcast.19), calls=%async_computation.1 | async-start | bytes 1310720 | tf_op jit(solution)/shard_map/all_to_all | solution.py:36
  83.0 3.4 %collective-permute-start.1 = (bf16[416,128]{1,0:T(8,128)(2,1)S(1)}, bf16[416,128]{1,0:T(8,128)(2,1)S(1)}, u32[]{:S(2)}, u32[]{:S(2)}) collective-permute-start(bf16[416,128]{1,0:T(8,128)(2,1)S(1)} %get-tuple-element.18.refs_1_), channel_id=1, source_target_pairs={{0,32},{32,0},{1,33},{33,1},{2,34},{34,2},{3,35},{35,3},{4,36},{36... | collective-permute-start | bytes 319496 | tf_op jit(solution)/shard_map/ppermute | solution.py:24
  86.4 8.0 %collective-permute-done.1.refs_2_ = bf16[416,128]{1,0:T(8,128)(2,1)S(1)} collective-permute-done((bf16[416,128]{1,0:T(8,128)(2,1)S(1)}, bf16[416,128]{1,0:T(8,128)(2,1)S(1)}, u32[]{:S(2)}, u32[]{:S(2)}) %collective-permute-start.1) | collective-permute-done | bytes 106528 | tf_op jit(solution)/shard_map/ppermute | solution.py:24
  94.4 0.6 copy-done.9
  95.1 0.0 all-to-all-done.1
  95.1 1.1 copy-done.1
  96.2 0.9 copy-done.10
  97.1 3.9 %attend.1 = (bf16[64,128]{1,0:T(8,128)(2,1)S(1)}, bf16[64,128]{1,0:T(8,128)(2,1)}) custom-call(s32[5]{0:T(128)S(1)} %stack.23.place.refs_0_, bf16[416,128]{1,0:T(8,128)(2,1)S(1)} %get-tuple-element.18.refs_1_, bf16[416,128]{1,0:T(8,128)(2,1)S(1)} %copy-done.10, bf16[16,384,128]{2,1,0:T(8,128)(2,1)S(1)} %all-to-all-done.refs_3_.received, ...), custom_call_target="tpu_custom_call" | custom-call | flops 1000000000 | bytes 5000000 | tf_op jit(solution)/shard_map/attend/pallas_call | solution.py:357
  100.9 12.5 %collective-permute-start.7 = (bf16[64,128]{1,0:T(8,128)(2,1)}, bf16[64,128]{1,0:T(8,128)(2,1)S(1)}, u32[]{:S(2)}, u32[]{:S(2)}) collective-permute-start(bf16[64,128]{1,0:T(8,128)(2,1)} %get-tuple-element.27), channel_id=1, source_target_pairs={{0,16},{16,0},{1,17},{17,1},{2,18},{18,2},{3,19},{19,3},{4,20},{20... | collective-permute-start | bytes 49160 | tf_op jit(solution)/shard_map/ppermute | solution.py:24
  113.4 2.1 %collective-permute-done.7 = bf16[64,128]{1,0:T(8,128)(2,1)S(1)} collective-permute-done((bf16[64,128]{1,0:T(8,128)(2,1)}, bf16[64,128]{1,0:T(8,128)(2,1)S(1)}, u32[]{:S(2)}, u32[]{:S(2)}) %collective-permute-start.7) | collective-permute-done | bytes 16416 | tf_op jit(solution)/shard_map/ppermute | solution.py:24
  115.5 11.0 %all_to_all.26.values = bf16[8,64,256]{2,1,0:T(8,128)(2,1)S(1)} all-to-all(bf16[8,64,256]{2,1,0:T(8,128)(2,1)S(1)} %broadcast_in_dim.2), channel_id=1, replica_groups=mesh['xh'=2,'xl'=2,'yh'=2,'yl'=2,'zh'=2,'zlh'=4,'zll'=2,'c'=2] {'xl','yh..., dimensions={0} | all-to-all | bytes 524288 | tf_op jit(solution)/shard_map/all_to_all | solution.py:36
  126.5 1.5 project.1
  128.0 1.9 %collective-permute-start.8 = (bf16[8,2,16,448]{3,2,1,0:T(8,128)(2,1)S(1)}, bf16[8,2,16,448]{3,2,1,0:T(8,128)(2,1)S(1)}, u32[]{:S(2)}, u32[]{:S(2)}) collective-permute-start(bf16[8,2,16,448]{3,2,1,0:T(8,128)(2,1)S(1)} %get-tuple-element.30), channel_id=1, source_target_pairs={{0,1},{1,0},{2,3},{3,2},{4,5},{5,4},{6,7},{7,6},{8,9},{9,8},{10,11... | collective-permute-start | bytes 688136 | tf_op jit(solution)/shard_map/ppermute | solution.py:24
  130.0 1.5 collective-permute-done.8
  131.5 0.1 add_convert_fusion
  131.6 10.2 %all_to_all.27 = bf16[8,2,16,448]{3,2,1,0:T(8,128)(2,1)S(1)} all-to-all(bf16[8,2,16,448]{3,2,1,0:T(8,128)(2,1)S(1)} %add_convert_fusion), channel_id=1, replica_groups=mesh['xh'=2,'xl'=2,'yh'=2,'yl'=2,'zh'=2,'zlh'=4,'zll'=2,'c'=2] {'xl','yh..., dimensions={0} | all-to-all | bytes 458752 | tf_op jit(solution)/shard_map/all_to_all | solution.py:36
  141.8 29.1 %all_to_all.28 = bf16[16,16,448]{2,1,0:T(8,128)(2,1)S(1)} all-to-all(bf16[16,16,448]{2,1,0:T(8,128)(2,1)S(1)} %bitcast.21), channel_id=1, replica_groups=mesh['xh'=2,'xl'=2,'yh'=2,'yl'=2,'zh'=2,'zlh'=4,'zll'=2,'c'=2] {'zh','zl..., dimensions={0} | all-to-all | bytes 458752 | tf_op jit(solution)/shard_map/all_to_all | solution.py:36
  170.9 0.7 reduce_sum.12
  (27 shorter events, 0.2 us)
Async XLA Ops:
  0.0 24.5 %copy-start.4 = (bf16[8,48,128]{2,1,0:T(8,128)(2,1)S(1)}, bf16[8,48,128]{2,1,0:T(8,128)(2,1)}, u32[]{:S(2)}) copy-start(bf16[8,48,128]{2,1,0:T(8,128)(2,1)} %w_uq.3) | copy-start | bytes 294916
  0.0 24.5 %copy-start.6 = (bf16[8,16,128]{2,1,0:T(8,128)(2,1)S(1)}, bf16[8,16,128]{2,1,0:T(8,128)(2,1)}, u32[]{:S(2)}) copy-start(bf16[8,16,128]{2,1,0:T(8,128)(2,1)} %w_uk.3) | copy-start | bytes 98308
  0.0 24.5 %copy-start.8 = (bf16[8,16,128]{2,1,0:T(8,128)(2,1)S(1)}, bf16[8,16,128]{2,1,0:T(8,128)(2,1)}, u32[]{:S(2)}) copy-start(bf16[8,16,128]{2,1,0:T(8,128)(2,1)} %w_uv.3) | copy-start | bytes 98308
  1.0 36.5 %collective-permute-start.2 = (bf16[576,128]{1,0:T(8,128)(2,1)S(1)}, bf16[576,128]{1,0:T(8,128)(2,1)S(1)}, u32[]{:S(2)}, u32[]{:S(2)}) collective-permute-start(bf16[576,128]{1,0:T(8,128)(2,1)S(1)} %dynamic-slice_bitcast_fusion), channel_id=1, source_target_pairs={{0,16},{16,0},{1,17},{17,1},{2,18},{18,2},{3,19},{19,3},{4,20},{20... | collective-permute-start | bytes 442376 | tf_op jit(solution)/shard_map/ppermute | solution.py:24
  16.8 0.9 copy-start.3
  17.7 0.8 copy-start.5
  18.5 0.8 copy-start.7
  19.2 0.8 copy-start.11
  20.0 0.8 copy-start.13
  21.4 25.3 %collective-permute-start = (bf16[544,128]{1,0:T(8,128)(2,1)S(1)}, bf16[544,128]{1,0:T(8,128)(2,1)S(1)}, u32[]{:S(2)}, u32[]{:S(2)}) collective-permute-start(bf16[544,128]{1,0:T(8,128)(2,1)S(1)} %pack.1), channel_id=1, source_target_pairs={{0,16},{16,0},{1,17},{17,1},{2,18},{18,2},{3,19},{19,3},{4,20},{20... | collective-permute-start | bytes 417800 | tf_op jit(solution)/shard_map/ppermute | solution.py:24
  26.5 7.6 %copy-start = (bf16[512,576]{0,1:T(8,128)(2,1)S(1)}, bf16[512,576]{0,1:T(8,128)(2,1)}, u32[]{:S(2)}) copy-start(bf16[512,576]{0,1:T(8,128)(2,1)} %param.11) | copy-start | bytes 1769476
  26.5 11.0 %copy-start.15 = (s32[512]{0:T(512)S(1)}, s32[512]{0:T(512)}, u32[]{:S(2)}) copy-start(s32[512]{0:T(512)} %param.10) | copy-start | bytes 6148
  26.5 20.3 %copy-start.12 = (bf16[16,1536]{1,0:T(8,128)(2,1)S(1)}, bf16[16,1536]{1,0:T(8,128)(2,1)}, u32[]{:S(2)}) copy-start(bf16[16,1536]{1,0:T(8,128)(2,1)} %refs_2_.1) | copy-start | bytes 147460
  26.5 20.3 %copy-start.14 = (bf16[16,8,64]{2,1,0:T(8,128)(2,1)S(1)}, bf16[16,8,64]{2,1,0:T(8,128)(2,1)}, u32[]{:S(2)}) copy-start(bf16[16,8,64]{2,1,0:T(8,128)(2,1)} %refs_3_.1) | copy-start | bytes 49156
  26.5 49.5 %all-to-all-start = ((bf16[16,384,128]{2,1,0:T(8,128)(2,1)}), bf16[16,384,128]{2,1,0:T(8,128)(2,1)S(1)}, u32[]{:S(2)}, u32[]{:S(2)}) async-start(bf16[16,384,128]{2,1,0:T(8,128)(2,1)} %spread.1), calls=%async_computation | async-start | bytes 3145728 | tf_op jit(solution)/shard_map/all_to_all | solution.py:36
  34.0 41.9 %collective-permute-start.6 = (bf16[576,512]{1,0:T(8,128)(2,1)S(1)}, bf16[576,512]{1,0:T(8,128)(2,1)}, u32[]{:S(2)}, u32[]{:S(2)}) collective-permute-start(bf16[576,512]{1,0:T(8,128)(2,1)S(1)} %bitcast.17), channel_id=1, source_target_pairs={{0,32},{32,0},{1,33},{33,1},{2,34},{34,2},{3,35},{35,3},{4,36},{36... | collective-permute-start | bytes 1769480 | tf_op jit(solution)/shard_map/ppermute | solution.py:24
  37.5 33.9 %collective-permute-start.3 = (bf16[576,128]{1,0:T(8,128)(2,1)S(1)}, bf16[576,128]{1,0:T(8,128)(2,1)S(1)}, u32[]{:S(2)}, u32[]{:S(2)}) collective-permute-start(bf16[576,128]{1,0:T(8,128)(2,1)S(1)} %collective-permute-done.2), channel_id=1, source_target_pairs={{0,32},{32,0},{1,33},{33,1},{2,34},{34,2},{3,35},{35,3},{4,36},{36... | collective-permute-start | bytes 442376 | tf_op jit(solution)/shard_map/ppermute | solution.py:24
  40.0 31.5 %collective-permute-start.5 = (bf16[576,128]{1,0:T(8,128)(2,1)S(1)}, bf16[576,128]{1,0:T(8,128)(2,1)S(1)}, u32[]{:S(2)}, u32[]{:S(2)}) collective-permute-start(bf16[576,128]{1,0:T(8,128)(2,1)S(1)} %collective-permute-done.2), channel_id=1, source_target_pairs={{0,34},{2,32},{32,2},{34,0},{1,35},{3,33},{33,3},{35,1},{4,38},{6,... | collective-permute-start | bytes 442376 | tf_op jit(solution)/shard_map/ppermute | solution.py:345
  43.8 27.6 %collective-permute-start.4 = (bf16[576,128]{1,0:T(8,128)(2,1)S(1)}, bf16[576,128]{1,0:T(8,128)(2,1)S(1)}, u32[]{:S(2)}, u32[]{:S(2)}) collective-permute-start(bf16[576,128]{1,0:T(8,128)(2,1)S(1)} %collective-permute-done.2), channel_id=1, source_target_pairs={{0,2},{2,0},{1,3},{3,1},{4,6},{6,4},{5,7},{7,5},{8,10},{10,8},{9,1... | collective-permute-start | bytes 442376 | tf_op jit(solution)/shard_map/ppermute | solution.py:24
  47.5 28.5 %copy-start.2 = (bf16[8,4,80,128]{3,2,1,0:T(8,128)(2,1)}, bf16[8,4,80,128]{3,2,1,0:T(8,128)(2,1)S(1)}, u32[]{:S(2)}) copy-start(bf16[8,4,80,128]{3,2,1,0:T(8,128)(2,1)S(1)} %get-tuple-element.21) | copy-start | bytes 1966084
  76.0 19.1 %all-to-all-start.1 = ((bf16[32,80,128]{2,1,0:T(8,128)(2,1)}), bf16[32,80,128]{2,1,0:T(8,128)(2,1)S(1)}, u32[]{:S(2)}, u32[]{:S(2)}) async-start(bf16[32,80,128]{2,1,0:T(8,128)(2,1)} %bitcast.19), calls=%async_computation.1 | async-start | bytes 1310720 | tf_op jit(solution)/shard_map/all_to_all | solution.py:36
  83.0 11.4 %collective-permute-start.1 = (bf16[416,128]{1,0:T(8,128)(2,1)S(1)}, bf16[416,128]{1,0:T(8,128)(2,1)S(1)}, u32[]{:S(2)}, u32[]{:S(2)}) collective-permute-start(bf16[416,128]{1,0:T(8,128)(2,1)S(1)} %get-tuple-element.18.refs_1_), channel_id=1, source_target_pairs={{0,32},{32,0},{1,33},{33,1},{2,34},{34,2},{3,35},{35,3},{4,36},{36... | collective-permute-start | bytes 319496 | tf_op jit(solution)/shard_map/ppermute | solution.py:24
  94.4 0.6 copy-start.9
  95.1 1.1 copy-start.1
  96.2 0.9 copy-start.10
  100.9 14.5 %collective-permute-start.7 = (bf16[64,128]{1,0:T(8,128)(2,1)}, bf16[64,128]{1,0:T(8,128)(2,1)S(1)}, u32[]{:S(2)}, u32[]{:S(2)}) collective-permute-start(bf16[64,128]{1,0:T(8,128)(2,1)} %get-tuple-element.27), channel_id=1, source_target_pairs={{0,16},{16,0},{1,17},{17,1},{2,18},{18,2},{3,19},{19,3},{4,20},{20... | collective-permute-start | bytes 49160 | tf_op jit(solution)/shard_map/ppermute | solution.py:24
  128.0 3.4 %collective-permute-start.8 = (bf16[8,2,16,448]{3,2,1,0:T(8,128)(2,1)S(1)}, bf16[8,2,16,448]{3,2,1,0:T(8,128)(2,1)S(1)}, u32[]{:S(2)}, u32[]{:S(2)}) collective-permute-start(bf16[8,2,16,448]{3,2,1,0:T(8,128)(2,1)S(1)} %get-tuple-element.30), channel_id=1, source_target_pairs={{0,1},{1,0},{2,3},{3,2},{4,5},{5,4},{6,7},{7,6},{8,9},{9,8},{10,11... | collective-permute-start | bytes 688136 | tf_op jit(solution)/shard_map/ppermute | solution.py:24

commit v11 on v10

--- a/solution.py
+++ b/solution.py
@@ -17,7 +17,7 @@
 BF16 = jnp.bfloat16
 F32 = jnp.float32
 VMEM_LIMIT = 12 * 1024 * 1024
-UNPACK_FLOPS = 2 * 10**10
+UNPACK_FLOPS = 145 * 10**8
 
 
 def swap(block, axis):
@@ -149,7 +149,7 @@
     temper,
 ):
     rows, heads, n_uq, n_uk, n_uv, width = sizes
-    caches = [kv0, kv1] + [kv.at[c] for kv in (kv2, kv3) for c in range(2)]
+    caches = [kv0] + [kv.at[c] for kv in (kv1, kv2, kv3) for c in range(2)]
     spans, tokens = [], 0
     for cache in caches:
         spans.append((tokens, tokens + cache.shape[1]))
@@ -303,7 +303,8 @@
     )(place, *weights, *queries)
     piece = lax.dynamic_slice_in_dim(cache, (core * 2 + zll) * quarter, quarter, 1)
     far_piece = swap(piece, "zh")
-    near = swap(cache, "yl")
+    near = swap(lax.dynamic_slice_in_dim(cache, core * (tokens // 2), tokens // 2, 1), "yl")
+    near, w_out = lax.optimization_barrier((near, w_out))
     received = swap(packed, "zh")
 
     vpart, width = w_out.shape[1:]
@@ -343,14 +344,16 @@
     piece_y = swap(far_piece, "yl")
     piece_z = swap(far_piece, "zll")
     piece_yz = lax.ppermute(far_piece, ("yl", "zll"), [(0, 3), (1, 2), (2, 1), (3, 0)])
+    sent, spread, piece_y, piece_z, piece_yz, row_lengths = lax.optimization_barrier(
+        (sent, spread, piece_y, piece_z, piece_yz, row_lengths)
+    )
+
+    weights_far = exchange(sent.reshape(plane * heads, n_all, lanes), PLANE)
+    weights_far = weights_far.reshape(plane, heads, n_all, lanes)
+
+    near = lax.all_gather(near, "c", axis=0)
     far = lax.all_gather(jnp.concatenate([far_piece, piece_y], axis=1), "c", axis=0)
     far_z = lax.all_gather(jnp.concatenate([piece_z, piece_yz], axis=1), "c", axis=0)
-    sent, spread, far, far_z, near, row_lengths = lax.optimization_barrier(
-        (sent, spread, far, far_z, near, row_lengths)
-    )
-
-    weights_far = exchange(sent.reshape(plane * heads, n_all, lanes), PLANE)
-    weights_far = weights_far.reshape(plane, heads, n_all, lanes)
 
     packed_y = swap(packed, "yl")
 

time: 174 us -> 158 us (0.908)
  the two profiles are of different devices: /device:TPU:6 before, /device:TPU:32 now
where the time goes in v11:
time: 158 us; the launch traced here: 157 us
  starting transfers between devices  59.5 us (38%)
  blocking collectives  56.9 us (36%)
  waiting for transfers between devices  20.7 us (13%)
  Pallas kernels  9.29 us (6%)
  local copies, waits for them, and re-layouts  8.4 us (5%)
  other arithmetic  1.8 us (1%)
    all_to_all x3, blocking collectives, exchange(): return lax.all_to_all(blocks, axes, 0, 0, tiled=True)  50 us
    ppermute x8, starting transfers between devices, swap(): return lax.ppermute(block, axis, [(0, 1), (1, 0)])  41.9 us
    ppermute x8, waiting for transfers between devices, swap(): return lax.ppermute(block, axis, [(0, 1), (1, 0)])  16.4 us
    all_to_all x2, starting transfers between devices, exchange(): return lax.all_to_all(blocks, axes, 0, 0, tiled=True)  13.3 us
    unnamed x32, local copies, waits for them, and re-layouts  6.12 us
    all_to_all x2, waiting for transfers between devices, exchange(): return lax.all_to_all(blocks, axes, 0, 0, tiled=True)  4.31 us
    ppermute x1, starting transfers between devices, local(): lax.ppermute(far_piece, ('yl', 'zll'), [(0, 3), (1, 2), (2, 1), (3, 0)])  4.3 us
    pallas_call x1, Pallas kernels, local(): pl.pallas_call(lambda *refs: attend_kernel(*refs, sizes=(rows, heads, n_u...  3.69 us
  transfers between devices with their start and end apart: 11, of which 5 were waited for; matrix products, arithmetic and copies ran while one was open for 1% of the time, Pallas kernels for 3%

profile of v11, /device:TPU:32, one launch (start us, length us, event | category | flops | bytes accessed | tf_op | source)
XLA Modules:
  0.0 156.9 jit_solution(4177071034891191807)
XLA Ops:
  0.0 1.0 dynamic-slice_bitcast_fusion
  1.1 3.5 %collective-permute-start.2 = (bf16[576,256]{1,0:T(8,128)(2,1)S(1)}, bf16[576,256]{1,0:T(8,128)(2,1)S(1)}, u32[]{:S(2)}, u32[]{:S(2)}) collective-permute-start(bf16[576,256]{1,0:T(8,128)(2,1)S(1)} %dynamic-slice_bitcast_fusion), channel_id=1, source_target_pairs={{0,32},{32,0},{1,33},{33,1},{2,34},{34,2},{3,35},{35,3},{4,36},{36... | collective-permute-start | bytes 884744 | tf_op jit(solution)/shard_map/ppermute | solution.py:24
  4.6 0.9 dynamic-slice_bitcast_fusion.1
  5.5 14.8 %collective-permute-start.3 = (bf16[576,128]{1,0:T(8,128)(2,1)S(1)}, bf16[576,128]{1,0:T(8,128)(2,1)S(1)}, u32[]{:S(2)}, u32[]{:S(2)}) collective-permute-start(bf16[576,128]{1,0:T(8,128)(2,1)S(1)} %dynamic-slice_bitcast_fusion.1), channel_id=1, source_target_pairs={{0,16},{16,0},{1,17},{17,1},{2,18},{18,2},{3,19},{19,3},{4,20},{20... | collective-permute-start | bytes 442376 | tf_op jit(solution)/shard_map/ppermute | solution.py:24
  20.3 0.1 stack.23.place.refs_0_
  20.4 0.9 copy-done.2
  21.3 0.8 copy-done.4
  22.1 0.8 copy-done.6
  22.8 0.8 copy-done.8
  23.6 0.8 copy-done.10
  24.4 0.6 pack.1
  25.0 1.9 %collective-permute-start = (bf16[544,128]{1,0:T(8,128)(2,1)S(1)}, bf16[544,128]{1,0:T(8,128)(2,1)S(1)}, u32[]{:S(2)}, u32[]{:S(2)}) collective-permute-start(bf16[544,128]{1,0:T(8,128)(2,1)S(1)} %pack.1), channel_id=1, source_target_pairs={{0,16},{16,0},{1,17},{17,1},{2,18},{18,2},{3,19},{19,3},{4,20},{20... | collective-permute-start | bytes 417800 | tf_op jit(solution)/shard_map/ppermute | solution.py:24
  27.0 0.0 collective-permute-done.2
  27.0 0.1 reshape.50.w_out
  27.1 2.0 %spread.1 = bf16[16,384,128]{2,1,0:T(8,128)(2,1)} custom-call(s32[5]{0:T(128)S(1)} %stack.23.place.refs_0_, bf16[8,48,128]{2,1,0:T(8,128)(2,1)S(1)} %copy-done.3, bf16[8,16,128]{2,1,0:T(8,128)(2,1)S(1)} %copy-done.5, bf16[8,16,128]{2,1,0:T(8,128)(2,1)S(1)} %copy-done.7, bf16[32,7168]{1,0:T(8,128)(2,1)S(1)} %reshape.50.w_out), custom_call_target="tpu_custom_call" | custom-call | flops 1000000 | bytes 1000000 | tf_op jit(solution)/shard_map/spread/pallas_call | solution.py:314
  29.1 6.9 %all-to-all-start = ((bf16[16,384,128]{2,1,0:T(8,128)(2,1)}), bf16[16,384,128]{2,1,0:T(8,128)(2,1)S(1)}, u32[]{:S(2)}, u32[]{:S(2)}) async-start(bf16[16,384,128]{2,1,0:T(8,128)(2,1)} %spread.1), calls=%async_computation | async-start | bytes 3145728 | tf_op jit(solution)/shard_map/all_to_all | solution.py:36
  36.0 0.1 reshape.51.refs_6_
  36.1 1.8 %collective-permute-done.3 = bf16[576,128]{1,0:T(8,128)(2,1)S(1)} collective-permute-done((bf16[576,128]{1,0:T(8,128)(2,1)S(1)}, bf16[576,128]{1,0:T(8,128)(2,1)S(1)}, u32[]{:S(2)}, u32[]{:S(2)}) %collective-permute-start.3) | collective-permute-done | bytes 147488 | tf_op jit(solution)/shard_map/ppermute | solution.py:24
  37.9 2.3 %collective-permute-start.4 = (bf16[576,128]{1,0:T(8,128)(2,1)S(1)}, bf16[576,128]{1,0:T(8,128)(2,1)S(1)}, u32[]{:S(2)}, u32[]{:S(2)}) collective-permute-start(bf16[576,128]{1,0:T(8,128)(2,1)S(1)} %collective-permute-done.3), channel_id=1, source_target_pairs={{0,32},{32,0},{1,33},{33,1},{2,34},{34,2},{3,35},{35,3},{4,36},{36... | collective-permute-start | bytes 442376 | tf_op jit(solution)/shard_map/ppermute | solution.py:24
  40.3 2.6 %collective-permute-start.5 = (bf16[576,128]{1,0:T(8,128)(2,1)S(1)}, bf16[576,128]{1,0:T(8,128)(2,1)}, u32[]{:S(2)}, u32[]{:S(2)}) collective-permute-start(bf16[576,128]{1,0:T(8,128)(2,1)S(1)} %collective-permute-done.3), channel_id=1, source_target_pairs={{0,2},{2,0},{1,3},{3,1},{4,6},{6,4},{5,7},{7,5},{8,10},{10,8},{9,1... | collective-permute-start | bytes 442376 | tf_op jit(solution)/shard_map/ppermute | solution.py:24
  42.8 4.3 %collective-permute-start.6 = (bf16[576,128]{1,0:T(8,128)(2,1)S(1)}, bf16[576,128]{1,0:T(8,128)(2,1)}, u32[]{:S(2)}, u32[]{:S(2)}) collective-permute-start(bf16[576,128]{1,0:T(8,128)(2,1)S(1)} %collective-permute-done.3), channel_id=1, source_target_pairs={{0,34},{2,32},{32,2},{34,0},{1,35},{3,33},{33,3},{35,1},{4,38},{6,... | collective-permute-start | bytes 442376 | tf_op jit(solution)/shard_map/ppermute | solution.py:346
  47.1 0.0 collective-permute-done.refs_1_
  47.2 1.5 unpack.1
  48.7 2.5 %collective-permute-start.1 = (bf16[416,128]{1,0:T(8,128)(2,1)S(1)}, bf16[416,128]{1,0:T(8,128)(2,1)}, u32[]{:S(2)}, u32[]{:S(2)}) collective-permute-start(bf16[416,128]{1,0:T(8,128)(2,1)S(1)} %get-tuple-element.20.refs_1_), channel_id=1, source_target_pairs={{0,32},{32,0},{1,33},{33,1},{2,34},{34,2},{3,35},{35,3},{4,36},{36... | collective-permute-start | bytes 319496 | tf_op jit(solution)/shard_map/ppermute | solution.py:24
  51.2 10.9 %collective-permute-done.4 = bf16[576,128]{1,0:T(8,128)(2,1)S(1)} collective-permute-done((bf16[576,128]{1,0:T(8,128)(2,1)S(1)}, bf16[576,128]{1,0:T(8,128)(2,1)S(1)}, u32[]{:S(2)}, u32[]{:S(2)}) %collective-permute-start.4) | collective-permute-done | bytes 147488 | tf_op jit(solution)/shard_map/ppermute | solution.py:24
  62.0 0.0 collective-permute-done.5
  62.0 0.0 collective-permute-done.6
  62.0 0.0 all-to-all-done.refs_3_.received
  62.0 6.5 %all-to-all-start.1 = ((bf16[32,80,128]{2,1,0:T(8,128)(2,1)}), bf16[32,80,128]{2,1,0:T(8,128)(2,1)S(1)}, u32[]{:S(2)}, u32[]{:S(2)}) async-start(bf16[32,80,128]{2,1,0:T(8,128)(2,1)} %bitcast.7), calls=%async_computation.1 | async-start | bytes 1310720 | tf_op jit(solution)/shard_map/all_to_all | solution.py:36
  68.5 2.2 %all-gather = bf16[1152,256]{1,0:T(8,128)(2,1)S(1)} all-gather(bf16[576,256]{1,0:T(8,128)(2,1)S(1)} %collective-permute-done.2), channel_id=2, replica_groups=mesh['xh'=2,'xl'=2,'yh'=2,'yl'=2,'zh'=2,'zlh'=4,'zll'=2,'c'=2] {'c'}, dimensions={0}, use_global_device_ids=true | all-gather | bytes 884736 | tf_op jit(solution)/shard_map/all_gather | solution.py:354
  70.8 1.0 pad_maximum_fusion.1
  71.8 2.2 %all-gather.2 = bf16[1152,256]{1,0:T(8,128)(2,1)S(1)} all-gather(bf16[576,256]{1,0:T(8,128)(2,1)S(1)} %pad_maximum_fusion.1), channel_id=4, replica_groups=mesh['xh'=2,'xl'=2,'yh'=2,'yl'=2,'zh'=2,'zlh'=4,'zll'=2,'c'=2] {'c'}, dimensions={0}, use_global_device_ids=true | all-gather | bytes 884736 | tf_op jit(solution)/shard_map/all_gather | solution.py:356
  74.1 2.3 %all-gather.1 = bf16[1152,256]{1,0:T(8,128)(2,1)} all-gather(bf16[576,256]{1,0:T(8,128)(2,1)S(1)} %pad_maximum_fusion), channel_id=3, replica_groups=mesh['xh'=2,'xl'=2,'yh'=2,'yl'=2,'zh'=2,'zlh'=4,'zll'=2,'c'=2] {'c'}, dimensions={0}, use_global_device_ids=true | all-gather | bytes 884736 | tf_op jit(solution)/shard_map/all_gather | solution.py:355
  76.4 0.0 collective-permute-done.1.refs_2_
  76.4 4.3 %all-to-all-done.1 = bf16[32,80,128]{2,1,0:T(8,128)(2,1)S(1)} async-done(((bf16[32,80,128]{2,1,0:T(8,128)(2,1)}), bf16[32,80,128]{2,1,0:T(8,128)(2,1)S(1)}, u32[]{:S(2)}, u32[]{:S(2)}) %all-to-all-start.1) | async-done | bytes 655392 | tf_op jit(solution)/shard_map/all_to_all | solution.py:36
  80.7 1.1 copy-done
  81.8 1.1 copy-done.1
  82.8 3.7 %attend.1 = (bf16[64,128]{1,0:T(8,128)(2,1)S(1)}, bf16[64,128]{1,0:T(8,128)(2,1)}) custom-call(s32[5]{0:T(128)S(1)} %stack.23.place.refs_0_, bf16[416,128]{1,0:T(8,128)(2,1)S(1)} %get-tuple-element.20.refs_1_, bf16[416,128]{1,0:T(8,128)(2,1)} %collective-permute-done.1.refs_2_, bf16[16,384,128]{2,1,0:T(8,128)(2,1)S(1)} %all-to-all-done.refs_3_.received, ...), custom_call_target="tpu_custom_call" | custom-call | flops 1000000000 | bytes 5000000 | tf_op jit(solution)/shard_map/attend/pallas_call | solution.py:360
  86.5 12.3 %collective-permute-start.7 = (bf16[64,128]{1,0:T(8,128)(2,1)}, bf16[64,128]{1,0:T(8,128)(2,1)S(1)}, u32[]{:S(2)}, u32[]{:S(2)}) collective-permute-start(bf16[64,128]{1,0:T(8,128)(2,1)} %get-tuple-element.31), channel_id=1, source_target_pairs={{0,16},{16,0},{1,17},{17,1},{2,18},{18,2},{3,19},{19,3},{4,20},{20... | collective-permute-start | bytes 49160 | tf_op jit(solution)/shard_map/ppermute | solution.py:24
  98.9 2.2 %collective-permute-done.7 = bf16[64,128]{1,0:T(8,128)(2,1)S(1)} collective-permute-done((bf16[64,128]{1,0:T(8,128)(2,1)}, bf16[64,128]{1,0:T(8,128)(2,1)S(1)}, u32[]{:S(2)}, u32[]{:S(2)}) %collective-permute-start.7) | collective-permute-done | bytes 16416 | tf_op jit(solution)/shard_map/ppermute | solution.py:24
  101.1 9.6 %all_to_all.26.values = bf16[8,64,256]{2,1,0:T(8,128)(2,1)S(1)} all-to-all(bf16[8,64,256]{2,1,0:T(8,128)(2,1)S(1)} %broadcast_in_dim.2), channel_id=1, replica_groups=mesh['xh'=2,'xl'=2,'yh'=2,'yl'=2,'zh'=2,'zlh'=4,'zll'=2,'c'=2] {'xl','yh..., dimensions={0} | all-to-all | bytes 524288 | tf_op jit(solution)/shard_map/all_to_all | solution.py:36
  110.8 1.5 project.1
  112.3 1.9 %collective-permute-start.8 = (bf16[8,2,16,448]{3,2,1,0:T(8,128)(2,1)S(1)}, bf16[8,2,16,448]{3,2,1,0:T(8,128)(2,1)S(1)}, u32[]{:S(2)}, u32[]{:S(2)}) collective-permute-start(bf16[8,2,16,448]{3,2,1,0:T(8,128)(2,1)S(1)} %get-tuple-element.34), channel_id=1, source_target_pairs={{0,1},{1,0},{2,3},{3,2},{4,5},{5,4},{6,7},{7,6},{8,9},{9,8},{10,11... | collective-permute-start | bytes 688136 | tf_op jit(solution)/shard_map/ppermute | solution.py:24
  114.2 1.5 collective-permute-done.8
  115.7 0.1 add_convert_fusion
  115.8 10.2 %all_to_all.27 = bf16[8,2,16,448]{3,2,1,0:T(8,128)(2,1)S(1)} all-to-all(bf16[8,2,16,448]{3,2,1,0:T(8,128)(2,1)S(1)} %add_convert_fusion), channel_id=1, replica_groups=mesh['xh'=2,'xl'=2,'yh'=2,'yl'=2,'zh'=2,'zlh'=4,'zll'=2,'c'=2] {'xl','yh..., dimensions={0} | all-to-all | bytes 458752 | tf_op jit(solution)/shard_map/all_to_all | solution.py:36
  126.0 30.2 %all_to_all.28 = bf16[16,16,448]{2,1,0:T(8,128)(2,1)S(1)} all-to-all(bf16[16,16,448]{2,1,0:T(8,128)(2,1)S(1)} %bitcast.23), channel_id=1, replica_groups=mesh['xh'=2,'xl'=2,'yh'=2,'yl'=2,'zh'=2,'zlh'=4,'zll'=2,'c'=2] {'zh','zl..., dimensions={0} | all-to-all | bytes 458752 | tf_op jit(solution)/shard_map/all_to_all | solution.py:36
  156.2 0.7 reduce_sum.12
  (29 shorter events, 0.1 us)
Async XLA Ops:
  0.0 27.1 %copy-start.3 = (bf16[8,48,128]{2,1,0:T(8,128)(2,1)S(1)}, bf16[8,48,128]{2,1,0:T(8,128)(2,1)}, u32[]{:S(2)}) copy-start(bf16[8,48,128]{2,1,0:T(8,128)(2,1)} %w_uq.3) | copy-start | bytes 294916
  0.0 27.1 %copy-start.5 = (bf16[8,16,128]{2,1,0:T(8,128)(2,1)S(1)}, bf16[8,16,128]{2,1,0:T(8,128)(2,1)}, u32[]{:S(2)}) copy-start(bf16[8,16,128]{2,1,0:T(8,128)(2,1)} %w_uk.3) | copy-start | bytes 98308
  0.0 27.1 %copy-start.7 = (bf16[8,16,128]{2,1,0:T(8,128)(2,1)S(1)}, bf16[8,16,128]{2,1,0:T(8,128)(2,1)}, u32[]{:S(2)}) copy-start(bf16[8,16,128]{2,1,0:T(8,128)(2,1)} %w_uv.3) | copy-start | bytes 98308
  0.0 27.0 %copy-start.12 = (bf16[8,4,7168]{2,1,0:T(4,128)(2,1)S(1)}, bf16[8,4,7168]{2,1,0:T(4,128)(2,1)}, u32[]{:S(2)}) copy-start(bf16[8,4,7168]{2,1,0:T(4,128)(2,1)} %param.15) | copy-start | bytes 1376260
  1.1 25.9 %collective-permute-start.2 = (bf16[576,256]{1,0:T(8,128)(2,1)S(1)}, bf16[576,256]{1,0:T(8,128)(2,1)S(1)}, u32[]{:S(2)}, u32[]{:S(2)}) collective-permute-start(bf16[576,256]{1,0:T(8,128)(2,1)S(1)} %dynamic-slice_bitcast_fusion), channel_id=1, source_target_pairs={{0,32},{32,0},{1,33},{33,1},{2,34},{34,2},{3,35},{35,3},{4,36},{36... | collective-permute-start | bytes 884744 | tf_op jit(solution)/shard_map/ppermute | solution.py:24
  5.5 32.4 %collective-permute-start.3 = (bf16[576,128]{1,0:T(8,128)(2,1)S(1)}, bf16[576,128]{1,0:T(8,128)(2,1)S(1)}, u32[]{:S(2)}, u32[]{:S(2)}) collective-permute-start(bf16[576,128]{1,0:T(8,128)(2,1)S(1)} %dynamic-slice_bitcast_fusion.1), channel_id=1, source_target_pairs={{0,16},{16,0},{1,17},{17,1},{2,18},{18,2},{3,19},{19,3},{4,20},{20... | collective-permute-start | bytes 442376 | tf_op jit(solution)/shard_map/ppermute | solution.py:24
  20.4 0.9 copy-start.2
  21.3 0.8 copy-start.4
  22.1 0.8 copy-start.6
  22.8 0.8 copy-start.8
  23.6 0.8 copy-start.10
  25.0 22.1 %collective-permute-start = (bf16[544,128]{1,0:T(8,128)(2,1)S(1)}, bf16[544,128]{1,0:T(8,128)(2,1)S(1)}, u32[]{:S(2)}, u32[]{:S(2)}) collective-permute-start(bf16[544,128]{1,0:T(8,128)(2,1)S(1)} %pack.1), channel_id=1, source_target_pairs={{0,16},{16,0},{1,17},{17,1},{2,18},{18,2},{3,19},{19,3},{4,20},{20... | collective-permute-start | bytes 417800 | tf_op jit(solution)/shard_map/ppermute | solution.py:24
  29.1 6.9 %copy-start.15 = (s32[512]{0:T(512)S(1)}, s32[512]{0:T(512)}, u32[]{:S(2)}) copy-start(s32[512]{0:T(512)} %param.10) | copy-start | bytes 6148
  29.1 18.0 %copy-start.9 = (bf16[16,1536]{1,0:T(8,128)(2,1)S(1)}, bf16[16,1536]{1,0:T(8,128)(2,1)}, u32[]{:S(2)}) copy-start(bf16[16,1536]{1,0:T(8,128)(2,1)} %refs_2_.1) | copy-start | bytes 147460
  29.1 18.1 %copy-start.11 = (bf16[16,8,64]{2,1,0:T(8,128)(2,1)S(1)}, bf16[16,8,64]{2,1,0:T(8,128)(2,1)}, u32[]{:S(2)}) copy-start(bf16[16,8,64]{2,1,0:T(8,128)(2,1)} %refs_3_.1) | copy-start | bytes 49156
  29.1 32.9 %all-to-all-start = ((bf16[16,384,128]{2,1,0:T(8,128)(2,1)}), bf16[16,384,128]{2,1,0:T(8,128)(2,1)S(1)}, u32[]{:S(2)}, u32[]{:S(2)}) async-start(bf16[16,384,128]{2,1,0:T(8,128)(2,1)} %spread.1), calls=%async_computation | async-start | bytes 3145728 | tf_op jit(solution)/shard_map/all_to_all | solution.py:36
  37.9 10.8 %copy-start.13 = (bf16[576,128]{1,0:T(8,128)(2,1)}, bf16[576,128]{1,0:T(8,128)(2,1)S(1)}, u32[]{:S(2)}) copy-start(bf16[576,128]{1,0:T(8,128)(2,1)S(1)} %collective-permute-done.3) | copy-start | bytes 442372
  37.9 24.1 %collective-permute-start.4 = (bf16[576,128]{1,0:T(8,128)(2,1)S(1)}, bf16[576,128]{1,0:T(8,128)(2,1)S(1)}, u32[]{:S(2)}, u32[]{:S(2)}) collective-permute-start(bf16[576,128]{1,0:T(8,128)(2,1)S(1)} %collective-permute-done.3), channel_id=1, source_target_pairs={{0,32},{32,0},{1,33},{33,1},{2,34},{34,2},{3,35},{35,3},{4,36},{36... | collective-permute-start | bytes 442376 | tf_op jit(solution)/shard_map/ppermute | solution.py:24
  40.3 21.8 %collective-permute-start.5 = (bf16[576,128]{1,0:T(8,128)(2,1)S(1)}, bf16[576,128]{1,0:T(8,128)(2,1)}, u32[]{:S(2)}, u32[]{:S(2)}) collective-permute-start(bf16[576,128]{1,0:T(8,128)(2,1)S(1)} %collective-permute-done.3), channel_id=1, source_target_pairs={{0,2},{2,0},{1,3},{3,1},{4,6},{6,4},{5,7},{7,5},{8,10},{10,8},{9,1... | collective-permute-start | bytes 442376 | tf_op jit(solution)/shard_map/ppermute | solution.py:24
  42.8 19.2 %collective-permute-start.6 = (bf16[576,128]{1,0:T(8,128)(2,1)S(1)}, bf16[576,128]{1,0:T(8,128)(2,1)}, u32[]{:S(2)}, u32[]{:S(2)}) collective-permute-start(bf16[576,128]{1,0:T(8,128)(2,1)S(1)} %collective-permute-done.3), channel_id=1, source_target_pairs={{0,34},{2,32},{32,2},{34,0},{1,35},{3,33},{33,3},{35,1},{4,38},{6,... | collective-permute-start | bytes 442376 | tf_op jit(solution)/shard_map/ppermute | solution.py:346
  48.7 23.1 %copy-start.14 = (bf16[576,128]{1,0:T(8,128)(2,1)S(1)}, bf16[576,128]{1,0:T(8,128)(2,1)}, u32[]{:S(2)}) copy-start(bf16[576,128]{1,0:T(8,128)(2,1)} %copy-done.13) | copy-start | bytes 442372
  48.7 27.7 %collective-permute-start.1 = (bf16[416,128]{1,0:T(8,128)(2,1)S(1)}, bf16[416,128]{1,0:T(8,128)(2,1)}, u32[]{:S(2)}, u32[]{:S(2)}) collective-permute-start(bf16[416,128]{1,0:T(8,128)(2,1)S(1)} %get-tuple-element.20.refs_1_), channel_id=1, source_target_pairs={{0,32},{32,0},{1,33},{33,1},{2,34},{34,2},{3,35},{35,3},{4,36},{36... | collective-permute-start | bytes 319496 | tf_op jit(solution)/shard_map/ppermute | solution.py:24
  62.0 18.7 %all-to-all-start.1 = ((bf16[32,80,128]{2,1,0:T(8,128)(2,1)}), bf16[32,80,128]{2,1,0:T(8,128)(2,1)S(1)}, u32[]{:S(2)}, u32[]{:S(2)}) async-start(bf16[32,80,128]{2,1,0:T(8,128)(2,1)} %bitcast.7), calls=%async_computation.1 | async-start | bytes 1310720 | tf_op jit(solution)/shard_map/all_to_all | solution.py:36
  80.7 1.1 copy-start
  81.8 1.1 copy-start.1
  86.5 14.5 %collective-permute-start.7 = (bf16[64,128]{1,0:T(8,128)(2,1)}, bf16[64,128]{1,0:T(8,128)(2,1)S(1)}, u32[]{:S(2)}, u32[]{:S(2)}) collective-permute-start(bf16[64,128]{1,0:T(8,128)(2,1)} %get-tuple-element.31), channel_id=1, source_target_pairs={{0,16},{16,0},{1,17},{17,1},{2,18},{18,2},{3,19},{19,3},{4,20},{20... | collective-permute-start | bytes 49160 | tf_op jit(solution)/shard_map/ppermute | solution.py:24
  112.3 3.4 %collective-permute-start.8 = (bf16[8,2,16,448]{3,2,1,0:T(8,128)(2,1)S(1)}, bf16[8,2,16,448]{3,2,1,0:T(8,128)(2,1)S(1)}, u32[]{:S(2)}, u32[]{:S(2)}) collective-permute-start(bf16[8,2,16,448]{3,2,1,0:T(8,128)(2,1)S(1)} %get-tuple-element.34), channel_id=1, source_target_pairs={{0,1},{1,0},{2,3},{3,2},{4,5},{5,4},{6,7},{7,6},{8,9},{9,8},{10,11... | collective-permute-start | bytes 688136 | tf_op jit(solution)/shard_map/ppermute | solution.py:24

commit v12 on v11

--- a/solution.py
+++ b/solution.py
@@ -17,7 +17,8 @@
 BF16 = jnp.bfloat16
 F32 = jnp.float32
 VMEM_LIMIT = 12 * 1024 * 1024
-UNPACK_FLOPS = 145 * 10**8
+UNPACK_FLOPS = 139 * 10**8
+HOLD_FLOPS = 4 * 10**9
 
 
 def swap(block, axis):
@@ -124,6 +125,10 @@
     rope_out[theirs] = stay[1]
     packed[pl.ds(pl.multiple_of(to + zh * own_rows, 16), own_rows)] = go[0]
     packed[pl.ds(pl.multiple_of(to + (1 - zh) * own_rows, 16), own_rows)] = go[1]
+
+
+def hold_kernel(piece, out):
+    out[...] = piece[...]
 
 
 def attend_kernel(
@@ -292,20 +297,10 @@
     queries = (query_latent, query_rope)
     latent_chunks = query_latent.shape[1] // lanes
     n_sent = four * n_all + (latent_chunks + 2) * own_rows
-    packed = pl.pallas_call(
-        pack_kernel,
-        out_shape=jax.ShapeDtypeStruct((n_sent, lanes), BF16),
-        in_specs=[smem] + [vmem] * 5,
-        out_specs=vmem,
-        compiler_params=pltpu.CompilerParams(vmem_limit_bytes=VMEM_LIMIT),
-        cost_estimate=pl.CostEstimate(flops=10**6, bytes_accessed=10**6, transcendentals=0),
-        name="pack",
-    )(place, *weights, *queries)
     piece = lax.dynamic_slice_in_dim(cache, (core * 2 + zll) * quarter, quarter, 1)
     far_piece = swap(piece, "zh")
     near = swap(lax.dynamic_slice_in_dim(cache, core * (tokens // 2), tokens // 2, 1), "yl")
     near, w_out = lax.optimization_barrier((near, w_out))
-    received = swap(packed, "zh")
 
     vpart, width = w_out.shape[1:]
     columns = width // 8
@@ -320,7 +315,18 @@
         cost_estimate=pl.CostEstimate(flops=10**6, bytes_accessed=10**6, transcendentals=0),
         name="spread",
     )(place, *weights, w_out.reshape(w_rows, width))
+    queries_after, spread = lax.optimization_barrier((query_latent, spread))
     spread = exchange(spread, PLANE)
+    packed = pl.pallas_call(
+        pack_kernel,
+        out_shape=jax.ShapeDtypeStruct((n_sent, lanes), BF16),
+        in_specs=[smem] + [vmem] * 5,
+        out_specs=vmem,
+        compiler_params=pltpu.CompilerParams(vmem_limit_bytes=VMEM_LIMIT),
+        cost_estimate=pl.CostEstimate(flops=10**6, bytes_accessed=10**6, transcendentals=0),
+        name="pack",
+    )(place, *weights, queries_after, query_rope)
+    received = swap(packed, "zh")
 
     n_pack = (2 * latent_chunks + 2) * own_rows
     sent, packed, rope_kept = pl.pallas_call(
@@ -341,6 +347,15 @@
     rows = 4 * own_rows
     row_lengths = lengths.reshape(-1, rows)
 
+    far_piece = pl.pallas_call(
+        hold_kernel,
+        out_shape=jax.ShapeDtypeStruct(far_piece.shape, BF16),
+        in_specs=[vmem],
+        out_specs=vmem,
+        compiler_params=pltpu.CompilerParams(vmem_limit_bytes=VMEM_LIMIT),
+        cost_estimate=pl.CostEstimate(flops=HOLD_FLOPS, bytes_accessed=10**6, transcendentals=0),
+        name="hold",
+    )(far_piece)
     piece_y = swap(far_piece, "yl")
     piece_z = swap(far_piece, "zll")
     piece_yz = lax.ppermute(far_piece, ("yl", "zll"), [(0, 3), (1, 2), (2, 1), (3, 0)])

time: 158 us -> 153 us (0.968)
  the two profiles are of different devices: /device:TPU:32 before, /device:TPU:6 now
where the time goes in v12:
time: 153 us; the launch traced here: 151 us
  starting transfers between devices  63.2 us (41%)
  blocking collectives  53.3 us (35%)
  waiting for transfers between devices  15.2 us (10%)
  Pallas kernels  8.93 us (6%)
  local copies, waits for them, and re-layouts  8.42 us (6%)
  other arithmetic  1.73 us (1%)
    all_to_all x3, blocking collectives, exchange(): return lax.all_to_all(blocks, axes, 0, 0, tiled=True)  46.3 us
    ppermute x8, starting transfers between devices, swap(): return lax.ppermute(block, axis, [(0, 1), (1, 0)])  43.8 us
    all_to_all x2, starting transfers between devices, exchange(): return lax.all_to_all(blocks, axes, 0, 0, tiled=True)  15.5 us
    ppermute x8, waiting for transfers between devices, swap(): return lax.ppermute(block, axis, [(0, 1), (1, 0)])  15.2 us
    unnamed x24, local copies, waits for them, and re-layouts  4.37 us
    ppermute x1, starting transfers between devices, local(): lax.ppermute(far_piece, ('yl', 'zll'), [(0, 3), (1, 2), (2, 1), (3, 0)])  3.83 us
    pallas_call x1, Pallas kernels, local(): pl.pallas_call(lambda *refs: attend_kernel(*refs, sizes=(rows, heads, n_u...  3.33 us
  transfers between devices with their start and end apart: 11, of which 4 were waited for; matrix products, arithmetic and copies ran while one was open for 3% of the time, Pallas kernels for 3%

profile of v12, /device:TPU:6, one launch (start us, length us, event | category | flops | bytes accessed | tf_op | source)
XLA Modules:
  0.0 151.0 jit_solution(752491909369501549)
XLA Ops:
  0.0 1.0 dynamic-slice_bitcast_fusion
  1.0 3.5 %collective-permute-start = (bf16[576,256]{1,0:T(8,128)(2,1)S(1)}, bf16[576,256]{1,0:T(8,128)(2,1)S(1)}, u32[]{:S(2)}, u32[]{:S(2)}) collective-permute-start(bf16[576,256]{1,0:T(8,128)(2,1)S(1)} %dynamic-slice_bitcast_fusion), channel_id=1, source_target_pairs={{0,32},{32,0},{1,33},{33,1},{2,34},{34,2},{3,35},{35,3},{4,36},{36... | collective-permute-start | bytes 884744 | tf_op jit(solution)/shard_map/ppermute | solution.py:25
  4.5 0.9 dynamic-slice_bitcast_fusion.1
  5.5 15.7 %collective-permute-start.3 = (bf16[576,128]{1,0:T(8,128)(2,1)S(1)}, bf16[576,128]{1,0:T(8,128)(2,1)S(1)}, u32[]{:S(2)}, u32[]{:S(2)}) collective-permute-start(bf16[576,128]{1,0:T(8,128)(2,1)S(1)} %dynamic-slice_bitcast_fusion.1), channel_id=1, source_target_pairs={{0,16},{16,0},{1,17},{17,1},{2,18},{18,2},{3,19},{19,3},{4,20},{20... | collective-permute-start | bytes 442376 | tf_op jit(solution)/shard_map/ppermute | solution.py:25
  21.2 0.8 reshape.51.refs_6_
  22.0 0.1 stack.23.place.refs_0_
  22.1 0.0 collective-permute-done
  22.1 1.2 reshape.50.w_out
  23.3 0.0 copy-done.4
  23.3 0.0 copy-done.3
  23.3 1.9 %spread.1 = bf16[16,384,128]{2,1,0:T(8,128)(2,1)} custom-call(s32[5]{0:T(128)S(1)} %stack.23.place.refs_0_, bf16[8,48,128]{2,1,0:T(8,128)(2,1)S(1)} %copy-done.2, bf16[8,16,128]{2,1,0:T(8,128)(2,1)S(1)} %copy-done.3, bf16[8,16,128]{2,1,0:T(8,128)(2,1)S(1)} %copy-done.4, bf16[32,7168]{1,0:T(8,128)(2,1)S(1)} %reshape.50.w_out), custom_call_target="tpu_custom_call" | custom-call | flops 1000000 | bytes 1000000 | tf_op jit(solution)/shard_map/spread/pallas_call | solution.py:309
  25.3 7.3 %all-to-all-start = ((bf16[16,384,128]{2,1,0:T(8,128)(2,1)}), bf16[16,384,128]{2,1,0:T(8,128)(2,1)S(1)}, u32[]{:S(2)}, u32[]{:S(2)}) async-start(bf16[16,384,128]{2,1,0:T(8,128)(2,1)} %spread.1), calls=%async_computation | async-start | bytes 3145728 | tf_op jit(solution)/shard_map/all_to_all | solution.py:37
  32.6 0.6 pack.1
  33.2 5.6 %collective-permute-start.1 = (bf16[544,128]{1,0:T(8,128)(2,1)S(1)}, bf16[544,128]{1,0:T(8,128)(2,1)S(1)}, u32[]{:S(2)}, u32[]{:S(2)}) collective-permute-start(bf16[544,128]{1,0:T(8,128)(2,1)S(1)} %pack.1), channel_id=1, source_target_pairs={{0,16},{16,0},{1,17},{17,1},{2,18},{18,2},{3,19},{19,3},{4,20},{20... | collective-permute-start | bytes 417800 | tf_op jit(solution)/shard_map/ppermute | solution.py:25
  38.9 0.0 collective-permute-done.3.piece
  38.9 3.8 %collective-permute-start.6 = (bf16[576,128]{1,0:T(8,128)(2,1)S(1)}, bf16[576,128]{1,0:T(8,128)(2,1)S(1)}, u32[]{:S(2)}, u32[]{:S(2)}) collective-permute-start(bf16[576,128]{1,0:T(8,128)(2,1)S(1)} %hold.1), channel_id=1, source_target_pairs={{0,34},{2,32},{32,2},{34,0},{1,35},{3,33},{33,3},{35,1},{4,38},{6,... | collective-permute-start | bytes 442376 | tf_op jit(solution)/shard_map/ppermute | solution.py:361
  42.7 2.9 %collective-permute-start.5 = (bf16[576,128]{1,0:T(8,128)(2,1)S(1)}, bf16[576,128]{1,0:T(8,128)(2,1)S(1)}, u32[]{:S(2)}, u32[]{:S(2)}) collective-permute-start(bf16[576,128]{1,0:T(8,128)(2,1)S(1)} %hold.1), channel_id=1, source_target_pairs={{0,2},{2,0},{1,3},{3,1},{4,6},{6,4},{5,7},{7,5},{8,10},{10,8},{9,1... | collective-permute-start | bytes 442376 | tf_op jit(solution)/shard_map/ppermute | solution.py:25
  45.6 2.5 %collective-permute-start.4 = (bf16[576,128]{1,0:T(8,128)(2,1)S(1)}, bf16[576,128]{1,0:T(8,128)(2,1)}, u32[]{:S(2)}, u32[]{:S(2)}) collective-permute-start(bf16[576,128]{1,0:T(8,128)(2,1)S(1)} %hold.1), channel_id=1, source_target_pairs={{0,32},{32,0},{1,33},{33,1},{2,34},{34,2},{3,35},{35,3},{4,36},{36... | collective-permute-start | bytes 442376 | tf_op jit(solution)/shard_map/ppermute | solution.py:25
  48.1 6.7 %collective-permute-done.1.refs_1_ = bf16[544,128]{1,0:T(8,128)(2,1)S(1)} collective-permute-done((bf16[544,128]{1,0:T(8,128)(2,1)S(1)}, bf16[544,128]{1,0:T(8,128)(2,1)S(1)}, u32[]{:S(2)}, u32[]{:S(2)}) %collective-permute-start.1) | collective-permute-done | bytes 139296 | tf_op jit(solution)/shard_map/ppermute | solution.py:25
  54.8 1.5 unpack.1
  56.3 0.0 collective-permute-done.6
  56.3 0.8 collective-permute-done.5
  57.1 0.7 copy-done.10
  57.7 0.0 collective-permute-done.4
  57.7 0.0 all-to-all-done.refs_3_.received
  57.8 8.3 %all-to-all-start.1 = ((bf16[32,80,128]{2,1,0:T(8,128)(2,1)}), bf16[32,80,128]{2,1,0:T(8,128)(2,1)S(1)}, u32[]{:S(2)}, u32[]{:S(2)}) async-start(bf16[32,80,128]{2,1,0:T(8,128)(2,1)} %bitcast.7), calls=%async_computation.1 | async-start | bytes 1310720 | tf_op jit(solution)/shard_map/all_to_all | solution.py:37
  66.0 2.4 %all-gather = bf16[1152,256]{1,0:T(8,128)(2,1)S(1)} all-gather(bf16[576,256]{1,0:T(8,128)(2,1)} %copy-done.9), channel_id=2, replica_groups=mesh['xh'=2,'xl'=2,'yh'=2,'yl'=2,'zh'=2,'zlh'=4,'zll'=2,'c'=2] {'c'}, dimensions={0}, use_global_device_ids=true | all-gather | bytes 884736 | tf_op jit(solution)/shard_map/all_gather | solution.py:369
  68.5 3.4 %collective-permute-start.2 = (bf16[416,128]{1,0:T(8,128)(2,1)S(1)}, bf16[416,128]{1,0:T(8,128)(2,1)S(1)}, u32[]{:S(2)}, u32[]{:S(2)}) collective-permute-start(bf16[416,128]{1,0:T(8,128)(2,1)S(1)} %get-tuple-element.24.refs_1_), channel_id=1, source_target_pairs={{0,32},{32,0},{1,33},{33,1},{2,34},{34,2},{3,35},{35,3},{4,36},{36... | collective-permute-start | bytes 319496 | tf_op jit(solution)/shard_map/ppermute | solution.py:25
  71.8 0.9 pad_maximum_fusion
  72.8 2.2 %all-gather.1 = bf16[1152,256]{1,0:T(8,128)(2,1)S(1)} all-gather(bf16[576,256]{1,0:T(8,128)(2,1)S(1)} %pad_maximum_fusion), channel_id=3, replica_groups=mesh['xh'=2,'xl'=2,'yh'=2,'yl'=2,'zh'=2,'zlh'=4,'zll'=2,'c'=2] {'c'}, dimensions={0}, use_global_device_ids=true | all-gather | bytes 884736 | tf_op jit(solution)/shard_map/all_gather | solution.py:370
  75.1 2.3 %all-gather.2 = bf16[1152,256]{1,0:T(8,128)(2,1)} all-gather(bf16[576,256]{1,0:T(8,128)(2,1)S(1)} %pad_maximum_fusion.1), channel_id=4, replica_groups=mesh['xh'=2,'xl'=2,'yh'=2,'yl'=2,'zh'=2,'zlh'=4,'zll'=2,'c'=2] {'c'}, dimensions={0}, use_global_device_ids=true | all-gather | bytes 884736 | tf_op jit(solution)/shard_map/all_gather | solution.py:371
  77.4 0.0 collective-permute-done.2.refs_2_
  77.4 0.7 copy-done.5
  78.1 0.0 all-to-all-done.1
  78.1 1.1 copy-done
  79.1 1.1 copy-done.1
  80.2 0.9 copy-done.6
  81.1 3.3 %attend.1 = (bf16[64,128]{1,0:T(8,128)(2,1)S(1)}, bf16[64,128]{1,0:T(8,128)(2,1)}) custom-call(s32[5]{0:T(128)S(1)} %stack.23.place.refs_0_, bf16[416,128]{1,0:T(8,128)(2,1)S(1)} %get-tuple-element.24.refs_1_, bf16[416,128]{1,0:T(8,128)(2,1)S(1)} %copy-done.6, bf16[16,384,128]{2,1,0:T(8,128)(2,1)S(1)} %all-to-all-done.refs_3_.received, ...), custom_call_target="tpu_custom_call" | custom-call | flops 1000000000 | bytes 5000000 | tf_op jit(solution)/shard_map/attend/pallas_call | solution.py:375
  84.4 8.3 %collective-permute-start.7 = (bf16[64,128]{1,0:T(8,128)(2,1)}, bf16[64,128]{1,0:T(8,128)(2,1)S(1)}, u32[]{:S(2)}, u32[]{:S(2)}) collective-permute-start(bf16[64,128]{1,0:T(8,128)(2,1)} %get-tuple-element.35), channel_id=1, source_target_pairs={{0,16},{16,0},{1,17},{17,1},{2,18},{18,2},{3,19},{19,3},{4,20},{20... | collective-permute-start | bytes 49160 | tf_op jit(solution)/shard_map/ppermute | solution.py:25
  92.7 6.2 %collective-permute-done.7 = bf16[64,128]{1,0:T(8,128)(2,1)S(1)} collective-permute-done((bf16[64,128]{1,0:T(8,128)(2,1)}, bf16[64,128]{1,0:T(8,128)(2,1)S(1)}, u32[]{:S(2)}, u32[]{:S(2)}) %collective-permute-start.7) | collective-permute-done | bytes 16416 | tf_op jit(solution)/shard_map/ppermute | solution.py:25
  99.0 11.0 %all_to_all.26.values = bf16[8,64,256]{2,1,0:T(8,128)(2,1)S(1)} all-to-all(bf16[8,64,256]{2,1,0:T(8,128)(2,1)S(1)} %broadcast_in_dim.2), channel_id=1, replica_groups=mesh['xh'=2,'xl'=2,'yh'=2,'yl'=2,'zh'=2,'zlh'=4,'zll'=2,'c'=2] {'xl','yh..., dimensions={0} | all-to-all | bytes 524288 | tf_op jit(solution)/shard_map/all_to_all | solution.py:37
  110.0 1.5 project.1
  111.5 1.9 %collective-permute-start.8 = (bf16[8,2,16,448]{3,2,1,0:T(8,128)(2,1)S(1)}, bf16[8,2,16,448]{3,2,1,0:T(8,128)(2,1)S(1)}, u32[]{:S(2)}, u32[]{:S(2)}) collective-permute-start(bf16[8,2,16,448]{3,2,1,0:T(8,128)(2,1)S(1)} %get-tuple-element.38), channel_id=1, source_target_pairs={{0,1},{1,0},{2,3},{3,2},{4,5},{5,4},{6,7},{7,6},{8,9},{9,8},{10,11... | collective-permute-start | bytes 688136 | tf_op jit(solution)/shard_map/ppermute | solution.py:25
  113.5 1.5 collective-permute-done.8
  115.0 0.1 add_convert_fusion
  115.1 10.2 %all_to_all.27 = bf16[8,2,16,448]{3,2,1,0:T(8,128)(2,1)S(1)} all-to-all(bf16[8,2,16,448]{3,2,1,0:T(8,128)(2,1)S(1)} %add_convert_fusion), channel_id=1, replica_groups=mesh['xh'=2,'xl'=2,'yh'=2,'yl'=2,'zh'=2,'zlh'=4,'zll'=2,'c'=2] {'xl','yh..., dimensions={0} | all-to-all | bytes 458752 | tf_op jit(solution)/shard_map/all_to_all | solution.py:37
  125.3 25.0 %all_to_all.28 = bf16[16,16,448]{2,1,0:T(8,128)(2,1)S(1)} all-to-all(bf16[16,16,448]{2,1,0:T(8,128)(2,1)S(1)} %bitcast.23), channel_id=1, replica_groups=mesh['xh'=2,'xl'=2,'yh'=2,'yl'=2,'zh'=2,'zlh'=4,'zll'=2,'c'=2] {'zh','zl..., dimensions={0} | all-to-all | bytes 458752 | tf_op jit(solution)/shard_map/all_to_all | solution.py:37
  150.3 0.7 reduce_sum.12
  (22 shorter events, 0.1 us)
Async XLA Ops:
  0.0 23.3 %copy-start.4 = (bf16[8,16,128]{2,1,0:T(8,128)(2,1)S(1)}, bf16[8,16,128]{2,1,0:T(8,128)(2,1)}, u32[]{:S(2)}) copy-start(bf16[8,16,128]{2,1,0:T(8,128)(2,1)} %w_uv.3) | copy-start | bytes 98308
  0.0 23.3 %copy-start.3 = (bf16[8,16,128]{2,1,0:T(8,128)(2,1)S(1)}, bf16[8,16,128]{2,1,0:T(8,128)(2,1)}, u32[]{:S(2)}) copy-start(bf16[8,16,128]{2,1,0:T(8,128)(2,1)} %w_uk.3) | copy-start | bytes 98308
  0.0 23.3 %copy-start.2 = (bf16[8,48,128]{2,1,0:T(8,128)(2,1)S(1)}, bf16[8,48,128]{2,1,0:T(8,128)(2,1)}, u32[]{:S(2)}) copy-start(bf16[8,48,128]{2,1,0:T(8,128)(2,1)} %w_uq.3) | copy-start | bytes 294916
  1.0 21.0 %collective-permute-start = (bf16[576,256]{1,0:T(8,128)(2,1)S(1)}, bf16[576,256]{1,0:T(8,128)(2,1)S(1)}, u32[]{:S(2)}, u32[]{:S(2)}) collective-permute-start(bf16[576,256]{1,0:T(8,128)(2,1)S(1)} %dynamic-slice_bitcast_fusion), channel_id=1, source_target_pairs={{0,32},{32,0},{1,33},{33,1},{2,34},{34,2},{3,35},{35,3},{4,36},{36... | collective-permute-start | bytes 884744 | tf_op jit(solution)/shard_map/ppermute | solution.py:25
  5.5 33.4 %collective-permute-start.3 = (bf16[576,128]{1,0:T(8,128)(2,1)S(1)}, bf16[576,128]{1,0:T(8,128)(2,1)S(1)}, u32[]{:S(2)}, u32[]{:S(2)}) collective-permute-start(bf16[576,128]{1,0:T(8,128)(2,1)S(1)} %dynamic-slice_bitcast_fusion.1), channel_id=1, source_target_pairs={{0,16},{16,0},{1,17},{17,1},{2,18},{18,2},{3,19},{19,3},{4,20},{20... | collective-permute-start | bytes 442376 | tf_op jit(solution)/shard_map/ppermute | solution.py:25
  22.1 10.5 %copy-start.9 = (bf16[576,256]{1,0:T(8,128)(2,1)}, bf16[576,256]{1,0:T(8,128)(2,1)S(1)}, u32[]{:S(2)}) copy-start(bf16[576,256]{1,0:T(8,128)(2,1)S(1)} %collective-permute-done) | copy-start | bytes 884740
  25.3 7.3 %copy-start.7 = (bf16[16,1536]{1,0:T(8,128)(2,1)S(1)}, bf16[16,1536]{1,0:T(8,128)(2,1)}, u32[]{:S(2)}) copy-start(bf16[16,1536]{1,0:T(8,128)(2,1)} %refs_2_.1) | copy-start | bytes 147460
  25.3 7.3 %copy-start.8 = (bf16[16,8,64]{2,1,0:T(8,128)(2,1)S(1)}, bf16[16,8,64]{2,1,0:T(8,128)(2,1)}, u32[]{:S(2)}) copy-start(bf16[16,8,64]{2,1,0:T(8,128)(2,1)} %refs_3_.1) | copy-start | bytes 49156
  25.3 32.5 %all-to-all-start = ((bf16[16,384,128]{2,1,0:T(8,128)(2,1)}), bf16[16,384,128]{2,1,0:T(8,128)(2,1)S(1)}, u32[]{:S(2)}, u32[]{:S(2)}) async-start(bf16[16,384,128]{2,1,0:T(8,128)(2,1)} %spread.1), calls=%async_computation | async-start | bytes 3145728 | tf_op jit(solution)/shard_map/all_to_all | solution.py:37
  33.2 21.6 %collective-permute-start.1 = (bf16[544,128]{1,0:T(8,128)(2,1)S(1)}, bf16[544,128]{1,0:T(8,128)(2,1)S(1)}, u32[]{:S(2)}, u32[]{:S(2)}) collective-permute-start(bf16[544,128]{1,0:T(8,128)(2,1)S(1)} %pack.1), channel_id=1, source_target_pairs={{0,16},{16,0},{1,17},{17,1},{2,18},{18,2},{3,19},{19,3},{4,20},{20... | collective-permute-start | bytes 417800 | tf_op jit(solution)/shard_map/ppermute | solution.py:25
  38.9 17.4 %collective-permute-start.6 = (bf16[576,128]{1,0:T(8,128)(2,1)S(1)}, bf16[576,128]{1,0:T(8,128)(2,1)S(1)}, u32[]{:S(2)}, u32[]{:S(2)}) collective-permute-start(bf16[576,128]{1,0:T(8,128)(2,1)S(1)} %hold.1), channel_id=1, source_target_pairs={{0,34},{2,32},{32,2},{34,0},{1,35},{3,33},{33,3},{35,1},{4,38},{6,... | collective-permute-start | bytes 442376 | tf_op jit(solution)/shard_map/ppermute | solution.py:361
  42.7 14.4 %collective-permute-start.5 = (bf16[576,128]{1,0:T(8,128)(2,1)S(1)}, bf16[576,128]{1,0:T(8,128)(2,1)S(1)}, u32[]{:S(2)}, u32[]{:S(2)}) collective-permute-start(bf16[576,128]{1,0:T(8,128)(2,1)S(1)} %hold.1), channel_id=1, source_target_pairs={{0,2},{2,0},{1,3},{3,1},{4,6},{6,4},{5,7},{7,5},{8,10},{10,8},{9,1... | collective-permute-start | bytes 442376 | tf_op jit(solution)/shard_map/ppermute | solution.py:25
  45.6 12.1 %collective-permute-start.4 = (bf16[576,128]{1,0:T(8,128)(2,1)S(1)}, bf16[576,128]{1,0:T(8,128)(2,1)}, u32[]{:S(2)}, u32[]{:S(2)}) collective-permute-start(bf16[576,128]{1,0:T(8,128)(2,1)S(1)} %hold.1), channel_id=1, source_target_pairs={{0,32},{32,0},{1,33},{33,1},{2,34},{34,2},{3,35},{35,3},{4,36},{36... | collective-permute-start | bytes 442376 | tf_op jit(solution)/shard_map/ppermute | solution.py:25
  57.1 0.7 copy-start.10
  57.7 15.0 %copy-start.11 = (bf16[576,128]{1,0:T(8,128)(2,1)S(1)}, bf16[576,128]{1,0:T(8,128)(2,1)}, u32[]{:S(2)}) copy-start(bf16[576,128]{1,0:T(8,128)(2,1)} %copy-done.10) | copy-start | bytes 442372
  57.8 20.3 %all-to-all-start.1 = ((bf16[32,80,128]{2,1,0:T(8,128)(2,1)}), bf16[32,80,128]{2,1,0:T(8,128)(2,1)S(1)}, u32[]{:S(2)}, u32[]{:S(2)}) async-start(bf16[32,80,128]{2,1,0:T(8,128)(2,1)} %bitcast.7), calls=%async_computation.1 | async-start | bytes 1310720 | tf_op jit(solution)/shard_map/all_to_all | solution.py:37
  68.5 8.9 %collective-permute-start.2 = (bf16[416,128]{1,0:T(8,128)(2,1)S(1)}, bf16[416,128]{1,0:T(8,128)(2,1)S(1)}, u32[]{:S(2)}, u32[]{:S(2)}) collective-permute-start(bf16[416,128]{1,0:T(8,128)(2,1)S(1)} %get-tuple-element.24.refs_1_), channel_id=1, source_target_pairs={{0,32},{32,0},{1,33},{33,1},{2,34},{34,2},{3,35},{35,3},{4,36},{36... | collective-permute-start | bytes 319496 | tf_op jit(solution)/shard_map/ppermute | solution.py:25
  77.4 0.7 copy-start.5
  78.1 1.1 copy-start
  79.1 1.1 copy-start.1
  80.2 0.9 copy-start.6
  84.4 14.5 %collective-permute-start.7 = (bf16[64,128]{1,0:T(8,128)(2,1)}, bf16[64,128]{1,0:T(8,128)(2,1)S(1)}, u32[]{:S(2)}, u32[]{:S(2)}) collective-permute-start(bf16[64,128]{1,0:T(8,128)(2,1)} %get-tuple-element.35), channel_id=1, source_target_pairs={{0,16},{16,0},{1,17},{17,1},{2,18},{18,2},{3,19},{19,3},{4,20},{20... | collective-permute-start | bytes 49160 | tf_op jit(solution)/shard_map/ppermute | solution.py:25
  111.5 3.4 %collective-permute-start.8 = (bf16[8,2,16,448]{3,2,1,0:T(8,128)(2,1)S(1)}, bf16[8,2,16,448]{3,2,1,0:T(8,128)(2,1)S(1)}, u32[]{:S(2)}, u32[]{:S(2)}) collective-permute-start(bf16[8,2,16,448]{3,2,1,0:T(8,128)(2,1)S(1)} %get-tuple-element.38), channel_id=1, source_target_pairs={{0,1},{1,0},{2,3},{3,2},{4,5},{5,4},{6,7},{7,6},{8,9},{9,8},{10,11... | collective-permute-start | bytes 688136 | tf_op jit(solution)/shard_map/ppermute | solution.py:25

commit v13 on v12

--- a/solution.py
+++ b/solution.py
@@ -359,8 +359,9 @@
     piece_y = swap(far_piece, "yl")
     piece_z = swap(far_piece, "zll")
     piece_yz = lax.ppermute(far_piece, ("yl", "zll"), [(0, 3), (1, 2), (2, 1), (3, 0)])
-    sent, spread, piece_y, piece_z, piece_yz, row_lengths = lax.optimization_barrier(
-        (sent, spread, piece_y, piece_z, piece_yz, row_lengths)
+    packed_y = swap(packed, "yl")
+    sent, spread, piece_y, piece_z, piece_yz, row_lengths, packed_y = lax.optimization_barrier(
+        (sent, spread, piece_y, piece_z, piece_yz, row_lengths, packed_y)
     )
 
     weights_far = exchange(sent.reshape(plane * heads, n_all, lanes), PLANE)
@@ -369,8 +370,6 @@
     near = lax.all_gather(near, "c", axis=0)
     far = lax.all_gather(jnp.concatenate([far_piece, piece_y], axis=1), "c", axis=0)
     far_z = lax.all_gather(jnp.concatenate([piece_z, piece_yz], axis=1), "c", axis=0)
-
-    packed_y = swap(packed, "yl")
 
     keep, give = pl.pallas_call(
         lambda *refs: attend_kernel(

time: 153 us -> 154 us (level)
  waiting for transfers between devices: 15.2 us -> 20.7 us
  local copies, waits for them, and re-layouts: 8.42 us -> 6.44 us
    ppermute x8, waiting for transfers between devices: 15.2 us -> 18.9 us  [swap(): return lax.ppermute(block, axis, [(0, 1), (1, 0)])]
    all_to_all x2, waiting for transfers between devices: 0.01 us -> 1.81 us  [exchange(): return lax.all_to_all(blocks, axes, 0, 0, tiled=True)]
    all_to_all x3, blocking collectives: 46.3 us -> 44.6 us  [exchange(): return lax.all_to_all(blocks, axes, 0, 0, tiled=True)]
    unnamed x24 -> x30, local copies, waits for them, and re-layouts: 4.37 us -> 3.07 us
  transfers between devices with their start and end apart: 11 -> 11, of which waited for: 4 -> 5; matrix products, arithmetic and copies ran while one was open for 3% -> 2% of each run, Pallas kernels for 3% -> 3%
where the time goes in v13:
time: 154 us; the launch traced here: 152 us
  starting transfers between devices  61.7 us (40%)
  blocking collectives  51.8 us (34%)
  waiting for transfers between devices  20.7 us (13%)
  Pallas kernels  8.92 us (6%)
  local copies, waits for them, and re-layouts  6.44 us (4%)
  other arithmetic  1.73 us (1%)
    all_to_all x3, blocking collectives, exchange(): return lax.all_to_all(blocks, axes, 0, 0, tiled=True)  44.6 us
    ppermute x8, starting transfers between devices, swap(): return lax.ppermute(block, axis, [(0, 1), (1, 0)])  43.4 us
    ppermute x8, waiting for transfers between devices, swap(): return lax.ppermute(block, axis, [(0, 1), (1, 0)])  18.9 us
    all_to_all x2, starting transfers between devices, exchange(): return lax.all_to_all(blocks, axes, 0, 0, tiled=True)  14.5 us
    ppermute x1, starting transfers between devices, local(): lax.ppermute(far_piece, ('yl', 'zll'), [(0, 3), (1, 2), (2, 1), (3, 0)])  3.83 us
    pallas_call x1, Pallas kernels, local(): pl.pallas_call(lambda *refs: attend_kernel(*refs, sizes=(rows, heads, n_u...  3.33 us
  transfers between devices with their start and end apart: 11, of which 5 were waited for; matrix products, arithmetic and copies ran while one was open for 2% of the time, Pallas kernels for 3%

profile of v13, /device:TPU:6, one launch (start us, length us, event | category | flops | bytes accessed | tf_op | source)
XLA Modules:
  0.0 151.6 jit_solution(4639364754279695253)
XLA Ops:
  0.0 1.0 dynamic-slice_bitcast_fusion
  1.0 3.5 %collective-permute-start = (bf16[576,256]{1,0:T(8,128)(2,1)S(1)}, bf16[576,256]{1,0:T(8,128)(2,1)S(1)}, u32[]{:S(2)}, u32[]{:S(2)}) collective-permute-start(bf16[576,256]{1,0:T(8,128)(2,1)S(1)} %dynamic-slice_bitcast_fusion), channel_id=1, source_target_pairs={{0,32},{32,0},{1,33},{33,1},{2,34},{34,2},{3,35},{35,3},{4,36},{36... | collective-permute-start | bytes 884744 | tf_op jit(solution)/shard_map/ppermute | solution.py:25
  4.5 0.9 dynamic-slice_bitcast_fusion.1
  5.5 15.7 %collective-permute-start.2 = (bf16[576,128]{1,0:T(8,128)(2,1)S(1)}, bf16[576,128]{1,0:T(8,128)(2,1)S(1)}, u32[]{:S(2)}, u32[]{:S(2)}) collective-permute-start(bf16[576,128]{1,0:T(8,128)(2,1)S(1)} %dynamic-slice_bitcast_fusion.1), channel_id=1, source_target_pairs={{0,16},{16,0},{1,17},{17,1},{2,18},{18,2},{3,19},{19,3},{4,20},{20... | collective-permute-start | bytes 442376 | tf_op jit(solution)/shard_map/ppermute | solution.py:25
  21.2 0.1 stack.23.place.refs_0_
  21.3 0.0 collective-permute-done
  21.3 1.2 reshape.50.w_out
  22.5 0.0 copy-done.4
  22.5 0.0 copy-done.3
  22.6 0.0 copy-done.2
  22.6 1.9 %spread.1 = bf16[16,384,128]{2,1,0:T(8,128)(2,1)} custom-call(s32[5]{0:T(128)S(1)} %stack.23.place.refs_0_, bf16[8,48,128]{2,1,0:T(8,128)(2,1)S(1)} %copy-done.2, bf16[8,16,128]{2,1,0:T(8,128)(2,1)S(1)} %copy-done.3, bf16[8,16,128]{2,1,0:T(8,128)(2,1)S(1)} %copy-done.4, bf16[32,7168]{1,0:T(8,128)(2,1)S(1)} %reshape.50.w_out), custom_call_target="tpu_custom_call" | custom-call | flops 1000000 | bytes 1000000 | tf_op jit(solution)/shard_map/spread/pallas_call | solution.py:309
  24.5 7.3 %all-to-all-start = ((bf16[16,384,128]{2,1,0:T(8,128)(2,1)}), bf16[16,384,128]{2,1,0:T(8,128)(2,1)S(1)}, u32[]{:S(2)}, u32[]{:S(2)}) async-start(bf16[16,384,128]{2,1,0:T(8,128)(2,1)} %spread.1), calls=%async_computation | async-start | bytes 3145728 | tf_op jit(solution)/shard_map/all_to_all | solution.py:37
  31.8 0.6 pack.1
  32.5 6.4 %collective-permute-start.1 = (bf16[544,128]{1,0:T(8,128)(2,1)S(1)}, bf16[544,128]{1,0:T(8,128)(2,1)S(1)}, u32[]{:S(2)}, u32[]{:S(2)}) collective-permute-start(bf16[544,128]{1,0:T(8,128)(2,1)S(1)} %pack.1), channel_id=1, source_target_pairs={{0,16},{16,0},{1,17},{17,1},{2,18},{18,2},{3,19},{19,3},{4,20},{20... | collective-permute-start | bytes 417800 | tf_op jit(solution)/shard_map/ppermute | solution.py:25
  38.9 0.0 collective-permute-done.2.piece
  38.9 0.0 copy-start.14
  38.9 3.8 %collective-permute-start.5 = (bf16[576,128]{1,0:T(8,128)(2,1)S(1)}, bf16[576,128]{1,0:T(8,128)(2,1)S(1)}, u32[]{:S(2)}, u32[]{:S(2)}) collective-permute-start(bf16[576,128]{1,0:T(8,128)(2,1)S(1)} %hold.1), channel_id=1, source_target_pairs={{0,34},{2,32},{32,2},{34,0},{1,35},{3,33},{33,3},{35,1},{4,38},{6,... | collective-permute-start | bytes 442376 | tf_op jit(solution)/shard_map/ppermute | solution.py:361
  42.7 2.9 %collective-permute-start.4 = (bf16[576,128]{1,0:T(8,128)(2,1)S(1)}, bf16[576,128]{1,0:T(8,128)(2,1)S(1)}, u32[]{:S(2)}, u32[]{:S(2)}) collective-permute-start(bf16[576,128]{1,0:T(8,128)(2,1)S(1)} %hold.1), channel_id=1, source_target_pairs={{0,2},{2,0},{1,3},{3,1},{4,6},{6,4},{5,7},{7,5},{8,10},{10,8},{9,1... | collective-permute-start | bytes 442376 | tf_op jit(solution)/shard_map/ppermute | solution.py:25
  45.7 2.5 %collective-permute-start.3 = (bf16[576,128]{1,0:T(8,128)(2,1)S(1)}, bf16[576,128]{1,0:T(8,128)(2,1)}, u32[]{:S(2)}, u32[]{:S(2)}) collective-permute-start(bf16[576,128]{1,0:T(8,128)(2,1)S(1)} %hold.1), channel_id=1, source_target_pairs={{0,32},{32,0},{1,33},{33,1},{2,34},{34,2},{3,35},{35,3},{4,36},{36... | collective-permute-start | bytes 442376 | tf_op jit(solution)/shard_map/ppermute | solution.py:25
  48.1 6.5 %collective-permute-done.1.refs_1_ = bf16[544,128]{1,0:T(8,128)(2,1)S(1)} collective-permute-done((bf16[544,128]{1,0:T(8,128)(2,1)S(1)}, bf16[544,128]{1,0:T(8,128)(2,1)S(1)}, u32[]{:S(2)}, u32[]{:S(2)}) %collective-permute-start.1) | collective-permute-done | bytes 139296 | tf_op jit(solution)/shard_map/ppermute | solution.py:25
  54.7 1.5 unpack.1
  56.2 3.3 %collective-permute-start.6 = (bf16[416,128]{1,0:T(8,128)(2,1)S(1)}, bf16[416,128]{1,0:T(8,128)(2,1)S(1)}, u32[]{:S(2)}, u32[]{:S(2)}) collective-permute-start(bf16[416,128]{1,0:T(8,128)(2,1)S(1)} %get-tuple-element.25.refs_1_), channel_id=1, source_target_pairs={{0,32},{32,0},{1,33},{33,1},{2,34},{34,2},{3,35},{35,3},{4,36},{36... | collective-permute-start | bytes 319496 | tf_op jit(solution)/shard_map/ppermute | solution.py:25
  59.5 0.1 reshape.51.refs_6_
  59.6 0.0 collective-permute-done.5
  59.6 0.0 collective-permute-done.4
  59.6 0.0 collective-permute-done.3
  59.6 3.2 %collective-permute-done.6.refs_2_ = bf16[416,128]{1,0:T(8,128)(2,1)S(1)} collective-permute-done((bf16[416,128]{1,0:T(8,128)(2,1)S(1)}, bf16[416,128]{1,0:T(8,128)(2,1)S(1)}, u32[]{:S(2)}, u32[]{:S(2)}) %collective-permute-start.6) | collective-permute-done | bytes 106528 | tf_op jit(solution)/shard_map/ppermute | solution.py:25
  62.9 0.0 all-to-all-done.refs_3_.received
  62.9 7.2 %all-to-all-start.1 = ((bf16[32,80,128]{2,1,0:T(8,128)(2,1)}), bf16[32,80,128]{2,1,0:T(8,128)(2,1)S(1)}, u32[]{:S(2)}, u32[]{:S(2)}) async-start(bf16[32,80,128]{2,1,0:T(8,128)(2,1)} %bitcast.7), calls=%async_computation.1 | async-start | bytes 1310720 | tf_op jit(solution)/shard_map/all_to_all | solution.py:37
  70.1 2.6 %all-gather = bf16[1152,256]{1,0:T(8,128)(2,1)S(1)} all-gather(bf16[576,256]{1,0:T(8,128)(2,1)} %copy-done.9), channel_id=2, replica_groups=mesh['xh'=2,'xl'=2,'yh'=2,'yl'=2,'zh'=2,'zlh'=4,'zll'=2,'c'=2] {'c'}, dimensions={0}, use_global_device_ids=true | all-gather | bytes 884736 | tf_op jit(solution)/shard_map/all_gather | solution.py:370
  72.7 0.9 pad_maximum_fusion
  73.7 2.2 %all-gather.1 = bf16[1152,256]{1,0:T(8,128)(2,1)S(1)} all-gather(bf16[576,256]{1,0:T(8,128)(2,1)S(1)} %pad_maximum_fusion), channel_id=3, replica_groups=mesh['xh'=2,'xl'=2,'yh'=2,'yl'=2,'zh'=2,'zlh'=4,'zll'=2,'c'=2] {'c'}, dimensions={0}, use_global_device_ids=true | all-gather | bytes 884736 | tf_op jit(solution)/shard_map/all_gather | solution.py:371
  75.9 2.3 %all-gather.2 = bf16[1152,256]{1,0:T(8,128)(2,1)} all-gather(bf16[576,256]{1,0:T(8,128)(2,1)S(1)} %pad_maximum_fusion.1), channel_id=4, replica_groups=mesh['xh'=2,'xl'=2,'yh'=2,'yl'=2,'zh'=2,'zlh'=4,'zll'=2,'c'=2] {'c'}, dimensions={0}, use_global_device_ids=true | all-gather | bytes 884736 | tf_op jit(solution)/shard_map/all_gather | solution.py:372
  78.3 1.8 %all-to-all-done.1 = bf16[32,80,128]{2,1,0:T(8,128)(2,1)S(1)} async-done(((bf16[32,80,128]{2,1,0:T(8,128)(2,1)}), bf16[32,80,128]{2,1,0:T(8,128)(2,1)S(1)}, u32[]{:S(2)}, u32[]{:S(2)}) %all-to-all-start.1) | async-done | bytes 655392 | tf_op jit(solution)/shard_map/all_to_all | solution.py:37
  80.1 1.1 copy-done
  81.2 1.1 copy-done.1
  82.2 0.9 copy-done.6
  83.1 3.3 %attend.1 = (bf16[64,128]{1,0:T(8,128)(2,1)S(1)}, bf16[64,128]{1,0:T(8,128)(2,1)}) custom-call(s32[5]{0:T(128)S(1)} %stack.23.place.refs_0_, bf16[416,128]{1,0:T(8,128)(2,1)S(1)} %get-tuple-element.25.refs_1_, bf16[416,128]{1,0:T(8,128)(2,1)S(1)} %copy-done.6, bf16[16,384,128]{2,1,0:T(8,128)(2,1)S(1)} %all-to-all-done.refs_3_.received, ...), custom_call_target="tpu_custom_call" | custom-call | flops 1000000000 | bytes 5000000 | tf_op jit(solution)/shard_map/attend/pallas_call | solution.py:374
  86.5 7.2 %collective-permute-start.7 = (bf16[64,128]{1,0:T(8,128)(2,1)}, bf16[64,128]{1,0:T(8,128)(2,1)S(1)}, u32[]{:S(2)}, u32[]{:S(2)}) collective-permute-start(bf16[64,128]{1,0:T(8,128)(2,1)} %get-tuple-element.37), channel_id=1, source_target_pairs={{0,16},{16,0},{1,17},{17,1},{2,18},{18,2},{3,19},{19,3},{4,20},{20... | collective-permute-start | bytes 49160 | tf_op jit(solution)/shard_map/ppermute | solution.py:25
  93.6 7.6 %collective-permute-done.7 = bf16[64,128]{1,0:T(8,128)(2,1)S(1)} collective-permute-done((bf16[64,128]{1,0:T(8,128)(2,1)}, bf16[64,128]{1,0:T(8,128)(2,1)S(1)}, u32[]{:S(2)}, u32[]{:S(2)}) %collective-permute-start.7) | collective-permute-done | bytes 16416 | tf_op jit(solution)/shard_map/ppermute | solution.py:25
  101.3 9.3 %all_to_all.26.values = bf16[8,64,256]{2,1,0:T(8,128)(2,1)S(1)} all-to-all(bf16[8,64,256]{2,1,0:T(8,128)(2,1)S(1)} %broadcast_in_dim.2), channel_id=1, replica_groups=mesh['xh'=2,'xl'=2,'yh'=2,'yl'=2,'zh'=2,'zlh'=4,'zll'=2,'c'=2] {'xl','yh..., dimensions={0} | all-to-all | bytes 524288 | tf_op jit(solution)/shard_map/all_to_all | solution.py:37
  110.6 1.5 project.1
  112.1 1.9 %collective-permute-start.8 = (bf16[8,2,16,448]{3,2,1,0:T(8,128)(2,1)S(1)}, bf16[8,2,16,448]{3,2,1,0:T(8,128)(2,1)S(1)}, u32[]{:S(2)}, u32[]{:S(2)}) collective-permute-start(bf16[8,2,16,448]{3,2,1,0:T(8,128)(2,1)S(1)} %get-tuple-element.40), channel_id=1, source_target_pairs={{0,1},{1,0},{2,3},{3,2},{4,5},{5,4},{6,7},{7,6},{8,9},{9,8},{10,11... | collective-permute-start | bytes 688136 | tf_op jit(solution)/shard_map/ppermute | solution.py:25
  114.0 1.5 collective-permute-done.8
  115.5 0.1 add_convert_fusion
  115.6 10.2 %all_to_all.27 = bf16[8,2,16,448]{3,2,1,0:T(8,128)(2,1)S(1)} all-to-all(bf16[8,2,16,448]{3,2,1,0:T(8,128)(2,1)S(1)} %add_convert_fusion), channel_id=1, replica_groups=mesh['xh'=2,'xl'=2,'yh'=2,'yl'=2,'zh'=2,'zlh'=4,'zll'=2,'c'=2] {'xl','yh..., dimensions={0} | all-to-all | bytes 458752 | tf_op jit(solution)/shard_map/all_to_all | solution.py:37
  125.8 25.1 %all_to_all.28 = bf16[16,16,448]{2,1,0:T(8,128)(2,1)S(1)} all-to-all(bf16[16,16,448]{2,1,0:T(8,128)(2,1)S(1)} %bitcast.23), channel_id=1, replica_groups=mesh['xh'=2,'xl'=2,'yh'=2,'yl'=2,'zh'=2,'zlh'=4,'zll'=2,'c'=2] {'zh','zl..., dimensions={0} | all-to-all | bytes 458752 | tf_op jit(solution)/shard_map/all_to_all | solution.py:37
  150.9 0.7 reduce_sum.12
  (28 shorter events, 0.1 us)
Async XLA Ops:
  0.0 22.5 %copy-start.4 = (bf16[8,16,128]{2,1,0:T(8,128)(2,1)S(1)}, bf16[8,16,128]{2,1,0:T(8,128)(2,1)}, u32[]{:S(2)}) copy-start(bf16[8,16,128]{2,1,0:T(8,128)(2,1)} %w_uv.3) | copy-start | bytes 98308
  0.0 22.5 %copy-start.3 = (bf16[8,16,128]{2,1,0:T(8,128)(2,1)S(1)}, bf16[8,16,128]{2,1,0:T(8,128)(2,1)}, u32[]{:S(2)}) copy-start(bf16[8,16,128]{2,1,0:T(8,128)(2,1)} %w_uk.3) | copy-start | bytes 98308
  0.0 22.6 %copy-start.2 = (bf16[8,48,128]{2,1,0:T(8,128)(2,1)S(1)}, bf16[8,48,128]{2,1,0:T(8,128)(2,1)}, u32[]{:S(2)}) copy-start(bf16[8,48,128]{2,1,0:T(8,128)(2,1)} %w_uq.3) | copy-start | bytes 294916
  1.0 20.3 %collective-permute-start = (bf16[576,256]{1,0:T(8,128)(2,1)S(1)}, bf16[576,256]{1,0:T(8,128)(2,1)S(1)}, u32[]{:S(2)}, u32[]{:S(2)}) collective-permute-start(bf16[576,256]{1,0:T(8,128)(2,1)S(1)} %dynamic-slice_bitcast_fusion), channel_id=1, source_target_pairs={{0,32},{32,0},{1,33},{33,1},{2,34},{34,2},{3,35},{35,3},{4,36},{36... | collective-permute-start | bytes 884744 | tf_op jit(solution)/shard_map/ppermute | solution.py:25
  5.5 33.4 %collective-permute-start.2 = (bf16[576,128]{1,0:T(8,128)(2,1)S(1)}, bf16[576,128]{1,0:T(8,128)(2,1)S(1)}, u32[]{:S(2)}, u32[]{:S(2)}) collective-permute-start(bf16[576,128]{1,0:T(8,128)(2,1)S(1)} %dynamic-slice_bitcast_fusion.1), channel_id=1, source_target_pairs={{0,16},{16,0},{1,17},{17,1},{2,18},{18,2},{3,19},{19,3},{4,20},{20... | collective-permute-start | bytes 442376 | tf_op jit(solution)/shard_map/ppermute | solution.py:25
  21.3 10.5 %copy-start.9 = (bf16[576,256]{1,0:T(8,128)(2,1)}, bf16[576,256]{1,0:T(8,128)(2,1)S(1)}, u32[]{:S(2)}) copy-start(bf16[576,256]{1,0:T(8,128)(2,1)S(1)} %collective-permute-done) | copy-start | bytes 884740
  24.5 7.3 %copy-start.7 = (bf16[16,1536]{1,0:T(8,128)(2,1)S(1)}, bf16[16,1536]{1,0:T(8,128)(2,1)}, u32[]{:S(2)}) copy-start(bf16[16,1536]{1,0:T(8,128)(2,1)} %refs_2_.1) | copy-start | bytes 147460
  24.5 7.3 %copy-start.8 = (bf16[16,8,64]{2,1,0:T(8,128)(2,1)S(1)}, bf16[16,8,64]{2,1,0:T(8,128)(2,1)}, u32[]{:S(2)}) copy-start(bf16[16,8,64]{2,1,0:T(8,128)(2,1)} %refs_3_.1) | copy-start | bytes 49156
  24.5 38.4 %all-to-all-start = ((bf16[16,384,128]{2,1,0:T(8,128)(2,1)}), bf16[16,384,128]{2,1,0:T(8,128)(2,1)S(1)}, u32[]{:S(2)}, u32[]{:S(2)}) async-start(bf16[16,384,128]{2,1,0:T(8,128)(2,1)} %spread.1), calls=%async_computation | async-start | bytes 3145728 | tf_op jit(solution)/shard_map/all_to_all | solution.py:37
  32.5 22.2 %collective-permute-start.1 = (bf16[544,128]{1,0:T(8,128)(2,1)S(1)}, bf16[544,128]{1,0:T(8,128)(2,1)S(1)}, u32[]{:S(2)}, u32[]{:S(2)}) collective-permute-start(bf16[544,128]{1,0:T(8,128)(2,1)S(1)} %pack.1), channel_id=1, source_target_pairs={{0,16},{16,0},{1,17},{17,1},{2,18},{18,2},{3,19},{19,3},{4,20},{20... | collective-permute-start | bytes 417800 | tf_op jit(solution)/shard_map/ppermute | solution.py:25
  38.9 20.6 %copy-start.14 = (s32[512]{0:T(512)S(1)}, s32[512]{0:T(512)}, u32[]{:S(2)}) copy-start(s32[512]{0:T(512)} %param.10) | copy-start | bytes 6148
  38.9 20.7 %collective-permute-start.5 = (bf16[576,128]{1,0:T(8,128)(2,1)S(1)}, bf16[576,128]{1,0:T(8,128)(2,1)S(1)}, u32[]{:S(2)}, u32[]{:S(2)}) collective-permute-start(bf16[576,128]{1,0:T(8,128)(2,1)S(1)} %hold.1), channel_id=1, source_target_pairs={{0,34},{2,32},{32,2},{34,0},{1,35},{3,33},{33,3},{35,1},{4,38},{6,... | collective-permute-start | bytes 442376 | tf_op jit(solution)/shard_map/ppermute | solution.py:361
  42.7 16.9 %collective-permute-start.4 = (bf16[576,128]{1,0:T(8,128)(2,1)S(1)}, bf16[576,128]{1,0:T(8,128)(2,1)S(1)}, u32[]{:S(2)}, u32[]{:S(2)}) collective-permute-start(bf16[576,128]{1,0:T(8,128)(2,1)S(1)} %hold.1), channel_id=1, source_target_pairs={{0,2},{2,0},{1,3},{3,1},{4,6},{6,4},{5,7},{7,5},{8,10},{10,8},{9,1... | collective-permute-start | bytes 442376 | tf_op jit(solution)/shard_map/ppermute | solution.py:25
  45.7 14.0 %collective-permute-start.3 = (bf16[576,128]{1,0:T(8,128)(2,1)S(1)}, bf16[576,128]{1,0:T(8,128)(2,1)}, u32[]{:S(2)}, u32[]{:S(2)}) collective-permute-start(bf16[576,128]{1,0:T(8,128)(2,1)S(1)} %hold.1), channel_id=1, source_target_pairs={{0,32},{32,0},{1,33},{33,1},{2,34},{34,2},{3,35},{35,3},{4,36},{36... | collective-permute-start | bytes 442376 | tf_op jit(solution)/shard_map/ppermute | solution.py:25
  56.2 6.7 %collective-permute-start.6 = (bf16[416,128]{1,0:T(8,128)(2,1)S(1)}, bf16[416,128]{1,0:T(8,128)(2,1)S(1)}, u32[]{:S(2)}, u32[]{:S(2)}) collective-permute-start(bf16[416,128]{1,0:T(8,128)(2,1)S(1)} %get-tuple-element.25.refs_1_), channel_id=1, source_target_pairs={{0,32},{32,0},{1,33},{33,1},{2,34},{34,2},{3,35},{35,3},{4,36},{36... | collective-permute-start | bytes 319496 | tf_op jit(solution)/shard_map/ppermute | solution.py:25
  59.6 3.3 %copy-start.10 = (bf16[576,128]{1,0:T(8,128)(2,1)}, bf16[576,128]{1,0:T(8,128)(2,1)S(1)}, u32[]{:S(2)}) copy-start(bf16[576,128]{1,0:T(8,128)(2,1)S(1)} %collective-permute-done.5) | copy-start | bytes 442372
  59.6 3.3 %copy-start.12 = (bf16[576,128]{1,0:T(8,128)(2,1)}, bf16[576,128]{1,0:T(8,128)(2,1)S(1)}, u32[]{:S(2)}) copy-start(bf16[576,128]{1,0:T(8,128)(2,1)S(1)} %collective-permute-done.4) | copy-start | bytes 442372
  62.9 10.8 %copy-start.5 = (bf16[416,128]{1,0:T(8,128)(2,1)}, bf16[416,128]{1,0:T(8,128)(2,1)S(1)}, u32[]{:S(2)}) copy-start(bf16[416,128]{1,0:T(8,128)(2,1)S(1)} %collective-permute-done.6.refs_2_) | copy-start | bytes 319492
  62.9 17.2 %all-to-all-start.1 = ((bf16[32,80,128]{2,1,0:T(8,128)(2,1)}), bf16[32,80,128]{2,1,0:T(8,128)(2,1)S(1)}, u32[]{:S(2)}, u32[]{:S(2)}) async-start(bf16[32,80,128]{2,1,0:T(8,128)(2,1)} %bitcast.7), calls=%async_computation.1 | async-start | bytes 1310720 | tf_op jit(solution)/shard_map/all_to_all | solution.py:37
  70.1 3.5 %copy-start.11 = (bf16[576,128]{1,0:T(8,128)(2,1)S(1)}, bf16[576,128]{1,0:T(8,128)(2,1)}, u32[]{:S(2)}) copy-start(bf16[576,128]{1,0:T(8,128)(2,1)} %copy-done.10) | copy-start | bytes 442372
  70.1 3.6 %copy-start.13 = (bf16[576,128]{1,0:T(8,128)(2,1)S(1)}, bf16[576,128]{1,0:T(8,128)(2,1)}, u32[]{:S(2)}) copy-start(bf16[576,128]{1,0:T(8,128)(2,1)} %copy-done.12) | copy-start | bytes 442372
  80.1 1.1 copy-start
  81.2 1.1 copy-start.1
  82.2 0.9 copy-start.6
  86.5 14.8 %collective-permute-start.7 = (bf16[64,128]{1,0:T(8,128)(2,1)}, bf16[64,128]{1,0:T(8,128)(2,1)S(1)}, u32[]{:S(2)}, u32[]{:S(2)}) collective-permute-start(bf16[64,128]{1,0:T(8,128)(2,1)} %get-tuple-element.37), channel_id=1, source_target_pairs={{0,16},{16,0},{1,17},{17,1},{2,18},{18,2},{3,19},{19,3},{4,20},{20... | collective-permute-start | bytes 49160 | tf_op jit(solution)/shard_map/ppermute | solution.py:25
  112.1 3.4 %collective-permute-start.8 = (bf16[8,2,16,448]{3,2,1,0:T(8,128)(2,1)S(1)}, bf16[8,2,16,448]{3,2,1,0:T(8,128)(2,1)S(1)}, u32[]{:S(2)}, u32[]{:S(2)}) collective-permute-start(bf16[8,2,16,448]{3,2,1,0:T(8,128)(2,1)S(1)} %get-tuple-element.40), channel_id=1, source_target_pairs={{0,1},{1,0},{2,3},{3,2},{4,5},{5,4},{6,7},{7,6},{8,9},{9,8},{10,11... | collective-permute-start | bytes 688136 | tf_op jit(solution)/shard_map/ppermute | solution.py:25
